TPU v7x, 32 devices: a whole 2x2x4 slice. The times are simulated.
32 devices in a mesh: ctx: 8 (over z, core), exp: 4 (over y, x).
Axes of the slice: x: 2, y: 2, z: 4, core: 2. Of those that a mesh axis runs over, the one named last changes fastest.
Arguments:
- block_input: bfloat16 [4, 2048, 1280], P('exp', 'ctx'), may hold values from -6 to 6
- cotangent: bfloat16 [4, 2048, 1280], P('exp', 'ctx'), may hold values from -6 to 6
- routes: int32 [4, 2048, 7], P('exp', 'ctx'), may hold values from 0 to 15, all different within a row; in each aligned block of 256 rows (0 to 255, 256 to 511, ..., all dimensions but the last counted through in order) at most 168 rows name the same one
- attn_gain: bfloat16 [1280], P(('ctx', 'exp')), may hold values from 0.25 to 1.75
- query_key_value_weight: bfloat16 [1280, 3840], P(('ctx', 'exp')), may hold values from -0.15625 to 0.15625
- attention_output_weight: bfloat16 [1280, 1280], P(('ctx', 'exp')), may hold values from -2.5 to 2.5
- ffn_gain: bfloat16 [1280], P(('ctx', 'exp')), may hold values from 0.25 to 1.75
- routing_weight: bfloat16 [1280, 16], P(('ctx', 'exp')), may hold values from -0.078125 to 0.078125
- common_expert_gate_up_weight: bfloat16 [1280, 1792], P(('ctx', 'exp')), may hold values from -0.15625 to 0.15625
- common_expert_down_weight: bfloat16 [896, 1280], P(('ctx', 'exp')), may hold values from -0.25 to 0.25
- expert_gate_up: bfloat16 [16, 1280, 1792], P('exp', 'ctx'), may hold values from -0.15625 to 0.15625
- expert_down: bfloat16 [16, 896, 1280], P('exp', 'ctx'), may hold values from -0.75 to 0.75
Outputs:
- layer_out: bfloat16 [4, 2048, 1280], P('exp', 'ctx')
- input_grad: float32 [4, 2048, 1280], P('exp', 'ctx')
- attn_gain_grad: float32 [1280], P(('ctx', 'exp'))
- qkv_weight_grad: float32 [1280, 3840], P(('ctx', 'exp'))
- out_weight_grad: float32 [1280, 1280], P(('ctx', 'exp'))
- ffn_gain_grad: float32 [1280], P(('ctx', 'exp'))
- router_weight_grad: float32 [1280, 16], P(('ctx', 'exp'))
- shared_gate_up_grad: float32 [1280, 1792], P(('ctx', 'exp'))
- shared_down_grad: float32 [896, 1280], P(('ctx', 'exp'))
- expert_gate_up_grad: float32 [16, 1280, 1792], P('exp', 'ctx')
- expert_down_grad: float32 [16, 896, 1280], P('exp', 'ctx')
Inputs may be any that keep to these rules, and one draw needn't show every extreme that they name: `routes`: the 7 experts of a token differ. Among the 256 rows of one device no expert is named by more than 168 rows, and in every draw some expert is named by exactly 168 rows of some device.
All inputs are finite; a program needn't handle non-finite values.
Results may differ from a plain program's by a relative error of at most 0.019.
Values may be sent and summed in bfloat16 or wider, within the bound.
No kernel may reach another device: no remote copies, remote signals or barrier semaphores. Data moves between devices by JAX's collectives and lax.ppermute only.
A program may use at most 320 MiB of HBM per device.

v0:
```python
import jax
import jax.numpy as jnp
from jax import lax
from jax.sharding import PartitionSpec as P

HEADS = 10
HEAD_DIM = 128
FF = 896
TOP = 7


norm_eps = 1e-06
rope_base = 10000.0
masked_value = -1000000000.0


def dealt_positions(row_index, tok_dev, n_ctx):
    halfway = tok_dev // 2
    device = row_index // tok_dev
    within = row_index % tok_dev
    early_pos = device * halfway + within
    late_pos = (2 * n_ctx - 1 - device) * halfway + within - halfway
    return jnp.where(within < halfway, early_pos, late_pos)


def rope_tables(positions, head_dim):
    halfway = head_dim // 2
    frequency = rope_base ** (-(jnp.arange(halfway).astype(jnp.float32) * 2.0 / head_dim))
    angles = positions.astype(jnp.float32)[:, None] * frequency[None, :]
    angles = jnp.concatenate([angles, angles], axis=1)
    return (jnp.cos(angles), jnp.sin(angles))


def rotate(vector, cosines, sine_table):
    halfway = vector.shape[-1] // 2
    turned = jnp.concatenate([-vector[..., halfway:], vector[..., :halfway]], axis=-1)
    return vector * cosines + turned * sine_table


def unrotate(gradient, cosines, sine_table):
    halfway = gradient.shape[-1] // 2
    moved_part = gradient * sine_table
    turned = jnp.concatenate([moved_part[..., halfway:], -moved_part[..., :halfway]], axis=-1)
    return gradient * cosines + turned


def rms_scale(values):
    return lax.rsqrt(jnp.mean(values * values, axis=1, keepdims=True) + norm_eps)


def norm_back(grad_in, values, inv_rms, gain_vec):
    scaled = grad_in * gain_vec
    return inv_rms * scaled - values * inv_rms**3 * jnp.mean(scaled * values, axis=1, keepdims=True)


def heads_first(matrix):
    return jnp.moveaxis(matrix.reshape(matrix.shape[0], HEADS, HEAD_DIM), 1, 0)


def heads_last(stacked):
    return jnp.moveaxis(stacked, 0, 1).reshape(stacked.shape[1], HEADS * HEAD_DIM)


def head_pairs(stacked):
    return stacked.reshape((HEADS // 2, 2) + stacked.shape[1:])


def head_probs(queries, key_rows, allowed):
    scores = jnp.einsum(
        "htd,hld->htl", queries, key_rows, preferred_element_type=jnp.float32
    ) * HEAD_DIM ** (-0.5)
    scores = jnp.where(allowed[None], scores, masked_value)
    row_peak = jnp.max(scores, axis=2, keepdims=True)
    raised = jnp.exp(scores - row_peak)
    return raised / jnp.sum(raised, axis=2, keepdims=True)


def attend_forward(query_heads, key_heads, value_heads, allowed):

    def per_pair(element):
        queries, key_rows, value_rows = element
        probabilities = head_probs(queries, key_rows, allowed)
        return jnp.einsum(
            "htl,hld->htd",
            probabilities.astype(jnp.bfloat16),
            value_rows,
            preferred_element_type=jnp.float32,
        )

    result = lax.map(
        per_pair, (head_pairs(query_heads), head_pairs(key_heads), head_pairs(value_heads))
    )
    return result.reshape((HEADS,) + result.shape[2:])


def attend_backward(query_heads, key_heads, value_heads, grad_heads, allowed):
    head_scale = HEAD_DIM ** (-0.5)

    def per_pair(element):
        queries, key_rows, value_rows, grad_rows = element
        probabilities = head_probs(queries, key_rows, allowed)
        probs_low = probabilities.astype(jnp.bfloat16)
        grad_probs = jnp.einsum(
            "htd,hld->htl", grad_rows, value_rows, preferred_element_type=jnp.float32
        )
        delta_rows = jnp.sum(probabilities * grad_probs, axis=2, keepdims=True)
        grad_scores = (probabilities * (grad_probs - delta_rows)).astype(jnp.bfloat16)
        grad_query = (
            jnp.einsum("htl,hld->htd", grad_scores, key_rows, preferred_element_type=jnp.float32)
            * head_scale
        )
        grad_key = (
            jnp.einsum("htl,htd->hld", grad_scores, queries, preferred_element_type=jnp.float32)
            * head_scale
        )
        grad_value = jnp.einsum(
            "htl,htd->hld", probs_low, grad_rows, preferred_element_type=jnp.float32
        )
        return (grad_query, grad_key, grad_value)

    parts = lax.map(
        per_pair,
        (
            head_pairs(query_heads),
            head_pairs(key_heads),
            head_pairs(value_heads),
            head_pairs(grad_heads),
        ),
    )
    return tuple((member.reshape((HEADS,) + member.shape[2:]) for member in parts))


def fetch_dense(
    attn_gain,
    query_key_value_weight,
    attention_output_weight,
    ffn_gain,
    routing_weight,
    common_expert_gate_up_weight,
    common_expert_down_weight,
):
    return (
        lax.all_gather(attn_gain, ("ctx", "exp"), axis=0, tiled=True),
        lax.all_gather(query_key_value_weight, ("ctx", "exp"), axis=0, tiled=True),
        lax.all_gather(attention_output_weight, ("ctx", "exp"), axis=0, tiled=True),
        lax.all_gather(ffn_gain, ("ctx", "exp"), axis=0, tiled=True),
        lax.all_gather(routing_weight, ("ctx", "exp"), axis=0, tiled=True),
        lax.all_gather(common_expert_gate_up_weight, ("ctx", "exp"), axis=0, tiled=True),
        lax.all_gather(common_expert_down_weight, ("ctx", "exp"), axis=0, tiled=True),
    )


def body(
    block_input,
    cotangent,
    routes,
    attn_gain,
    query_key_value_weight,
    attention_output_weight,
    ffn_gain,
    routing_weight,
    common_expert_gate_up_weight,
    common_expert_down_weight,
    expert_gate_up,
    expert_down,
):
    n_ctx = lax.axis_size("ctx")
    n_exp = lax.axis_size("exp")
    ctx_rank = lax.axis_index("ctx")
    tok_dev = block_input.shape[1]
    model_width = block_input.shape[2]
    exp_dev = expert_gate_up.shape[0]
    experts = exp_dev * n_exp
    capacity = min(tok_dev, 3 * TOP * tok_dev // (2 * experts))
    local_pos = dealt_positions(
        ctx_rank * tok_dev + jnp.arange(tok_dev, dtype=jnp.int32), tok_dev, n_ctx
    )
    key_pos = dealt_positions(jnp.arange(tok_dev * n_ctx, dtype=jnp.int32), tok_dev, n_ctx)
    allowed = key_pos[None, :] <= local_pos[:, None]
    cosines, sine_table = rope_tables(local_pos, HEAD_DIM)
    cosines = cosines[:, None, :]
    sine_table = sine_table[:, None, :]
    tokens_in = block_input[0].astype(jnp.float32)
    grad_low = cotangent[0]
    out_grad = grad_low.astype(jnp.float32)
    routed = routes[0]
    route_table = (
        routed[:, :, None] == jnp.arange(experts, dtype=jnp.int32)[None, None, :]
    ).astype(jnp.float32)
    flat_expert = routed.reshape(-1)
    onehot_int = (flat_expert[:, None] == jnp.arange(experts, dtype=jnp.int32)[None, :]).astype(
        jnp.int32
    )
    earlier = jnp.cumsum(onehot_int, axis=0) - onehot_int
    slot_pos = jnp.sum(earlier * onehot_int, axis=1)
    destination = flat_expert * capacity + slot_pos

    def pack_rows(row_block):
        buffer = (
            jnp.zeros((experts * capacity, model_width), jnp.bfloat16)
            .at[destination]
            .set(row_block)
        )
        return buffer.reshape(n_exp, exp_dev, capacity, model_width)

    def unpack_rows(buffer):
        return buffer.reshape(experts * capacity, model_width)[destination].reshape(
            tok_dev, TOP, model_width
        )

    def front_part(dense_set):
        inv_one = rms_scale(tokens_in)
        first_normalized = (tokens_in * inv_one * dense_set[0].astype(jnp.float32)).astype(
            jnp.bfloat16
        )
        attention_projected = jnp.dot(
            first_normalized, dense_set[1], preferred_element_type=jnp.float32
        )
        head_shape = (tok_dev, HEADS, HEAD_DIM)
        queries = (
            rotate(attention_projected[:, :model_width].reshape(head_shape), cosines, sine_table)
            .astype(jnp.bfloat16)
            .reshape(tok_dev, model_width)
        )
        key_rows = (
            rotate(
                attention_projected[:, model_width : 2 * model_width].reshape(head_shape),
                cosines,
                sine_table,
            )
            .astype(jnp.bfloat16)
            .reshape(tok_dev, model_width)
        )
        value_rows = attention_projected[:, 2 * model_width :].astype(jnp.bfloat16)
        return (inv_one, first_normalized, queries, key_rows, value_rows)

    def middle_part(dense_set, mixed_low):
        residual = tokens_in + jnp.dot(mixed_low, dense_set[2], preferred_element_type=jnp.float32)
        inv_two = rms_scale(residual)
        second_normalized = (residual * inv_two * dense_set[3].astype(jnp.float32)).astype(
            jnp.bfloat16
        )
        common_expert_preactivation = jnp.dot(
            second_normalized, dense_set[5], preferred_element_type=jnp.float32
        )
        common_expert_hidden = (
            jax.nn.silu(common_expert_preactivation[:, :FF]) * common_expert_preactivation[:, FF:]
        ).astype(jnp.bfloat16)
        router_scores = jnp.dot(second_normalized, dense_set[4], preferred_element_type=jnp.float32)
        chosen = jnp.sum(route_table * router_scores[:, None, :], axis=2)
        gate_weights = jax.nn.softmax(chosen, axis=1)
        return (
            residual,
            inv_two,
            second_normalized,
            common_expert_preactivation,
            common_expert_hidden,
            gate_weights,
        )

    dense_set = fetch_dense(
        attn_gain,
        query_key_value_weight,
        attention_output_weight,
        ffn_gain,
        routing_weight,
        common_expert_gate_up_weight,
        common_expert_down_weight,
    )
    expert_full = (
        lax.all_gather(expert_gate_up, "ctx", axis=1, tiled=True),
        lax.all_gather(expert_down, "ctx", axis=1, tiled=True),
    )
    inv_one, first_normalized, queries, key_rows, value_rows = front_part(dense_set)
    all_keys, all_values = (
        lax.all_gather(key_rows, "ctx", axis=0, tiled=True),
        lax.all_gather(value_rows, "ctx", axis=0, tiled=True),
    )
    key_heads = heads_first(all_keys)
    value_heads = heads_first(all_values)
    mixed_low = heads_last(
        attend_forward(heads_first(queries), key_heads, value_heads, allowed)
    ).astype(jnp.bfloat16)
    (
        residual,
        inv_two,
        second_normalized,
        common_expert_preactivation,
        common_expert_hidden,
        gate_weights,
    ) = middle_part(dense_set, mixed_low)
    common_expert_output = jnp.dot(
        common_expert_hidden, dense_set[6], preferred_element_type=jnp.float32
    )
    attention_projected = jnp.einsum(
        "sjcd,jdf->sjcf",
        lax.all_to_all(
            pack_rows(jnp.repeat(second_normalized, TOP, axis=0)),
            "exp",
            split_axis=0,
            concat_axis=0,
            tiled=True,
        ),
        expert_full[0],
        preferred_element_type=jnp.float32,
    )
    hidden = (jax.nn.silu(attention_projected[..., :FF]) * attention_projected[..., FF:]).astype(
        jnp.bfloat16
    )
    output = jnp.einsum(
        "sjcf,jfd->sjcd", hidden, expert_full[1], preferred_element_type=jnp.float32
    ).astype(jnp.bfloat16)
    returned = lax.all_to_all(output, "exp", split_axis=0, concat_axis=0, tiled=True)
    expert_rows = unpack_rows(returned).astype(jnp.float32)
    routed_sum = jnp.sum(gate_weights[:, :, None] * expert_rows, axis=1)
    layer_out = (residual + common_expert_output + routed_sum).astype(jnp.bfloat16)
    dense_back = fetch_dense(
        attn_gain,
        query_key_value_weight,
        attention_output_weight,
        ffn_gain,
        routing_weight,
        common_expert_gate_up_weight,
        common_expert_down_weight,
    )
    expert_back = (
        lax.all_gather(expert_gate_up, "ctx", axis=1, tiled=True),
        lax.all_gather(expert_down, "ctx", axis=1, tiled=True),
    )
    inv_one, first_normalized, queries, key_rows, value_rows = front_part(dense_back)
    keys_back, values_back = (
        lax.all_gather(key_rows, "ctx", axis=0, tiled=True),
        lax.all_gather(value_rows, "ctx", axis=0, tiled=True),
    )
    key_heads = heads_first(keys_back)
    value_heads = heads_first(values_back)
    query_heads = heads_first(queries)
    mixed_low = heads_last(attend_forward(query_heads, key_heads, value_heads, allowed)).astype(
        jnp.bfloat16
    )
    (
        residual,
        inv_two,
        second_normalized,
        common_expert_preactivation,
        common_expert_hidden,
        gate_weights,
    ) = middle_part(dense_back, mixed_low)
    gated_grad = (
        (gate_weights[:, :, None] * out_grad[:, None, :])
        .astype(jnp.bfloat16)
        .reshape(tok_dev * TOP, model_width)
    )
    rows_in, grad_in = (
        lax.all_to_all(
            pack_rows(jnp.repeat(second_normalized, TOP, axis=0)),
            "exp",
            split_axis=0,
            concat_axis=0,
            tiled=True,
        ),
        lax.all_to_all(pack_rows(gated_grad), "exp", split_axis=0, concat_axis=0, tiled=True),
    )
    attention_projected = jnp.einsum(
        "sjcd,jdf->sjcf", rows_in, expert_back[0], preferred_element_type=jnp.float32
    )
    gate_part = attention_projected[..., :FF]
    up_part = attention_projected[..., FF:]
    sigmoid_gate = jax.nn.sigmoid(gate_part)
    activated = gate_part * sigmoid_gate
    hidden = (activated * up_part).astype(jnp.bfloat16)
    output = jnp.einsum(
        "sjcf,jfd->sjcd", hidden, expert_back[1], preferred_element_type=jnp.float32
    ).astype(jnp.bfloat16)
    grad_hidden = jnp.einsum(
        "sjcd,jfd->sjcf", grad_in, expert_back[1], preferred_element_type=jnp.float32
    )
    down_grad = jnp.einsum("sjcf,sjcd->jfd", hidden, grad_in, preferred_element_type=jnp.float32)
    grad_pre = jnp.concatenate(
        [
            grad_hidden * up_part * sigmoid_gate * (1.0 + gate_part * (1.0 - sigmoid_gate)),
            grad_hidden * activated,
        ],
        axis=-1,
    ).astype(jnp.bfloat16)
    gate_up_grad = jnp.einsum(
        "sjcd,sjcf->jdf", rows_in, grad_pre, preferred_element_type=jnp.float32
    )
    grad_rows_in = jnp.einsum(
        "sjcf,jdf->sjcd", grad_pre, expert_back[0], preferred_element_type=jnp.float32
    ).astype(jnp.bfloat16)
    back_rows, back_output = (
        lax.all_to_all(grad_rows_in, "exp", split_axis=0, concat_axis=0, tiled=True),
        lax.all_to_all(output, "exp", split_axis=0, concat_axis=0, tiled=True),
    )
    routed_grad = jnp.sum(unpack_rows(back_rows).astype(jnp.float32), axis=1)
    grad_gates = jnp.sum(
        out_grad[:, None, :] * unpack_rows(back_output).astype(jnp.float32), axis=2
    )
    grad_chosen = gate_weights * (
        grad_gates - jnp.sum(gate_weights * grad_gates, axis=1, keepdims=True)
    )
    grad_logits = jnp.sum(route_table * grad_chosen[:, :, None], axis=1).astype(jnp.bfloat16)
    router_grad = jnp.dot(second_normalized.T, grad_logits, preferred_element_type=jnp.float32)
    shared_hidden_grad = jnp.dot(grad_low, dense_back[6].T, preferred_element_type=jnp.float32)
    shared_down_grad = jnp.dot(common_expert_hidden.T, grad_low, preferred_element_type=jnp.float32)
    shared_gate = common_expert_preactivation[:, :FF]
    shared_up = common_expert_preactivation[:, FF:]
    shared_sigmoid = jax.nn.sigmoid(shared_gate)
    shared_pre_grad = jnp.concatenate(
        [
            shared_hidden_grad
            * shared_up
            * shared_sigmoid
            * (1.0 + shared_gate * (1.0 - shared_sigmoid)),
            shared_hidden_grad * shared_gate * shared_sigmoid,
        ],
        axis=1,
    ).astype(jnp.bfloat16)
    shared_gate_up_grad = jnp.dot(
        second_normalized.T, shared_pre_grad, preferred_element_type=jnp.float32
    )
    normed_two_grad = (
        jnp.dot(shared_pre_grad, dense_back[5].T, preferred_element_type=jnp.float32)
        + jnp.dot(grad_logits, dense_back[4].T, preferred_element_type=jnp.float32)
        + routed_grad
    )
    ffn_gain_grad = jnp.sum(normed_two_grad * residual * inv_two, axis=0)
    residual_grad = out_grad + norm_back(
        normed_two_grad, residual, inv_two, dense_back[3].astype(jnp.float32)
    )
    mixed_grad = residual_grad.astype(jnp.bfloat16)
    out_weight_grad = jnp.dot(mixed_low.T, mixed_grad, preferred_element_type=jnp.float32)
    mixed_back = jnp.dot(mixed_grad, dense_back[2].T, preferred_element_type=jnp.float32).astype(
        jnp.bfloat16
    )
    grad_query, grad_key, grad_value = attend_backward(
        query_heads, key_heads, value_heads, heads_first(mixed_back), allowed
    )
    key_part, value_part = (
        lax.psum_scatter(grad_key, "ctx", scatter_dimension=1, tiled=True),
        lax.psum_scatter(grad_value, "ctx", scatter_dimension=1, tiled=True),
    )
    query_back = unrotate(jnp.moveaxis(grad_query, 0, 1), cosines, sine_table).reshape(
        tok_dev, model_width
    )
    key_back = unrotate(jnp.moveaxis(key_part, 0, 1), cosines, sine_table).reshape(
        tok_dev, model_width
    )
    value_back = jnp.moveaxis(value_part, 0, 1).reshape(tok_dev, model_width)
    qkv_grad_low = jnp.concatenate([query_back, key_back, value_back], axis=1).astype(jnp.bfloat16)
    qkv_weight_grad = jnp.dot(first_normalized.T, qkv_grad_low, preferred_element_type=jnp.float32)
    normed_grad = jnp.dot(qkv_grad_low, dense_back[1].T, preferred_element_type=jnp.float32)
    attn_gain_grad = jnp.sum(normed_grad * tokens_in * inv_one, axis=0)
    input_grad = residual_grad + norm_back(
        normed_grad, tokens_in, inv_one, dense_back[0].astype(jnp.float32)
    )
    dense_grads = (
        lax.psum_scatter(attn_gain_grad, ("ctx", "exp"), scatter_dimension=0, tiled=True),
        lax.psum_scatter(qkv_weight_grad, ("ctx", "exp"), scatter_dimension=0, tiled=True),
        lax.psum_scatter(out_weight_grad, ("ctx", "exp"), scatter_dimension=0, tiled=True),
        lax.psum_scatter(ffn_gain_grad, ("ctx", "exp"), scatter_dimension=0, tiled=True),
        lax.psum_scatter(router_grad, ("ctx", "exp"), scatter_dimension=0, tiled=True),
        lax.psum_scatter(shared_gate_up_grad, ("ctx", "exp"), scatter_dimension=0, tiled=True),
        lax.psum_scatter(shared_down_grad, ("ctx", "exp"), scatter_dimension=0, tiled=True),
    )
    expert_grads = (
        lax.psum_scatter(
            gate_up_grad.astype(jnp.bfloat16), "ctx", scatter_dimension=1, tiled=True
        ).astype(jnp.float32),
        lax.psum_scatter(
            down_grad.astype(jnp.bfloat16), "ctx", scatter_dimension=1, tiled=True
        ).astype(jnp.float32),
    )
    return (
        layer_out[None],
        input_grad[None],
        dense_grads[0],
        dense_grads[1],
        dense_grads[2],
        dense_grads[3],
        dense_grads[4],
        dense_grads[5],
        dense_grads[6],
        expert_grads[0],
        expert_grads[1],
    )


def solution(mesh):
    in_specs = (
        P("exp", "ctx", None),
        P("exp", "ctx", None),
        P("exp", "ctx", None),
        P(("ctx", "exp")),
        P(("ctx", "exp"), None),
        P(("ctx", "exp"), None),
        P(("ctx", "exp")),
        P(("ctx", "exp"), None),
        P(("ctx", "exp"), None),
        P(("ctx", "exp"), None),
        P("exp", "ctx", None),
        P("exp", "ctx", None),
    )
    out_specs = (
        P("exp", "ctx", None),
        P("exp", "ctx", None),
        P(("ctx", "exp")),
        P(("ctx", "exp"), None),
        P(("ctx", "exp"), None),
        P(("ctx", "exp")),
        P(("ctx", "exp"), None),
        P(("ctx", "exp"), None),
        P(("ctx", "exp"), None),
        P("exp", "ctx", None),
        P("exp", "ctx", None),
    )
    return jax.shard_map(body, mesh=mesh, in_specs=in_specs, out_specs=out_specs, check_vma=False)
```

profile of v0, /device:TPU:0, one launch (start us, length us, event | category | flops | bytes accessed | tf_op | source)
XLA Modules:
  0.0 2162.8 jit_solution(10618153087231468623)
XLA Ops:
  9.7 42.5 %all-reduce.8 = (bf16[1280]{0:T(1024)(128)(2,1)S(1)}, bf16[1280]{0:T(1024)(128)(2,1)}) all-reduce(bf16[1280]{0:T(1024)(128)(2,1)S(1)} %dynamic-update-slice, bf16[1280]{0:T(1024)(128)(2,1)S(1)} %dynamic-update-slice.1), channel_id=1, replica_groups=mesh['ctx'=8,'exp'=4] {'ctx','exp'}, use_global_device_ids=true, to_apply=%add | all-reduce | flops 2560 | bytes 10240
  54.6 43.7 %all-gather.11.cloned.1.call-done = bf16[1280,3840]{1,0:T(8,128)(2,1)} async-done(((bf16[40,3840]{1,0:T(8,128)(2,1)}), bf16[1280,3840]{1,0:T(8,128)(2,1)}) %all-gather.11.cloned.1.call-update) | async-done | bytes 9830416 | tf_op jit(solution)/shard_map/all_gather | solution.py:144
  126.8 42.5 %all-gather.13.cloned.1.call-done = bf16[2048,1280]{1,0:T(8,128)(2,1)} async-done(((bf16[256,1280]{1,0:T(8,128)(2,1)}), bf16[2048,1280]{1,0:T(8,128)(2,1)}) %all-gather.13.cloned.1.call-update) | async-done | bytes 5242896 | tf_op jit(solution)/shard_map/all_gather | solution.py:276
  185.4 41.0 %all-gather.15.cloned.1.call-done = bf16[2048,1280]{1,0:T(8,128)(2,1)} async-done(((bf16[256,1280]{1,0:T(8,128)(2,1)}), bf16[2048,1280]{1,0:T(8,128)(2,1)}) %all-gather.15.cloned.1.call-update) | async-done | bytes 5242896 | tf_op jit(solution)/shard_map/all_gather | solution.py:277
  242.4 34.0 %while.30 = (s32[]{:T(128)}, bf16[5,2,256,128]{3,2,1,0:T(8,128)(2,1)S(1)}, bf16[5,2,256,128]{3,2,1,0:T(8,128)(2,1)S(1)}, bf16[5,2,2048,128]{3,2,1,0:T(8,128)(2,1...) while((s32[]{:T(128)}, ...), condition=%wide.region_4.5_spmd.clone, body=%wide.region_1.4_spmd.clone.sunk | while | flops 815272448 | bytes 5259349 | solution.py:90
  277.6 9.7 all-gather.17.cloned.1.call-done
  302.6 16.0 scatter_custom_fusion
  324.9 136.9 %all-gather.1 = bf16[32,40,16]{1,2,0:T(8,128)(2,1)S(1)} all-gather(bf16[1,40,16]{1,2,0:T(8,128)(2,1)S(1)} %bitcast.328), channel_id=1, replica_groups=mesh['ctx'=8,'exp'=4] {'ctx','exp'}, dimensions={0}, use_global_device_ids=true | all-gather | bytes 42240 | tf_op jit(solution)/shard_map/all_gather | solution.py:147
  467.7 10.4 mul.489
  479.0 23.0 %scatter_custom_fusion.1 = bf16[2688,1280]{1,0:T(8,128)(2,1)} fusion(s32[1792]{0:T(1024)S(1)} %copy-done.52, f32[1792,1280]{1,0:T(8,128)} %mul.489, f32[1792]{0:T(1024)S(1)} %div.108, bf16[]{:T(256)} %constant.157.clone.1), kind=kCustom, calls=%fused_computation.111 | custom fusion | flops 4587520 | bytes 16064514 | tf_op jit(solution)/shard_map/scatter | solution.py:202
  508.2 23.0 %fusion.121 = f32[4,4,168,1792]{3,2,0,1:T(8,128)} fusion(bf16[4,1280,1792]{2,1,0:T(8,128)(2,1)} %all-gather.21.cloned.1.call-done, bf16[4,4,168,1280]{3,2,1,0:T(8,128)(2,1)} %all-to-all-done), kind=kOutput, calls=%fused_computation.105 | convolution fusion | flops 12331253760 | bytes 44498944 | tf_op jit(solution)/shard_map/sjcd,jdf->sjcf/dot_general | solution.py:295
  540.4 40.3 %all-to-all-done.2 = bf16[4,4,168,1280]{3,2,1,0:T(8,128)(2,1)} async-done(((bf16[4,4,168,1280]{3,2,1,0:T(8,128)(2,1)}), bf16[4,4,168,1280]{3,2,1,0:T(8,128)(2,1)}, u32[]{:S(2)}, u32[]{:S(2)}) %all-to-all-start.2) | async-done | bytes 6881312 | tf_op jit(solution)/shard_map/all_to_all | solution.py:362
  580.7 22.0 %fusion.113 = (bf16[4,4,168,896]{3,2,0,1:T(8,128)(2,1)}, bf16[4,4,168,896]{3,2,0,1:T(8,128)(2,1)}, bf16[4,4,168,896]{3,2,0,1:T(8,128)(2,1)}) fusion(f32[4,4,168,1792]{3,2,0,1:T(8,128)} %fusion.121, bf16[4,896,1280]{2,1,0:T(8,128)(2,1)} %all-gather.23.cloned.1.call-done, bf16[4,4,168,1280]{3,2,1,0:T(8,128)(2,1)} %all-to-all-done.2), kind=kOutput, calls=%fused_computation.94 | convolution fusion | flops 6201753600 | bytes 49774592 | tf_op jit(solution)/shard_map/sjcd,jfd->sjcf/dot_general | solution.py:375
  602.8 11.8 convert_bitcast_fusion.1
  623.2 21.3 convert_bitcast_fusion
  650.8 57.3 %all-to-all-done.1 = bf16[4,4,168,1280]{3,2,1,0:T(8,128)(2,1)} async-done(((bf16[4,4,168,1280]{3,2,1,0:T(8,128)(2,1)}), bf16[4,4,168,1280]{3,2,1,0:T(8,128)(2,1)}, u32[]{:S(2)}, u32[]{:S(2)}) %all-to-all-start.1) | async-done | bytes 6881312 | tf_op jit(solution)/shard_map/all_to_all | solution.py:313
  731.9 14.1 gather_fusion
  763.1 22.9 %all-to-all-done.3 = bf16[4,4,168,1280]{3,2,1,0:T(8,128)(2,1)} async-done(((bf16[4,4,168,1280]{3,2,1,0:T(8,128)(2,1)}), bf16[4,4,168,1280]{3,2,1,0:T(8,128)(2,1)}, u32[]{:S(2)}, u32[]{:S(2)}) %all-to-all-start.3) | async-done | bytes 6881312 | tf_op jit(solution)/shard_map/all_to_all | solution.py:393
  786.0 14.1 gather_fusion.1
  821.9 126.8 %while.31 = (s32[]{:T(128)}, f32[5,2,256,128]{2,3,1,0:T(8,128)}, f32[5,2,2048,128]{2,3,1,0:T(8,128)}, f32[5,2,2048,128]{2,3,1,0:T(8,128)}, bf16[5,2,256,128]{3,2...) while((s32[]{:T(128)}, f32[5,2,256,128]{2,3,1,0:T(8,128)}, ...), condition=%wide.region_24.25_spmd.clone, body=%wide.region_20.24_spmd.clone.sunk | while | flops 1628508160 | bytes 64383628 | solution.py:121
  950.8 14.8 bitcast_convert_fusion.1
  965.7 21.3 bitcast_convert_fusion
  998.6 60.0 %reduce-scatter.13.cloned.1.call-done = f32[10,256,128]{1,2,0:T(8,128)} async-done(((f32[10,2048,128]{1,2,0:T(8,128)}), f32[10,256,128]{1,2,0:T(8,128)}) %reduce-scatter.13.cloned.1.call-update) | async-done | bytes 1310736 | tf_op jit(solution)/shard_map/reduce_scatter | solution.py:442
  1060.8 107.7 %reduce-scatter.11.cloned.1.call-done = f32[10,256,128]{1,2,0:T(8,128)} async-done(((f32[10,2048,128]{1,2,0:T(8,128)}), f32[10,256,128]{1,2,0:T(8,128)}) %reduce-scatter.11.cloned.1.call-update) | async-done | bytes 1310736 | tf_op jit(solution)/shard_map/reduce_scatter | solution.py:441
  1172.2 9.6 fusion.154
  1186.0 116.1 %fusion.4 = f32[32,1280]{1,0:T(8,128)S(1)} fusion(f32[896,1280]{1,0:T(8,128)} %fusion.156), kind=kCustom, calls=%all-reduce-scatter | all-reduce-scatter fusion | flops 1310721 | bytes 4751360
  1332.3 62.1 %reduce-scatter.23.cloned.1.call-done = bf16[4,112,1280]{2,1,0:T(8,128)(2,1)} async-done(((bf16[4,896,1280]{2,1,0:T(8,128)(2,1)}), bf16[4,112,1280]{2,1,0:T(8,128)(2,1)}) %reduce-scatter.23.cloned.1.call-update) | async-done | bytes 1146896 | tf_op jit(solution)/shard_map/reduce_scatter | solution.py:471
  1404.6 46.4 %all-reduce.7 = (f32[1280]{0:T(1024)S(1)}, f32[1280]{0:T(1024)S(1)}) all-reduce(f32[1280]{0:T(1024)S(1)} %get-tuple-element.222, f32[1280]{0:T(1024)S(1)} %copy-done.51), channel_id=4, replica_groups=mesh['ctx'=8,'exp'=4] {'ctx','exp'}, use_global_device_ids=true, to_apply=%region_29.30.clone | all-reduce | flops 2560 | bytes 20480
  1453.6 132.7 %reduce-scatter.21.cloned.1.call-done = bf16[4,160,1792]{2,1,0:T(8,128)(2,1)} async-done(((bf16[4,1280,1792]{2,1,0:T(8,128)(2,1)}), bf16[4,160,1792]{2,1,0:T(8,128)(2,1)}) %reduce-scatter.21.cloned.1.call-update) | async-done | bytes 2293776 | tf_op jit(solution)/shard_map/reduce_scatter | solution.py:468
  1590.5 197.0 %reduce-scatter.19.cloned.1.call-done = f32[40,1792]{1,0:T(8,128)} async-done(((f32[1280,1792]{1,0:T(8,128)}), f32[40,1792]{1,0:T(8,128)}) %reduce-scatter.19.cloned.1.call-update) | async-done | bytes 286736 | tf_op jit(solution)/shard_map/reduce_scatter | solution.py:464
  1787.5 151.2 %reduce-scatter.17.cloned.1.call-done = f32[40,1280]{1,0:T(8,128)} async-done(((f32[1280,1280]{1,0:T(8,128)}), f32[40,1280]{1,0:T(8,128)}) %reduce-scatter.17.cloned.1.call-update) | async-done | bytes 204816 | tf_op jit(solution)/shard_map/reduce_scatter | solution.py:461
  1938.7 217.1 %reduce-scatter.15.cloned.1.call-done = f32[40,3840]{1,0:T(8,128)} async-done(((f32[1280,3840]{1,0:T(8,128)}), f32[40,3840]{1,0:T(8,128)}) %reduce-scatter.15.cloned.1.call-update) | async-done | bytes 614416 | tf_op jit(solution)/shard_map/reduce_scatter | solution.py:460
  (360 shorter events, 418.7 us)
Async XLA Ops:
  7.2 91.1 %all-gather.11.cloned.1.call-start = ((), (), s32[]{:S(2)}) async-start(), calls=%async_computation.11 | async-start | bytes 10137600 | tf_op jit(solution)/shard_map/all_gather | solution.py:144
  7.9 161.4 %all-gather.13.cloned.1.call-start = ((), (), s32[]{:S(2)}) async-start(), calls=%async_computation.12 | async-start | bytes 5898240 | tf_op jit(solution)/shard_map/all_gather | solution.py:276
  53.3 72.8 %copy-start.28 = (f32[256,128]{0,1:T(8,128)}, f32[256,128]{0,1:T(8,128)S(1)}, u32[]{:S(2)}) copy-start(f32[256,128]{0,1:T(8,128)S(1)} %get-tuple-element.286) | copy-start | bytes 393220
  53.3 72.8 %copy-start.30 = (f32[256,128]{0,1:T(8,128)}, f32[256,128]{0,1:T(8,128)S(1)}, u32[]{:S(2)}) copy-start(f32[256,128]{0,1:T(8,128)S(1)} %get-tuple-element.287) | copy-start | bytes 393220
  114.6 111.8 %all-gather.15.cloned.1.call-start = ((), (), s32[]{:S(2)}) async-start(), calls=%async_computation.13 | async-start | bytes 5898240 | tf_op jit(solution)/shard_map/all_gather | solution.py:277
  116.9 170.4 %all-gather.17.cloned.1.call-start = ((), (), s32[]{:S(2)}) async-start(), calls=%async_computation.14 | async-start | bytes 3379200 | tf_op jit(solution)/shard_map/all_gather | solution.py:145
  117.5 390.7 %all-gather.21.cloned.1.call-start = ((), (), s32[]{:S(2)}) async-start(), calls=%async_computation.16 | async-start | bytes 20643840 | tf_op jit(solution)/shard_map/all_gather | solution.py:271
  118.0 422.4 %all-gather.23.cloned.1.call-start = ((), (), s32[]{:S(2)}) async-start(), calls=%async_computation.17 | async-start | bytes 10321920 | tf_op jit(solution)/shard_map/all_gather | solution.py:272
  119.2 171.8 %copy-start.43 = (f32[1280]{0:T(1024)}, f32[1280]{0:T(1024)S(1)}, u32[]{:S(2)}) copy-start(f32[1280]{0:T(1024)S(1)} %convert_element_type.168) | copy-start | bytes 15364
  291.7 431.1 %copy-start.4 = (bf16[256,1280]{1,0:T(8,128)(2,1)}, bf16[256,1280]{1,0:T(8,128)(2,1)S(1)}, u32[]{:S(2)}) copy-start(bf16[256,1280]{1,0:T(8,128)(2,1)S(1)} %multiply_convert_fusion.4) | copy-start | bytes 1966084
  318.6 143.4 %copy-start.13 = (bf16[1,256,1280]{2,1,0:T(8,128)(2,1)S(1)}, bf16[1,256,1280]{2,1,0:T(8,128)(2,1)}, u32[]{:S(2)}) copy-start(bf16[1,256,1280]{2,1,0:T(8,128)(2,1)} %param.17) | copy-start | bytes 1966084
  318.6 183.4 %all-to-all-start = ((bf16[4,4,168,1280]{3,2,1,0:T(8,128)(2,1)}), bf16[4,4,168,1280]{3,2,1,0:T(8,128)(2,1)}, u32[]{:S(2)}, u32[]{:S(2)}) async-start(bf16[4,4,168,1280]{3,2,1,0:T(8,128)(2,1)} %bitcast.302), calls=%async_computation | async-start | bytes 13762560 | tf_op jit(solution)/shard_map/all_to_all | solution.py:297
  324.1 389.4 %all-gather.25.cloned.1.call-start = ((), (), s32[]{:S(2)}) async-start(), calls=%async_computation.25 | async-start | bytes 2703360 | tf_op jit(solution)/shard_map/all_gather | solution.py:149
  502.0 78.8 %all-to-all-start.2 = ((bf16[4,4,168,1280]{3,2,1,0:T(8,128)(2,1)}), bf16[4,4,168,1280]{3,2,1,0:T(8,128)(2,1)}, u32[]{:S(2)}, u32[]{:S(2)}) async-start(bf16[4,4,168,1280]{3,2,1,0:T(8,128)(2,1)} %bitcast.303), calls=%async_computation.2 | async-start | bytes 13762560 | tf_op jit(solution)/shard_map/all_to_all | solution.py:362
  507.4 215.4 %all-gather.19.cloned.1.call-start = ((), (), s32[]{:S(2)}) async-start(), calls=%async_computation.15 | async-start | bytes 4730880 | tf_op jit(solution)/shard_map/all_gather | solution.py:148
  617.8 90.2 %all-to-all-start.1 = ((bf16[4,4,168,1280]{3,2,1,0:T(8,128)(2,1)}), bf16[4,4,168,1280]{3,2,1,0:T(8,128)(2,1)}, u32[]{:S(2)}, u32[]{:S(2)}) async-start(bf16[4,4,168,1280]{3,2,1,0:T(8,128)(2,1)} %copy.143), calls=%async_computation.1 | async-start | bytes 13762560 | tf_op jit(solution)/shard_map/all_to_all | solution.py:313
  708.1 77.9 %all-to-all-start.3 = ((bf16[4,4,168,1280]{3,2,1,0:T(8,128)(2,1)}), bf16[4,4,168,1280]{3,2,1,0:T(8,128)(2,1)}, u32[]{:S(2)}, u32[]{:S(2)}) async-start(bf16[4,4,168,1280]{3,2,1,0:T(8,128)(2,1)} %copy.148), calls=%async_computation.3 | async-start | bytes 13762560 | tf_op jit(solution)/shard_map/all_to_all | solution.py:393
  713.4 345.1 %reduce-scatter.13.cloned.1.call-start = ((), (), s32[]{:S(2)}) async-start(), calls=%async_computation.19 | async-start | bytes 11796480 | tf_op jit(solution)/shard_map/reduce_scatter | solution.py:442
  948.7 219.8 %reduce-scatter.11.cloned.1.call-start = ((), (), s32[]{:S(2)}) async-start(), calls=%async_computation.18 | async-start | bytes 11796480 | tf_op jit(solution)/shard_map/reduce_scatter | solution.py:441
  949.3 381.6 %all-reduce.11.cloned.1.call-start = ((), (), s32[]{:S(2)}) async-start(), calls=%async_computation.26 | async-start | bytes 163840
  950.7 443.7 %reduce-scatter.23.cloned.1.call-start = ((), (), s32[]{:S(2)}) async-start(), calls=%async_computation.24 | async-start | bytes 10321920 | tf_op jit(solution)/shard_map/reduce_scatter | solution.py:471
  965.6 620.7 %reduce-scatter.21.cloned.1.call-start = ((), (), s32[]{:S(2)}) async-start(), calls=%async_computation.23 | async-start | bytes 20643840 | tf_op jit(solution)/shard_map/reduce_scatter | solution.py:468
  987.0 800.5 %reduce-scatter.19.cloned.1.call-start = ((), (), s32[]{:S(2)}) async-start(), calls=%async_computation.22 | async-start | bytes 9461760 | tf_op jit(solution)/shard_map/reduce_scatter | solution.py:464
  993.0 945.7 %reduce-scatter.17.cloned.1.call-start = ((), (), s32[]{:S(2)}) async-start(), calls=%async_computation.21 | async-start | bytes 6758400 | tf_op jit(solution)/shard_map/reduce_scatter | solution.py:461
  998.3 170.3 %copy-start.19 = (f32[5,2,256,128]{2,3,1,0:T(8,128)S(1)}, f32[5,2,256,128]{2,3,1,0:T(8,128)}, u32[]{:S(2)}) copy-start(f32[5,2,256,128]{2,3,1,0:T(8,128)} %get-tuple-element.105) | copy-start | bytes 3932164
  998.3 170.3 %copy-start.31 = (f32[256,128]{0,1:T(8,128)S(1)}, f32[256,128]{0,1:T(8,128)}, u32[]{:S(2)}) copy-start(f32[256,128]{0,1:T(8,128)} %copy-done.30) | copy-start | bytes 393220
  998.3 1157.5 %reduce-scatter.15.cloned.1.call-start = ((), (), s32[]{:S(2)}) async-start(), calls=%async_computation.20 | async-start | bytes 20275200 | tf_op jit(solution)/shard_map/reduce_scatter | solution.py:460
  1186.0 141.1 %copy-start.3 = (f32[256,1280]{1,0:T(8,128)S(1)}, f32[256,1280]{1,0:T(8,128)}, u32[]{:S(2)}) copy-start(f32[256,1280]{1,0:T(8,128)} %copy-done.1) | copy-start | bytes 3932164
  1302.2 15.2 collective-permute-start
  1306.0 11.3 collective-permute-start.1
  1309.0 8.3 collective-permute-start.2
  1312.5 4.8 collective-permute-start.3
  (58 other events, 430.4 us)
Sparse Core Ops, SparseCore 0:
  10.9 87.3 all-gather.10
  114.7 54.5 all-gather.12
  171.6 54.7 all-gather.14
  229.1 58.1 all-gather.16
  288.7 163.4 all-gather.20
  453.7 86.7 all-gather.22
  543.3 82.0 all-gather.24
  628.3 94.3 all-gather.18
  948.9 109.6 reduce-scatter.12
  1060.7 107.7 reduce-scatter.10
  1174.1 119.0 all-reduce.10
  1295.4 98.9 reduce-scatter.22
  1396.8 189.4 reduce-scatter.20
  1589.1 198.3 reduce-scatter.18
  1790.2 148.4 reduce-scatter.16
  1945.6 210.1 reduce-scatter.14
where the time goes:
time: 2170 us; the launch traced here: 2160 us
  waiting for transfers between devices  1210 us (56%)
  blocking collectives  342 us (16%)
  matrix products  288 us (13%)
  local copies, waits for them, and re-layouts  203 us (9%)
  other arithmetic  71.9 us (3%)
  starting transfers between devices  36.6 us (2%)
    reduce_scatter x1, waiting for transfers between devices, body(): lax.psum_scatter(qkv_weight_grad, ('ctx', 'exp'), scatter_dimension=0, ti...  217 us
    unnamed x3, blocking collectives  205 us
    reduce_scatter x1, waiting for transfers between devices, body(): lax.psum_scatter(shared_gate_up_grad, ('ctx', 'exp'), scatter_dimension=0...  197 us
    reduce_scatter x1, waiting for transfers between devices, body(): lax.psum_scatter(out_weight_grad, ('ctx', 'exp'), scatter_dimension=0, ti...  151 us
    all_gather x1, blocking collectives, fetch_dense(): lax.all_gather(routing_weight, ('ctx', 'exp'), axis=0, tiled=True)  137 us
    reduce_scatter x1, waiting for transfers between devices, body(): lax.psum_scatter(gate_up_grad.astype(jnp.bfloat16), 'ctx', scatter_dimens...  133 us
    reduce_scatter x1, waiting for transfers between devices, body(): lax.psum_scatter(grad_key, 'ctx', scatter_dimension=1, tiled=True)  108 us
    reduce_scatter x1, waiting for transfers between devices, body(): lax.psum_scatter(down_grad.astype(jnp.bfloat16), 'ctx', scatter_dimension...  62.1 us
  transfers between devices with their start and end apart: 24, of which 17 were waited for; matrix products, arithmetic and copies ran while one was open for 23% of the time, Pallas kernels for 0%

commit v1 on v0

v1 whole, which is shorter than its diff:
```python
import functools

import jax
import jax.numpy as jnp
import numpy as np
from jax import lax
from jax.experimental import pallas as pl
from jax.experimental.pallas import tpu as pltpu
from jax.sharding import Mesh
from jax.sharding import PartitionSpec as P

HEADS = 10
HEAD_DIM = 128
FF = 896
TOP = 7

norm_eps = 1e-06
rope_base = 10000.0
masked_value = -1e30
LOG2E = 1.4426950408889634

BF = jnp.bfloat16
F32 = jnp.float32
VMEM_LIMIT = 56 * 1024 * 1024


def rope_tables(positions, head_dim):
    halfway = head_dim // 2
    frequency = rope_base ** (-(jnp.arange(halfway).astype(F32) * 2.0 / head_dim))
    angles = positions.astype(F32)[:, None] * frequency[None, :]
    angles = jnp.concatenate([angles, angles], axis=1)
    return (jnp.cos(angles), jnp.sin(angles))


def rotate(vector, cosines, sine_table):
    halfway = vector.shape[-1] // 2
    turned = jnp.concatenate([-vector[..., halfway:], vector[..., :halfway]], axis=-1)
    return vector * cosines + turned * sine_table


def unrotate(gradient, cosines, sine_table):
    halfway = gradient.shape[-1] // 2
    moved = gradient * sine_table
    turned = jnp.concatenate([moved[..., halfway:], -moved[..., :halfway]], axis=-1)
    return gradient * cosines + turned


def rms_scale(values):
    return lax.rsqrt(jnp.mean(values * values, axis=1, keepdims=True) + norm_eps)


def norm_back(grad_in, values, inv_rms, gain_vec):
    scaled = grad_in * gain_vec
    return inv_rms * scaled - values * inv_rms**3 * jnp.mean(scaled * values, axis=1, keepdims=True)


def dot(a, b, dims=((1,), (0,))):
    return lax.dot_general(a, b, (dims, ((), ())), preferred_element_type=F32)


NT = ((1,), (1,))
TN = ((0,), (0,))


def shift(value, axis):
    n = lax.axis_size(axis)
    return lax.ppermute(value, axis, [(i, (i + 1) % n) for i in range(n)])


def ring_gather(value, axis):
    parts = [value]
    for _ in range(1, lax.axis_size(axis)):
        parts.append(shift(parts[-1], axis))
    return parts


def ring_sum(blocks, axis):
    n = len(blocks)
    if n == 1:
        return blocks[0].astype(F32)
    moving = blocks[1].astype(BF)
    for k in range(2, n):
        moving = (shift(moving, axis).astype(F32) + blocks[k].astype(F32)).astype(BF)
    return shift(moving, axis).astype(F32) + blocks[0].astype(F32)


def to_order(parts, axis):
    n = len(parts)
    index = lax.axis_index(axis)
    if n == 1:
        return parts[0][None]
    if n == 2:
        first = jnp.where(index == 0, parts[0], parts[1])
        second = jnp.where(index == 0, parts[1], parts[0])
        return jnp.stack([first, second])
    back = parts[::-1]
    return lax.dynamic_slice_in_dim(jnp.stack(back + back), n - 1 - index, n, axis=0)


def ring_blocks(value, axis, dim):
    n = lax.axis_size(axis)
    index = lax.axis_index(axis)
    return [
        lax.dynamic_index_in_dim(value, lax.rem(index - k + n, n), dim, keepdims=False)
        for k in range(n)
    ]


def dense_gather(shard):
    rows, width = shard.shape
    along_q = to_order(ring_gather(shard, "q"), "q")
    nq = along_q.shape[0]
    half = nq // 2
    one = to_order(ring_gather(along_q[:half], "b"), "b")
    two = to_order(ring_gather(along_q[half:], "a"), "a")
    one = to_order(ring_gather(one, "a"), "a")
    two = to_order(ring_gather(two, "b"), "b")
    plane = jnp.concatenate(
        [jnp.moveaxis(one, 2, 0), jnp.moveaxis(jnp.swapaxes(two, 0, 1), 2, 0)], axis=0
    )
    whole = to_order(ring_gather(plane, "r"), "r")
    return jnp.moveaxis(whole, 0, 1).reshape(-1, width)


def dense_sum(whole, n_rows):
    width = whole.shape[1]
    nq, nr, na, nb = (lax.axis_size(axis) for axis in ("q", "r", "a", "b"))
    value = whole.reshape(nq, nr, na, nb, n_rows, width)
    value = ring_sum(ring_blocks(value, "r", 1), "r").astype(BF)
    half = nq // 2
    one, two = value[:half], value[half:]
    one = ring_sum(ring_blocks(one, "a", 1), "a").astype(BF)
    two = ring_sum(ring_blocks(two, "b", 2), "b").astype(BF)
    one = ring_sum(ring_blocks(one, "b", 1), "b")
    two = ring_sum(ring_blocks(two, "a", 1), "a")
    value = jnp.concatenate([one, two], axis=0).astype(BF)
    return ring_sum(ring_blocks(value, "q", 0), "q")


def plane_gather(rows):
    half = rows.shape[0] // 2
    one = jnp.stack(ring_gather(rows[:half], "b"))
    two = jnp.stack(ring_gather(rows[half:], "a"))
    return (jnp.stack(ring_gather(one, "a")), jnp.stack(ring_gather(two, "b")))


def plane_sum(one, two):
    na, nb = one.shape[:2]
    first = ring_sum([one[k] for k in range(na)], "a")
    second = ring_sum([two[k] for k in range(nb)], "b")
    first = ring_sum([first[k] for k in range(nb)], "b")
    second = ring_sum([second[k] for k in range(na)], "a")
    return jnp.concatenate([first, second], axis=0)


def allowed_mask(own, other, n_ctx, half):
    row = lax.broadcasted_iota(jnp.int32, (2 * half, 2 * half), 0)
    col = lax.broadcasted_iota(jnp.int32, (2 * half, 2 * half), 1)
    last = 2 * n_ctx - 1
    query = row + jnp.where(row < half, own * half, (last - own) * half - half)
    key = col + jnp.where(col < half, other * half, (last - other) * half - half)
    return key <= query


def attend_kernel(n_ctx, n_src, first, last, place_ref, q_ref, *refs):
    kv_refs, refs = refs[:n_src], refs[n_src:]
    if not first:
        acc_in, ml_in = refs[:2]
        refs = refs[2:]
    out_ref, ml_ref = refs
    queries = q_ref[...]
    tok = queries.shape[0]
    scores = []
    for s in range(n_src):
        raw = dot(queries, kv_refs[s][0], NT) * (HEAD_DIM ** (-0.5) * LOG2E)
        mask = allowed_mask(place_ref[0], place_ref[1 + s], n_ctx, tok // 2)
        scores.append(jnp.where(mask, raw, masked_value))
    peak = functools.reduce(jnp.maximum, [jnp.max(s, axis=1, keepdims=True) for s in scores])
    if not first:
        old_peak = ml_in[0][:, 0:1]
        old_sum = ml_in[0][:, 64:65]
        peak = jnp.maximum(peak, old_peak)
    total = jnp.zeros_like(peak)
    mixed = jnp.zeros((tok, HEAD_DIM), F32)
    for s in range(n_src):
        raised = jnp.exp2(scores[s] - peak)
        total = total + jnp.sum(raised, axis=1, keepdims=True)
        mixed = mixed + dot(raised.astype(BF), kv_refs[s][1])
    if not first:
        decay = jnp.exp2(old_peak - peak)
        total = total + old_sum * decay
        mixed = mixed + acc_in[...] * decay
    if last:
        out_ref[...] = (mixed / total).astype(BF)
        ml_ref[0] = jnp.broadcast_to(peak + jnp.log2(total), (tok, 128))
    else:
        out_ref[...] = mixed
        lane = lax.broadcasted_iota(jnp.int32, (tok, 128), 1)
        ml_ref[0] = jnp.where(lane < 64, peak, total)


def attend_chunk(places, queries, kv_list, state, last, n_ctx):
    tok, width = queries.shape
    head = pl.BlockSpec((tok, HEAD_DIM), lambda h, p: (0, h))
    pair = pl.BlockSpec((2, tok, HEAD_DIM), lambda h, p: (0, 0, h))
    rows = pl.BlockSpec((1, tok, 128), lambda h, p: (h, 0, 0))
    first = state is None
    n = len(kv_list)
    pairs = tok * tok * n * HEADS
    return pl.pallas_call(
        functools.partial(attend_kernel, n_ctx, n, first, last),
        grid_spec=pltpu.PrefetchScalarGridSpec(
            num_scalar_prefetch=1,
            grid=(HEADS,),
            in_specs=[head] + [pair] * n + ([] if first else [head, rows]),
            out_specs=[head, rows],
        ),
        out_shape=[
            jax.ShapeDtypeStruct((tok, width), BF if last else F32),
            jax.ShapeDtypeStruct((HEADS, tok, 128), F32),
        ],
        compiler_params=pltpu.CompilerParams(vmem_limit_bytes=VMEM_LIMIT // 2),
        cost_estimate=pl.CostEstimate(
            flops=4 * pairs * HEAD_DIM * 4, bytes_accessed=8 * tok * width, transcendentals=pairs
        ),
        name="attend",
    )(places, queries, *kv_list, *(() if first else state))


def attend_back_kernel(n_ctx, n_src, first, place_ref, q_ref, do_ref, o_ref, lse_ref, *refs):
    kv_refs, refs = refs[:n_src], refs[n_src:]
    if not first:
        dq_in, refs = refs[0], refs[1:]
    dq_ref, dkv_refs = refs[0], refs[1:]
    queries = q_ref[...]
    grad = do_ref[...]
    tok = queries.shape[0]
    lse = lse_ref[0][:, 0:1]
    delta = jnp.sum(grad.astype(F32) * o_ref[...].astype(F32), axis=1, keepdims=True)
    scale = HEAD_DIM ** (-0.5)
    grad_query = jnp.zeros((tok, HEAD_DIM), F32)
    for s in range(n_src):
        keys, values = kv_refs[s][0], kv_refs[s][1]
        raw = dot(queries, keys, NT) * (scale * LOG2E)
        mask = allowed_mask(place_ref[0], place_ref[1 + s], n_ctx, tok // 2)
        probs = jnp.exp2(jnp.where(mask, raw, masked_value) - lse)
        grad_probs = dot(grad, values, NT)
        grad_scores = (probs * (grad_probs - delta)).astype(BF)
        grad_query = grad_query + dot(grad_scores, keys)
        dkv_refs[s][0] = (dot(grad_scores, queries, TN) * scale).astype(dkv_refs[s].dtype)
        dkv_refs[s][1] = dot(probs.astype(BF), grad, TN).astype(dkv_refs[s].dtype)
    grad_query = grad_query * scale
    if not first:
        grad_query = grad_query + dq_in[...]
    dq_ref[...] = grad_query


def attend_back_chunk(places, queries, grad, mixed, lse, kv_list, dq, n_ctx):
    tok, width = queries.shape
    head = pl.BlockSpec((tok, HEAD_DIM), lambda h, p: (0, h))
    pair = pl.BlockSpec((2, tok, HEAD_DIM), lambda h, p: (0, 0, h))
    rows = pl.BlockSpec((1, tok, 128), lambda h, p: (h, 0, 0))
    first = dq is None
    n = len(kv_list)
    pairs = tok * tok * n * HEADS
    out = pl.pallas_call(
        functools.partial(attend_back_kernel, n_ctx, n, first),
        grid_spec=pltpu.PrefetchScalarGridSpec(
            num_scalar_prefetch=1,
            grid=(HEADS,),
            in_specs=[head, head, head, rows] + [pair] * n + ([] if first else [head]),
            out_specs=[head] + [pair] * n,
        ),
        out_shape=[jax.ShapeDtypeStruct((tok, width), F32)]
        + [jax.ShapeDtypeStruct((2, tok, width), F32 if s == 0 else BF) for s in range(n)],
        compiler_params=pltpu.CompilerParams(vmem_limit_bytes=VMEM_LIMIT // 2),
        cost_estimate=pl.CostEstimate(
            flops=10 * pairs * HEAD_DIM * 4, bytes_accessed=16 * tok * width, transcendentals=pairs
        ),
        name="attend_back",
    )(places, queries, grad, mixed, lse, *kv_list, *(() if first else (dq,)))
    return out[0], out[1:]


def expert_kernel(
    slots, e_ref, rank_ref, c0, c1, g0, g1, wr_ref, w1_ref, w2_ref,
    y0, y1, d0, d1, dg_ref, x_ref, h_ref, dey_ref, deg_ref,
):
    n_src = c0.shape[1]
    half = c0.shape[2]
    tok = 2 * half
    experts = wr_ref.shape[0]
    me = e_ref[0]
    picks, rows, grads, weights = [], [], [], []
    own = lax.broadcasted_iota(jnp.int32, (experts, tok), 0) == me
    slot = lax.broadcasted_iota(jnp.int32, (slots, tok), 0).astype(F32)
    for s in range(n_src):
        tokens = jnp.concatenate([c0[0, s], c1[s, 0]], axis=0)
        cot = jnp.concatenate([g0[0, s], g1[s, 0]], axis=0)
        rank = rank_ref[0, s, 0]
        logits = dot(wr_ref[...], tokens, NT)
        logits = jnp.where(rank >= 0, logits, masked_value)
        raised = jnp.where(rank >= 0, jnp.exp(logits - jnp.max(logits, axis=0, keepdims=True)), 0.0)
        gates = raised / jnp.sum(raised, axis=0, keepdims=True)
        gate_row = jnp.sum(jnp.where(own, gates, 0.0), axis=0, keepdims=True)
        rank_row = jnp.sum(jnp.where(own, rank, 0.0), axis=0, keepdims=True)
        pick = jnp.where(slot == rank_row, 1.0, 0.0)
        weights.append(jnp.sum(pick * gate_row, axis=1, keepdims=True))
        pick_low = pick.astype(BF)
        picks.append((pick, pick_low))
        rows.append(dot(pick_low, tokens).astype(BF))
        grads.append(dot(pick_low, cot))
    x = jnp.concatenate(rows, axis=0)
    grad = jnp.concatenate(grads, axis=0)
    weight = jnp.concatenate(weights, axis=0)
    x_ref[...] = x
    dey = (weight * grad).astype(BF)
    dey_ref[...] = dey
    pre = dot(x, w1_ref[...])
    gate, up = pre[:, :FF], pre[:, FF:]
    sig = jax.nn.sigmoid(gate)
    act = gate * sig
    hidden = (act * up).astype(BF)
    h_ref[...] = hidden
    grad_hidden = dot(dey, w2_ref[...], NT)
    deg = jnp.concatenate(
        [
            (grad_hidden * up * sig * (1.0 + gate * (1.0 - sig))).astype(BF),
            (grad_hidden * act).astype(BF),
        ],
        axis=1,
    )
    deg_ref[...] = deg
    dec = dot(deg, w1_ref[...], NT).astype(BF)
    ey = dot(hidden, w2_ref[...]).astype(BF).astype(F32)
    dgate = jnp.sum(grad * ey, axis=1, keepdims=True)
    weighted = (weight * ey).astype(BF)
    for s in range(n_src):
        part = slice(s * slots, (s + 1) * slots)
        pick, pick_low = picks[s]
        back = dot(pick_low, dec[part], TN).astype(BF)
        d0[0, s] = back[:half]
        d1[s, 0] = back[half:]
        back = dot(pick_low, weighted[part], TN).astype(BF)
        y0[0, s] = back[:half]
        y1[s, 0] = back[half:]
        dg_ref[0, s] = jnp.sum(pick * dgate[part], axis=0, keepdims=True)


def expert_chunk(chunk, expert, ranks, c, g, router_t, w1, w2, slots):
    na, nb, half, width = c[0].shape
    experts = router_t.shape[0]
    one = pl.BlockSpec((1, nb, half, width), lambda i, e: (i, 0, 0, 0))
    two = pl.BlockSpec((nb, 1, half, width), lambda i, e: (0, i, 0, 0))

    def fixed(shape):
        return pl.BlockSpec(shape, lambda i, e: (0,) * len(shape), pipeline_mode=pl.Buffered(1))

    def by_rows(n):
        return pl.BlockSpec((nb * slots, n), lambda i, e: (i, 0))

    n_rows = na * nb * slots
    return pl.pallas_call(
        functools.partial(expert_kernel, slots),
        grid_spec=pltpu.PrefetchScalarGridSpec(
            num_scalar_prefetch=1,
            grid=(na,),
            in_specs=[
                pl.BlockSpec((1, nb, 1, experts, 2 * half), lambda i, e: (i, 0, chunk, 0, 0)),
                one, two, one, two,
                fixed(router_t.shape), fixed(w1.shape), fixed(w2.shape),
            ],
            out_specs=[
                one, two, one, two,
                pl.BlockSpec((1, nb, 1, 2 * half), lambda i, e: (i, 0, 0, 0)),
                by_rows(width), by_rows(FF), by_rows(width), by_rows(2 * FF),
            ],
        ),
        out_shape=[
            jax.ShapeDtypeStruct((na, nb, half, width), BF),
            jax.ShapeDtypeStruct((nb, na, half, width), BF),
            jax.ShapeDtypeStruct((na, nb, half, width), BF),
            jax.ShapeDtypeStruct((nb, na, half, width), BF),
            jax.ShapeDtypeStruct((na, nb, 1, 2 * half), F32),
            jax.ShapeDtypeStruct((n_rows, width), BF),
            jax.ShapeDtypeStruct((n_rows, FF), BF),
            jax.ShapeDtypeStruct((n_rows, width), BF),
            jax.ShapeDtypeStruct((n_rows, 2 * FF), BF),
        ],
        compiler_params=pltpu.CompilerParams(vmem_limit_bytes=VMEM_LIMIT),
        cost_estimate=pl.CostEstimate(
            flops=n_rows * width * FF * 12, bytes_accessed=30_000_000, transcendentals=n_rows * FF
        ),
        name="experts",
    )(expert, ranks, *c, *g, router_t, w1, w2)


def body(
    n_experts,
    block_input,
    cotangent,
    routes,
    attn_gain,
    query_key_value_weight,
    attention_output_weight,
    ffn_gain,
    routing_weight,
    common_expert_gate_up_weight,
    common_expert_down_weight,
    expert_gate_up,
    expert_down,
):
    nq, nr, na, nb = (lax.axis_size(axis) for axis in ("q", "r", "a", "b"))
    q_at, r_at, a_at, b_at = (lax.axis_index(axis) for axis in ("q", "r", "a", "b"))
    n_ctx = nq * nr
    n_exp = na * nb
    ctx_rank = q_at * nr + r_at
    exp_rank = a_at * nb + b_at
    tok = block_input.shape[1]
    width = block_input.shape[2]
    half = tok // 2
    capacity = min(tok, 3 * TOP * tok // (2 * n_experts))
    slots = -(-capacity // 16) * 16
    row = jnp.arange(tok, dtype=jnp.int32)
    local_pos = jnp.where(
        row < half, ctx_rank * half + row, (2 * n_ctx - 1 - ctx_rank) * half + row - half
    )
    cosines, sine_table = rope_tables(local_pos, HEAD_DIM)
    cosines = cosines[:, None, :]
    sine_table = sine_table[:, None, :]
    head_shape = (tok, HEADS, HEAD_DIM)
    tokens_in = block_input[0].astype(F32)
    grad_low = cotangent[0]
    out_grad = grad_low.astype(F32)

    named = jnp.any(
        routes[0][:, :, None] == jnp.arange(n_experts, dtype=jnp.int32)[None, None, :], axis=1
    )
    before = (row[:, None] < row[None, :]).astype(BF)
    rank = dot(named.astype(BF).T, before)
    rank = jnp.where(named.T, rank, -1.0)
    ranks = jnp.stack(ring_gather(rank, "q"))
    ranks = jnp.stack(ring_gather(ranks, "b"))
    ranks = jnp.stack(ring_gather(ranks, "a"))

    own_rows = query_key_value_weight.shape[0]
    small = jnp.concatenate(
        [
            attn_gain[:, None],
            ffn_gain[:, None],
            routing_weight,
            jnp.zeros((own_rows, 126 - n_experts), BF),
        ],
        axis=1,
    )
    small = dense_gather(small)
    gain_one = small[:, 0].astype(F32)
    gain_two = small[:, 1].astype(F32)
    router = small[:, 2 : 2 + n_experts]
    qkv_weight = dense_gather(query_key_value_weight)
    out_weight = dense_gather(attention_output_weight)
    shared_in = dense_gather(common_expert_gate_up_weight)
    shared_out = dense_gather(common_expert_down_weight)

    def own_expert(stack):
        rows = lax.all_to_all(stack, "q", split_axis=0, concat_axis=0, tiled=True)
        whole = to_order(ring_gather(rows, "r"), "r")
        return jnp.moveaxis(whole, 0, 1).reshape(-1, stack.shape[2])

    w1 = own_expert(expert_gate_up)
    w2 = own_expert(expert_down)

    inv_one = rms_scale(tokens_in)
    normed = (tokens_in * inv_one * gain_one).astype(BF)
    projected = dot(normed, qkv_weight)
    queries = rotate(projected[:, :width].reshape(head_shape), cosines, sine_table)
    queries = queries.astype(BF).reshape(tok, width)
    keys = rotate(projected[:, width : 2 * width].reshape(head_shape), cosines, sine_table)
    keys = keys.astype(BF).reshape(tok, width)
    kv_own = jnp.stack([keys, projected[:, 2 * width :].astype(BF)])
    kv_chunks = [ring_gather(part, "r") for part in ring_gather(kv_own, "q")]
    places = [
        jnp.stack(
            [ctx_rank]
            + [
                lax.rem(q_at - k + nq, nq) * nr + lax.rem(r_at - s + nr, nr)
                for s in range(nr)
            ]
        ).astype(jnp.int32)
        for k in range(nq)
    ]
    state = None
    for k in range(nq):
        state = attend_chunk(places[k], queries, kv_chunks[k], state, k == nq - 1, n_ctx)
    mixed, lse = state

    g_planes = [plane_gather(part) for part in ring_gather(grad_low, "q")]

    residual = tokens_in + dot(mixed, out_weight)
    inv_two = rms_scale(residual)
    second = (residual * inv_two * gain_two).astype(BF)
    c_planes = [plane_gather(part) for part in ring_gather(second, "q")]
    expert = (exp_rank * nq + q_at).astype(jnp.int32).reshape(1)
    results = [
        expert_chunk(k, expert, ranks, c_planes[k], g_planes[k], router.T, w1, w2, slots)
        for k in range(nq)
    ]
    dec_sums = [None] * nq
    for k in list(range(1, nq)) + [0]:
        dec_sums[k] = plane_sum(results[k][2], results[k][3])
    routed_grad = ring_sum(dec_sums, "q")
    y_sums = [plane_sum(result[0], result[1]) for result in results]
    routed_sum = ring_sum(y_sums, "q")

    shared_pre = dot(second, shared_in)
    shared_gate, shared_up = shared_pre[:, :FF], shared_pre[:, FF:]
    shared_sig = jax.nn.sigmoid(shared_gate)
    shared_hidden = (shared_gate * shared_sig * shared_up).astype(BF)
    layer_out = (residual + dot(shared_hidden, shared_out) + routed_sum).astype(BF)

    logits = jnp.where(named, dot(second, router), masked_value)
    raised = jnp.where(named, jnp.exp(logits - jnp.max(logits, axis=1, keepdims=True)), 0.0)
    gates = raised / jnp.sum(raised, axis=1, keepdims=True)
    dgate = jnp.stack([result[4].reshape(na, nb, tok) for result in results])
    dgate = to_order([dgate[k] for k in range(nq)], "q")
    dgate = to_order([dgate[:, k] for k in range(na)], "a")
    dgate = to_order([dgate[:, :, k] for k in range(nb)], "b")
    dgate = jnp.transpose(dgate, (2, 1, 0, 3))
    dgate = lax.all_to_all(dgate, "q", split_axis=0, concat_axis=0, tiled=True)
    dgate = lax.all_to_all(dgate, "a", split_axis=1, concat_axis=1, tiled=True)
    dgate = lax.all_to_all(dgate, "b", split_axis=2, concat_axis=2, tiled=True)
    dgate = jnp.transpose(dgate, (1, 2, 0, 3)).reshape(n_experts, tok).T
    grad_logits = gates * (dgate - jnp.sum(gates * dgate, axis=1, keepdims=True))
    grad_logits = grad_logits.astype(BF)

    shared_hidden_grad = dot(grad_low, shared_out, NT)
    shared_pre_grad = jnp.concatenate(
        [
            shared_hidden_grad * shared_up * shared_sig * (1.0 + shared_gate * (1.0 - shared_sig)),
            shared_hidden_grad * shared_gate * shared_sig,
        ],
        axis=1,
    ).astype(BF)
    second_grad = (
        dot(shared_pre_grad, shared_in, NT) + dot(grad_logits, router, NT) + routed_grad
    )
    ffn_gain_grad = jnp.sum(second_grad * residual * inv_two, axis=0)
    residual_grad = out_grad + norm_back(second_grad, residual, inv_two, gain_two)
    mixed_grad = residual_grad.astype(BF)
    heads_grad = dot(mixed_grad, out_weight, NT).astype(BF)

    dq = None
    kv_sums = [None] * nq
    for k in list(range(1, nq)) + [0]:
        dq, parts = attend_back_chunk(
            places[k], queries, heads_grad, mixed, lse, kv_chunks[k], dq, n_ctx
        )
        kv_sums[k] = ring_sum(parts, "r")
    kv_grad = ring_sum(kv_sums, "q")

    xs, hs, deys, degs = (
        jnp.concatenate([result[i] for result in results], axis=0) for i in range(5, 9)
    )

    def expert_rows(whole):
        value = whole.reshape(nq, nr, -1, whole.shape[1])
        value = ring_sum(ring_blocks(value, "r", 1), "r").astype(BF)
        return lax.all_to_all(value, "q", split_axis=0, concat_axis=0, tiled=True).astype(F32)

    gate_up_grad = expert_rows(dot(xs, degs, TN).astype(BF))
    down_grad = expert_rows(dot(hs, deys, TN).astype(BF))

    down_rows = common_expert_down_weight.shape[0]
    shared_down_grad = dense_sum(dot(shared_hidden, grad_low, TN).astype(BF), down_rows)
    shared_in_grad = dense_sum(dot(second, shared_pre_grad, TN).astype(BF), own_rows)
    out_weight_grad = dense_sum(dot(mixed, mixed_grad, TN).astype(BF), own_rows)
    router_grad = dot(second, grad_logits, TN)

    query_back = unrotate(dq.reshape(head_shape), cosines, sine_table).reshape(tok, width)
    key_back = unrotate(kv_grad[0].reshape(head_shape), cosines, sine_table).reshape(tok, width)
    qkv_back = jnp.concatenate([query_back, key_back, kv_grad[1]], axis=1).astype(BF)
    normed_grad = dot(qkv_back, qkv_weight, NT)
    attn_gain_grad = jnp.sum(normed_grad * tokens_in * inv_one, axis=0)
    input_grad = residual_grad + norm_back(normed_grad, tokens_in, inv_one, gain_one)
    qkv_weight_grad = dense_sum(dot(normed, qkv_back, TN).astype(BF), own_rows)
    small_grad = jnp.concatenate(
        [
            attn_gain_grad[:, None],
            ffn_gain_grad[:, None],
            router_grad,
            jnp.zeros((width, 126 - n_experts), F32),
        ],
        axis=1,
    )
    small_grad = dense_sum(small_grad, own_rows)
    return (
        layer_out[None],
        input_grad[None],
        small_grad[:, 0],
        qkv_weight_grad,
        out_weight_grad,
        small_grad[:, 1],
        small_grad[:, 2 : 2 + n_experts],
        shared_in_grad,
        shared_down_grad,
        gate_up_grad,
        down_grad,
    )


def solution(mesh):
    n_ctx, n_exp = mesh.shape["ctx"], mesh.shape["exp"]

    def layer(*args):
        n_experts = args[10].shape[0]
        nq = n_experts // n_exp
        nb = 2
        fine = Mesh(
            np.asarray(mesh.devices).reshape(nq, n_ctx // nq, n_exp // nb, nb), ("q", "r", "a", "b")
        )
        ctx, exp, every = ("q", "r"), ("a", "b"), ("q", "r", "a", "b")
        tokens, flat, rows = P(exp, ctx, None), P(every), P(every, None)
        run = jax.shard_map(
            functools.partial(body, n_experts),
            mesh=fine,
            in_specs=(
                tokens, tokens, tokens, flat, rows, rows, flat, rows, rows, rows, tokens, tokens,
            ),
            out_specs=(tokens, tokens, flat, rows, rows, flat, rows, rows, rows, tokens, tokens),
            check_vma=False,
        )
        return run(*args)

    return layer
```

time: 2170 us -> 1500 us (0.69)
  waiting for transfers between devices: 1210 us -> 724 us
  blocking collectives: 342 us -> 0 us
  matrix products: 288 us -> 88.2 us
  starting transfers between devices: 36.6 us -> 214 us
  Pallas kernels: 0 us -> 161 us
  other arithmetic: 71.9 us -> 165 us
  local copies, waits for them, and re-layouts: 203 us -> 133 us
    reduce_scatter x7 -> x0, waiting for transfers between devices: 928 us -> none  [the longest x1 217 us: body(): lax.psum_scatter(qkv_weight_grad, ('ctx', 'exp'), scatter_dimension=0, ti...]
    ppermute x0 -> x179, waiting for transfers between devices: none -> 698 us  [shift(): return lax.ppermute(value, axis, [(i, (i + 1) % n) for i in range(n)])]
    unnamed x3 -> x0, blocking collectives: 205 us -> none
    ppermute x0 -> x179, starting transfers between devices: none -> 184 us  [shift(): return lax.ppermute(value, axis, [(i, (i + 1) % n) for i in range(n)])]
    dot_general x46 -> x17, matrix products: 250 us -> 85.7 us  [dot(): return lax.dot_general(a, b, (dims, ((), ())), preferred_element_type=F32)]
    pallas_call x0 -> x12, Pallas kernels: none -> 161 us  [the longest x4 86 us: expert_chunk(): pl.pallas_call(functools.partial(expert_kernel, slots), grid_spec=pltpu.P...]
    all_gather x8 -> x0, waiting for transfers between devices: 152 us -> none  [the longest x1 43.7 us: fetch_dense(): lax.all_gather(query_key_value_weight, ('ctx', 'exp'), axis=0, tiled=True)]
    all_gather x1 -> x0, blocking collectives: 137 us -> none  [fetch_dense(): lax.all_gather(routing_weight, ('ctx', 'exp'), axis=0, tiled=True)]
  transfers between devices with their start and end apart: 24 -> 186, of which waited for: 17 -> 91; matrix products, arithmetic and copies ran while one was open for 23% -> 24% of each run, Pallas kernels for 0% -> 10%
where the time goes in v1:
time: 1500 us; the launch traced here: 1490 us
  waiting for transfers between devices  724 us (48%)
  starting transfers between devices  214 us (14%)
  other arithmetic  165 us (11%)
  Pallas kernels  161 us (11%)
  local copies, waits for them, and re-layouts  133 us (9%)
  matrix products  88.2 us (6%)
    ppermute x179, waiting for transfers between devices, shift(): return lax.ppermute(value, axis, [(i, (i + 1) % n) for i in range(n)])  698 us
    ppermute x179, starting transfers between devices, shift(): return lax.ppermute(value, axis, [(i, (i + 1) % n) for i in range(n)])  184 us
    pallas_call x4, Pallas kernels, expert_chunk(): pl.pallas_call(functools.partial(expert_kernel, slots), grid_spec=pltpu.P...  86 us
    dot_general x17, matrix products, dot(): return lax.dot_general(a, b, (dims, ((), ())), preferred_element_type=F32)  85.7 us
    pallas_call x4, Pallas kernels, attend_back_chunk(): pl.pallas_call(functools.partial(attend_back_kernel, n_ctx, n, first), gr...  43.2 us
    another operation x32, other arithmetic, plane_gather(): return (jnp.stack(ring_gather(one, 'a')), jnp.stack(ring_gather(two, 'b')))  41.2 us
    pallas_call x4, Pallas kernels, attend_chunk(): pl.pallas_call(functools.partial(attend_kernel, n_ctx, n, first, last), g...  31.6 us
    unnamed x396, local copies, waits for them, and re-layouts  31.5 us
  transfers between devices with their start and end apart: 186, of which 91 were waited for; matrix products, arithmetic and copies ran while one was open for 24% of the time, Pallas kernels for 10%

profile of v1, /device:TPU:0, one launch (start us, length us, event | category | flops | bytes accessed | tf_op | source)
XLA Modules:
  0.0 1490.2 jit_solution(1352479613379306834)
XLA Ops:
  22.1 29.4 %collective-permute-done.1 = bf16[40,128]{1,0:T(8,128)(2,1)S(1)} collective-permute-done((bf16[40,128]{1,0:T(8,128)(2,1)S(1)}, bf16[40,128]{1,0:T(8,128)(2,1)S(1)}, u32[]{:S(2)}, u32[]{:S(2)}) %collective-permute-start.1) | collective-permute-done | bytes 10272 | tf_op jit(solution)/shard_map/ppermute | solution.py:67
  143.0 11.9 collective-permute-done.45
  185.3 14.8 collective-permute-done.13
  203.7 25.3 %collective-permute-done.14 = bf16[2,2,40,3840]{3,2,0,1:T(8,128)(2,1)S(1)} collective-permute-done((bf16[2,2,40,3840]{3,2,0,1:T(8,128)(2,1)S(1)}, bf16[2,2,40,3840]{3,2,0,1:T(8,128)(2,1)S(1)}, u32[]{:S(2)}, u32[]{:S(2)}) %collective-permute-start.14) | collective-permute-done | bytes 1228832 | tf_op jit(solution)/shard_map/ppermute | solution.py:67
  240.1 11.3 collective-permute-done.37
  348.1 46.2 %collective-permute-done.16.refs_0_ = bf16[2,256,1280]{2,1,0:T(8,128)(2,1)S(1)} collective-permute-done((bf16[2,256,1280]{2,1,0:T(8,128)(2,1)S(1)}, bf16[2,256,1280]{2,1,0:T(8,128)(2,1)S(1)}, u32[]{:S(2)}, u32[]{:S(2)}) %collective-permute-start.16) | collective-permute-done | bytes 1310752 | tf_op jit(solution)/shard_map/ppermute | solution.py:67
  394.3 11.8 collective-permute-start.17
  410.1 23.6 %all-to-all-done = bf16[4,160,1792]{2,1,0:T(8,128)(2,1)} async-done(((bf16[4,160,1792]{2,1,0:T(8,128)(2,1)}), bf16[4,160,1792]{2,1,0:T(8,128)(2,1)}, u32[]{:S(2)}, u32[]{:S(2)}) %all-to-all-start) | async-done | bytes 2293792 | tf_op jit(solution)/shard_map/all_to_all | solution.py:466
  446.2 24.6 %collective-permute-done.18.refs_0_ = bf16[2,256,1280]{2,1,0:T(8,128)(2,1)S(1)} collective-permute-done((bf16[2,256,1280]{2,1,0:T(8,128)(2,1)}, bf16[2,256,1280]{2,1,0:T(8,128)(2,1)S(1)}, u32[]{:S(2)}, u32[]{:S(2)}) %collective-permute-start.18) | collective-permute-done | bytes 1310752 | tf_op jit(solution)/shard_map/ppermute | solution.py:67
  553.2 13.8 collective-permute-done.53
  571.7 21.2 %experts.7 = (bf16[2,2,128,1280]{3,2,1,0:T(8,128)(2,1)}, bf16[2,2,128,1280]{3,2,1,0:T(8,128)(2,1)}, bf16[2,2,128,1280]{3,2,1,0:T(8,128)(2,1)}, bf16[2,2,128,1280...) custom-call(s32[1]{0:T(128)} %bitcast.120.e_ref, ...), custom_call_target="tpu_custom_call" | custom-call | flops 9688842240 | bytes 30000000 | tf_op jit(solution)/shard_map/experts/pallas_call | solution.py:363
  611.0 10.4 collective-permute-done.170
  642.2 21.7 %experts.4 = (bf16[2,2,128,1280]{3,2,1,0:T(8,128)(2,1)}, bf16[2,2,128,1280]{3,2,1,0:T(8,128)(2,1)}, bf16[2,2,128,1280]{3,2,1,0:T(8,128)(2,1)}, bf16[2,2,128,1280...) custom-call(s32[1]{0:T(128)} %bitcast.120.e_ref, ...), custom_call_target="tpu_custom_call" | custom-call | flops 9688842240 | bytes 30000000 | tf_op jit(solution)/shard_map/experts/pallas_call | solution.py:363
  759.1 15.6 %collective-permute-done.87 = bf16[128,1280]{1,0:T(8,128)(2,1)S(1)} collective-permute-done((bf16[128,1280]{1,0:T(8,128)(2,1)S(1)}, bf16[128,1280]{1,0:T(8,128)(2,1)S(1)}, u32[]{:S(2)}, u32[]{:S(2)}) %collective-permute-start.87) | collective-permute-done | bytes 327712 | tf_op jit(solution)/shard_map/ppermute | solution.py:67
  790.2 21.6 %experts.5 = (bf16[2,2,128,1280]{3,2,1,0:T(8,128)(2,1)}, bf16[2,2,128,1280]{3,2,1,0:T(8,128)(2,1)}, bf16[2,2,128,1280]{3,2,1,0:T(8,128)(2,1)}, bf16[2,2,128,1280...) custom-call(s32[1]{0:T(128)} %bitcast.120.e_ref, ...), custom_call_target="tpu_custom_call" | custom-call | flops 9688842240 | bytes 30000000 | tf_op jit(solution)/shard_map/experts/pallas_call | solution.py:363
  828.2 10.6 collective-permute-done.114
  870.0 21.5 %experts.6 = (bf16[2,2,128,1280]{3,2,1,0:T(8,128)(2,1)}, bf16[2,2,128,1280]{3,2,1,0:T(8,128)(2,1)}, bf16[2,2,128,1280]{3,2,1,0:T(8,128)(2,1)}, bf16[2,2,128,1280...) custom-call(s32[1]{0:T(128)} %bitcast.120.e_ref, ...), custom_call_target="tpu_custom_call" | custom-call | flops 9688842240 | bytes 30000000 | tf_op jit(solution)/shard_map/experts/pallas_call | solution.py:363
  898.6 12.4 fusion.36
  911.1 29.1 %fusion.9 = bf16[1280,1792]{1,0:T(8,128)(2,1)} fusion(bf16[704,1792]{1,0:T(8,128)(2,1)} %get-tuple-element.114, bf16[704,1792]{1,0:T(8,128)(2,1)} %get-tuple-element.113, bf16[704,1792]{1,0:T(8,128)(2,1)} %get-tuple-element.112, bf16[704,1792]{1,0:T(8,128)(2,1)} %get-tuple-element.111, bf16[704,1280]{1,0:T(8,128)(2,1)} %get-tuple-element.110, ...), kind=kOutput, calls=%fused_computation.12 | convolution fusion | flops 12989956096 | bytes 21889024 | tf_op jit(solution)/shard_map/dot_general | solution.py:58
  1090.8 9.7 collective-permute-done.125
  1113.9 10.9 attend_back.4
  1126.3 11.4 attend_back.5
  1140.2 10.5 attend_back.6
  1154.0 10.5 attend_back.7
  1173.8 29.2 %collective-permute-done.131 = bf16[2,256,1280]{2,1,0:T(8,128)(2,1)S(1)} collective-permute-done((bf16[2,256,1280]{2,1,0:T(8,128)(2,1)S(1)}, bf16[2,256,1280]{2,1,0:T(8,128)(2,1)S(1)}, u32[]{:S(2)}, u32[]{:S(2)}) %collective-permute-start.131) | collective-permute-done | bytes 1310752 | tf_op jit(solution)/shard_map/ppermute | solution.py:67
  1214.8 21.5 %collective-permute-done.133 = bf16[2,256,1280]{2,1,0:T(8,128)(2,1)S(1)} collective-permute-done((bf16[2,256,1280]{2,1,0:T(8,128)(2,1)S(1)}, bf16[2,256,1280]{2,1,0:T(8,128)(2,1)S(1)}, u32[]{:S(2)}, u32[]{:S(2)}) %collective-permute-start.133) | collective-permute-done | bytes 1310752 | tf_op jit(solution)/shard_map/ppermute | solution.py:67
  1247.9 20.7 %collective-permute-done.135 = bf16[2,256,1280]{2,1,0:T(8,128)(2,1)S(1)} collective-permute-done((bf16[2,256,1280]{2,1,0:T(8,128)(2,1)S(1)}, bf16[2,256,1280]{2,1,0:T(8,128)(2,1)S(1)}, u32[]{:S(2)}, u32[]{:S(2)}) %collective-permute-start.135) | collective-permute-done | bytes 1310752 | tf_op jit(solution)/shard_map/ppermute | solution.py:67
  1317.7 32.9 %collective-permute-done.159 = bf16[40,1280]{1,0:T(8,128)(2,1)S(1)} collective-permute-done((bf16[40,1280]{1,0:T(8,128)(2,1)S(1)}, bf16[40,1280]{1,0:T(8,128)(2,1)S(1)}, u32[]{:S(2)}, u32[]{:S(2)}) %collective-permute-start.159) | collective-permute-done | bytes 102432 | tf_op jit(solution)/shard_map/ppermute | solution.py:67
  1350.7 10.2 collective-permute-start.160
  1389.4 25.5 %collective-permute-done.139 = bf16[2,40,128]{2,1,0:T(8,128)(2,1)S(1)} collective-permute-done((bf16[2,40,128]{2,1,0:T(8,128)(2,1)S(1)}, bf16[2,40,128]{2,1,0:T(8,128)(2,1)S(1)}, u32[]{:S(2)}, u32[]{:S(2)}) %collective-permute-start.139) | collective-permute-done | bytes 20512 | tf_op jit(solution)/shard_map/ppermute | solution.py:67
  1420.1 27.5 %collective-permute-done.146 = bf16[2,2,40,3840]{3,2,0,1:T(8,128)(2,1)S(1)} collective-permute-done((bf16[2,2,40,3840]{3,2,0,1:T(8,128)(2,1)S(1)}, bf16[2,2,40,3840]{3,2,0,1:T(8,128)(2,1)S(1)}, u32[]{:S(2)}, u32[]{:S(2)}) %collective-permute-start.146) | collective-permute-done | bytes 1228832 | tf_op jit(solution)/shard_map/ppermute | solution.py:67
  1458.7 9.9 collective-permute-done.150
  (1110 shorter events, 878.7 us)
Async XLA Ops:
  0.7 100.5 %collective-permute-start.23 = (bf16[40,1280]{1,0:T(8,128)(2,1)}, bf16[40,1280]{1,0:T(8,128)(2,1)S(1)}, u32[]{:S(2)}, u32[]{:S(2)}) collective-permute-start(bf16[40,1280]{1,0:T(8,128)(2,1)} %param.17), channel_id=1, source_target_pairs={{0,8},{8,16},{16,24},{24,0},{1,9},{9,17},{17,25},{25,1},{2,10},{10... | collective-permute-start | bytes 307208 | tf_op jit(solution)/shard_map/ppermute | solution.py:67
  7.8 124.5 %collective-permute-start.8 = (bf16[40,3840]{1,0:T(8,128)(2,1)}, bf16[40,3840]{1,0:T(8,128)(2,1)}, u32[]{:S(2)}, u32[]{:S(2)}) collective-permute-start(bf16[40,3840]{1,0:T(8,128)(2,1)} %param.16), channel_id=1, source_target_pairs={{0,8},{8,16},{16,24},{24,0},{1,9},{9,17},{17,25},{25,1},{2,10},{10... | collective-permute-start | bytes 921608 | tf_op jit(solution)/shard_map/ppermute | solution.py:67
  10.3 312.4 %all-to-all-start.1 = ((bf16[4,112,1280]{2,1,0:T(8,128)(2,1)}), bf16[4,112,1280]{2,1,0:T(8,128)(2,1)}, u32[]{:S(2)}, u32[]{:S(2)}) async-start(bf16[4,112,1280]{2,1,0:T(8,128)(2,1)} %param.23), calls=%async_computation.1 | async-start | bytes 2293760 | tf_op jit(solution)/shard_map/all_to_all | solution.py:466
  15.4 150.5 %collective-permute-start.57 = (bf16[256,1280]{1,0:T(8,128)(2,1)S(1)}, bf16[256,1280]{1,0:T(8,128)(2,1)}, u32[]{:S(2)}, u32[]{:S(2)}) collective-permute-start(bf16[256,1280]{1,0:T(8,128)(2,1)S(1)} %bitcast.932), channel_id=1, source_target_pairs={{0,8},{8,16},{16,24},{24,0},{1,9},{9,17},{17,25},{25,1},{2,10},{10... | collective-permute-start | bytes 1966088 | tf_op jit(solution)/shard_map/ppermute | solution.py:67
  136.1 98.6 %collective-permute-start.104 = (bf16[2,128,1280]{2,1,0:T(8,128)(2,1)S(1)}, bf16[2,128,1280]{2,1,0:T(8,128)(2,1)S(1)}, u32[]{:S(2)}, u32[]{:S(2)}) collective-permute-start(bf16[2,128,1280]{2,1,0:T(8,128)(2,1)S(1)} %get-tuple-element.297), channel_id=1, source_target_pairs={{0,2},{2,0},{1,3},{3,1},{4,6},{6,4},{5,7},{7,5},{8,10},{10,8},{9,1... | collective-permute-start | bytes 1966088 | tf_op jit(solution)/shard_map/ppermute | solution.py:67
  139.7 98.7 %collective-permute-start.106 = (bf16[2,128,1280]{2,1,0:T(8,128)(2,1)S(1)}, bf16[2,128,1280]{2,1,0:T(8,128)(2,1)S(1)}, u32[]{:S(2)}, u32[]{:S(2)}) collective-permute-start(bf16[2,128,1280]{2,1,0:T(8,128)(2,1)S(1)} %get-tuple-element.291), channel_id=1, source_target_pairs={{0,1},{1,0},{2,3},{3,2},{4,5},{5,4},{6,7},{7,6},{8,9},{9,8},{10,11... | collective-permute-start | bytes 1966088 | tf_op jit(solution)/shard_map/ppermute | solution.py:67
  181.4 98.7 %collective-permute-start.46 = (bf16[4,2,2,28,1280]{4,0,3,2,1:T(4,128)(2,1)S(1)}, bf16[4,2,2,28,1280]{4,0,3,2,1:T(4,128)(2,1)S(1)}, u32[]{:S(2)}, u32[]{:S(2)}) collective-permute-start(bf16[4,2,2,28,1280]{4,0,3,2,1:T(4,128)(2,1)S(1)} %copy.371), channel_id=1, source_target_pairs={{0,4},{4,0},{1,5},{5,1},{2,6},{6,2},{3,7},{7,3},{8,12},{12,8},{9,1... | collective-permute-start | bytes 3440648 | tf_op jit(solution)/shard_map/ppermute | solution.py:67
  274.5 73.3 %collective-permute-start.30 = (bf16[4,2,2,40,1280]{4,3,2,1,0:T(8,128)(2,1)}, bf16[4,2,2,40,1280]{4,3,2,1,0:T(8,128)(2,1)}, u32[]{:S(2)}, u32[]{:S(2)}) collective-permute-start(bf16[4,2,2,40,1280]{4,3,2,1,0:T(8,128)(2,1)} %pad_maximum_fusion.6), channel_id=1, source_target_pairs={{0,4},{4,0},{1,5},{5,1},{2,6},{6,2},{3,7},{7,3},{8,12},{12,8},{9,1... | collective-permute-start | bytes 4915208 | tf_op jit(solution)/shard_map/ppermute | solution.py:67
  275.7 166.8 %collective-permute-start.38 = (bf16[4,2,2,40,1792]{4,3,2,1,0:T(8,128)(2,1)}, bf16[4,2,2,40,1792]{4,3,2,1,0:T(8,128)(2,1)}, u32[]{:S(2)}, u32[]{:S(2)}) collective-permute-start(bf16[4,2,2,40,1792]{4,3,2,1,0:T(8,128)(2,1)} %pad_maximum_fusion.4), channel_id=1, source_target_pairs={{0,4},{4,0},{1,5},{5,1},{2,6},{6,2},{3,7},{7,3},{8,12},{12,8},{9,1... | collective-permute-start | bytes 6881288 | tf_op jit(solution)/shard_map/ppermute | solution.py:67
  322.8 110.9 %all-to-all-start = ((bf16[4,160,1792]{2,1,0:T(8,128)(2,1)}), bf16[4,160,1792]{2,1,0:T(8,128)(2,1)}, u32[]{:S(2)}, u32[]{:S(2)}) async-start(bf16[4,160,1792]{2,1,0:T(8,128)(2,1)} %param.22), calls=%async_computation | async-start | bytes 4587520 | tf_op jit(solution)/shard_map/all_to_all | solution.py:466
  346.6 91.0 %collective-permute-start.91 = (bf16[2,128,1280]{2,1,0:T(8,128)(2,1)}, bf16[2,128,1280]{2,1,0:T(8,128)(2,1)}, u32[]{:S(2)}, u32[]{:S(2)}) collective-permute-start(bf16[2,128,1280]{2,1,0:T(8,128)(2,1)} %get-tuple-element.281), channel_id=1, source_target_pairs={{0,2},{2,0},{1,3},{3,1},{4,6},{6,4},{5,7},{7,5},{8,10},{10,8},{9,1... | collective-permute-start | bytes 1966088 | tf_op jit(solution)/shard_map/ppermute | solution.py:67
  347.8 92.3 %collective-permute-start.93 = (bf16[2,128,1280]{2,1,0:T(8,128)(2,1)}, bf16[2,128,1280]{2,1,0:T(8,128)(2,1)}, u32[]{:S(2)}, u32[]{:S(2)}) collective-permute-start(bf16[2,128,1280]{2,1,0:T(8,128)(2,1)} %get-tuple-element.275), channel_id=1, source_target_pairs={{0,1},{1,0},{2,3},{3,2},{4,5},{5,4},{6,7},{7,6},{8,9},{9,8},{10,11... | collective-permute-start | bytes 1966088 | tf_op jit(solution)/shard_map/ppermute | solution.py:67
  534.9 220.7 %collective-permute-start.161 = (bf16[4,2,2,40,1792]{4,3,0,1,2:T(8,128)(2,1)}, bf16[4,2,2,40,1792]{4,3,0,1,2:T(8,128)(2,1)}, u32[]{:S(2)}, u32[]{:S(2)}) collective-permute-start(bf16[4,2,2,40,1792]{4,3,0,1,2:T(8,128)(2,1)} %bitcast.919), channel_id=1, source_target_pairs={{0,4},{4,0},{1,5},{5,1},{2,6},{6,2},{3,7},{7,3},{8,12},{12,8},{9,1... | collective-permute-start | bytes 6881288 | tf_op jit(solution)/shard_map/ppermute | solution.py:67
  569.9 69.8 %collective-permute-start.54 = (bf16[2,128,1280]{2,1,0:T(8,128)(2,1)}, bf16[2,128,1280]{2,1,0:T(8,128)(2,1)}, u32[]{:S(2)}, u32[]{:S(2)}) collective-permute-start(bf16[2,128,1280]{2,1,0:T(8,128)(2,1)} %get-tuple-element.257), channel_id=1, source_target_pairs={{0,2},{2,0},{1,3},{3,1},{4,6},{6,4},{5,7},{7,5},{8,10},{10,8},{9,1... | collective-permute-start | bytes 1966088 | tf_op jit(solution)/shard_map/ppermute | solution.py:67
  675.0 70.8 %collective-permute-start.84 = (bf16[256,1280]{1,0:T(8,128)(2,1)}, bf16[256,1280]{1,0:T(8,128)(2,1)S(1)}, u32[]{:S(2)}, u32[]{:S(2)}) collective-permute-start(bf16[256,1280]{1,0:T(8,128)(2,1)} %collective-permute-done.69), channel_id=1, source_target_pairs={{0,8},{8,16},{16,24},{24,0},{1,9},{9,17},{17,25},{25,1},{2,10},{10... | collective-permute-start | bytes 1966088 | tf_op jit(solution)/shard_map/ppermute | solution.py:67
  681.3 95.6 %collective-permute-start.73 = (bf16[2,128,1280]{2,1,0:T(8,128)(2,1)S(1)}, bf16[2,128,1280]{2,1,0:T(8,128)(2,1)S(1)}, u32[]{:S(2)}, u32[]{:S(2)}) collective-permute-start(bf16[2,128,1280]{2,1,0:T(8,128)(2,1)S(1)} %get-tuple-element.267), channel_id=1, source_target_pairs={{0,1},{1,0},{2,3},{3,2},{4,5},{5,4},{6,7},{7,6},{8,9},{9,8},{10,11... | collective-permute-start | bytes 1966088 | tf_op jit(solution)/shard_map/ppermute | solution.py:67
  685.6 102.8 %collective-permute-start.71 = (bf16[2,128,1280]{2,1,0:T(8,128)(2,1)S(1)}, bf16[2,128,1280]{2,1,0:T(8,128)(2,1)S(1)}, u32[]{:S(2)}, u32[]{:S(2)}) collective-permute-start(bf16[2,128,1280]{2,1,0:T(8,128)(2,1)S(1)} %get-tuple-element.273), channel_id=1, source_target_pairs={{0,2},{2,0},{1,3},{3,1},{4,6},{6,4},{5,7},{7,5},{8,10},{10,8},{9,1... | collective-permute-start | bytes 1966088 | tf_op jit(solution)/shard_map/ppermute | solution.py:67
  783.5 77.6 %collective-permute-start.88 = (bf16[2,128,1280]{2,1,0:T(8,128)(2,1)}, bf16[2,128,1280]{2,1,0:T(8,128)(2,1)}, u32[]{:S(2)}, u32[]{:S(2)}) collective-permute-start(bf16[2,128,1280]{2,1,0:T(8,128)(2,1)} %get-tuple-element.283), channel_id=1, source_target_pairs={{0,1},{1,0},{2,3},{3,2},{4,5},{5,4},{6,7},{7,6},{8,9},{9,8},{10,11... | collective-permute-start | bytes 1966088 | tf_op jit(solution)/shard_map/ppermute | solution.py:67
  785.8 78.3 %collective-permute-start.86 = (bf16[2,128,1280]{2,1,0:T(8,128)(2,1)}, bf16[2,128,1280]{2,1,0:T(8,128)(2,1)}, u32[]{:S(2)}, u32[]{:S(2)}) collective-permute-start(bf16[2,128,1280]{2,1,0:T(8,128)(2,1)} %get-tuple-element.289), channel_id=1, source_target_pairs={{0,2},{2,0},{1,3},{3,1},{4,6},{6,4},{5,7},{7,5},{8,10},{10,8},{9,1... | collective-permute-start | bytes 1966088 | tf_op jit(solution)/shard_map/ppermute | solution.py:67
  852.9 90.3 %collective-permute-start.116 = (bf16[2,128,1280]{2,1,0:T(8,128)(2,1)}, bf16[2,128,1280]{2,1,0:T(8,128)(2,1)}, u32[]{:S(2)}, u32[]{:S(2)}) collective-permute-start(bf16[2,128,1280]{2,1,0:T(8,128)(2,1)} %slice_bitcast_fusion.21), channel_id=1, source_target_pairs={{0,2},{2,0},{1,3},{3,1},{4,6},{6,4},{5,7},{7,5},{8,10},{10,8},{9,1... | collective-permute-start | bytes 1966088 | tf_op jit(solution)/shard_map/ppermute | solution.py:67
  854.8 93.3 %collective-permute-start.118 = (bf16[2,128,1280]{2,1,0:T(8,128)(2,1)}, bf16[2,128,1280]{2,1,0:T(8,128)(2,1)}, u32[]{:S(2)}, u32[]{:S(2)}) collective-permute-start(bf16[2,128,1280]{2,1,0:T(8,128)(2,1)} %slice_bitcast_fusion.20), channel_id=1, source_target_pairs={{0,1},{1,0},{2,3},{3,2},{4,5},{5,4},{6,7},{7,6},{8,9},{9,8},{10,11... | collective-permute-start | bytes 1966088 | tf_op jit(solution)/shard_map/ppermute | solution.py:67
  858.1 94.5 %collective-permute-start.79 = (bf16[2,128,1280]{2,1,0:T(8,128)(2,1)}, bf16[2,128,1280]{2,1,0:T(8,128)(2,1)}, u32[]{:S(2)}, u32[]{:S(2)}) collective-permute-start(bf16[2,128,1280]{2,1,0:T(8,128)(2,1)} %slice_bitcast_fusion.29), channel_id=1, source_target_pairs={{0,2},{2,0},{1,3},{3,1},{4,6},{6,4},{5,7},{7,5},{8,10},{10,8},{9,1... | collective-permute-start | bytes 1966088 | tf_op jit(solution)/shard_map/ppermute | solution.py:67
  861.1 94.6 %collective-permute-start.81 = (bf16[2,128,1280]{2,1,0:T(8,128)(2,1)}, bf16[2,128,1280]{2,1,0:T(8,128)(2,1)}, u32[]{:S(2)}, u32[]{:S(2)}) collective-permute-start(bf16[2,128,1280]{2,1,0:T(8,128)(2,1)} %slice_bitcast_fusion.28), channel_id=1, source_target_pairs={{0,1},{1,0},{2,3},{3,2},{4,5},{5,4},{6,7},{7,6},{8,9},{9,8},{10,11... | collective-permute-start | bytes 1966088 | tf_op jit(solution)/shard_map/ppermute | solution.py:67
  864.1 152.0 %collective-permute-start.115 = (bf16[256,1280]{1,0:T(8,128)(2,1)}, bf16[256,1280]{1,0:T(8,128)(2,1)}, u32[]{:S(2)}, u32[]{:S(2)}) collective-permute-start(bf16[256,1280]{1,0:T(8,128)(2,1)} %pad_maximum_fusion.49), channel_id=1, source_target_pairs={{0,8},{8,16},{16,24},{24,0},{1,9},{9,17},{17,25},{25,1},{2,10},{10... | collective-permute-start | bytes 1966088 | tf_op jit(solution)/shard_map/ppermute | solution.py:67
  943.2 81.4 %collective-permute-start.68 = (bf16[256,1280]{1,0:T(8,128)(2,1)}, bf16[256,1280]{1,0:T(8,128)(2,1)}, u32[]{:S(2)}, u32[]{:S(2)}) collective-permute-start(bf16[256,1280]{1,0:T(8,128)(2,1)} %pad_maximum_fusion.36), channel_id=1, source_target_pairs={{0,8},{8,16},{16,24},{24,0},{1,9},{9,17},{17,25},{25,1},{2,10},{10... | collective-permute-start | bytes 1966088 | tf_op jit(solution)/shard_map/ppermute | solution.py:67
  955.7 127.6 %collective-permute-start.178 = (bf16[4,112,1280]{2,1,0:T(8,128)(2,1)}, bf16[4,112,1280]{2,1,0:T(8,128)(2,1)}, u32[]{:S(2)}, u32[]{:S(2)}) collective-permute-start(bf16[4,112,1280]{2,1,0:T(8,128)(2,1)} %dynamic-slice_bitcast_fusion.4), channel_id=1, source_target_pairs={{0,4},{4,0},{1,5},{5,1},{2,6},{6,2},{3,7},{7,3},{8,12},{12,8},{9,1... | collective-permute-start | bytes 3440648 | tf_op jit(solution)/shard_map/ppermute | solution.py:67
  978.9 225.9 %collective-permute-start.177 = (bf16[4,160,1792]{2,1,0:T(8,128)(2,1)}, bf16[4,160,1792]{2,1,0:T(8,128)(2,1)}, u32[]{:S(2)}, u32[]{:S(2)}) collective-permute-start(bf16[4,160,1792]{2,1,0:T(8,128)(2,1)} %dynamic-slice_bitcast_fusion), channel_id=1, source_target_pairs={{0,4},{4,0},{1,5},{5,1},{2,6},{6,2},{3,7},{7,3},{8,12},{12,8},{9,1... | collective-permute-start | bytes 6881288 | tf_op jit(solution)/shard_map/ppermute | solution.py:67
  1073.3 233.6 %collective-permute-start.168 = (bf16[40,1792]{1,0:T(8,128)(2,1)}, bf16[40,1792]{1,0:T(8,128)(2,1)}, u32[]{:S(2)}, u32[]{:S(2)}) collective-permute-start(bf16[40,1792]{1,0:T(8,128)(2,1)} %fusion.148), channel_id=1, source_target_pairs={{0,8},{8,16},{16,24},{24,0},{1,9},{9,17},{17,25},{25,1},{2,10},{10... | collective-permute-start | bytes 430088 | tf_op jit(solution)/shard_map/ppermute | solution.py:67
  1082.9 227.9 %collective-permute-start.98 = (bf16[256,1280]{1,0:T(8,128)(2,1)}, bf16[256,1280]{1,0:T(8,128)(2,1)}, u32[]{:S(2)}, u32[]{:S(2)}) collective-permute-start(bf16[256,1280]{1,0:T(8,128)(2,1)} %fusion.65), channel_id=1, source_target_pairs={{0,8},{8,16},{16,24},{24,0},{1,9},{9,17},{17,25},{25,1},{2,10},{10... | collective-permute-start | bytes 1966088 | tf_op jit(solution)/shard_map/ppermute | solution.py:67
  1086.3 215.5 %all-to-all-start.6 = ((bf16[4,112,1280]{2,1,0:T(8,128)(2,1)}), bf16[4,112,1280]{2,1,0:T(8,128)(2,1)}, u32[]{:S(2)}, u32[]{:S(2)}) async-start(bf16[4,112,1280]{2,1,0:T(8,128)(2,1)} %fusion.46), calls=%async_computation.6 | async-start | bytes 2293760 | tf_op jit(solution)/shard_map/all_to_all | solution.py:568
  1301.6 80.1 %collective-permute-start.145 = (bf16[4,2,2,40,3840]{4,3,0,1,2:T(8,128)(2,1)}, bf16[4,2,2,40,3840]{4,3,0,1,2:T(8,128)(2,1)}, u32[]{:S(2)}, u32[]{:S(2)}) collective-permute-start(bf16[4,2,2,40,3840]{4,3,0,1,2:T(8,128)(2,1)} %bitcast.918), channel_id=1, source_target_pairs={{0,4},{4,0},{1,5},{5,1},{2,6},{6,2},{3,7},{7,3},{8,12},{12,8},{9,1... | collective-permute-start | bytes 14745608 | tf_op jit(solution)/shard_map/ppermute | solution.py:67
  1301.8 71.6 %all-to-all-start.5 = ((bf16[4,160,1792]{2,1,0:T(8,128)(2,1)}), bf16[4,160,1792]{2,1,0:T(8,128)(2,1)S(1)}, u32[]{:S(2)}, u32[]{:S(2)}) async-start(bf16[4,160,1792]{2,1,0:T(8,128)(2,1)} %fusion.34), calls=%async_computation.5 | async-start | bytes 4587520 | tf_op jit(solution)/shard_map/all_to_all | solution.py:568
  (332 other events, 6672.1 us)

commit v2 on v1

--- a/solution.py
+++ b/solution.py
@@ -32,19 +32,6 @@
     return (jnp.cos(angles), jnp.sin(angles))
 
 
-def rotate(vector, cosines, sine_table):
-    halfway = vector.shape[-1] // 2
-    turned = jnp.concatenate([-vector[..., halfway:], vector[..., :halfway]], axis=-1)
-    return vector * cosines + turned * sine_table
-
-
-def unrotate(gradient, cosines, sine_table):
-    halfway = gradient.shape[-1] // 2
-    moved = gradient * sine_table
-    turned = jnp.concatenate([moved[..., halfway:], -moved[..., :halfway]], axis=-1)
-    return gradient * cosines + turned
-
-
 def rms_scale(values):
     return lax.rsqrt(jnp.mean(values * values, axis=1, keepdims=True) + norm_eps)
 
@@ -84,73 +71,200 @@
     return shift(moving, axis).astype(F32) + blocks[0].astype(F32)
 
 
-def to_order(parts, axis):
-    n = len(parts)
-    index = lax.axis_index(axis)
-    if n == 1:
-        return parts[0][None]
-    if n == 2:
-        first = jnp.where(index == 0, parts[0], parts[1])
-        second = jnp.where(index == 0, parts[1], parts[0])
-        return jnp.stack([first, second])
-    back = parts[::-1]
-    return lax.dynamic_slice_in_dim(jnp.stack(back + back), n - 1 - index, n, axis=0)
-
-
-def ring_blocks(value, axis, dim):
+def ring_blocks(arrays, axis, dim):
     n = lax.axis_size(axis)
     index = lax.axis_index(axis)
-    return [
-        lax.dynamic_index_in_dim(value, lax.rem(index - k + n, n), dim, keepdims=False)
-        for k in range(n)
+    out = []
+    for k in range(n):
+        at = lax.rem(index - k + n, n)
+        parts = [lax.dynamic_index_in_dim(v, at, dim, keepdims=False) for v in arrays]
+        out.append(parts[0] if len(parts) == 1 else jnp.concatenate(parts, axis=-1))
+    return out
+
+
+def after(value, *events):
+    return lax.optimization_barrier((value, *events))[0]
+
+
+def place_kernel(counts, columns, index_ref, *refs):
+    n = len(counts)
+    pieces, outs, sems = refs[:n], refs[n:-1], refs[-1]
+    t = 0
+    for piece, count in zip(pieces, counts):
+        for j in range(count):
+            at = index_ref[t]
+            t += 1
+            for o, (low, high) in enumerate(columns):
+                pltpu.make_async_copy(
+                    piece.at[j, :, pl.ds(low, high - low)], outs[o].at[at], sems.at[o]
+                ).start()
+    for o in range(len(columns)):
+        pltpu.make_async_copy(outs[o], outs[o], sems.at[o]).wait()
+
+
+def place(index, pieces, widths):
+    rows, total = pieces[0].shape[-2:]
+    pieces = [piece.reshape(-1, rows, total) for piece in pieces]
+    counts = [piece.shape[0] for piece in pieces]
+    edges = np.cumsum([0] + list(widths))
+    columns = [(int(low), int(high)) for low, high in zip(edges[:-1], edges[1:])]
+    n = sum(counts)
+    anywhere = pl.BlockSpec(memory_space=pl.ANY)
+    outs = pl.pallas_call(
+        functools.partial(place_kernel, counts, columns),
+        grid_spec=pltpu.PrefetchScalarGridSpec(
+            num_scalar_prefetch=1,
+            grid=(1,),
+            in_specs=[anywhere] * len(pieces),
+            out_specs=[anywhere] * len(widths),
+            scratch_shapes=[pltpu.SemaphoreType.DMA((len(widths),))],
+        ),
+        out_shape=[jax.ShapeDtypeStruct((n, rows, w), pieces[0].dtype) for w in widths],
+        cost_estimate=pl.CostEstimate(
+            flops=0, bytes_accessed=4 * n * rows * total, transcendentals=0
+        ),
+        name="place",
+    )(index, *pieces)
+    return [out.reshape(n * rows, w) for out, w in zip(outs, widths)]
+
+
+def dense_rings(along_q):
+    half = len(along_q) // 2
+    na, nb = lax.axis_size("a"), lax.axis_size("b")
+    one = jnp.stack(ring_gather(jnp.stack(along_q[:half]), "b"))
+    two = jnp.stack(ring_gather(jnp.stack(along_q[half:]), "a"))
+    pieces = ring_gather(one, "a") + ring_gather(two, "b")
+    steps = [[(kq, ka, kb) for kb in range(nb) for kq in range(half)] for ka in range(na)]
+    steps += [
+        [(kq, ka, kb) for ka in range(na) for kq in range(half, len(along_q))] for kb in range(nb)
     ]
-
-
-def dense_gather(shard):
-    rows, width = shard.shape
-    along_q = to_order(ring_gather(shard, "q"), "q")
-    nq = along_q.shape[0]
-    half = nq // 2
-    one = to_order(ring_gather(along_q[:half], "b"), "b")
-    two = to_order(ring_gather(along_q[half:], "a"), "a")
-    one = to_order(ring_gather(one, "a"), "a")
-    two = to_order(ring_gather(two, "b"), "b")
-    plane = jnp.concatenate(
-        [jnp.moveaxis(one, 2, 0), jnp.moveaxis(jnp.swapaxes(two, 0, 1), 2, 0)], axis=0
-    )
-    whole = to_order(ring_gather(plane, "r"), "r")
-    return jnp.moveaxis(whole, 0, 1).reshape(-1, width)
-
-
-def dense_sum(whole, n_rows):
-    width = whole.shape[1]
+    return pieces, steps
+
+
+def dense_place(pieces, steps, widths):
     nq, nr, na, nb = (lax.axis_size(axis) for axis in ("q", "r", "a", "b"))
-    value = whole.reshape(nq, nr, na, nb, n_rows, width)
-    value = ring_sum(ring_blocks(value, "r", 1), "r").astype(BF)
+    moved = [ring_gather(piece, "r") for piece in pieces]
+    order = [(k, *s) for k in range(nr) for part in steps for s in part]
+    kr, kq, ka, kb = (np.array(column, np.int32) for column in zip(*order))
+    index = lax.rem(lax.axis_index("q") - kq + nq, nq) * nr
+    index = index + lax.rem(lax.axis_index("r") - kr + nr, nr)
+    index = index * na + lax.rem(lax.axis_index("a") - ka + na, na)
+    index = index * nb + lax.rem(lax.axis_index("b") - kb + nb, nb)
+    arrays = [moved[p][k] for k in range(nr) for p in range(len(pieces))]
+    return place(index.astype(jnp.int32), arrays, widths)
+
+
+def dense_sum(wholes, n_rows):
+    nq, nr, na, nb = (lax.axis_size(axis) for axis in ("q", "r", "a", "b"))
+    values = [whole.reshape(nq, nr, na, nb, n_rows, whole.shape[1]) for whole in wholes]
+    value = ring_sum(ring_blocks(values, "r", 1), "r").astype(BF)
     half = nq // 2
     one, two = value[:half], value[half:]
-    one = ring_sum(ring_blocks(one, "a", 1), "a").astype(BF)
-    two = ring_sum(ring_blocks(two, "b", 2), "b").astype(BF)
-    one = ring_sum(ring_blocks(one, "b", 1), "b")
-    two = ring_sum(ring_blocks(two, "a", 1), "a")
+    one = ring_sum(ring_blocks([one], "a", 1), "a").astype(BF)
+    two = ring_sum(ring_blocks([two], "b", 2), "b").astype(BF)
+    one = ring_sum(ring_blocks([one], "b", 1), "b")
+    two = ring_sum(ring_blocks([two], "a", 1), "a")
     value = jnp.concatenate([one, two], axis=0).astype(BF)
-    return ring_sum(ring_blocks(value, "q", 0), "q")
+    return ring_sum(ring_blocks([value], "q", 0), "q")
 
 
 def plane_gather(rows):
-    half = rows.shape[0] // 2
-    one = jnp.stack(ring_gather(rows[:half], "b"))
-    two = jnp.stack(ring_gather(rows[half:], "a"))
-    return (jnp.stack(ring_gather(one, "a")), jnp.stack(ring_gather(two, "b")))
-
-
-def plane_sum(one, two):
-    na, nb = one.shape[:2]
-    first = ring_sum([one[k] for k in range(na)], "a")
-    second = ring_sum([two[k] for k in range(nb)], "b")
-    first = ring_sum([first[k] for k in range(nb)], "b")
-    second = ring_sum([second[k] for k in range(na)], "a")
-    return jnp.concatenate([first, second], axis=0)
+    half = rows.shape[-2] // 2
+    one = jnp.stack(ring_gather(rows[..., :half, :], "b"))
+    two = jnp.stack(ring_gather(rows[..., half:, :], "a"))
+    return (jnp.stack(ring_gather(one, "a")), ring_gather(two, "b"))
+
+
+def plane_sum(one, two, dim=0):
+    first = ring_sum(one, "a")
+    second = ring_sum(two, "b")
+    first = ring_sum([lax.index_in_dim(first, k, dim, False) for k in range(len(two))], "b")
+    second = ring_sum([lax.index_in_dim(second, k, dim, False) for k in range(len(one))], "a")
+    return jnp.concatenate([first, second], axis=-2)
+
+
+def project_kernel(n_query, x_ref, w_ref, cos_ref, sin_ref, q_ref, kv_ref):
+    j = pl.program_id(0)
+    made = dot(x_ref[...], w_ref[...])
+
+    def turned():
+        parts = []
+        for low in range(0, made.shape[1], HEAD_DIM):
+            u = made[:, low : low + HEAD_DIM]
+            parts.append(u * cos_ref[...] + pltpu.roll(u, HEAD_DIM // 2, 1) * sin_ref[...])
+        return jnp.concatenate(parts, axis=1).astype(BF)
+
+    @pl.when(j < n_query)
+    def _():
+        q_ref[...] = turned()
+
+    @pl.when((j >= n_query) & (j < 2 * n_query))
+    def _():
+        kv_ref[0] = turned()
+
+    @pl.when(j >= 2 * n_query)
+    def _():
+        kv_ref[0] = made.astype(BF)
+
+
+def project(normed, weight, cosines, signed_sine):
+    tok, width = normed.shape
+    block = 2 * HEAD_DIM
+    n = width // block
+    table = pl.BlockSpec((tok, HEAD_DIM), lambda j: (0, 0))
+    return pl.pallas_call(
+        functools.partial(project_kernel, n),
+        grid=(3 * n,),
+        in_specs=[
+            pl.BlockSpec((tok, width), lambda j: (0, 0)),
+            pl.BlockSpec((width, block), lambda j: (0, j)),
+            table,
+            table,
+        ],
+        out_specs=[
+            pl.BlockSpec((tok, block), lambda j: (0, jnp.minimum(j, n - 1))),
+            pl.BlockSpec(
+                (1, tok, block),
+                lambda j: (jnp.maximum(j - n, 0) // n, 0, jnp.maximum(j - n, 0) % n),
+            ),
+        ],
+        out_shape=[
+            jax.ShapeDtypeStruct((tok, width), BF),
+            jax.ShapeDtypeStruct((2, tok, width), BF),
+        ],
+        compiler_params=pltpu.CompilerParams(vmem_limit_bytes=VMEM_LIMIT // 2),
+        cost_estimate=pl.CostEstimate(
+            flops=6 * tok * width * width, bytes_accessed=6 * width * width, transcendentals=0
+        ),
+        name="project",
+    )(normed, weight, cosines, signed_sine)
+
+
+def turn_back(grad, cos, signed_sine):
+    return grad * cos - pltpu.roll(grad, HEAD_DIM // 2, 1) * signed_sine
+
+
+def finish_kernel(moved_ref, own_ref, cos_ref, sin_ref, out_ref):
+    keys = moved_ref[0].astype(F32) + own_ref[0]
+    out_ref[0] = turn_back(keys, cos_ref[...], sin_ref[...]).astype(BF)
+    out_ref[1] = (moved_ref[1].astype(F32) + own_ref[1]).astype(BF)
+
+
+def finish_keys(moved, own, cosines, signed_sine):
+    _, tok, width = own.shape
+    pair = pl.BlockSpec((2, tok, HEAD_DIM), lambda h: (0, 0, h))
+    table = pl.BlockSpec((tok, HEAD_DIM), lambda h: (0, 0))
+    return pl.pallas_call(
+        finish_kernel,
+        grid=(width // HEAD_DIM,),
+        in_specs=[pair, pair, table, table],
+        out_specs=pair,
+        out_shape=jax.ShapeDtypeStruct((2, tok, width), BF),
+        cost_estimate=pl.CostEstimate(
+            flops=10 * tok * width, bytes_accessed=16 * tok * width, transcendentals=0
+        ),
+        name="finish_keys",
+    )(moved, own, cosines, signed_sine)
 
 
 def allowed_mask(own, other, n_ctx, half):
@@ -227,7 +341,9 @@
     )(places, queries, *kv_list, *(() if first else state))
 
 
-def attend_back_kernel(n_ctx, n_src, first, place_ref, q_ref, do_ref, o_ref, lse_ref, *refs):
+def attend_back_kernel(
+    n_ctx, n_src, first, last, place_ref, q_ref, do_ref, o_ref, lse_ref, cos_ref, sin_ref, *refs
+):
     kv_refs, refs = refs[:n_src], refs[n_src:]
     if not first:
         dq_in, refs = refs[0], refs[1:]
@@ -252,51 +368,58 @@
     grad_query = grad_query * scale
     if not first:
         grad_query = grad_query + dq_in[...]
+    if last:
+        grad_query = turn_back(grad_query, cos_ref[...], sin_ref[...]).astype(BF)
     dq_ref[...] = grad_query
 
 
-def attend_back_chunk(places, queries, grad, mixed, lse, kv_list, dq, n_ctx):
+def attend_back_chunk(places, queries, grad, mixed, lse, tables, kv_list, dq, last, n_ctx):
     tok, width = queries.shape
     head = pl.BlockSpec((tok, HEAD_DIM), lambda h, p: (0, h))
     pair = pl.BlockSpec((2, tok, HEAD_DIM), lambda h, p: (0, 0, h))
     rows = pl.BlockSpec((1, tok, 128), lambda h, p: (h, 0, 0))
+    table = pl.BlockSpec((tok, HEAD_DIM), lambda h, p: (0, 0))
     first = dq is None
     n = len(kv_list)
     pairs = tok * tok * n * HEADS
     out = pl.pallas_call(
-        functools.partial(attend_back_kernel, n_ctx, n, first),
+        functools.partial(attend_back_kernel, n_ctx, n, first, last),
         grid_spec=pltpu.PrefetchScalarGridSpec(
             num_scalar_prefetch=1,
             grid=(HEADS,),
-            in_specs=[head, head, head, rows] + [pair] * n + ([] if first else [head]),
+            in_specs=[head, head, head, rows, table, table] + [pair] * n + ([] if first else [head]),
             out_specs=[head] + [pair] * n,
         ),
-        out_shape=[jax.ShapeDtypeStruct((tok, width), F32)]
+        out_shape=[jax.ShapeDtypeStruct((tok, width), BF if last else F32)]
         + [jax.ShapeDtypeStruct((2, tok, width), F32 if s == 0 else BF) for s in range(n)],
         compiler_params=pltpu.CompilerParams(vmem_limit_bytes=VMEM_LIMIT // 2),
         cost_estimate=pl.CostEstimate(
             flops=10 * pairs * HEAD_DIM * 4, bytes_accessed=16 * tok * width, transcendentals=pairs
         ),
         name="attend_back",
-    )(places, queries, grad, mixed, lse, *kv_list, *(() if first else (dq,)))
+    )(places, queries, grad, mixed, lse, *tables, *kv_list, *(() if first else (dq,)))
     return out[0], out[1:]
 
 
-def expert_kernel(
-    slots, e_ref, rank_ref, c0, c1, g0, g1, wr_ref, w1_ref, w2_ref,
-    y0, y1, d0, d1, dg_ref, x_ref, h_ref, dey_ref, deg_ref,
-):
-    n_src = c0.shape[1]
+def expert_kernel(slots, na, nb, n_kept, e_ref, rank_ref, c0, *refs):
+    c1, refs = refs[:nb], refs[nb:]
+    g0, g1, refs = refs[0], refs[1 : 1 + nb], refs[1 + nb :]
+    wr_ref, w1_ref, w2_ref = refs[:3]
+    refs = refs[3 + n_kept :]
+    d0, d1, refs = refs[:na], refs[na : na + nb], refs[na + nb :]
+    dg_ref, x_ref, h_ref, dey_ref, deg_ref = refs[:5]
+    y0, y1 = refs[5 : 5 + na], refs[5 + na :]
     half = c0.shape[2]
     tok = 2 * half
     experts = wr_ref.shape[0]
     me = e_ref[0]
+    step = pl.program_id(0)
     picks, rows, grads, weights = [], [], [], []
     own = lax.broadcasted_iota(jnp.int32, (experts, tok), 0) == me
     slot = lax.broadcasted_iota(jnp.int32, (slots, tok), 0).astype(F32)
-    for s in range(n_src):
-        tokens = jnp.concatenate([c0[0, s], c1[s, 0]], axis=0)
-        cot = jnp.concatenate([g0[0, s], g1[s, 0]], axis=0)
+    for s in range(nb):
+        tokens = jnp.concatenate([c0[0, s], c1[s][0]], axis=0)
+        cot = jnp.concatenate([g0[0, s, 0], g1[s][0, 0]], axis=0)
         rank = rank_ref[0, s, 0]
         logits = dot(wr_ref[...], tokens, NT)
         logits = jnp.where(rank >= 0, logits, masked_value)
@@ -335,64 +458,81 @@
     ey = dot(hidden, w2_ref[...]).astype(BF).astype(F32)
     dgate = jnp.sum(grad * ey, axis=1, keepdims=True)
     weighted = (weight * ey).astype(BF)
-    for s in range(n_src):
+    d_first, y_first = [], []
+    for s in range(nb):
         part = slice(s * slots, (s + 1) * slots)
         pick, pick_low = picks[s]
         back = dot(pick_low, dec[part], TN).astype(BF)
-        d0[0, s] = back[:half]
-        d1[s, 0] = back[half:]
+        d_first.append(back[:half])
+        d1[s][0] = back[half:]
         back = dot(pick_low, weighted[part], TN).astype(BF)
-        y0[0, s] = back[:half]
-        y1[s, 0] = back[half:]
+        y_first.append(back[:half])
+        y1[s][0, 0] = back[half:]
         dg_ref[0, s] = jnp.sum(pick * dgate[part], axis=0, keepdims=True)
-
-
-def expert_chunk(chunk, expert, ranks, c, g, router_t, w1, w2, slots):
+    for k in range(na):
+
+        @pl.when(step == k)
+        def _(k=k):
+            for s in range(nb):
+                d0[k][s] = d_first[s]
+                y0[k][0, s] = y_first[s]
+
+
+def expert_chunk(chunk, nq, expert, ranks, c, g, router_t, w1, w2, kept, slots):
     na, nb, half, width = c[0].shape
     experts = router_t.shape[0]
     one = pl.BlockSpec((1, nb, half, width), lambda i, e: (i, 0, 0, 0))
-    two = pl.BlockSpec((nb, 1, half, width), lambda i, e: (0, i, 0, 0))
+    two = pl.BlockSpec((1, half, width), lambda i, e: (i, 0, 0))
+    g_one = pl.BlockSpec((1, nb, 1, half, width), lambda i, e: (i, 0, chunk, 0, 0))
+    g_two = pl.BlockSpec((1, 1, half, width), lambda i, e: (i, chunk, 0, 0))
 
     def fixed(shape):
         return pl.BlockSpec(shape, lambda i, e: (0,) * len(shape), pipeline_mode=pl.Buffered(1))
 
     def by_rows(n):
-        return pl.BlockSpec((nb * slots, n), lambda i, e: (i, 0))
+        return pl.BlockSpec((nb * slots, n), lambda i, e: (chunk * na + i, 0))
 
     n_rows = na * nb * slots
-    return pl.pallas_call(
-        functools.partial(expert_kernel, slots),
+    kept_shapes = (
+        [jax.ShapeDtypeStruct((nq * n_rows, n), BF) for n in (width, FF, width, 2 * FF)]
+        + [jax.ShapeDtypeStruct((nq, nb, half, width), BF)] * na
+        + [jax.ShapeDtypeStruct((nq, na, half, width), BF)] * nb
+    )
+    n_kept = 0 if kept is None else len(kept)
+    n_in = 1 + 1 + (1 + nb) * 2 + 3
+    n_out = na + nb + 1
+    out = pl.pallas_call(
+        functools.partial(expert_kernel, slots, na, nb, n_kept),
         grid_spec=pltpu.PrefetchScalarGridSpec(
             num_scalar_prefetch=1,
             grid=(na,),
             in_specs=[
                 pl.BlockSpec((1, nb, 1, experts, 2 * half), lambda i, e: (i, 0, chunk, 0, 0)),
-                one, two, one, two,
+                one, *[two] * nb, g_one, *[g_two] * nb,
                 fixed(router_t.shape), fixed(w1.shape), fixed(w2.shape),
+                *[pl.BlockSpec(memory_space=pl.ANY)] * n_kept,
             ],
             out_specs=[
-                one, two, one, two,
+                *[pl.BlockSpec((nb, half, width), lambda i, e: (0, 0, 0))] * na,
+                *[two] * nb,
                 pl.BlockSpec((1, nb, 1, 2 * half), lambda i, e: (i, 0, 0, 0)),
                 by_rows(width), by_rows(FF), by_rows(width), by_rows(2 * FF),
+                *[pl.BlockSpec((1, nb, half, width), lambda i, e: (chunk, 0, 0, 0))] * na,
+                *[pl.BlockSpec((1, 1, half, width), lambda i, e: (chunk, i, 0, 0))] * nb,
             ],
         ),
-        out_shape=[
-            jax.ShapeDtypeStruct((na, nb, half, width), BF),
-            jax.ShapeDtypeStruct((nb, na, half, width), BF),
-            jax.ShapeDtypeStruct((na, nb, half, width), BF),
-            jax.ShapeDtypeStruct((nb, na, half, width), BF),
-            jax.ShapeDtypeStruct((na, nb, 1, 2 * half), F32),
-            jax.ShapeDtypeStruct((n_rows, width), BF),
-            jax.ShapeDtypeStruct((n_rows, FF), BF),
-            jax.ShapeDtypeStruct((n_rows, width), BF),
-            jax.ShapeDtypeStruct((n_rows, 2 * FF), BF),
-        ],
+        out_shape=[jax.ShapeDtypeStruct((nb, half, width), BF)] * na
+        + [jax.ShapeDtypeStruct((na, half, width), BF)] * nb
+        + [jax.ShapeDtypeStruct((na, nb, 1, 2 * half), F32)]
+        + kept_shapes,
+        input_output_aliases={n_in + k: n_out + k for k in range(n_kept)},
         compiler_params=pltpu.CompilerParams(vmem_limit_bytes=VMEM_LIMIT),
         cost_estimate=pl.CostEstimate(
             flops=n_rows * width * FF * 12, bytes_accessed=30_000_000, transcendentals=n_rows * FF
         ),
         name="experts",
-    )(expert, ranks, *c, *g, router_t, w1, w2)
+    )(expert, ranks, c[0], *c[1], g[0], *g[1], router_t, w1, w2, *(() if kept is None else kept))
+    return out[:na], out[na : na + nb], out[na + nb], out[n_out:]
 
 
 def body(
@@ -425,13 +565,18 @@
     local_pos = jnp.where(
         row < half, ctx_rank * half + row, (2 * n_ctx - 1 - ctx_rank) * half + row - half
     )
-    cosines, sine_table = rope_tables(local_pos, HEAD_DIM)
-    cosines = cosines[:, None, :]
-    sine_table = sine_table[:, None, :]
-    head_shape = (tok, HEADS, HEAD_DIM)
+    cosines, sines = rope_tables(local_pos, HEAD_DIM)
+    sines = jnp.where(jnp.arange(HEAD_DIM)[None, :] < HEAD_DIM // 2, -sines, sines)
+    tables = (cosines, sines)
     tokens_in = block_input[0].astype(F32)
     grad_low = cotangent[0]
     out_grad = grad_low.astype(F32)
+    own_rows = query_key_value_weight.shape[0]
+    down_rows = common_expert_down_weight.shape[0]
+
+    zeros = jnp.zeros((own_rows, 127), BF)
+    front = jnp.concatenate([query_key_value_weight, attn_gain[:, None], zeros], axis=1)
+    front_q = ring_gather(front, "q")
 
     named = jnp.any(
         routes[0][:, :, None] == jnp.arange(n_experts, dtype=jnp.int32)[None, None, :], axis=1
@@ -443,42 +588,43 @@
     ranks = jnp.stack(ring_gather(ranks, "b"))
     ranks = jnp.stack(ring_gather(ranks, "a"))
 
-    own_rows = query_key_value_weight.shape[0]
-    small = jnp.concatenate(
+    rest = jnp.concatenate(
         [
-            attn_gain[:, None],
+            attention_output_weight,
+            common_expert_gate_up_weight,
+            common_expert_down_weight.reshape(own_rows, -1),
             ffn_gain[:, None],
             routing_weight,
-            jnp.zeros((own_rows, 126 - n_experts), BF),
+            zeros[:, n_experts:],
         ],
         axis=1,
     )
-    small = dense_gather(small)
-    gain_one = small[:, 0].astype(F32)
-    gain_two = small[:, 1].astype(F32)
-    router = small[:, 2 : 2 + n_experts]
-    qkv_weight = dense_gather(query_key_value_weight)
-    out_weight = dense_gather(attention_output_weight)
-    shared_in = dense_gather(common_expert_gate_up_weight)
-    shared_out = dense_gather(common_expert_down_weight)
+    flat = common_expert_down_weight.size // own_rows
+    g_q = ring_gather(after(grad_low, front_q[-1]), "q")
+    rest_q = ring_gather(after(rest, g_q[-1]), "q")
+    front_pieces, front_steps = dense_rings(front_q)
+    rest_pieces, rest_steps = dense_rings([after(part, *front_pieces) for part in rest_q])
+    g_stack = after(jnp.stack(g_q), *rest_pieces)
+    g_one, g_two = plane_gather(g_stack)
 
     def own_expert(stack):
         rows = lax.all_to_all(stack, "q", split_axis=0, concat_axis=0, tiled=True)
-        whole = to_order(ring_gather(rows, "r"), "r")
-        return jnp.moveaxis(whole, 0, 1).reshape(-1, stack.shape[2])
-
-    w1 = own_expert(expert_gate_up)
-    w2 = own_expert(expert_down)
-
+        parts = ring_gather(rows, "r")
+        kr = np.repeat(np.arange(nr, dtype=np.int32), nq)
+        kq = np.tile(np.arange(nq, dtype=np.int32), nr)
+        index = kq * nr + lax.rem(r_at - kr + nr, nr)
+        return place(index.astype(jnp.int32), parts, [stack.shape[2]])[0]
+
+    w2 = own_expert(after(expert_down, rest_q[-1]))
+
+    qkv_weight, front_small = dense_place(front_pieces, front_steps, [3 * width, 128])
+    gain_one = front_small[:, 0].astype(F32)
     inv_one = rms_scale(tokens_in)
     normed = (tokens_in * inv_one * gain_one).astype(BF)
-    projected = dot(normed, qkv_weight)
-    queries = rotate(projected[:, :width].reshape(head_shape), cosines, sine_table)
-    queries = queries.astype(BF).reshape(tok, width)
-    keys = rotate(projected[:, width : 2 * width].reshape(head_shape), cosines, sine_table)
-    keys = keys.astype(BF).reshape(tok, width)
-    kv_own = jnp.stack([keys, projected[:, 2 * width :].astype(BF)])
-    kv_chunks = [ring_gather(part, "r") for part in ring_gather(kv_own, "q")]
+    queries, kv_own = project(normed, qkv_weight, *tables)
+    kv_q = ring_gather(kv_own, "q")
+    kv_chunks = [ring_gather(part, "r") for part in kv_q]
+    w1 = own_expert(after(expert_gate_up, kv_q[-1]))
     places = [
         jnp.stack(
             [ctx_rank]
@@ -494,23 +640,35 @@
         state = attend_chunk(places[k], queries, kv_chunks[k], state, k == nq - 1, n_ctx)
     mixed, lse = state
 
-    g_planes = [plane_gather(part) for part in ring_gather(grad_low, "q")]
-
+    out_weight, shared_in, shared_out, rest_small = dense_place(
+        rest_pieces, rest_steps, [width, 2 * FF, flat, 128]
+    )
+    shared_out = shared_out.reshape(-1, width)
+    gain_two = rest_small[:, 0].astype(F32)
+    router = rest_small[:, 1 : 1 + n_experts]
     residual = tokens_in + dot(mixed, out_weight)
     inv_two = rms_scale(residual)
     second = (residual * inv_two * gain_two).astype(BF)
     c_planes = [plane_gather(part) for part in ring_gather(second, "q")]
     expert = (exp_rank * nq + q_at).astype(jnp.int32).reshape(1)
-    results = [
-        expert_chunk(k, expert, ranks, c_planes[k], g_planes[k], router.T, w1, w2, slots)
-        for k in range(nq)
-    ]
+    router_t = router.T
+    kept = None
+    dec_parts, dgates = [], []
+    for k in range(nq):
+        one, two, dgate, kept = expert_chunk(
+            k, nq, expert, ranks, c_planes[k], (g_one, g_two), router_t, w1, w2, kept, slots
+        )
+        dec_parts.append((one, two))
+        dgates.append(dgate.reshape(na * nb, tok))
     dec_sums = [None] * nq
     for k in list(range(1, nq)) + [0]:
-        dec_sums[k] = plane_sum(results[k][2], results[k][3])
+        dec_sums[k] = plane_sum(*dec_parts[k])
     routed_grad = ring_sum(dec_sums, "q")
-    y_sums = [plane_sum(result[0], result[1]) for result in results]
-    routed_sum = ring_sum(y_sums, "q")
+    y_one, y_two = kept[4 : 4 + na], kept[4 + na :]
+    y_one = [after(y_one[0], routed_grad)] + [after(v, routed_grad) for v in y_one[1:]]
+    y_two = [after(y_two[0], routed_grad)] + [after(v, routed_grad) for v in y_two[1:]]
+    y_sums = plane_sum(y_one, y_two, 1)
+    routed_sum = ring_sum([y_sums[k] for k in range(nq)], "q")
 
     shared_pre = dot(second, shared_in)
     shared_gate, shared_up = shared_pre[:, :FF], shared_pre[:, FF:]
@@ -521,15 +679,16 @@
     logits = jnp.where(named, dot(second, router), masked_value)
     raised = jnp.where(named, jnp.exp(logits - jnp.max(logits, axis=1, keepdims=True)), 0.0)
     gates = raised / jnp.sum(raised, axis=1, keepdims=True)
-    dgate = jnp.stack([result[4].reshape(na, nb, tok) for result in results])
-    dgate = to_order([dgate[k] for k in range(nq)], "q")
-    dgate = to_order([dgate[:, k] for k in range(na)], "a")
-    dgate = to_order([dgate[:, :, k] for k in range(nb)], "b")
-    dgate = jnp.transpose(dgate, (2, 1, 0, 3))
-    dgate = lax.all_to_all(dgate, "q", split_axis=0, concat_axis=0, tiled=True)
-    dgate = lax.all_to_all(dgate, "a", split_axis=1, concat_axis=1, tiled=True)
-    dgate = lax.all_to_all(dgate, "b", split_axis=2, concat_axis=2, tiled=True)
-    dgate = jnp.transpose(dgate, (1, 2, 0, 3)).reshape(n_experts, tok).T
+    n_all = nq * na * nb
+    spot = np.arange(n_all, dtype=np.int32)
+    spot = (
+        lax.rem(q_at - spot // (na * nb) + nq, nq) * (na * nb)
+        + lax.rem(a_at - spot // nb % na + na, na) * nb
+        + lax.rem(b_at - spot % nb + nb, nb)
+    )
+    dgate = jnp.concatenate(dgates, axis=0)[spot]
+    dgate = lax.all_to_all(dgate, ("q", "a", "b"), split_axis=0, concat_axis=0, tiled=True)
+    dgate = jnp.swapaxes(dgate.reshape(nq, na * nb, tok), 0, 1).reshape(n_experts, tok).T
     grad_logits = gates * (dgate - jnp.sum(gates * dgate, axis=1, keepdims=True))
     grad_logits = grad_logits.astype(BF)
 
@@ -550,59 +709,71 @@
     heads_grad = dot(mixed_grad, out_weight, NT).astype(BF)
 
     dq = None
-    kv_sums = [None] * nq
+    moving = None
     for k in list(range(1, nq)) + [0]:
         dq, parts = attend_back_chunk(
-            places[k], queries, heads_grad, mixed, lse, kv_chunks[k], dq, n_ctx
+            places[k], queries, heads_grad, mixed, lse, tables, kv_chunks[k], dq, k == 0, n_ctx
         )
-        kv_sums[k] = ring_sum(parts, "r")
-    kv_grad = ring_sum(kv_sums, "q")
-
-    xs, hs, deys, degs = (
-        jnp.concatenate([result[i] for result in results], axis=0) for i in range(5, 9)
-    )
+        term = ring_sum(parts, "r")
+        if k == 1:
+            moving = term.astype(BF)
+        elif k:
+            moving = (shift(moving, "q").astype(F32) + term).astype(BF)
+    kv_back = finish_keys(shift(moving, "q"), term, *tables)
+
+    xs, hs, deys, degs = kept[:4]
 
     def expert_rows(whole):
         value = whole.reshape(nq, nr, -1, whole.shape[1])
-        value = ring_sum(ring_blocks(value, "r", 1), "r").astype(BF)
+        value = ring_sum(ring_blocks([value], "r", 1), "r").astype(BF)
         return lax.all_to_all(value, "q", split_axis=0, concat_axis=0, tiled=True).astype(F32)
 
     gate_up_grad = expert_rows(dot(xs, degs, TN).astype(BF))
     down_grad = expert_rows(dot(hs, deys, TN).astype(BF))
 
-    down_rows = common_expert_down_weight.shape[0]
-    shared_down_grad = dense_sum(dot(shared_hidden, grad_low, TN).astype(BF), down_rows)
-    shared_in_grad = dense_sum(dot(second, shared_pre_grad, TN).astype(BF), own_rows)
-    out_weight_grad = dense_sum(dot(mixed, mixed_grad, TN).astype(BF), own_rows)
-    router_grad = dot(second, grad_logits, TN)
-
-    query_back = unrotate(dq.reshape(head_shape), cosines, sine_table).reshape(tok, width)
-    key_back = unrotate(kv_grad[0].reshape(head_shape), cosines, sine_table).reshape(tok, width)
-    qkv_back = jnp.concatenate([query_back, key_back, kv_grad[1]], axis=1).astype(BF)
-    normed_grad = dot(qkv_back, qkv_weight, NT)
+    rest_grad = dense_sum(
+        [
+            dot(mixed, mixed_grad, TN).astype(BF),
+            dot(second, shared_pre_grad, TN).astype(BF),
+            dot(shared_hidden, grad_low, TN).astype(BF).reshape(width, flat),
+            jnp.concatenate(
+                [
+                    ffn_gain_grad[:, None],
+                    dot(second, grad_logits, TN),
+                    jnp.zeros((width, 127 - n_experts), F32),
+                ],
+                axis=1,
+            ).astype(BF),
+        ],
+        own_rows,
+    )
+    query_grad = dense_sum([dot(normed, dq, TN).astype(BF)], own_rows)
+    normed_grad = dot(dq, qkv_weight[:, :width], NT)
+    normed_grad += dot(kv_back[0], qkv_weight[:, width : 2 * width], NT)
+    normed_grad += dot(kv_back[1], qkv_weight[:, 2 * width :], NT)
     attn_gain_grad = jnp.sum(normed_grad * tokens_in * inv_one, axis=0)
     input_grad = residual_grad + norm_back(normed_grad, tokens_in, inv_one, gain_one)
-    qkv_weight_grad = dense_sum(dot(normed, qkv_back, TN).astype(BF), own_rows)
-    small_grad = jnp.concatenate(
+    kv_weight_grad = dense_sum(
         [
-            attn_gain_grad[:, None],
-            ffn_gain_grad[:, None],
-            router_grad,
-            jnp.zeros((width, 126 - n_experts), F32),
+            dot(normed, kv_back[0], TN).astype(BF),
+            dot(normed, kv_back[1], TN).astype(BF),
+            jnp.concatenate(
+                [attn_gain_grad[:, None], jnp.zeros((width, 127), F32)], axis=1
+            ).astype(BF),
         ],
-        axis=1,
-    )
-    small_grad = dense_sum(small_grad, own_rows)
+        own_rows,
+    )
+    at_in, at_out = width + 2 * FF, width + 2 * FF + flat
     return (
         layer_out[None],
         input_grad[None],
-        small_grad[:, 0],
-        qkv_weight_grad,
-        out_weight_grad,
-        small_grad[:, 1],
-        small_grad[:, 2 : 2 + n_experts],
-        shared_in_grad,
-        shared_down_grad,
+        kv_weight_grad[:, 2 * width],
+        jnp.concatenate([query_grad, kv_weight_grad[:, : 2 * width]], axis=1),
+        rest_grad[:, :width],
+        rest_grad[:, at_out],
+        rest_grad[:, at_out + 1 : at_out + 1 + n_experts],
+        rest_grad[:, width:at_in],
+        rest_grad[:, at_in:at_out].reshape(down_rows, width),
         gate_up_grad,
         down_grad,
     )

time: 1500 us -> 2000 us (1.33)
  Pallas kernels: 161 us -> 1030 us
  waiting for transfers between devices: 724 us -> 552 us
  other arithmetic: 165 us -> 97.5 us
  starting transfers between devices: 214 us -> 151 us
  local copies, waits for them, and re-layouts: 133 us -> 95.5 us
  matrix products: 88.2 us -> 61.8 us
    pallas_call x8 -> x14, Pallas kernels: 129 us -> 991 us  [the longest x4 841 us: place(): pl.pallas_call(functools.partial(place_kernel, counts, columns), grid_spe...]
    ppermute x179 -> x121, waiting for transfers between devices: 698 us -> 552 us  [shift(): return lax.ppermute(value, axis, [(i, (i + 1) % n) for i in range(n)])]
    ppermute x179 -> x121, starting transfers between devices: 184 us -> 127 us  [shift(): return lax.ppermute(value, axis, [(i, (i + 1) % n) for i in range(n)])]
    another operation x79 -> x24, other arithmetic: 71.8 us -> 33.9 us  [the longest x10 16.6 us: plane_gather(): return (jnp.stack(ring_gather(one, 'a')), ring_gather(two, 'b'))]
    squeeze x40 -> x16, local copies, waits for them, and re-layouts: 31.2 us -> 5.86 us  [ring_blocks(): lax.dynamic_index_in_dim(v, at, dim, keepdims=False)]
    dot_general x17 -> x21, matrix products: 85.7 us -> 61.8 us  [dot(): return lax.dot_general(a, b, (dims, ((), ())), preferred_element_type=F32)]
    all_to_all x2, waiting for transfers between devices: 23.6 us -> 0.01 us  [own_expert(): rows = lax.all_to_all(stack, 'q', split_axis=0, concat_axis=0, tiled=True)]
    unnamed x396 -> x304, local copies, waits for them, and re-layouts: 31.5 us -> 41.9 us
  transfers between devices with their start and end apart: 186 -> 126, of which waited for: 91 -> 59; matrix products, arithmetic and copies ran while one was open for 24% -> 10% of each run, Pallas kernels for 10% -> 51%
where the time goes in v2:
time: 2000 us; the launch traced here: 1990 us
  Pallas kernels  1030 us (52%)
  waiting for transfers between devices  552 us (28%)
  starting transfers between devices  151 us (8%)
  other arithmetic  97.5 us (5%)
  local copies, waits for them, and re-layouts  95.5 us (5%)
  matrix products  61.8 us (3%)
    pallas_call x4, Pallas kernels, place(): pl.pallas_call(functools.partial(place_kernel, counts, columns), grid_spe...  841 us
    ppermute x121, waiting for transfers between devices, shift(): return lax.ppermute(value, axis, [(i, (i + 1) % n) for i in range(n)])  552 us
    ppermute x121, starting transfers between devices, shift(): return lax.ppermute(value, axis, [(i, (i + 1) % n) for i in range(n)])  127 us
    pallas_call x4, Pallas kernels, expert_chunk(): pl.pallas_call(functools.partial(expert_kernel, slots, na, nb, n_kept), g...  89.3 us
    dot_general x21, matrix products, dot(): return lax.dot_general(a, b, (dims, ((), ())), preferred_element_type=F32)  61.8 us
    pallas_call x4, Pallas kernels, attend_back_chunk(): pl.pallas_call(functools.partial(attend_back_kernel, n_ctx, n, first, las...  44.6 us
    unnamed x304, local copies, waits for them, and re-layouts  41.9 us
  transfers between devices with their start and end apart: 126, of which 59 were waited for; matrix products, arithmetic and copies ran while one was open for 10% of the time, Pallas kernels for 51%

profile of v2, /device:TPU:0, one launch (start us, length us, event | category | flops | bytes accessed | tf_op | source)
XLA Modules:
  0.0 1986.7 jit_solution(16588247146760258607)
XLA Ops:
  54.7 11.7 collective-permute-done.19
  70.0 11.5 collective-permute-done.20
  92.9 11.5 collective-permute-done.24
  118.0 309.5 %place.4 = (bf16[32,40,3840]{2,1,0:T(8,128)(2,1)}, bf16[32,40,128]{2,1,0:T(8,128)(2,1)}) custom-call(s32[32]{0:T(128)} %fusion.135.index_ref, bf16[4,40,3968]{2,1,0:T(8,128)(2,1)} %bitcast.517, bf16[4,40,3968]{2,1,0:T(8,128)(2,1)} %bitcast.10.refs_1_, bf16[4,40,3968]{2,1,0:T(8,128)(2,1)} %bitcast.15.refs_2_, bf16[4,40,3968]{2,1,0:T(8,128)(2,1)} %bitcast.16.refs_3_, ...), custom_call_target="tpu_custom_call" | custom-call | bytes 20316160 | tf_op jit(solution)/shard_map/place/pallas_call | solution.py:113
  454.8 28.9 %collective-permute-done.32 = f32[16,256]{1,0:T(8,128)S(1)} collective-permute-done((f32[16,256]{1,0:T(8,128)S(1)}, f32[16,256]{1,0:T(8,128)S(1)}, u32[]{:S(2)}, u32[]{:S(2)}) %collective-permute-start.32) | collective-permute-done | bytes 16416 | tf_op jit(solution)/shard_map/ppermute | solution.py:54
  511.7 20.7 %collective-permute-done.12.refs_0_ = bf16[2,256,1280]{2,1,0:T(8,128)(2,1)} collective-permute-done((bf16[2,256,1280]{2,1,0:T(8,128)(2,1)S(1)}, bf16[2,256,1280]{2,1,0:T(8,128)(2,1)}, u32[]{:S(2)}, u32[]{:S(2)}) %collective-permute-start.12) | collective-permute-done | bytes 1310752 | tf_op jit(solution)/shard_map/ppermute | solution.py:54
  540.6 24.2 %collective-permute-done.13.refs_0_ = bf16[2,256,1280]{2,1,0:T(8,128)(2,1)} collective-permute-done((bf16[2,256,1280]{2,1,0:T(8,128)(2,1)}, bf16[2,256,1280]{2,1,0:T(8,128)(2,1)}, u32[]{:S(2)}, u32[]{:S(2)}) %collective-permute-start.13) | collective-permute-done | bytes 1310752 | tf_op jit(solution)/shard_map/ppermute | solution.py:54
  583.7 71.4 %place.7 = bf16[8,112,1280]{2,1,0:T(8,128)(2,1)} custom-call(s32[8]{0:T(128)} %fusion.137.index_ref, bf16[4,112,1280]{2,1,0:T(8,128)(2,1)} %all-to-all-done.1.refs_0_, bf16[4,112,1280]{2,1,0:T(8,128)(2,1)} %collective-permute-done.49.refs_1_), custom_call_target="tpu_custom_call" | custom-call | bytes 4587520 | tf_op jit(solution)/shard_map/place/pallas_call | solution.py:113
  664.0 319.5 %place.5 = (bf16[32,40,1280]{2,1,0:T(8,128)(2,1)}, bf16[32,40,1792]{2,1,0:T(8,128)(2,1)}, bf16[32,40,896]{2,1,0:T(8,128)(2,1)}, bf16[32,40,128]{2,1,0:T(8,128)(2,1)}) custom-call(s32[32]{0:T(128)} %fusion.135.index_ref, bf16[4,40,4096]{2,1,0:T(8,128)(2,1)} %bitcast.35.refs_0_, bf16[4,40,4096]{2,1,0:T(8,128)(2,1)} %bitcast.36.refs_1_, ...), custom_call_target="tpu_custom_call" | custom-call | bytes 20971520 | tf_op jit(solution)/shard_map/place/pallas_call | solution.py:113
  1033.0 18.1 collective-permute-done.37
  1081.2 11.6 collective-permute-done.39
  1108.2 12.6 collective-permute-done.42
  1137.4 140.7 %place.6 = bf16[8,160,1792]{2,1,0:T(8,128)(2,1)} custom-call(s32[8]{0:T(128)} %fusion.137.index_ref, bf16[4,160,1792]{2,1,0:T(8,128)(2,1)} %all-to-all-done.refs_0_, bf16[4,160,1792]{2,1,0:T(8,128)(2,1)} %collective-permute-done.48.refs_1_), custom_call_target="tpu_custom_call" | custom-call | bytes 9175040 | tf_op jit(solution)/shard_map/place/pallas_call | solution.py:113
  1278.1 22.1 %experts.4 = (bf16[2,128,1280]{2,1,0:T(8,128)(2,1)}, bf16[2,128,1280]{2,1,0:T(8,128)(2,1)}, bf16[2,128,1280]{2,1,0:T(8,128)(2,1)}, bf16[2,128,1280]{2,1,0:T(8,12...) custom-call(s32[1]{0:T(128)} %bitcast.50.e_ref, ...), custom_call_target="tpu_custom_call" | custom-call | flops 9688842240 | bytes 30000000 | tf_op jit(solution)/shard_map/experts/pallas_call | solution.py:504
  1300.2 22.6 %experts.5 = (bf16[2,128,1280]{2,1,0:T(8,128)(2,1)}, bf16[2,128,1280]{2,1,0:T(8,128)(2,1)}, bf16[2,128,1280]{2,1,0:T(8,128)(2,1)}, bf16[2,128,1280]{2,1,0:T(8,12...) custom-call(s32[1]{0:T(128)} %bitcast.50.e_ref, ...), custom_call_target="tpu_custom_call", output_to_operand_aliasing={{5}: (11, {}), {6}: (12, {}), {7}: (13, {}), {8}: (14, {}),... | custom-call | flops 9688842240 | bytes 30000000 | tf_op jit(solution)/shard_map/experts/pallas_call | solution.py:504
  1322.9 22.2 %experts.6 = (bf16[2,128,1280]{2,1,0:T(8,128)(2,1)}, bf16[2,128,1280]{2,1,0:T(8,128)(2,1)}, bf16[2,128,1280]{2,1,0:T(8,128)(2,1)}, bf16[2,128,1280]{2,1,0:T(8,12...) custom-call(s32[1]{0:T(128)} %bitcast.50.e_ref, ...), custom_call_target="tpu_custom_call", output_to_operand_aliasing={{5}: (11, {}), {6}: (12, {}), {7}: (13, {}), {8}: (14, {}),... | custom-call | flops 9688842240 | bytes 30000000 | tf_op jit(solution)/shard_map/experts/pallas_call | solution.py:504
  1345.0 22.5 %experts.7 = (bf16[2,128,1280]{2,1,0:T(8,128)(2,1)}, bf16[2,128,1280]{2,1,0:T(8,128)(2,1)}, bf16[2,128,1280]{2,1,0:T(8,128)(2,1)}, bf16[2,128,1280]{2,1,0:T(8,12...) custom-call(s32[1]{0:T(128)} %bitcast.50.e_ref, ...), custom_call_target="tpu_custom_call", output_to_operand_aliasing={{5}: (11, {}), {6}: (12, {}), {7}: (13, {}), {8}: (14, {}),... | custom-call | flops 9688842240 | bytes 30000000 | tf_op jit(solution)/shard_map/experts/pallas_call | solution.py:504
  1367.5 11.4 convolution_convert_fusion.6
  1389.8 18.6 convolution_convert_fusion
  1417.3 11.8 collective-permute-done.64
  1459.8 11.3 collective-permute-done.79
  1472.8 12.0 collective-permute-done.68
  1498.5 12.9 collective-permute-done.66
  1513.2 14.2 collective-permute-done.71
  1571.8 11.2 attend_back.5
  1586.0 11.9 attend_back.6
  1708.2 36.2 %collective-permute-done.81 = bf16[4,2,128,1280]{3,2,0,1:T(8,128)(2,1)S(1)} collective-permute-done((bf16[4,2,128,1280]{3,2,0,1:T(8,128)(2,1)S(1)}, bf16[4,2,128,1280]{3,2,0,1:T(8,128)(2,1)S(1)}, u32[]{:S(2)}, u32[]{:S(2)}) %collective-permute-start.81) | collective-permute-done | bytes 2621472 | tf_op jit(solution)/shard_map/ppermute | solution.py:54
  1761.5 19.2 collective-permute-done.89
  1796.1 20.1 %collective-permute-done.91 = bf16[2,256,1280]{2,1,0:T(8,128)(2,1)} collective-permute-done((bf16[2,256,1280]{2,1,0:T(8,128)(2,1)}, bf16[2,256,1280]{2,1,0:T(8,128)(2,1)}, u32[]{:S(2)}, u32[]{:S(2)}) %collective-permute-start.91) | collective-permute-done | bytes 1310752 | tf_op jit(solution)/shard_map/ppermute | solution.py:54
  1842.7 25.7 %collective-permute-done.86 = bf16[256,1280]{1,0:T(8,128)(2,1)S(1)} collective-permute-done((bf16[256,1280]{1,0:T(8,128)(2,1)S(1)}, bf16[256,1280]{1,0:T(8,128)(2,1)S(1)}, u32[]{:S(2)}, u32[]{:S(2)}) %collective-permute-start.86) | collective-permute-done | bytes 655392 | tf_op jit(solution)/shard_map/ppermute | solution.py:54
  1905.1 12.9 collective-permute-done.115
  1924.2 16.1 collective-permute-done.98
  (778 shorter events, 656.6 us)
Async XLA Ops:
  40.5 41.7 %collective-permute-start.2 = (bf16[2,2,40,3968]{3,2,1,0:T(8,128)(2,1)S(1)}, bf16[2,2,40,3968]{3,2,1,0:T(8,128)(2,1)}, u32[]{:S(2)}, u32[]{:S(2)}) collective-permute-start(bf16[2,2,40,3968]{3,2,1,0:T(8,128)(2,1)S(1)} %pad_maximum_fusion.13), channel_id=1, source_target_pairs={{0,2},{2,0},{1,3},{3,1},{4,6},{6,4},{5,7},{7,5},{8,10},{10,8},{9,1... | collective-permute-start | bytes 3809288 | tf_op jit(solution)/shard_map/ppermute | solution.py:54
  113.3 328.1 %collective-permute-start.22 = (bf16[2,40,4096]{2,1,0:T(8,128)(2,1)}, bf16[2,40,4096]{2,1,0:T(8,128)(2,1)}, u32[]{:S(2)}, u32[]{:S(2)}) collective-permute-start(bf16[2,40,4096]{2,1,0:T(8,128)(2,1)} %get-tuple-element.310), channel_id=1, source_target_pairs={{0,1},{1,0},{2,3},{3,2},{4,5},{5,4},{6,7},{7,6},{8,9},{9,8},{10,11... | collective-permute-start | bytes 1966088 | tf_op jit(solution)/shard_map/ppermute | solution.py:54
  116.5 328.4 %collective-permute-start.26 = (bf16[2,40,4096]{2,1,0:T(8,128)(2,1)}, bf16[2,40,4096]{2,1,0:T(8,128)(2,1)}, u32[]{:S(2)}, u32[]{:S(2)}) collective-permute-start(bf16[2,40,4096]{2,1,0:T(8,128)(2,1)} %get-tuple-element.308), channel_id=1, source_target_pairs={{0,2},{2,0},{1,3},{3,1},{4,6},{6,4},{5,7},{7,5},{8,10},{10,8},{9,1... | collective-permute-start | bytes 1966088 | tf_op jit(solution)/shard_map/ppermute | solution.py:54
  441.3 58.0 %collective-permute-start.11 = (bf16[2,256,1280]{2,1,0:T(8,128)(2,1)S(1)}, bf16[2,256,1280]{2,1,0:T(8,128)(2,1)S(1)}, u32[]{:S(2)}, u32[]{:S(2)}) collective-permute-start(bf16[2,256,1280]{2,1,0:T(8,128)(2,1)S(1)} %get-tuple-element.107.refs_0_), channel_id=1, source_target_pairs={{0,8},{8,16},{16,24},{24,0},{1,9},{9,17},{17,25},{25,1},{2,10},{10... | collective-permute-start | bytes 3932168 | tf_op jit(solution)/shard_map/ppermute | solution.py:54
  444.4 57.5 %collective-permute-start.23 = (bf16[2,2,40,4096]{3,2,1,0:T(8,128)(2,1)}, bf16[2,2,40,4096]{3,2,1,0:T(8,128)(2,1)}, u32[]{:S(2)}, u32[]{:S(2)}) collective-permute-start(bf16[2,2,40,4096]{3,2,1,0:T(8,128)(2,1)} %pad_maximum_fusion.7), channel_id=1, source_target_pairs={{0,2},{2,0},{1,3},{3,1},{4,6},{6,4},{5,7},{7,5},{8,10},{10,8},{9,1... | collective-permute-start | bytes 3932168 | tf_op jit(solution)/shard_map/ppermute | solution.py:54
  447.3 55.4 %collective-permute-start.27 = (bf16[2,2,40,4096]{3,2,1,0:T(8,128)(2,1)}, bf16[2,2,40,4096]{3,2,1,0:T(8,128)(2,1)}, u32[]{:S(2)}, u32[]{:S(2)}) collective-permute-start(bf16[2,2,40,4096]{3,2,1,0:T(8,128)(2,1)} %pad_maximum_fusion.8), channel_id=1, source_target_pairs={{0,1},{1,0},{2,3},{3,2},{4,5},{5,4},{6,7},{7,6},{8,9},{9,8},{10,11... | collective-permute-start | bytes 3932168 | tf_op jit(solution)/shard_map/ppermute | solution.py:54
  448.4 63.3 %all-to-all-start.1 = ((bf16[4,112,1280]{2,1,0:T(8,128)(2,1)}), bf16[4,112,1280]{2,1,0:T(8,128)(2,1)}, u32[]{:S(2)}, u32[]{:S(2)}) async-start(bf16[4,112,1280]{2,1,0:T(8,128)(2,1)} %param.38), calls=%async_computation.1 | async-start | bytes 2293760 | tf_op jit(solution)/shard_map/all_to_all | solution.py:611
  533.3 129.1 %collective-permute-start.30 = (bf16[2,2,40,4096]{3,2,1,0:T(8,128)(2,1)}, bf16[2,2,40,4096]{3,2,1,0:T(8,128)(2,1)}, u32[]{:S(2)}, u32[]{:S(2)}) collective-permute-start(bf16[2,2,40,4096]{3,2,1,0:T(8,128)(2,1)} %pad_maximum_fusion.8), channel_id=1, source_target_pairs={{0,4},{4,0},{1,5},{5,1},{2,6},{6,2},{3,7},{7,3},{8,12},{12,8},{9,1... | collective-permute-start | bytes 3932168 | tf_op jit(solution)/shard_map/ppermute | solution.py:54
  533.3 129.6 %collective-permute-start.29 = (bf16[2,2,40,4096]{3,2,1,0:T(8,128)(2,1)}, bf16[2,2,40,4096]{3,2,1,0:T(8,128)(2,1)}, u32[]{:S(2)}, u32[]{:S(2)}) collective-permute-start(bf16[2,2,40,4096]{3,2,1,0:T(8,128)(2,1)} %collective-permute-done.23), channel_id=1, source_target_pairs={{0,4},{4,0},{1,5},{5,1},{2,6},{6,2},{3,7},{7,3},{8,12},{12,8},{9,1... | collective-permute-start | bytes 3932168 | tf_op jit(solution)/shard_map/ppermute | solution.py:54
  538.6 125.4 %collective-permute-start.31 = (bf16[2,2,40,4096]{3,2,1,0:T(8,128)(2,1)}, bf16[2,2,40,4096]{3,2,1,0:T(8,128)(2,1)}, u32[]{:S(2)}, u32[]{:S(2)}) collective-permute-start(bf16[2,2,40,4096]{3,2,1,0:T(8,128)(2,1)} %collective-permute-done.27), channel_id=1, source_target_pairs={{0,4},{4,0},{1,5},{5,1},{2,6},{6,2},{3,7},{7,3},{8,12},{12,8},{9,1... | collective-permute-start | bytes 3932168 | tf_op jit(solution)/shard_map/ppermute | solution.py:54
  539.9 455.7 %collective-permute-start.15 = (bf16[2,256,1280]{2,1,0:T(8,128)(2,1)}, bf16[2,256,1280]{2,1,0:T(8,128)(2,1)}, u32[]{:S(2)}, u32[]{:S(2)}) collective-permute-start(bf16[2,256,1280]{2,1,0:T(8,128)(2,1)} %collective-permute-done.12.refs_0_), channel_id=1, source_target_pairs={{0,4},{4,0},{1,5},{5,1},{2,6},{6,2},{3,7},{7,3},{8,12},{12,8},{9,1... | collective-permute-start | bytes 3932168 | tf_op jit(solution)/shard_map/ppermute | solution.py:54
  564.9 441.7 %collective-permute-start.14 = (bf16[2,256,1280]{2,1,0:T(8,128)(2,1)}, bf16[2,256,1280]{2,1,0:T(8,128)(2,1)}, u32[]{:S(2)}, u32[]{:S(2)}) collective-permute-start(bf16[2,256,1280]{2,1,0:T(8,128)(2,1)} %collective-permute-done.13.refs_0_), channel_id=1, source_target_pairs={{0,4},{4,0},{1,5},{5,1},{2,6},{6,2},{3,7},{7,3},{8,12},{12,8},{9,1... | collective-permute-start | bytes 3932168 | tf_op jit(solution)/shard_map/ppermute | solution.py:54
  662.4 615.8 %collective-permute-start.47 = (bf16[2,4,128,1280]{3,2,1,0:T(8,128)(2,1)}, bf16[2,4,128,1280]{3,2,1,0:T(8,128)(2,1)}, u32[]{:S(2)}, u32[]{:S(2)}) collective-permute-start(bf16[2,4,128,1280]{3,2,1,0:T(8,128)(2,1)} %pad_maximum_fusion.5.refs_3_), channel_id=1, source_target_pairs={{0,1},{1,0},{2,3},{3,2},{4,5},{5,4},{6,7},{7,6},{8,9},{9,8},{10,11... | collective-permute-start | bytes 7864328 | tf_op jit(solution)/shard_map/ppermute | solution.py:54
  662.9 399.3 %collective-permute-start.45 = (bf16[2,4,128,1280]{3,2,1,0:T(8,128)(2,1)}, bf16[2,4,128,1280]{3,2,1,0:T(8,128)(2,1)}, u32[]{:S(2)}, u32[]{:S(2)}) collective-permute-start(bf16[2,4,128,1280]{3,2,1,0:T(8,128)(2,1)} %get-tuple-element.277), channel_id=1, source_target_pairs={{0,2},{2,0},{1,3},{3,1},{4,6},{6,4},{5,7},{7,5},{8,10},{10,8},{9,1... | collective-permute-start | bytes 7864328 | tf_op jit(solution)/shard_map/ppermute | solution.py:54
  990.8 102.0 %all-to-all-start = ((bf16[4,160,1792]{2,1,0:T(8,128)(2,1)}), bf16[4,160,1792]{2,1,0:T(8,128)(2,1)}, u32[]{:S(2)}, u32[]{:S(2)}) async-start(bf16[4,160,1792]{2,1,0:T(8,128)(2,1)} %param.37), calls=%async_computation | async-start | bytes 4587520 | tf_op jit(solution)/shard_map/all_to_all | solution.py:611
  1092.8 43.5 %collective-permute-start.48 = (bf16[4,160,1792]{2,1,0:T(8,128)(2,1)}, bf16[4,160,1792]{2,1,0:T(8,128)(2,1)}, u32[]{:S(2)}, u32[]{:S(2)}) collective-permute-start(bf16[4,160,1792]{2,1,0:T(8,128)(2,1)} %all-to-all-done.refs_0_), channel_id=1, source_target_pairs={{0,4},{4,0},{1,5},{5,1},{2,6},{6,2},{3,7},{7,3},{8,12},{12,8},{9,1... | collective-permute-start | bytes 6881288 | tf_op jit(solution)/shard_map/ppermute | solution.py:54
  1120.9 157.3 %collective-permute-start.61 = (bf16[2,128,1280]{2,1,0:T(8,128)(2,1)}, bf16[2,128,1280]{2,1,0:T(8,128)(2,1)}, u32[]{:S(2)}, u32[]{:S(2)}) collective-permute-start(bf16[2,128,1280]{2,1,0:T(8,128)(2,1)} %pad_maximum_fusion.25.refs_0_), channel_id=1, source_target_pairs={{0,1},{1,0},{2,3},{3,2},{4,5},{5,4},{6,7},{7,6},{8,9},{9,8},{10,11... | collective-permute-start | bytes 1966088 | tf_op jit(solution)/shard_map/ppermute | solution.py:54
  1121.9 178.3 %collective-permute-start.57 = (bf16[2,128,1280]{2,1,0:T(8,128)(2,1)S(1)}, bf16[2,128,1280]{2,1,0:T(8,128)(2,1)}, u32[]{:S(2)}, u32[]{:S(2)}) collective-permute-start(bf16[2,128,1280]{2,1,0:T(8,128)(2,1)S(1)} %pad_maximum_fusion.23.refs_0_), channel_id=1, source_target_pairs={{0,1},{1,0},{2,3},{3,2},{4,5},{5,4},{6,7},{7,6},{8,9},{9,8},{10,11... | collective-permute-start | bytes 1966088 | tf_op jit(solution)/shard_map/ppermute | solution.py:54
  1134.2 188.7 %collective-permute-start.53 = (bf16[2,128,1280]{2,1,0:T(8,128)(2,1)}, bf16[2,128,1280]{2,1,0:T(8,128)(2,1)}, u32[]{:S(2)}, u32[]{:S(2)}) collective-permute-start(bf16[2,128,1280]{2,1,0:T(8,128)(2,1)} %pad_maximum_fusion.21.refs_0_), channel_id=1, source_target_pairs={{0,1},{1,0},{2,3},{3,2},{4,5},{5,4},{6,7},{7,6},{8,9},{9,8},{10,11... | collective-permute-start | bytes 1966088 | tf_op jit(solution)/shard_map/ppermute | solution.py:54
  1136.3 208.7 %collective-permute-start.43 = (bf16[2,128,1280]{2,1,0:T(8,128)(2,1)S(1)}, bf16[2,128,1280]{2,1,0:T(8,128)(2,1)}, u32[]{:S(2)}, u32[]{:S(2)}) collective-permute-start(bf16[2,128,1280]{2,1,0:T(8,128)(2,1)S(1)} %pad_maximum_fusion.19.refs_0_), channel_id=1, source_target_pairs={{0,1},{1,0},{2,3},{3,2},{4,5},{5,4},{6,7},{7,6},{8,9},{9,8},{10,11... | collective-permute-start | bytes 1966088 | tf_op jit(solution)/shard_map/ppermute | solution.py:54
  1381.4 148.0 %collective-permute-start.120 = (bf16[4,112,1280]{2,1,0:T(8,128)(2,1)}, bf16[4,112,1280]{2,1,0:T(8,128)(2,1)}, u32[]{:S(2)}, u32[]{:S(2)}) collective-permute-start(bf16[4,112,1280]{2,1,0:T(8,128)(2,1)} %dynamic-slice_bitcast_fusion.3), channel_id=1, source_target_pairs={{0,4},{4,0},{1,5},{5,1},{2,6},{6,2},{3,7},{7,3},{8,12},{12,8},{9,1... | collective-permute-start | bytes 3440648 | tf_op jit(solution)/shard_map/ppermute | solution.py:54
  1411.2 223.4 %collective-permute-start.119 = (bf16[4,160,1792]{2,1,0:T(8,128)(2,1)}, bf16[4,160,1792]{2,1,0:T(8,128)(2,1)}, u32[]{:S(2)}, u32[]{:S(2)}) collective-permute-start(bf16[4,160,1792]{2,1,0:T(8,128)(2,1)} %dynamic-slice_bitcast_fusion), channel_id=1, source_target_pairs={{0,4},{4,0},{1,5},{5,1},{2,6},{6,2},{3,7},{7,3},{8,12},{12,8},{9,1... | collective-permute-start | bytes 6881288 | tf_op jit(solution)/shard_map/ppermute | solution.py:54
  1531.9 107.0 %all-to-all-start.4 = ((bf16[4,112,1280]{2,1,0:T(8,128)(2,1)}), bf16[4,112,1280]{2,1,0:T(8,128)(2,1)}, u32[]{:S(2)}, u32[]{:S(2)}) async-start(bf16[4,112,1280]{2,1,0:T(8,128)(2,1)} %fusion.22), calls=%async_computation.4 | async-start | bytes 2293760 | tf_op jit(solution)/shard_map/all_to_all | solution.py:729
  1638.9 146.0 %all-to-all-start.3 = ((bf16[4,160,1792]{2,1,0:T(8,128)(2,1)}), bf16[4,160,1792]{2,1,0:T(8,128)(2,1)}, u32[]{:S(2)}, u32[]{:S(2)}) async-start(bf16[4,160,1792]{2,1,0:T(8,128)(2,1)} %fusion), calls=%async_computation.3 | async-start | bytes 4587520 | tf_op jit(solution)/shard_map/all_to_all | solution.py:729
  1677.6 153.4 %collective-permute-start.111 = (bf16[4,2,2,40,4096]{4,3,0,1,2:T(8,128)(2,1)}, bf16[4,2,2,40,4096]{4,3,0,1,2:T(8,128)(2,1)}, u32[]{:S(2)}, u32[]{:S(2)}) collective-permute-start(bf16[4,2,2,40,4096]{4,3,0,1,2:T(8,128)(2,1)} %pad_maximum_fusion.1), channel_id=1, source_target_pairs={{0,4},{4,0},{1,5},{5,1},{2,6},{6,2},{3,7},{7,3},{8,12},{12,8},{9,1... | collective-permute-start | bytes 15728648 | tf_op jit(solution)/shard_map/ppermute | solution.py:54
  1680.1 80.5 %collective-permute-start.90 = (bf16[2,256,1280]{2,1,0:T(8,128)(2,1)S(1)}, bf16[2,256,1280]{2,1,0:T(8,128)(2,1)S(1)}, u32[]{:S(2)}, u32[]{:S(2)}) collective-permute-start(bf16[2,256,1280]{2,1,0:T(8,128)(2,1)S(1)} %copy-done.25), channel_id=1, source_target_pairs={{0,4},{4,0},{1,5},{5,1},{2,6},{6,2},{3,7},{7,3},{8,12},{12,8},{9,1... | collective-permute-start | bytes 3932168 | tf_op jit(solution)/shard_map/ppermute | solution.py:54
  1686.9 57.5 %collective-permute-start.81 = (bf16[4,2,128,1280]{3,2,0,1:T(8,128)(2,1)S(1)}, bf16[4,2,128,1280]{3,2,0,1:T(8,128)(2,1)S(1)}, u32[]{:S(2)}, u32[]{:S(2)}) collective-permute-start(bf16[4,2,128,1280]{3,2,0,1:T(8,128)(2,1)S(1)} %copy.189), channel_id=1, source_target_pairs={{0,2},{2,0},{1,3},{3,1},{4,6},{6,4},{5,7},{7,5},{8,10},{10,8},{9,1... | collective-permute-start | bytes 7864328 | tf_op jit(solution)/shard_map/ppermute | solution.py:54
  1700.1 56.8 %collective-permute-start.83 = (bf16[4,2,128,1280]{3,2,0,1:T(8,128)(2,1)S(1)}, bf16[4,2,128,1280]{3,2,0,1:T(8,128)(2,1)S(1)}, u32[]{:S(2)}, u32[]{:S(2)}) collective-permute-start(bf16[4,2,128,1280]{3,2,0,1:T(8,128)(2,1)S(1)} %copy.191), channel_id=1, source_target_pairs={{0,1},{1,0},{2,3},{3,2},{4,5},{5,4},{6,7},{7,6},{8,9},{9,8},{10,11... | collective-permute-start | bytes 7864328 | tf_op jit(solution)/shard_map/ppermute | solution.py:54
  1708.2 88.0 %collective-permute-start.92 = (bf16[2,256,1280]{2,1,0:T(8,128)(2,1)}, bf16[2,256,1280]{2,1,0:T(8,128)(2,1)}, u32[]{:S(2)}, u32[]{:S(2)}) collective-permute-start(bf16[2,256,1280]{2,1,0:T(8,128)(2,1)} %get-tuple-element.189), channel_id=1, source_target_pairs={{0,4},{4,0},{1,5},{5,1},{2,6},{6,2},{3,7},{7,3},{8,12},{12,8},{9,1... | collective-permute-start | bytes 3932168 | tf_op jit(solution)/shard_map/ppermute | solution.py:54
  1818.4 51.8 %collective-permute-start.93 = (bf16[2,256,1280]{2,1,0:T(8,128)(2,1)S(1)}, bf16[2,256,1280]{2,1,0:T(8,128)(2,1)}, u32[]{:S(2)}, u32[]{:S(2)}) collective-permute-start(bf16[2,256,1280]{2,1,0:T(8,128)(2,1)S(1)} %add_convert_fusion.2), channel_id=1, source_target_pairs={{0,8},{8,16},{16,24},{24,0},{1,9},{9,17},{17,25},{25,1},{2,10},{10... | collective-permute-start | bytes 3932168 | tf_op jit(solution)/shard_map/ppermute | solution.py:54
  1839.0 59.9 %collective-permute-start.114 = (bf16[2,2,40,4096]{3,2,0,1:T(8,128)(2,1)}, bf16[2,2,40,4096]{3,2,0,1:T(8,128)(2,1)}, u32[]{:S(2)}, u32[]{:S(2)}) collective-permute-start(bf16[2,2,40,4096]{3,2,0,1:T(8,128)(2,1)} %dynamic-slice_bitcast_fusion.1), channel_id=1, source_target_pairs={{0,1},{1,0},{2,3},{3,2},{4,5},{5,4},{6,7},{7,6},{8,9},{9,8},{10,11... | collective-permute-start | bytes 3932168 | tf_op jit(solution)/shard_map/ppermute | solution.py:54
  1841.2 60.6 %collective-permute-start.112 = (bf16[2,2,40,4096]{3,2,0,1:T(8,128)(2,1)}, bf16[2,2,40,4096]{3,2,0,1:T(8,128)(2,1)}, u32[]{:S(2)}, u32[]{:S(2)}) collective-permute-start(bf16[2,2,40,4096]{3,2,0,1:T(8,128)(2,1)} %dynamic-slice_bitcast_fusion.2), channel_id=1, source_target_pairs={{0,2},{2,0},{1,3},{3,1},{4,6},{6,4},{5,7},{7,5},{8,10},{10,8},{9,1... | collective-permute-start | bytes 3932168 | tf_op jit(solution)/shard_map/ppermute | solution.py:54
  (243 other events, 6995.2 us)

commit v3 on v2

--- a/solution.py
+++ b/solution.py
@@ -109,17 +109,14 @@
     edges = np.cumsum([0] + list(widths))
     columns = [(int(low), int(high)) for low, high in zip(edges[:-1], edges[1:])]
     n = sum(counts)
-    anywhere = pl.BlockSpec(memory_space=pl.ANY)
     outs = pl.pallas_call(
         functools.partial(place_kernel, counts, columns),
-        grid_spec=pltpu.PrefetchScalarGridSpec(
-            num_scalar_prefetch=1,
-            grid=(1,),
-            in_specs=[anywhere] * len(pieces),
-            out_specs=[anywhere] * len(widths),
-            scratch_shapes=[pltpu.SemaphoreType.DMA((len(widths),))],
-        ),
+        in_specs=[pl.BlockSpec(memory_space=pltpu.SMEM)]
+        + [pl.BlockSpec(memory_space=pl.ANY)] * len(pieces),
+        out_specs=[pl.BlockSpec(memory_space=pltpu.VMEM)] * len(widths),
+        scratch_shapes=[pltpu.SemaphoreType.DMA((len(widths),))],
         out_shape=[jax.ShapeDtypeStruct((n, rows, w), pieces[0].dtype) for w in widths],
+        compiler_params=pltpu.CompilerParams(vmem_limit_bytes=VMEM_LIMIT // 2),
         cost_estimate=pl.CostEstimate(
             flops=0, bytes_accessed=4 * n * rows * total, transcendentals=0
         ),

time: 2000 us -> 1180 us (0.59)
  Pallas kernels: 1030 us -> 201 us
    pallas_call x4, Pallas kernels: 841 us -> 11.1 us  [place(): pl.pallas_call(functools.partial(place_kernel, counts, columns), in_specs...]
    unnamed x304 -> x324, local copies, waits for them, and re-layouts: 41.9 us -> 52.5 us
  transfers between devices with their start and end apart: 126 -> 126, of which waited for: 59 -> 60; matrix products, arithmetic and copies ran while one was open for 10% -> 17% of each run, Pallas kernels for 51% -> 15%
where the time goes in v3:
time: 1180 us; the launch traced here: 1170 us
  waiting for transfers between devices  554 us (47%)
  Pallas kernels  201 us (17%)
  starting transfers between devices  151 us (13%)
  local copies, waits for them, and re-layouts  106 us (9%)
  other arithmetic  94.7 us (8%)
  matrix products  60.5 us (5%)
    ppermute x121, waiting for transfers between devices, shift(): return lax.ppermute(value, axis, [(i, (i + 1) % n) for i in range(n)])  554 us
    ppermute x121, starting transfers between devices, shift(): return lax.ppermute(value, axis, [(i, (i + 1) % n) for i in range(n)])  127 us
    pallas_call x4, Pallas kernels, expert_chunk(): pl.pallas_call(functools.partial(expert_kernel, slots, na, nb, n_kept), g...  89.1 us
    dot_general x21, matrix products, dot(): return lax.dot_general(a, b, (dims, ((), ())), preferred_element_type=F32)  60.5 us
    unnamed x324, local copies, waits for them, and re-layouts  52.5 us
    pallas_call x4, Pallas kernels, attend_back_chunk(): pl.pallas_call(functools.partial(attend_back_kernel, n_ctx, n, first, las...  45.9 us
    pallas_call x4, Pallas kernels, attend_chunk(): pl.pallas_call(functools.partial(attend_kernel, n_ctx, n, first, last), g...  37.7 us
  transfers between devices with their start and end apart: 126, of which 60 were waited for; matrix products, arithmetic and copies ran while one was open for 17% of the time, Pallas kernels for 15%

profile of v3, /device:TPU:0, one launch (start us, length us, event | category | flops | bytes accessed | tf_op | source)
XLA Modules:
  0.0 1170.7 jit_solution(9403818801401802117)
XLA Ops:
  15.1 10.5 collective-permute-done.3
  53.8 12.7 %collective-permute-done.19 = bf16[256,1280]{1,0:T(8,128)(2,1)} collective-permute-done((bf16[256,1280]{1,0:T(8,128)(2,1)}, bf16[256,1280]{1,0:T(8,128)(2,1)}, u32[]{:S(2)}, u32[]{:S(2)}) %collective-permute-start.19) | collective-permute-done | bytes 655392 | tf_op jit(solution)/shard_map/ppermute | solution.py:54
  70.6 10.9 collective-permute-done.20
  92.9 11.5 collective-permute-done.24
  149.7 31.2 %collective-permute-done.32 = f32[16,256]{1,0:T(8,128)S(1)} collective-permute-done((f32[16,256]{1,0:T(8,128)S(1)}, f32[16,256]{1,0:T(8,128)S(1)}, u32[]{:S(2)}, u32[]{:S(2)}) %collective-permute-start.32) | collective-permute-done | bytes 16416 | tf_op jit(solution)/shard_map/ppermute | solution.py:54
  208.2 21.5 %collective-permute-done.12.refs_0_ = bf16[2,256,1280]{2,1,0:T(8,128)(2,1)} collective-permute-done((bf16[2,256,1280]{2,1,0:T(8,128)(2,1)}, bf16[2,256,1280]{2,1,0:T(8,128)(2,1)}, u32[]{:S(2)}, u32[]{:S(2)}) %collective-permute-start.12) | collective-permute-done | bytes 1310752 | tf_op jit(solution)/shard_map/ppermute | solution.py:54
  237.3 24.9 %collective-permute-done.13.refs_0_ = bf16[2,256,1280]{2,1,0:T(8,128)(2,1)} collective-permute-done((bf16[2,256,1280]{2,1,0:T(8,128)(2,1)}, bf16[2,256,1280]{2,1,0:T(8,128)(2,1)}, u32[]{:S(2)}, u32[]{:S(2)}) %collective-permute-start.13) | collective-permute-done | bytes 1310752 | tf_op jit(solution)/shard_map/ppermute | solution.py:54
  401.2 10.8 collective-permute-done.39
  426.7 13.5 %collective-permute-done.42 = bf16[128,1280]{1,0:T(8,128)(2,1)S(1)} collective-permute-done((bf16[128,1280]{1,0:T(8,128)(2,1)S(1)}, bf16[128,1280]{1,0:T(8,128)(2,1)S(1)}, u32[]{:S(2)}, u32[]{:S(2)}) %collective-permute-start.42) | collective-permute-done | bytes 327712 | tf_op jit(solution)/shard_map/ppermute | solution.py:54
  460.9 22.1 %experts.4 = (bf16[2,128,1280]{2,1,0:T(8,128)(2,1)}, bf16[2,128,1280]{2,1,0:T(8,128)(2,1)}, bf16[2,128,1280]{2,1,0:T(8,128)(2,1)}, bf16[2,128,1280]{2,1,0:T(8,12...) custom-call(s32[1]{0:T(128)} %bitcast.50.e_ref, ...), custom_call_target="tpu_custom_call" | custom-call | flops 9688842240 | bytes 30000000 | tf_op jit(solution)/shard_map/experts/pallas_call | solution.py:501
  483.9 22.5 %experts.5 = (bf16[2,128,1280]{2,1,0:T(8,128)(2,1)}, bf16[2,128,1280]{2,1,0:T(8,128)(2,1)}, bf16[2,128,1280]{2,1,0:T(8,128)(2,1)}, bf16[2,128,1280]{2,1,0:T(8,12...) custom-call(s32[1]{0:T(128)} %bitcast.50.e_ref, ...), custom_call_target="tpu_custom_call", output_to_operand_aliasing={{5}: (11, {}), {6}: (12, {}), {7}: (13, {}), {8}: (14, {}),... | custom-call | flops 9688842240 | bytes 30000000 | tf_op jit(solution)/shard_map/experts/pallas_call | solution.py:501
  507.2 22.1 %experts.6 = (bf16[2,128,1280]{2,1,0:T(8,128)(2,1)}, bf16[2,128,1280]{2,1,0:T(8,128)(2,1)}, bf16[2,128,1280]{2,1,0:T(8,128)(2,1)}, bf16[2,128,1280]{2,1,0:T(8,12...) custom-call(s32[1]{0:T(128)} %bitcast.50.e_ref, ...), custom_call_target="tpu_custom_call", output_to_operand_aliasing={{5}: (11, {}), {6}: (12, {}), {7}: (13, {}), {8}: (14, {}),... | custom-call | flops 9688842240 | bytes 30000000 | tf_op jit(solution)/shard_map/experts/pallas_call | solution.py:501
  530.3 22.4 %experts.7 = (bf16[2,128,1280]{2,1,0:T(8,128)(2,1)}, bf16[2,128,1280]{2,1,0:T(8,128)(2,1)}, bf16[2,128,1280]{2,1,0:T(8,128)(2,1)}, bf16[2,128,1280]{2,1,0:T(8,12...) custom-call(s32[1]{0:T(128)} %bitcast.50.e_ref, ...), custom_call_target="tpu_custom_call", output_to_operand_aliasing={{5}: (11, {}), {6}: (12, {}), {7}: (13, {}), {8}: (14, {}),... | custom-call | flops 9688842240 | bytes 30000000 | tf_op jit(solution)/shard_map/experts/pallas_call | solution.py:501
  552.7 11.4 convolution_convert_fusion.6
  575.0 18.6 %convolution_convert_fusion = bf16[1280,1792]{1,0:T(8,128)(2,1)S(1)} fusion(bf16[2816,1280]{1,0:T(8,128)(2,1)} %get-tuple-element.193, bf16[2816,1792]{1,0:T(8,128)(2,1)} %get-tuple-element.194), kind=kOutput, calls=%fused_computation.2 | convolution fusion | flops 12920750080 | bytes 21889024 | tf_op jit(solution)/shard_map/dot_general | solution.py:45
  601.5 12.7 %collective-permute-done.64 = bf16[2,128,1280]{2,1,0:T(8,128)(2,1)} collective-permute-done((bf16[2,128,1280]{2,1,0:T(8,128)(2,1)}, bf16[2,128,1280]{2,1,0:T(8,128)(2,1)}, u32[]{:S(2)}, u32[]{:S(2)}) %collective-permute-start.64) | collective-permute-done | bytes 655392 | tf_op jit(solution)/shard_map/ppermute | solution.py:54
  644.9 11.3 collective-permute-done.79
  657.9 12.0 %collective-permute-done.68 = bf16[128,1280]{1,0:T(8,128)(2,1)S(1)} collective-permute-done((bf16[128,1280]{1,0:T(8,128)(2,1)S(1)}, bf16[128,1280]{1,0:T(8,128)(2,1)S(1)}, u32[]{:S(2)}, u32[]{:S(2)}) %collective-permute-start.68) | collective-permute-done | bytes 327712 | tf_op jit(solution)/shard_map/ppermute | solution.py:54
  683.6 12.9 %collective-permute-done.66 = bf16[256,1280]{1,0:T(8,128)(2,1)S(1)} collective-permute-done((bf16[256,1280]{1,0:T(8,128)(2,1)S(1)}, bf16[256,1280]{1,0:T(8,128)(2,1)S(1)}, u32[]{:S(2)}, u32[]{:S(2)}) %collective-permute-start.66) | collective-permute-done | bytes 655392 | tf_op jit(solution)/shard_map/ppermute | solution.py:54
  698.3 14.2 %collective-permute-done.71 = bf16[256,1280]{1,0:T(8,128)(2,1)S(1)} collective-permute-done((bf16[256,1280]{1,0:T(8,128)(2,1)S(1)}, bf16[256,1280]{1,0:T(8,128)(2,1)S(1)}, u32[]{:S(2)}, u32[]{:S(2)}) %collective-permute-start.71) | collective-permute-done | bytes 655392 | tf_op jit(solution)/shard_map/ppermute | solution.py:54
  722.4 10.9 collective-permute-done.76
  742.7 11.1 attend_back.4
  756.3 11.2 attend_back.5
  768.6 12.4 %attend_back.6 = (f32[256,1280]{1,0:T(8,128)S(1)}, f32[2,256,1280]{2,1,0:T(8,128)S(1)}, bf16[2,256,1280]{2,1,0:T(8,128)(2,1)}) custom-call(s32[3]{0:T(128)S(1)} %pad_add_fusion.place_ref, bf16[256,1280]{1,0:T(8,128)(2,1)S(1)} %copy-done.42, bf16[256,1280]{1,0:T(8,128)(2,1)S(1)} %convolution_convert_fusion.8.do_ref, ...), custom_call_target="tpu_custom_call" | custom-call | flops 6710886400 | bytes 5242880 | tf_op jit(solution)/shard_map/attend_back/pallas_call | solution.py:382
  781.1 11.2 attend_back.7
  892.1 36.2 %collective-permute-done.81 = bf16[4,2,128,1280]{3,2,0,1:T(8,128)(2,1)S(1)} collective-permute-done((bf16[4,2,128,1280]{3,2,0,1:T(8,128)(2,1)S(1)}, bf16[4,2,128,1280]{3,2,0,1:T(8,128)(2,1)S(1)}, u32[]{:S(2)}, u32[]{:S(2)}) %collective-permute-start.81) | collective-permute-done | bytes 2621472 | tf_op jit(solution)/shard_map/ppermute | solution.py:54
  945.4 19.2 %collective-permute-done.89 = bf16[2,256,1280]{2,1,0:T(8,128)(2,1)S(1)} collective-permute-done((bf16[2,256,1280]{2,1,0:T(8,128)(2,1)S(1)}, bf16[2,256,1280]{2,1,0:T(8,128)(2,1)S(1)}, u32[]{:S(2)}, u32[]{:S(2)}) %collective-permute-start.89) | collective-permute-done | bytes 1310752 | tf_op jit(solution)/shard_map/ppermute | solution.py:54
  980.1 20.1 %collective-permute-done.91 = bf16[2,256,1280]{2,1,0:T(8,128)(2,1)} collective-permute-done((bf16[2,256,1280]{2,1,0:T(8,128)(2,1)}, bf16[2,256,1280]{2,1,0:T(8,128)(2,1)}, u32[]{:S(2)}, u32[]{:S(2)}) %collective-permute-start.91) | collective-permute-done | bytes 1310752 | tf_op jit(solution)/shard_map/ppermute | solution.py:54
  1003.0 11.1 collective-permute-done.85
  1026.6 25.7 %collective-permute-done.86 = bf16[256,1280]{1,0:T(8,128)(2,1)S(1)} collective-permute-done((bf16[256,1280]{1,0:T(8,128)(2,1)S(1)}, bf16[256,1280]{1,0:T(8,128)(2,1)S(1)}, u32[]{:S(2)}, u32[]{:S(2)}) %collective-permute-start.86) | collective-permute-done | bytes 655392 | tf_op jit(solution)/shard_map/ppermute | solution.py:54
  1089.1 12.9 %collective-permute-done.115 = bf16[2,40,4096]{2,1,0:T(8,128)(2,1)S(1)} collective-permute-done((bf16[2,40,4096]{2,1,0:T(8,128)(2,1)S(1)}, bf16[2,40,4096]{2,1,0:T(8,128)(2,1)S(1)}, u32[]{:S(2)}, u32[]{:S(2)}) %collective-permute-start.115) | collective-permute-done | bytes 655392 | tf_op jit(solution)/shard_map/ppermute | solution.py:54
  1108.1 16.1 %collective-permute-done.98 = bf16[2,2,40,2688]{3,2,0,1:T(8,128)(2,1)S(1)} collective-permute-done((bf16[2,2,40,2688]{3,2,0,1:T(8,128)(2,1)S(1)}, bf16[2,2,40,2688]{3,2,0,1:T(8,128)(2,1)S(1)}, u32[]{:S(2)}, u32[]{:S(2)}) %collective-permute-start.98) | collective-permute-done | bytes 860192 | tf_op jit(solution)/shard_map/ppermute | solution.py:54
  (798 shorter events, 639.6 us)
Async XLA Ops:
  40.5 41.7 %collective-permute-start.2 = (bf16[2,2,40,3968]{3,2,1,0:T(8,128)(2,1)S(1)}, bf16[2,2,40,3968]{3,2,1,0:T(8,128)(2,1)}, u32[]{:S(2)}, u32[]{:S(2)}) collective-permute-start(bf16[2,2,40,3968]{3,2,1,0:T(8,128)(2,1)S(1)} %pad_maximum_fusion.13), channel_id=1, source_target_pairs={{0,2},{2,0},{1,3},{3,1},{4,6},{6,4},{5,7},{7,5},{8,10},{10,8},{9,1... | collective-permute-start | bytes 3809288 | tf_op jit(solution)/shard_map/ppermute | solution.py:54
  138.2 58.2 %collective-permute-start.11 = (bf16[2,256,1280]{2,1,0:T(8,128)(2,1)}, bf16[2,256,1280]{2,1,0:T(8,128)(2,1)}, u32[]{:S(2)}, u32[]{:S(2)}) collective-permute-start(bf16[2,256,1280]{2,1,0:T(8,128)(2,1)} %get-tuple-element.107.refs_0_), channel_id=1, source_target_pairs={{0,8},{8,16},{16,24},{24,0},{1,9},{9,17},{17,25},{25,1},{2,10},{10... | collective-permute-start | bytes 3932168 | tf_op jit(solution)/shard_map/ppermute | solution.py:54
  139.8 58.7 %collective-permute-start.23 = (bf16[2,2,40,4096]{3,2,1,0:T(8,128)(2,1)S(1)}, bf16[2,2,40,4096]{3,2,1,0:T(8,128)(2,1)}, u32[]{:S(2)}, u32[]{:S(2)}) collective-permute-start(bf16[2,2,40,4096]{3,2,1,0:T(8,128)(2,1)S(1)} %pad_maximum_fusion.7), channel_id=1, source_target_pairs={{0,2},{2,0},{1,3},{3,1},{4,6},{6,4},{5,7},{7,5},{8,10},{10,8},{9,1... | collective-permute-start | bytes 3932168 | tf_op jit(solution)/shard_map/ppermute | solution.py:54
  141.6 57.5 %collective-permute-start.27 = (bf16[2,2,40,4096]{3,2,1,0:T(8,128)(2,1)S(1)}, bf16[2,2,40,4096]{3,2,1,0:T(8,128)(2,1)}, u32[]{:S(2)}, u32[]{:S(2)}) collective-permute-start(bf16[2,2,40,4096]{3,2,1,0:T(8,128)(2,1)S(1)} %pad_maximum_fusion.8), channel_id=1, source_target_pairs={{0,1},{1,0},{2,3},{3,2},{4,5},{5,4},{6,7},{7,6},{8,9},{9,8},{10,11... | collective-permute-start | bytes 3932168 | tf_op jit(solution)/shard_map/ppermute | solution.py:54
  142.7 65.5 %all-to-all-start.1 = ((bf16[4,112,1280]{2,1,0:T(8,128)(2,1)}), bf16[4,112,1280]{2,1,0:T(8,128)(2,1)}, u32[]{:S(2)}, u32[]{:S(2)}) async-start(bf16[4,112,1280]{2,1,0:T(8,128)(2,1)} %param.38), calls=%async_computation.1 | async-start | bytes 2293760 | tf_op jit(solution)/shard_map/all_to_all | solution.py:608
  230.0 63.5 %collective-permute-start.30 = (bf16[2,2,40,4096]{3,2,1,0:T(8,128)(2,1)S(1)}, bf16[2,2,40,4096]{3,2,1,0:T(8,128)(2,1)}, u32[]{:S(2)}, u32[]{:S(2)}) collective-permute-start(bf16[2,2,40,4096]{3,2,1,0:T(8,128)(2,1)S(1)} %pad_maximum_fusion.8), channel_id=1, source_target_pairs={{0,4},{4,0},{1,5},{5,1},{2,6},{6,2},{3,7},{7,3},{8,12},{12,8},{9,1... | collective-permute-start | bytes 3932168 | tf_op jit(solution)/shard_map/ppermute | solution.py:54
  230.1 63.9 %collective-permute-start.29 = (bf16[2,2,40,4096]{3,2,1,0:T(8,128)(2,1)}, bf16[2,2,40,4096]{3,2,1,0:T(8,128)(2,1)}, u32[]{:S(2)}, u32[]{:S(2)}) collective-permute-start(bf16[2,2,40,4096]{3,2,1,0:T(8,128)(2,1)} %collective-permute-done.23), channel_id=1, source_target_pairs={{0,4},{4,0},{1,5},{5,1},{2,6},{6,2},{3,7},{7,3},{8,12},{12,8},{9,1... | collective-permute-start | bytes 3932168 | tf_op jit(solution)/shard_map/ppermute | solution.py:54
  235.3 59.8 %collective-permute-start.31 = (bf16[2,2,40,4096]{3,2,1,0:T(8,128)(2,1)}, bf16[2,2,40,4096]{3,2,1,0:T(8,128)(2,1)}, u32[]{:S(2)}, u32[]{:S(2)}) collective-permute-start(bf16[2,2,40,4096]{3,2,1,0:T(8,128)(2,1)} %collective-permute-done.27), channel_id=1, source_target_pairs={{0,4},{4,0},{1,5},{5,1},{2,6},{6,2},{3,7},{7,3},{8,12},{12,8},{9,1... | collective-permute-start | bytes 3932168 | tf_op jit(solution)/shard_map/ppermute | solution.py:54
  236.6 78.2 %collective-permute-start.15 = (bf16[2,256,1280]{2,1,0:T(8,128)(2,1)}, bf16[2,256,1280]{2,1,0:T(8,128)(2,1)}, u32[]{:S(2)}, u32[]{:S(2)}) collective-permute-start(bf16[2,256,1280]{2,1,0:T(8,128)(2,1)} %collective-permute-done.12.refs_0_), channel_id=1, source_target_pairs={{0,4},{4,0},{1,5},{5,1},{2,6},{6,2},{3,7},{7,3},{8,12},{12,8},{9,1... | collective-permute-start | bytes 3932168 | tf_op jit(solution)/shard_map/ppermute | solution.py:54
  262.2 64.8 %collective-permute-start.14 = (bf16[2,256,1280]{2,1,0:T(8,128)(2,1)}, bf16[2,256,1280]{2,1,0:T(8,128)(2,1)}, u32[]{:S(2)}, u32[]{:S(2)}) collective-permute-start(bf16[2,256,1280]{2,1,0:T(8,128)(2,1)} %collective-permute-done.13.refs_0_), channel_id=1, source_target_pairs={{0,4},{4,0},{1,5},{5,1},{2,6},{6,2},{3,7},{7,3},{8,12},{12,8},{9,1... | collective-permute-start | bytes 3932168 | tf_op jit(solution)/shard_map/ppermute | solution.py:54
  293.5 166.6 %collective-permute-start.47 = (bf16[2,4,128,1280]{3,2,1,0:T(8,128)(2,1)}, bf16[2,4,128,1280]{3,2,1,0:T(8,128)(2,1)}, u32[]{:S(2)}, u32[]{:S(2)}) collective-permute-start(bf16[2,4,128,1280]{3,2,1,0:T(8,128)(2,1)} %pad_maximum_fusion.5.refs_3_), channel_id=1, source_target_pairs={{0,1},{1,0},{2,3},{3,2},{4,5},{5,4},{6,7},{7,6},{8,9},{9,8},{10,11... | collective-permute-start | bytes 7864328 | tf_op jit(solution)/shard_map/ppermute | solution.py:54
  294.1 87.3 %collective-permute-start.45 = (bf16[2,4,128,1280]{3,2,1,0:T(8,128)(2,1)}, bf16[2,4,128,1280]{3,2,1,0:T(8,128)(2,1)}, u32[]{:S(2)}, u32[]{:S(2)}) collective-permute-start(bf16[2,4,128,1280]{3,2,1,0:T(8,128)(2,1)} %get-tuple-element.277), channel_id=1, source_target_pairs={{0,2},{2,0},{1,3},{3,1},{4,6},{6,4},{5,7},{7,5},{8,10},{10,8},{9,1... | collective-permute-start | bytes 7864328 | tf_op jit(solution)/shard_map/ppermute | solution.py:54
  310.8 101.2 %all-to-all-start = ((bf16[4,160,1792]{2,1,0:T(8,128)(2,1)}), bf16[4,160,1792]{2,1,0:T(8,128)(2,1)S(1)}, u32[]{:S(2)}, u32[]{:S(2)}) async-start(bf16[4,160,1792]{2,1,0:T(8,128)(2,1)} %param.37), calls=%async_computation | async-start | bytes 4587520 | tf_op jit(solution)/shard_map/all_to_all | solution.py:608
  412.0 43.6 %collective-permute-start.48 = (bf16[4,160,1792]{2,1,0:T(8,128)(2,1)S(1)}, bf16[4,160,1792]{2,1,0:T(8,128)(2,1)S(1)}, u32[]{:S(2)}, u32[]{:S(2)}) collective-permute-start(bf16[4,160,1792]{2,1,0:T(8,128)(2,1)S(1)} %all-to-all-done.refs_0_), channel_id=1, source_target_pairs={{0,4},{4,0},{1,5},{5,1},{2,6},{6,2},{3,7},{7,3},{8,12},{12,8},{9,1... | collective-permute-start | bytes 6881288 | tf_op jit(solution)/shard_map/ppermute | solution.py:54
  441.2 41.8 %collective-permute-start.57 = (bf16[2,128,1280]{2,1,0:T(8,128)(2,1)S(1)}, bf16[2,128,1280]{2,1,0:T(8,128)(2,1)S(1)}, u32[]{:S(2)}, u32[]{:S(2)}) collective-permute-start(bf16[2,128,1280]{2,1,0:T(8,128)(2,1)S(1)} %copy-done.93), channel_id=1, source_target_pairs={{0,1},{1,0},{2,3},{3,2},{4,5},{5,4},{6,7},{7,6},{8,9},{9,8},{10,11... | collective-permute-start | bytes 1966088 | tf_op jit(solution)/shard_map/ppermute | solution.py:54
  453.4 52.9 %collective-permute-start.53 = (bf16[2,128,1280]{2,1,0:T(8,128)(2,1)S(1)}, bf16[2,128,1280]{2,1,0:T(8,128)(2,1)S(1)}, u32[]{:S(2)}, u32[]{:S(2)}) collective-permute-start(bf16[2,128,1280]{2,1,0:T(8,128)(2,1)S(1)} %pad_maximum_fusion.21.refs_0_), channel_id=1, source_target_pairs={{0,1},{1,0},{2,3},{3,2},{4,5},{5,4},{6,7},{7,6},{8,9},{9,8},{10,11... | collective-permute-start | bytes 1966088 | tf_op jit(solution)/shard_map/ppermute | solution.py:54
  455.6 73.8 %collective-permute-start.43 = (bf16[2,128,1280]{2,1,0:T(8,128)(2,1)S(1)}, bf16[2,128,1280]{2,1,0:T(8,128)(2,1)S(1)}, u32[]{:S(2)}, u32[]{:S(2)}) collective-permute-start(bf16[2,128,1280]{2,1,0:T(8,128)(2,1)S(1)} %pad_maximum_fusion.19.refs_0_), channel_id=1, source_target_pairs={{0,1},{1,0},{2,3},{3,2},{4,5},{5,4},{6,7},{7,6},{8,9},{9,8},{10,11... | collective-permute-start | bytes 1966088 | tf_op jit(solution)/shard_map/ppermute | solution.py:54
  566.5 147.9 %collective-permute-start.120 = (bf16[4,112,1280]{2,1,0:T(8,128)(2,1)}, bf16[4,112,1280]{2,1,0:T(8,128)(2,1)}, u32[]{:S(2)}, u32[]{:S(2)}) collective-permute-start(bf16[4,112,1280]{2,1,0:T(8,128)(2,1)} %dynamic-slice_bitcast_fusion.3), channel_id=1, source_target_pairs={{0,4},{4,0},{1,5},{5,1},{2,6},{6,2},{3,7},{7,3},{8,12},{12,8},{9,1... | collective-permute-start | bytes 3440648 | tf_op jit(solution)/shard_map/ppermute | solution.py:54
  596.4 222.2 %collective-permute-start.119 = (bf16[4,160,1792]{2,1,0:T(8,128)(2,1)}, bf16[4,160,1792]{2,1,0:T(8,128)(2,1)}, u32[]{:S(2)}, u32[]{:S(2)}) collective-permute-start(bf16[4,160,1792]{2,1,0:T(8,128)(2,1)} %dynamic-slice_bitcast_fusion), channel_id=1, source_target_pairs={{0,4},{4,0},{1,5},{5,1},{2,6},{6,2},{3,7},{7,3},{8,12},{12,8},{9,1... | collective-permute-start | bytes 6881288 | tf_op jit(solution)/shard_map/ppermute | solution.py:54
  717.0 105.7 %all-to-all-start.4 = ((bf16[4,112,1280]{2,1,0:T(8,128)(2,1)}), bf16[4,112,1280]{2,1,0:T(8,128)(2,1)}, u32[]{:S(2)}, u32[]{:S(2)}) async-start(bf16[4,112,1280]{2,1,0:T(8,128)(2,1)} %fusion.22), calls=%async_computation.4 | async-start | bytes 2293760 | tf_op jit(solution)/shard_map/all_to_all | solution.py:726
  822.7 146.1 %all-to-all-start.3 = ((bf16[4,160,1792]{2,1,0:T(8,128)(2,1)}), bf16[4,160,1792]{2,1,0:T(8,128)(2,1)}, u32[]{:S(2)}, u32[]{:S(2)}) async-start(bf16[4,160,1792]{2,1,0:T(8,128)(2,1)} %fusion), calls=%async_computation.3 | async-start | bytes 4587520 | tf_op jit(solution)/shard_map/all_to_all | solution.py:726
  833.0 38.9 %collective-permute-start.94 = (bf16[2,256,1280]{2,1,0:T(8,128)(2,1)S(1)}, bf16[2,256,1280]{2,1,0:T(8,128)(2,1)S(1)}, u32[]{:S(2)}, u32[]{:S(2)}) collective-permute-start(bf16[2,256,1280]{2,1,0:T(8,128)(2,1)S(1)} %copy-done.37), channel_id=1, source_target_pairs={{0,4},{4,0},{1,5},{5,1},{2,6},{6,2},{3,7},{7,3},{8,12},{12,8},{9,1... | collective-permute-start | bytes 3932168 | tf_op jit(solution)/shard_map/ppermute | solution.py:54
  861.5 153.4 %collective-permute-start.111 = (bf16[4,2,2,40,4096]{4,3,0,1,2:T(8,128)(2,1)}, bf16[4,2,2,40,4096]{4,3,0,1,2:T(8,128)(2,1)}, u32[]{:S(2)}, u32[]{:S(2)}) collective-permute-start(bf16[4,2,2,40,4096]{4,3,0,1,2:T(8,128)(2,1)} %pad_maximum_fusion.1), channel_id=1, source_target_pairs={{0,4},{4,0},{1,5},{5,1},{2,6},{6,2},{3,7},{7,3},{8,12},{12,8},{9,1... | collective-permute-start | bytes 15728648 | tf_op jit(solution)/shard_map/ppermute | solution.py:54
  864.0 80.5 %collective-permute-start.90 = (bf16[2,256,1280]{2,1,0:T(8,128)(2,1)S(1)}, bf16[2,256,1280]{2,1,0:T(8,128)(2,1)S(1)}, u32[]{:S(2)}, u32[]{:S(2)}) collective-permute-start(bf16[2,256,1280]{2,1,0:T(8,128)(2,1)S(1)} %copy-done.33), channel_id=1, source_target_pairs={{0,4},{4,0},{1,5},{5,1},{2,6},{6,2},{3,7},{7,3},{8,12},{12,8},{9,1... | collective-permute-start | bytes 3932168 | tf_op jit(solution)/shard_map/ppermute | solution.py:54
  870.8 57.5 %collective-permute-start.81 = (bf16[4,2,128,1280]{3,2,0,1:T(8,128)(2,1)S(1)}, bf16[4,2,128,1280]{3,2,0,1:T(8,128)(2,1)S(1)}, u32[]{:S(2)}, u32[]{:S(2)}) collective-permute-start(bf16[4,2,128,1280]{3,2,0,1:T(8,128)(2,1)S(1)} %copy.189), channel_id=1, source_target_pairs={{0,2},{2,0},{1,3},{3,1},{4,6},{6,4},{5,7},{7,5},{8,10},{10,8},{9,1... | collective-permute-start | bytes 7864328 | tf_op jit(solution)/shard_map/ppermute | solution.py:54
  884.0 56.8 %collective-permute-start.83 = (bf16[4,2,128,1280]{3,2,0,1:T(8,128)(2,1)S(1)}, bf16[4,2,128,1280]{3,2,0,1:T(8,128)(2,1)S(1)}, u32[]{:S(2)}, u32[]{:S(2)}) collective-permute-start(bf16[4,2,128,1280]{3,2,0,1:T(8,128)(2,1)S(1)} %copy.191), channel_id=1, source_target_pairs={{0,1},{1,0},{2,3},{3,2},{4,5},{5,4},{6,7},{7,6},{8,9},{9,8},{10,11... | collective-permute-start | bytes 7864328 | tf_op jit(solution)/shard_map/ppermute | solution.py:54
  892.1 88.0 %collective-permute-start.92 = (bf16[2,256,1280]{2,1,0:T(8,128)(2,1)}, bf16[2,256,1280]{2,1,0:T(8,128)(2,1)}, u32[]{:S(2)}, u32[]{:S(2)}) collective-permute-start(bf16[2,256,1280]{2,1,0:T(8,128)(2,1)} %get-tuple-element.189), channel_id=1, source_target_pairs={{0,4},{4,0},{1,5},{5,1},{2,6},{6,2},{3,7},{7,3},{8,12},{12,8},{9,1... | collective-permute-start | bytes 3932168 | tf_op jit(solution)/shard_map/ppermute | solution.py:54
  928.3 36.4 %collective-permute-start.89 = (bf16[2,256,1280]{2,1,0:T(8,128)(2,1)S(1)}, bf16[2,256,1280]{2,1,0:T(8,128)(2,1)S(1)}, u32[]{:S(2)}, u32[]{:S(2)}) collective-permute-start(bf16[2,256,1280]{2,1,0:T(8,128)(2,1)S(1)} %add_convert_fusion.4), channel_id=1, source_target_pairs={{0,8},{8,16},{16,24},{24,0},{1,9},{9,17},{17,25},{25,1},{2,10},{10... | collective-permute-start | bytes 3932168 | tf_op jit(solution)/shard_map/ppermute | solution.py:54
  1002.3 51.8 %collective-permute-start.93 = (bf16[2,256,1280]{2,1,0:T(8,128)(2,1)S(1)}, bf16[2,256,1280]{2,1,0:T(8,128)(2,1)}, u32[]{:S(2)}, u32[]{:S(2)}) collective-permute-start(bf16[2,256,1280]{2,1,0:T(8,128)(2,1)S(1)} %add_convert_fusion.2), channel_id=1, source_target_pairs={{0,8},{8,16},{16,24},{24,0},{1,9},{9,17},{17,25},{25,1},{2,10},{10... | collective-permute-start | bytes 3932168 | tf_op jit(solution)/shard_map/ppermute | solution.py:54
  1014.2 38.2 %collective-permute-start.86 = (bf16[256,1280]{1,0:T(8,128)(2,1)S(1)}, bf16[256,1280]{1,0:T(8,128)(2,1)S(1)}, u32[]{:S(2)}, u32[]{:S(2)}) collective-permute-start(bf16[256,1280]{1,0:T(8,128)(2,1)S(1)} %fusion.53), channel_id=1, source_target_pairs={{0,8},{8,16},{16,24},{24,0},{1,9},{9,17},{17,25},{25,1},{2,10},{10... | collective-permute-start | bytes 1966088 | tf_op jit(solution)/shard_map/ppermute | solution.py:54
  1023.0 59.9 %collective-permute-start.114 = (bf16[2,2,40,4096]{3,2,0,1:T(8,128)(2,1)}, bf16[2,2,40,4096]{3,2,0,1:T(8,128)(2,1)}, u32[]{:S(2)}, u32[]{:S(2)}) collective-permute-start(bf16[2,2,40,4096]{3,2,0,1:T(8,128)(2,1)} %dynamic-slice_bitcast_fusion.1), channel_id=1, source_target_pairs={{0,1},{1,0},{2,3},{3,2},{4,5},{5,4},{6,7},{7,6},{8,9},{9,8},{10,11... | collective-permute-start | bytes 3932168 | tf_op jit(solution)/shard_map/ppermute | solution.py:54
  1025.2 60.6 %collective-permute-start.112 = (bf16[2,2,40,4096]{3,2,0,1:T(8,128)(2,1)}, bf16[2,2,40,4096]{3,2,0,1:T(8,128)(2,1)}, u32[]{:S(2)}, u32[]{:S(2)}) collective-permute-start(bf16[2,2,40,4096]{3,2,0,1:T(8,128)(2,1)} %dynamic-slice_bitcast_fusion.2), channel_id=1, source_target_pairs={{0,2},{2,0},{1,3},{3,1},{4,6},{6,4},{5,7},{7,5},{8,10},{10,8},{9,1... | collective-permute-start | bytes 3932168 | tf_op jit(solution)/shard_map/ppermute | solution.py:54
  (253 other events, 3525.6 us)

commit v4 on v3

--- a/solution.py
+++ b/solution.py
@@ -59,6 +59,15 @@
     for _ in range(1, lax.axis_size(axis)):
         parts.append(shift(parts[-1], axis))
     return parts
+
+
+def shift_by(value, axis, k):
+    n = lax.axis_size(axis)
+    return lax.ppermute(value, axis, [(i, (i + k) % n) for i in range(n)])
+
+
+def direct_gather(value, axis):
+    return [value] + [shift_by(value, axis, k) for k in range(1, lax.axis_size(axis))]
 
 
 def ring_sum(blocks, axis):
@@ -83,6 +92,8 @@
 
 
 def after(value, *events):
+    if not events:
+        return value
     return lax.optimization_barrier((value, *events))[0]
 
 
@@ -125,17 +136,23 @@
     return [out.reshape(n * rows, w) for out, w in zip(outs, widths)]
 
 
-def dense_rings(along_q):
+def dense_steps(nq):
+    half, na, nb = nq // 2, lax.axis_size("a"), lax.axis_size("b")
+    steps = [[(kq, ka, kb) for kb in range(nb) for kq in range(half)] for ka in range(na)]
+    return steps + [
+        [(kq, ka, kb) for ka in range(na) for kq in range(half, nq)] for kb in range(nb)
+    ]
+
+
+def dense_start(along_q):
     half = len(along_q) // 2
-    na, nb = lax.axis_size("a"), lax.axis_size("b")
     one = jnp.stack(ring_gather(jnp.stack(along_q[:half]), "b"))
     two = jnp.stack(ring_gather(jnp.stack(along_q[half:]), "a"))
-    pieces = ring_gather(one, "a") + ring_gather(two, "b")
-    steps = [[(kq, ka, kb) for kb in range(nb) for kq in range(half)] for ka in range(na)]
-    steps += [
-        [(kq, ka, kb) for ka in range(na) for kq in range(half, len(along_q))] for kb in range(nb)
-    ]
-    return pieces, steps
+    return one, two
+
+
+def dense_end(one, two):
+    return ring_gather(one, "a") + ring_gather(two, "b")
 
 
 def dense_place(pieces, steps, widths):
@@ -151,7 +168,7 @@
     return place(index.astype(jnp.int32), arrays, widths)
 
 
-def dense_sum(wholes, n_rows):
+def dense_sum(wholes, n_rows, middle=(), late=()):
     nq, nr, na, nb = (lax.axis_size(axis) for axis in ("q", "r", "a", "b"))
     values = [whole.reshape(nq, nr, na, nb, n_rows, whole.shape[1]) for whole in wholes]
     value = ring_sum(ring_blocks(values, "r", 1), "r").astype(BF)
@@ -159,25 +176,29 @@
     one, two = value[:half], value[half:]
     one = ring_sum(ring_blocks([one], "a", 1), "a").astype(BF)
     two = ring_sum(ring_blocks([two], "b", 2), "b").astype(BF)
+    one, two = after(one, *middle), after(two, *middle)
     one = ring_sum(ring_blocks([one], "b", 1), "b")
     two = ring_sum(ring_blocks([two], "a", 1), "a")
-    value = jnp.concatenate([one, two], axis=0).astype(BF)
+    value = after(jnp.concatenate([one, two], axis=0).astype(BF), *late)
     return ring_sum(ring_blocks([value], "q", 0), "q")
 
 
-def plane_gather(rows):
-    half = rows.shape[-2] // 2
-    one = jnp.stack(ring_gather(rows[..., :half, :], "b"))
-    two = jnp.stack(ring_gather(rows[..., half:, :], "a"))
-    return (jnp.stack(ring_gather(one, "a")), ring_gather(two, "b"))
-
-
-def plane_sum(one, two, dim=0):
-    first = ring_sum(one, "a")
-    second = ring_sum(two, "b")
-    first = ring_sum([lax.index_in_dim(first, k, dim, False) for k in range(len(two))], "b")
-    second = ring_sum([lax.index_in_dim(second, k, dim, False) for k in range(len(one))], "a")
-    return jnp.concatenate([first, second], axis=-2)
+def plane_gather(rows, even, event=()):
+    inner, outer = ("b", "a") if even else ("a", "b")
+    first = after(jnp.stack(ring_gather(rows, inner)), *event)
+    parts = ring_gather(first, outer)
+    return [jnp.stack(parts)] if even else parts
+
+
+def sum_start(parts, even):
+    return ring_sum(parts, "a" if even else "b")
+
+
+def sum_end(first, even, dim=0):
+    n = first.shape[dim]
+    return ring_sum(
+        [lax.index_in_dim(first, k, dim, False) for k in range(n)], "b" if even else "a"
+    )
 
 
 def project_kernel(n_query, x_ref, w_ref, cos_ref, sin_ref, q_ref, kv_ref):
@@ -398,16 +419,15 @@
     return out[0], out[1:]
 
 
-def expert_kernel(slots, na, nb, n_kept, e_ref, rank_ref, c0, *refs):
-    c1, refs = refs[:nb], refs[nb:]
-    g0, g1, refs = refs[0], refs[1 : 1 + nb], refs[1 + nb :]
+def expert_kernel(slots, na, nb, even, n_kept, e_ref, rank_ref, *refs):
+    n_in, n_sum = (1, na) if even else (nb, nb)
+    c_refs, g_ref, refs = refs[:n_in], refs[n_in], refs[n_in + 1 :]
     wr_ref, w1_ref, w2_ref = refs[:3]
     refs = refs[3 + n_kept :]
-    d0, d1, refs = refs[:na], refs[na : na + nb], refs[na + nb :]
-    dg_ref, x_ref, h_ref, dey_ref, deg_ref = refs[:5]
-    y0, y1 = refs[5 : 5 + na], refs[5 + na :]
-    half = c0.shape[2]
-    tok = 2 * half
+    d_refs, dg_ref, refs = refs[:n_sum], refs[n_sum], refs[n_sum + 1 :]
+    x_ref, h_ref, dey_ref, deg_ref = refs[:4]
+    y_refs = refs[4:]
+    tok = g_ref.shape[3]
     experts = wr_ref.shape[0]
     me = e_ref[0]
     step = pl.program_id(0)
@@ -415,8 +435,8 @@
     own = lax.broadcasted_iota(jnp.int32, (experts, tok), 0) == me
     slot = lax.broadcasted_iota(jnp.int32, (slots, tok), 0).astype(F32)
     for s in range(nb):
-        tokens = jnp.concatenate([c0[0, s], c1[s][0]], axis=0)
-        cot = jnp.concatenate([g0[0, s, 0], g1[s][0, 0]], axis=0)
+        tokens = c_refs[0][0, s] if even else c_refs[s][0]
+        cot = g_ref[0, 0, lax.rem(e_ref[3] - s + nb, nb)]
         rank = rank_ref[0, s, 0]
         logits = dot(wr_ref[...], tokens, NT)
         logits = jnp.where(rank >= 0, logits, masked_value)
@@ -455,33 +475,36 @@
     ey = dot(hidden, w2_ref[...]).astype(BF).astype(F32)
     dgate = jnp.sum(grad * ey, axis=1, keepdims=True)
     weighted = (weight * ey).astype(BF)
-    d_first, y_first = [], []
+    d_all, y_all = [], []
     for s in range(nb):
         part = slice(s * slots, (s + 1) * slots)
         pick, pick_low = picks[s]
-        back = dot(pick_low, dec[part], TN).astype(BF)
-        d_first.append(back[:half])
-        d1[s][0] = back[half:]
-        back = dot(pick_low, weighted[part], TN).astype(BF)
-        y_first.append(back[:half])
-        y1[s][0, 0] = back[half:]
+        d_all.append(dot(pick_low, dec[part], TN).astype(BF))
+        y_all.append(dot(pick_low, weighted[part], TN).astype(BF))
+        if not even:
+            d_refs[s][0] = d_all[s]
+            y_refs[s][0, 0] = y_all[s]
         dg_ref[0, s] = jnp.sum(pick * dgate[part], axis=0, keepdims=True)
-    for k in range(na):
-
-        @pl.when(step == k)
-        def _(k=k):
-            for s in range(nb):
-                d0[k][s] = d_first[s]
-                y0[k][0, s] = y_first[s]
-
-
-def expert_chunk(chunk, nq, expert, ranks, c, g, router_t, w1, w2, kept, slots):
-    na, nb, half, width = c[0].shape
+    if even:
+        for k in range(na):
+
+            @pl.when(step == k)
+            def _(k=k):
+                for s in range(nb):
+                    d_refs[k][s] = d_all[s]
+                    y_refs[k][0, s] = y_all[s]
+
+
+def expert_chunk(chunk, nq, na, nb, expert, ranks, c, g, router_t, w1, w2, kept, y_kept, slots):
+    even = chunk % 2 == 0
+    tok, width = c[0].shape[-2:]
     experts = router_t.shape[0]
-    one = pl.BlockSpec((1, nb, half, width), lambda i, e: (i, 0, 0, 0))
-    two = pl.BlockSpec((1, half, width), lambda i, e: (i, 0, 0))
-    g_one = pl.BlockSpec((1, nb, 1, half, width), lambda i, e: (i, 0, chunk, 0, 0))
-    g_two = pl.BlockSpec((1, 1, half, width), lambda i, e: (i, chunk, 0, 0))
+    plane = pl.BlockSpec(
+        (1, 1, nb, tok, width),
+        lambda i, e: (lax.rem(e[1] - chunk + nq, nq), lax.rem(e[2] - i + na, na), 0, 0, 0),
+    )
+    one = pl.BlockSpec((1, nb, tok, width), lambda i, e: (i, 0, 0, 0))
+    two = pl.BlockSpec((1, tok, width), lambda i, e: (i, 0, 0))
 
     def fixed(shape):
         return pl.BlockSpec(shape, lambda i, e: (0,) * len(shape), pipeline_mode=pl.Buffered(1))
@@ -490,46 +513,56 @@
         return pl.BlockSpec((nb * slots, n), lambda i, e: (chunk * na + i, 0))
 
     n_rows = na * nb * slots
-    kept_shapes = (
-        [jax.ShapeDtypeStruct((nq * n_rows, n), BF) for n in (width, FF, width, 2 * FF)]
-        + [jax.ShapeDtypeStruct((nq, nb, half, width), BF)] * na
-        + [jax.ShapeDtypeStruct((nq, na, half, width), BF)] * nb
-    )
-    n_kept = 0 if kept is None else len(kept)
-    n_in = 1 + 1 + (1 + nb) * 2 + 3
-    n_out = na + nb + 1
+    n_half = nq // 2
+    if even:
+        d_specs = [pl.BlockSpec((nb, tok, width), lambda i, e: (0, 0, 0))] * na
+        y_specs = [pl.BlockSpec((1, nb, tok, width), lambda i, e: (chunk // 2, 0, 0, 0))] * na
+        d_shapes = [jax.ShapeDtypeStruct((nb, tok, width), BF)] * na
+        y_shapes = [jax.ShapeDtypeStruct((n_half, nb, tok, width), BF)] * na
+    else:
+        d_specs = [two] * nb
+        y_specs = [pl.BlockSpec((1, 1, tok, width), lambda i, e: (chunk // 2, i, 0, 0))] * nb
+        d_shapes = [jax.ShapeDtypeStruct((na, tok, width), BF)] * nb
+        y_shapes = [jax.ShapeDtypeStruct((n_half, na, tok, width), BF)] * nb
+    held = [*(kept or ()), *(y_kept or ())]
+    n_in = 1 + 1 + len(c) + 1 + 3
+    n_out = len(d_shapes) + 1
+    aliases = {n_in + k: n_out + k for k in range(len(kept or ()))}
+    for k in range(len(y_kept or ())):
+        aliases[n_in + len(kept or ()) + k] = n_out + 4 + k
     out = pl.pallas_call(
-        functools.partial(expert_kernel, slots, na, nb, n_kept),
+        functools.partial(expert_kernel, slots, na, nb, even, len(held)),
         grid_spec=pltpu.PrefetchScalarGridSpec(
             num_scalar_prefetch=1,
             grid=(na,),
             in_specs=[
-                pl.BlockSpec((1, nb, 1, experts, 2 * half), lambda i, e: (i, 0, chunk, 0, 0)),
-                one, *[two] * nb, g_one, *[g_two] * nb,
+                pl.BlockSpec((1, nb, 1, experts, tok), lambda i, e: (i, 0, chunk, 0, 0)),
+                *([one] if even else [two] * nb), plane,
                 fixed(router_t.shape), fixed(w1.shape), fixed(w2.shape),
-                *[pl.BlockSpec(memory_space=pl.ANY)] * n_kept,
+                *[pl.BlockSpec(memory_space=pl.ANY)] * len(held),
             ],
             out_specs=[
-                *[pl.BlockSpec((nb, half, width), lambda i, e: (0, 0, 0))] * na,
-                *[two] * nb,
-                pl.BlockSpec((1, nb, 1, 2 * half), lambda i, e: (i, 0, 0, 0)),
+                *d_specs,
+                pl.BlockSpec((1, nb, 1, tok), lambda i, e: (i, 0, 0, 0)),
                 by_rows(width), by_rows(FF), by_rows(width), by_rows(2 * FF),
-                *[pl.BlockSpec((1, nb, half, width), lambda i, e: (chunk, 0, 0, 0))] * na,
-                *[pl.BlockSpec((1, 1, half, width), lambda i, e: (chunk, i, 0, 0))] * nb,
+                *y_specs,
             ],
         ),
-        out_shape=[jax.ShapeDtypeStruct((nb, half, width), BF)] * na
-        + [jax.ShapeDtypeStruct((na, half, width), BF)] * nb
-        + [jax.ShapeDtypeStruct((na, nb, 1, 2 * half), F32)]
-        + kept_shapes,
-        input_output_aliases={n_in + k: n_out + k for k in range(n_kept)},
+        out_shape=[
+            *d_shapes,
+            jax.ShapeDtypeStruct((na, nb, 1, tok), F32),
+            *[jax.ShapeDtypeStruct((nq * n_rows, n), BF) for n in (width, FF, width, 2 * FF)],
+            *y_shapes,
+        ],
+        input_output_aliases=aliases,
         compiler_params=pltpu.CompilerParams(vmem_limit_bytes=VMEM_LIMIT),
         cost_estimate=pl.CostEstimate(
             flops=n_rows * width * FF * 12, bytes_accessed=30_000_000, transcendentals=n_rows * FF
         ),
         name="experts",
-    )(expert, ranks, c[0], *c[1], g[0], *g[1], router_t, w1, w2, *(() if kept is None else kept))
-    return out[:na], out[na : na + nb], out[na + nb], out[n_out:]
+    )(expert, ranks, *c, g, router_t, w1, w2, *held)
+    n_d = len(d_shapes)
+    return out[:n_d], out[n_d], out[n_out : n_out + 4], out[n_out + 4 :]
 
 
 def body(
@@ -571,20 +604,19 @@
     own_rows = query_key_value_weight.shape[0]
     down_rows = common_expert_down_weight.shape[0]
 
+    named = jnp.any(
+        routes[0][:, :, None] == jnp.arange(n_experts, dtype=jnp.int32)[None, None, :], axis=1
+    )
+    before = (row[:, None] < row[None, :]).astype(BF)
+    rank = dot(named.astype(BF).T, before)
+    rank = jnp.where(named.T, rank, -1.0)
+    ranks = jnp.stack(direct_gather(rank, "q"))
+    ranks = jnp.stack(ring_gather(ranks, "b"))
+    ranks = jnp.stack(ring_gather(ranks, "a"))
+
     zeros = jnp.zeros((own_rows, 127), BF)
     front = jnp.concatenate([query_key_value_weight, attn_gain[:, None], zeros], axis=1)
     front_q = ring_gather(front, "q")
-
-    named = jnp.any(
-        routes[0][:, :, None] == jnp.arange(n_experts, dtype=jnp.int32)[None, None, :], axis=1
-    )
-    before = (row[:, None] < row[None, :]).astype(BF)
-    rank = dot(named.astype(BF).T, before)
-    rank = jnp.where(named.T, rank, -1.0)
-    ranks = jnp.stack(ring_gather(rank, "q"))
-    ranks = jnp.stack(ring_gather(ranks, "b"))
-    ranks = jnp.stack(ring_gather(ranks, "a"))
-
     rest = jnp.concatenate(
         [
             attention_output_weight,
@@ -597,31 +629,32 @@
         axis=1,
     )
     flat = common_expert_down_weight.size // own_rows
-    g_q = ring_gather(after(grad_low, front_q[-1]), "q")
-    rest_q = ring_gather(after(rest, g_q[-1]), "q")
-    front_pieces, front_steps = dense_rings(front_q)
-    rest_pieces, rest_steps = dense_rings([after(part, *front_pieces) for part in rest_q])
-    g_stack = after(jnp.stack(g_q), *rest_pieces)
-    g_one, g_two = plane_gather(g_stack)
-
-    def own_expert(stack):
-        rows = lax.all_to_all(stack, "q", split_axis=0, concat_axis=0, tiled=True)
+    front_q[-1] = after(front_q[-1], ranks)
+    steps = dense_steps(nq)
+    front_first = dense_start(front_q)
+
+    def own_rows_of(stack, event):
+        return lax.all_to_all(after(stack, event), "q", split_axis=0, concat_axis=0, tiled=True)
+
+    def own_expert(rows):
         parts = ring_gather(rows, "r")
         kr = np.repeat(np.arange(nr, dtype=np.int32), nq)
         kq = np.tile(np.arange(nq, dtype=np.int32), nr)
         index = kq * nr + lax.rem(r_at - kr + nr, nr)
-        return place(index.astype(jnp.int32), parts, [stack.shape[2]])[0]
-
-    w2 = own_expert(after(expert_down, rest_q[-1]))
-
-    qkv_weight, front_small = dense_place(front_pieces, front_steps, [3 * width, 128])
+        return place(index.astype(jnp.int32), parts, [rows.shape[2]])[0]
+
+    w1_rows = own_rows_of(expert_gate_up, front_q[-1])
+    front_pieces = dense_end(*front_first)
+    qkv_weight, front_small = dense_place(front_pieces, steps, [3 * width, 128])
+    rest = lax.all_gather(rest, ("q", "r", "a", "b"), axis=0, tiled=True)
+    g_all = lax.all_gather(grad_low, ("q", "a", "b"), axis=0, tiled=True)
+    g_all = g_all.reshape(nq, na, nb, tok, width)
+
+    kv_chunks = []
     gain_one = front_small[:, 0].astype(F32)
     inv_one = rms_scale(tokens_in)
-    normed = (tokens_in * inv_one * gain_one).astype(BF)
+    normed = after((tokens_in * inv_one * gain_one).astype(BF), w1_rows)
     queries, kv_own = project(normed, qkv_weight, *tables)
-    kv_q = ring_gather(kv_own, "q")
-    kv_chunks = [ring_gather(part, "r") for part in kv_q]
-    w1 = own_expert(after(expert_gate_up, kv_q[-1]))
     places = [
         jnp.stack(
             [ctx_rank]
@@ -633,45 +666,66 @@
         for k in range(nq)
     ]
     state = None
+    arrived = kv_own
     for k in range(nq):
-        state = attend_chunk(places[k], queries, kv_chunks[k], state, k == nq - 1, n_ctx)
+        chunk = ring_gather(arrived, "r")
+        if k < nq - 1:
+            coming = shift(arrived, "q")
+        state = attend_chunk(places[k], queries, chunk, state, k == nq - 1, n_ctx)
+        kv_chunks.append(chunk)
+        if k < nq - 1:
+            arrived = after(coming, state[0]) if k < nq - 2 else coming
     mixed, lse = state
-
-    out_weight, shared_in, shared_out, rest_small = dense_place(
-        rest_pieces, rest_steps, [width, 2 * FF, flat, 128]
-    )
-    shared_out = shared_out.reshape(-1, width)
+    w1, w2 = own_expert(w1_rows), own_expert(own_rows_of(expert_down, arrived))
+
+    at_in, at_out = width + 2 * FF, width + 2 * FF + flat
+    out_weight, shared_in = rest[:, :width], rest[:, width:at_in]
+    shared_out = rest[:, at_in:at_out].reshape(-1, width)
+    rest_small = rest[:, at_out:]
     gain_two = rest_small[:, 0].astype(F32)
     router = rest_small[:, 1 : 1 + n_experts]
     residual = tokens_in + dot(mixed, out_weight)
     inv_two = rms_scale(residual)
     second = (residual * inv_two * gain_two).astype(BF)
-    c_planes = [plane_gather(part) for part in ring_gather(second, "q")]
-    expert = (exp_rank * nq + q_at).astype(jnp.int32).reshape(1)
+    expert = jnp.stack([exp_rank * nq + q_at, q_at, a_at, b_at]).astype(jnp.int32)
     router_t = router.T
     kept = None
+    ys = [None, None]
     dec_parts, dgates = [], []
+    c_q = ring_gather(second, "q")
     for k in range(nq):
-        one, two, dgate, kept = expert_chunk(
-            k, nq, expert, ranks, c_planes[k], (g_one, g_two), router_t, w1, w2, kept, slots
+        c = plane_gather(c_q[k], k % 2 == 0, () if k < 2 else (dgates[0],))
+        dec, dgate, kept, ys[k % 2] = expert_chunk(
+            k, nq, na, nb, expert, ranks, c, g_all, router_t, w1, w2, kept, ys[k % 2], slots
         )
-        dec_parts.append((one, two))
+        dec_parts.append(dec)
         dgates.append(dgate.reshape(na * nb, tok))
-    dec_sums = [None] * nq
-    for k in list(range(1, nq)) + [0]:
-        dec_sums[k] = plane_sum(*dec_parts[k])
-    routed_grad = ring_sum(dec_sums, "q")
-    y_one, y_two = kept[4 : 4 + na], kept[4 + na :]
-    y_one = [after(y_one[0], routed_grad)] + [after(v, routed_grad) for v in y_one[1:]]
-    y_two = [after(y_two[0], routed_grad)] + [after(v, routed_grad) for v in y_two[1:]]
-    y_sums = plane_sum(y_one, y_two, 1)
-    routed_sum = ring_sum([y_sums[k] for k in range(nq)], "q")
+    dec_parts[0] = [after(v, dgates[-1]) for v in dec_parts[0]]
+    firsts = [sum_start(dec_parts[k], k % 2 == 0) for k in range(nq)]
+    dec_sums = [sum_end(firsts[k], k % 2 == 0) for k in range(nq)]
+    xs, hs, deys, degs = kept[:4]
+    down_term = dot(after(hs, firsts[nq - 2]), deys, TN).astype(BF)
+    gate_up_term = dot(after(xs, firsts[nq - 1]), degs, TN).astype(BF)
+    moving = dec_sums[1].astype(BF)
+    for k in range(2, nq):
+        term = dec_sums[k]
+        if k >= nq - 2:
+            term = after(term, down_term if k == nq - 2 else gate_up_term)
+        moving = (shift(moving, "q").astype(F32) + term).astype(BF)
+    routed_grad = shift(moving, "q").astype(F32) + dec_sums[0]
+
+    def expert_rows(whole, *events):
+        value = whole.reshape(nq, nr, -1, whole.shape[1])
+        value = ring_sum(ring_blocks([value], "r", 1), "r").astype(BF)
+        value = after(value, *events)
+        return lax.all_to_all(value, "q", split_axis=0, concat_axis=0, tiled=True)
+
+    gate_up_rows_low = expert_rows(gate_up_term)
 
     shared_pre = dot(second, shared_in)
     shared_gate, shared_up = shared_pre[:, :FF], shared_pre[:, FF:]
     shared_sig = jax.nn.sigmoid(shared_gate)
     shared_hidden = (shared_gate * shared_sig * shared_up).astype(BF)
-    layer_out = (residual + dot(shared_hidden, shared_out) + routed_sum).astype(BF)
 
     logits = jnp.where(named, dot(second, router), masked_value)
     raised = jnp.where(named, jnp.exp(logits - jnp.max(logits, axis=1, keepdims=True)), 0.0)
@@ -697,6 +751,15 @@
         ],
         axis=1,
     ).astype(BF)
+    every = ("q", "r", "a", "b")
+    shared_grad = jnp.concatenate(
+        [
+            dot(second, shared_pre_grad, TN).astype(BF),
+            dot(shared_hidden, grad_low, TN).astype(BF).reshape(width, flat),
+        ],
+        axis=1,
+    )
+    shared_grad = lax.psum_scatter(shared_grad, every, scatter_dimension=0, tiled=True)
     second_grad = (
         dot(shared_pre_grad, shared_in, NT) + dot(grad_logits, router, NT) + routed_grad
     )
@@ -707,44 +770,38 @@
 
     dq = None
     moving = None
-    for k in list(range(1, nq)) + [0]:
+    held = after(heads_grad, shared_grad, gate_up_rows_low)
+    for step, k in enumerate(list(range(1, nq)) + [0]):
+        if step == 2:
+            held = after(held, moving)
         dq, parts = attend_back_chunk(
-            places[k], queries, heads_grad, mixed, lse, tables, kv_chunks[k], dq, k == 0, n_ctx
+            places[k], queries, held, mixed, lse, tables, kv_chunks[k], dq, k == 0, n_ctx
         )
         term = ring_sum(parts, "r")
         if k == 1:
             moving = term.astype(BF)
+            first_move = moving
         elif k:
             moving = (shift(moving, "q").astype(F32) + term).astype(BF)
+    last_move = moving
     kv_back = finish_keys(shift(moving, "q"), term, *tables)
 
-    xs, hs, deys, degs = kept[:4]
-
-    def expert_rows(whole):
-        value = whole.reshape(nq, nr, -1, whole.shape[1])
-        value = ring_sum(ring_blocks([value], "r", 1), "r").astype(BF)
-        return lax.all_to_all(value, "q", split_axis=0, concat_axis=0, tiled=True).astype(F32)
-
-    gate_up_grad = expert_rows(dot(xs, degs, TN).astype(BF))
-    down_grad = expert_rows(dot(hs, deys, TN).astype(BF))
-
-    rest_grad = dense_sum(
-        [
-            dot(mixed, mixed_grad, TN).astype(BF),
-            dot(second, shared_pre_grad, TN).astype(BF),
-            dot(shared_hidden, grad_low, TN).astype(BF).reshape(width, flat),
-            jnp.concatenate(
-                [
-                    ffn_gain_grad[:, None],
-                    dot(second, grad_logits, TN),
-                    jnp.zeros((width, 127 - n_experts), F32),
-                ],
-                axis=1,
-            ).astype(BF),
-        ],
-        own_rows,
-    )
-    query_grad = dense_sum([dot(normed, dq, TN).astype(BF)], own_rows)
+    y_sums = []
+    for even in (True, False):
+        first = sum_start([after(v, routed_grad) for v in ys[0 if even else 1]], even)
+        y_sums.append(sum_end(after(first, first_move), even, 1))
+    y_sums = after(y_sums, kv_back)
+    routed_sum = ring_sum([y_sums[k % 2][k // 2] for k in range(nq)], "q")
+    layer_out = (residual + dot(shared_hidden, shared_out) + routed_sum).astype(BF)
+
+
+    down_rows_low = expert_rows(down_term, last_move)
+    gate_up_grad, down_grad = gate_up_rows_low.astype(F32), down_rows_low.astype(F32)
+    out_part = lax.psum_scatter(
+        dot(mixed, mixed_grad, TN).astype(BF), every, scatter_dimension=0, tiled=True
+    )
+    shared_grad, out_part = shared_grad.astype(F32), out_part.astype(F32)
+    query_grad = dense_sum([after(dot(normed, dq, TN).astype(BF), last_move)], own_rows)
     normed_grad = dot(dq, qkv_weight[:, :width], NT)
     normed_grad += dot(kv_back[0], qkv_weight[:, width : 2 * width], NT)
     normed_grad += dot(kv_back[1], qkv_weight[:, 2 * width :], NT)
@@ -755,22 +812,27 @@
             dot(normed, kv_back[0], TN).astype(BF),
             dot(normed, kv_back[1], TN).astype(BF),
             jnp.concatenate(
-                [attn_gain_grad[:, None], jnp.zeros((width, 127), F32)], axis=1
+                [
+                    attn_gain_grad[:, None],
+                    ffn_gain_grad[:, None],
+                    dot(second, grad_logits, TN),
+                    jnp.zeros((width, 126 - n_experts), F32),
+                ],
+                axis=1,
             ).astype(BF),
         ],
         own_rows,
     )
-    at_in, at_out = width + 2 * FF, width + 2 * FF + flat
     return (
         layer_out[None],
         input_grad[None],
         kv_weight_grad[:, 2 * width],
         jnp.concatenate([query_grad, kv_weight_grad[:, : 2 * width]], axis=1),
-        rest_grad[:, :width],
-        rest_grad[:, at_out],
-        rest_grad[:, at_out + 1 : at_out + 1 + n_experts],
-        rest_grad[:, width:at_in],
-        rest_grad[:, at_in:at_out].reshape(down_rows, width),
+        out_part,
+        kv_weight_grad[:, 2 * width + 1],
+        kv_weight_grad[:, 2 * width + 2 : 2 * width + 2 + n_experts],
+        shared_grad[:, : 2 * FF],
+        shared_grad[:, 2 * FF :].reshape(down_rows, width),
         gate_up_grad,
         down_grad,
     )

time: 1180 us -> 1130 us (0.958)
  waiting for transfers between devices: 554 us -> 517 us
  starting transfers between devices: 151 us -> 124 us
  local copies, waits for them, and re-layouts: 106 us -> 81.3 us
  matrix products: 60.5 us -> 78.5 us
  between operations: 3.43 us -> 16.1 us
    ppermute x121 -> x76, waiting for transfers between devices: 554 us -> 405 us  [shift(): return lax.ppermute(value, axis, [(i, (i + 1) % n) for i in range(n)])]
    all_to_all x4, waiting for transfers between devices: 0.01 us -> 63.9 us  [the longest x2 45 us: own_rows_of(): lax.all_to_all(after(stack, event), 'q', split_axis=0, concat_axis=0, til...]
    ppermute x121 -> x76, starting transfers between devices: 127 us -> 94.5 us  [shift(): return lax.ppermute(value, axis, [(i, (i + 1) % n) for i in range(n)])]
    reduce_scatter x0 -> x1, waiting for transfers between devices: none -> 24.1 us  [body(): lax.psum_scatter(dot(mixed, mixed_grad, TN).astype(BF), every, scatter_di...]
    unnamed x324 -> x230, local copies, waits for them, and re-layouts: 52.5 us -> 32.2 us
    dot_general x21, matrix products: 60.5 us -> 78.5 us  [dot(): return lax.dot_general(a, b, (dims, ((), ())), preferred_element_type=F32)]
    dynamic_slice x15 -> x0, local copies, waits for them, and re-layouts: 16.8 us -> none  [ring_blocks(): lax.dynamic_index_in_dim(v, at, dim, keepdims=False)]
    another operation x7 -> x0, local copies, waits for them, and re-layouts: 15.6 us -> none  [the longest x1 5.47 us: dense_sum(): whole.reshape(nq, nr, na, nb, n_rows, whole.shape[1])]
  transfers between devices with their start and end apart: 126 -> 88, of which waited for: 60 -> 41; matrix products, arithmetic and copies ran while one was open for 17% -> 20% of each run, Pallas kernels for 15% -> 18%
where the time goes in v4:
time: 1130 us; the launch traced here: 1120 us
  waiting for transfers between devices  517 us (46%)
  Pallas kernels  200 us (18%)
  starting transfers between devices  124 us (11%)
  other arithmetic  102 us (9%)
  local copies, waits for them, and re-layouts  81.3 us (7%)
  matrix products  78.5 us (7%)
  between operations  16.1 us (1%)
    ppermute x76, waiting for transfers between devices, shift(): return lax.ppermute(value, axis, [(i, (i + 1) % n) for i in range(n)])  405 us
    ppermute x76, starting transfers between devices, shift(): return lax.ppermute(value, axis, [(i, (i + 1) % n) for i in range(n)])  94.5 us
    pallas_call x4, Pallas kernels, expert_chunk(): pl.pallas_call(functools.partial(expert_kernel, slots, na, nb, even, len(...  91.2 us
    dot_general x21, matrix products, dot(): return lax.dot_general(a, b, (dims, ((), ())), preferred_element_type=F32)  78.5 us
    pallas_call x4, Pallas kernels, attend_back_chunk(): pl.pallas_call(functools.partial(attend_back_kernel, n_ctx, n, first, las...  47.1 us
    all_to_all x2, waiting for transfers between devices, own_rows_of(): lax.all_to_all(after(stack, event), 'q', split_axis=0, concat_axis=0, til...  45 us
    pallas_call x4, Pallas kernels, attend_chunk(): pl.pallas_call(functools.partial(attend_kernel, n_ctx, n, first, last), g...  37.9 us
    unnamed x230, local copies, waits for them, and re-layouts  32.2 us
  transfers between devices with their start and end apart: 88, of which 41 were waited for; matrix products, arithmetic and copies ran while one was open for 20% of the time, Pallas kernels for 18%

profile of v4, /device:TPU:0, one launch (start us, length us, event | category | flops | bytes accessed | tf_op | source)
XLA Modules:
  0.0 1119.6 jit_solution(6586625769512120902)
XLA Ops:
  30.6 11.7 %collective-permute-done.5 = f32[16,256]{1,0:T(8,128)S(1)} collective-permute-done((f32[16,256]{1,0:T(8,128)S(1)}, f32[16,256]{1,0:T(8,128)S(1)}, u32[]{:S(2)}, u32[]{:S(2)}) %collective-permute-start.5) | collective-permute-done | bytes 16416 | tf_op jit(solution)/shard_map/ppermute | solution.py:66
  55.3 9.9 collective-permute-done.4
  93.0 32.8 %collective-permute-done.2 = bf16[2,2,40,3968]{3,2,1,0:T(8,128)(2,1)} collective-permute-done((bf16[2,2,40,3968]{3,2,1,0:T(8,128)(2,1)}, bf16[2,2,40,3968]{3,2,1,0:T(8,128)(2,1)}, u32[]{:S(2)}, u32[]{:S(2)}) %collective-permute-start.2) | collective-permute-done | bytes 1269792 | tf_op jit(solution)/shard_map/ppermute | solution.py:54
  139.6 18.0 %all-to-all-done.refs_0_ = bf16[4,160,1792]{2,1,0:T(8,128)(2,1)S(1)} async-done(((bf16[4,160,1792]{2,1,0:T(8,128)(2,1)}), bf16[4,160,1792]{2,1,0:T(8,128)(2,1)S(1)}, u32[]{:S(2)}, u32[]{:S(2)}) %all-to-all-start) | async-done | bytes 2293792 | tf_op jit(solution)/shard_map/all_to_all | solution.py:637
  186.8 35.9 %collective-permute-done.16.refs_0_ = bf16[2,256,1280]{2,1,0:T(8,128)(2,1)} collective-permute-done((bf16[2,256,1280]{2,1,0:T(8,128)(2,1)}, bf16[2,256,1280]{2,1,0:T(8,128)(2,1)}, u32[]{:S(2)}, u32[]{:S(2)}) %collective-permute-start.16) | collective-permute-done | bytes 1310752 | tf_op jit(solution)/shard_map/ppermute | solution.py:54
  247.7 41.3 %collective-permute-done.18.refs_0_ = bf16[2,256,1280]{2,1,0:T(8,128)(2,1)} collective-permute-done((bf16[2,256,1280]{2,1,0:T(8,128)(2,1)}, bf16[2,256,1280]{2,1,0:T(8,128)(2,1)}, u32[]{:S(2)}, u32[]{:S(2)}) %collective-permute-start.18) | collective-permute-done | bytes 1310752 | tf_op jit(solution)/shard_map/ppermute | solution.py:54
  289.0 24.4 %collective-permute-start.20 = (bf16[2,256,1280]{2,1,0:T(8,128)(2,1)}, bf16[2,256,1280]{2,1,0:T(8,128)(2,1)}, u32[]{:S(2)}, u32[]{:S(2)}) collective-permute-start(bf16[2,256,1280]{2,1,0:T(8,128)(2,1)} %collective-permute-done.18.refs_0_), channel_id=1, source_target_pairs={{0,8},{8,16},{16,24},{24,0},{1,9},{9,17},{17,25},{25,1},{2,10},{10... | collective-permute-start | bytes 3932168 | tf_op jit(solution)/shard_map/ppermute | solution.py:54
  313.4 38.1 %collective-permute-done.20.refs_0_ = bf16[2,256,1280]{2,1,0:T(8,128)(2,1)} collective-permute-done((bf16[2,256,1280]{2,1,0:T(8,128)(2,1)}, bf16[2,256,1280]{2,1,0:T(8,128)(2,1)}, u32[]{:S(2)}, u32[]{:S(2)}) %collective-permute-start.20) | collective-permute-done | bytes 1310752 | tf_op jit(solution)/shard_map/ppermute | solution.py:54
  356.6 27.0 %all-to-all-done.1.refs_0_ = bf16[4,112,1280]{2,1,0:T(8,128)(2,1)} async-done(((bf16[4,112,1280]{2,1,0:T(8,128)(2,1)}), bf16[4,112,1280]{2,1,0:T(8,128)(2,1)}, u32[]{:S(2)}, u32[]{:S(2)}) %all-to-all-start.1) | async-done | bytes 1146912 | tf_op jit(solution)/shard_map/all_to_all | solution.py:637
  398.7 10.1 attend.7
  457.1 13.0 %collective-permute-done.24 = bf16[256,1280]{1,0:T(8,128)(2,1)} collective-permute-done((bf16[256,1280]{1,0:T(8,128)(2,1)}, bf16[256,1280]{1,0:T(8,128)(2,1)}, u32[]{:S(2)}, u32[]{:S(2)}) %collective-permute-start.24) | collective-permute-done | bytes 655392 | tf_op jit(solution)/shard_map/ppermute | solution.py:54
  477.6 17.3 %collective-permute-done.31 = bf16[256,1280]{1,0:T(8,128)(2,1)} collective-permute-done((bf16[256,1280]{1,0:T(8,128)(2,1)}, bf16[256,1280]{1,0:T(8,128)(2,1)}, u32[]{:S(2)}, u32[]{:S(2)}) %collective-permute-start.31) | collective-permute-done | bytes 655392 | tf_op jit(solution)/shard_map/ppermute | solution.py:54
  504.3 23.3 %experts.4 = (bf16[2,256,1280]{2,1,0:T(8,128)(2,1)}, bf16[2,256,1280]{2,1,0:T(8,128)(2,1)}, f32[2,2,1,256]{3,2,1,0:T(1,128)}, bf16[2816,1280]{1,0:T(8,128)(2,1)}...) custom-call(s32[4]{0:T(128)} %pad_add_fusion.4.e_ref, ...), custom_call_target="tpu_custom_call" | custom-call | flops 9688842240 | bytes 30000000 | tf_op jit(solution)/shard_map/experts/pallas_call | solution.py:533
  528.3 29.2 %collective-permute-done.25 = bf16[256,1280]{1,0:T(8,128)(2,1)} collective-permute-done((bf16[256,1280]{1,0:T(8,128)(2,1)}, bf16[256,1280]{1,0:T(8,128)(2,1)}, u32[]{:S(2)}, u32[]{:S(2)}) %collective-permute-start.25) | collective-permute-done | bytes 655392 | tf_op jit(solution)/shard_map/ppermute | solution.py:54
  566.2 22.4 %experts.5 = (bf16[2,256,1280]{2,1,0:T(8,128)(2,1)}, bf16[2,256,1280]{2,1,0:T(8,128)(2,1)}, f32[2,2,1,256]{3,2,1,0:T(1,128)}, bf16[2816,1280]{1,0:T(8,128)(2,1)}...) custom-call(s32[4]{0:T(128)} %pad_add_fusion.4.e_ref, ...), custom_call_target="tpu_custom_call", output_to_operand_aliasing={{3}: (8, {}), {4}: (9, {}), {5}: (10, {}), {6}: (11, {})} | custom-call | flops 9688842240 | bytes 30000000 | tf_op jit(solution)/shard_map/experts/pallas_call | solution.py:533
  594.3 23.5 %experts.6 = (bf16[2,256,1280]{2,1,0:T(8,128)(2,1)}, bf16[2,256,1280]{2,1,0:T(8,128)(2,1)}, f32[2,2,1,256]{3,2,1,0:T(1,128)}, bf16[2816,1280]{1,0:T(8,128)(2,1)}...) custom-call(s32[4]{0:T(128)} %pad_add_fusion.4.e_ref, ...), custom_call_target="tpu_custom_call", output_to_operand_aliasing={{3}: (7, {}), {4}: (8, {}), {5}: (9, {}), {6}: (10, {}), {7... | custom-call | flops 9688842240 | bytes 30000000 | tf_op jit(solution)/shard_map/experts/pallas_call | solution.py:533
  619.1 22.1 %experts.7 = (bf16[2,256,1280]{2,1,0:T(8,128)(2,1)}, bf16[2,256,1280]{2,1,0:T(8,128)(2,1)}, f32[2,2,1,256]{3,2,1,0:T(1,128)}, bf16[2816,1280]{1,0:T(8,128)(2,1)}...) custom-call(s32[4]{0:T(128)} %pad_add_fusion.4.e_ref, ...), custom_call_target="tpu_custom_call", output_to_operand_aliasing={{3}: (8, {}), {4}: (9, {}), {5}: (10, {}), {6}: (11, {}), {... | custom-call | flops 9688842240 | bytes 30000000 | tf_op jit(solution)/shard_map/experts/pallas_call | solution.py:533
  656.6 11.9 %all-to-all-done.2 = f32[16,1,256]{2,1,0:T(1,128)S(1)} async-done(((f32[16,1,256]{2,1,0:T(1,128)}), f32[16,1,256]{2,1,0:T(1,128)S(1)}, u32[]{:S(2)}, u32[]{:S(2)}) %all-to-all-start.2) | async-done | bytes 16416 | tf_op jit(solution)/shard_map/all_to_all | solution.py:741
  677.3 13.5 %convolution_convert_fusion.7 = bf16[896,1280]{1,0:T(8,128)(2,1)} fusion(bf16[2816,896]{1,0:T(8,128)(2,1)} %get-tuple-element.139, bf16[2816,1280]{1,0:T(8,128)(2,1)} %get-tuple-element.140), kind=kOutput, calls=%fused_computation.18 | convolution fusion | flops 6460375040 | bytes 14548992 | tf_op jit(solution)/shard_map/dot_general | solution.py:45
  692.5 15.1 %convolution_convert_fusion.4 = bf16[1280,1792]{1,0:T(8,128)(2,1)} fusion(bf16[2816,1280]{1,0:T(8,128)(2,1)S(1)} %bitcast.327, bf16[2816,1792]{1,0:T(8,128)(2,1)S(1)} %bitcast.325), kind=kOutput, calls=%fused_computation.5 | convolution fusion | flops 12920750080 | bytes 21889024 | tf_op jit(solution)/shard_map/dot_general | solution.py:45
  718.7 12.0 %collective-permute-done.43 = bf16[256,1280]{1,0:T(8,128)(2,1)S(1)} collective-permute-done((bf16[256,1280]{1,0:T(8,128)(2,1)S(1)}, bf16[256,1280]{1,0:T(8,128)(2,1)S(1)}, u32[]{:S(2)}, u32[]{:S(2)}) %collective-permute-start.43) | collective-permute-done | bytes 655392 | tf_op jit(solution)/shard_map/ppermute | solution.py:54
  741.1 11.1 collective-permute-done.44
  784.0 18.9 %all-to-all-done.3 = bf16[4,160,1792]{2,1,0:T(8,128)(2,1)} async-done(((bf16[4,160,1792]{2,1,0:T(8,128)(2,1)}), bf16[4,160,1792]{2,1,0:T(8,128)(2,1)}, u32[]{:S(2)}, u32[]{:S(2)}) %all-to-all-start.3) | async-done | bytes 2293792 | tf_op jit(solution)/shard_map/all_to_all | solution.py:721
  804.2 11.3 %attend_back.4 = (f32[256,1280]{1,0:T(8,128)S(1)}, f32[2,256,1280]{2,1,0:T(8,128)S(1)}, bf16[2,256,1280]{2,1,0:T(8,128)(2,1)S(1)}) custom-call(s32[3]{0:T(128)S(1)} %pad_add_fusion.2.place_ref, bf16[256,1280]{1,0:T(8,128)(2,1)S(1)} %copy-done.23, bf16[256,1280]{1,0:T(8,128)(2,1)S(1)} %fusion.25.do_ref, bf16[256,1280]{1,0:T(8,128)(2,1)S(1)} %get-tuple-element.112.o_ref, ...), custom_call_target="tpu_custom_call" | custom-call | flops 6710886400 | bytes 5242880 | tf_op jit(solution)/shard_map/attend_back/pallas_call | solution.py:403
  815.7 39.9 %collective-permute-done.51 = bf16[2,2,256,1280]{3,2,0,1:T(8,128)(2,1)} collective-permute-done((bf16[2,2,256,1280]{3,2,0,1:T(8,128)(2,1)}, bf16[2,2,256,1280]{3,2,0,1:T(8,128)(2,1)}, u32[]{:S(2)}, u32[]{:S(2)}) %collective-permute-start.51) | collective-permute-done | bytes 2621472 | tf_op jit(solution)/shard_map/ppermute | solution.py:54
  858.0 12.0 %attend_back.5 = (f32[256,1280]{1,0:T(8,128)S(1)}, f32[2,256,1280]{2,1,0:T(8,128)S(1)}, bf16[2,256,1280]{2,1,0:T(8,128)(2,1)}) custom-call(s32[3]{0:T(128)S(1)} %copy-done.18, bf16[256,1280]{1,0:T(8,128)(2,1)S(1)} %copy-done.24, bf16[256,1280]{1,0:T(8,128)(2,1)S(1)} %copy-done.27, bf16[256,1280]{1,0:T(8,128)(2,1)S(1)} %copy-done.5, ...), custom_call_target="tpu_custom_call" | custom-call | flops 6710886400 | bytes 5242880 | tf_op jit(solution)/shard_map/attend_back/pallas_call | solution.py:403
  885.5 24.1 %reduce-scatter.5.cloned.1.call-done = bf16[40,1280]{1,0:T(8,128)(2,1)} async-done(((bf16[1280,1280]{1,0:T(8,128)(2,1)}), bf16[40,1280]{1,0:T(8,128)(2,1)}) %reduce-scatter.5.cloned.1.call-update) | async-done | bytes 102416 | tf_op jit(solution)/shard_map/reduce_scatter | solution.py:800
  918.1 11.2 attend_back.6
  929.4 12.6 %attend_back.7 = (bf16[256,1280]{1,0:T(8,128)(2,1)S(1)}, f32[2,256,1280]{2,1,0:T(8,128)S(1)}, bf16[2,256,1280]{2,1,0:T(8,128)(2,1)}) custom-call(s32[3]{0:T(128)S(1)} %copy-done.14, bf16[256,1280]{1,0:T(8,128)(2,1)S(1)} %copy-done.25, bf16[256,1280]{1,0:T(8,128)(2,1)S(1)} %copy-done.28, bf16[256,1280]{1,0:T(8,128)(2,1)S(1)} %copy-done.6, ...), custom_call_target="tpu_custom_call" | custom-call | flops 6710886400 | bytes 5242880 | tf_op jit(solution)/shard_map/attend_back/pallas_call | solution.py:403
  964.0 20.2 %collective-permute-done.57.moved_ref = bf16[2,256,1280]{2,1,0:T(8,128)(2,1)} collective-permute-done((bf16[2,256,1280]{2,1,0:T(8,128)(2,1)}, bf16[2,256,1280]{2,1,0:T(8,128)(2,1)}, u32[]{:S(2)}, u32[]{:S(2)}) %collective-permute-start.57) | collective-permute-done | bytes 1310752 | tf_op jit(solution)/shard_map/ppermute | solution.py:54
  1016.4 10.6 collective-permute-done.73
  1053.0 10.1 collective-permute-done.65
  (573 shorter events, 469.0 us)
Async XLA Ops:
  7.2 404.9 %all-gather.4.cloned.1.call-start = ((), (), s32[]{:S(2)}) async-start(), calls=%async_computation.7 | async-start | bytes 10813440 | tf_op jit(solution)/shard_map/all_gather | solution.py:649
  11.6 492.6 %all-gather.6.cloned.1.call-start = ((), (), s32[]{:S(2)}) async-start(), calls=%async_computation.9 | async-start | bytes 11141120 | tf_op jit(solution)/shard_map/all_gather | solution.py:650
  71.9 54.0 %collective-permute-start.2 = (bf16[2,2,40,3968]{3,2,1,0:T(8,128)(2,1)}, bf16[2,2,40,3968]{3,2,1,0:T(8,128)(2,1)}, u32[]{:S(2)}, u32[]{:S(2)}) collective-permute-start(bf16[2,2,40,3968]{3,2,1,0:T(8,128)(2,1)} %pad_maximum_fusion.8), channel_id=1, source_target_pairs={{0,2},{2,0},{1,3},{3,1},{4,6},{6,4},{5,7},{7,5},{8,10},{10,8},{9,1... | collective-permute-start | bytes 3809288 | tf_op jit(solution)/shard_map/ppermute | solution.py:54
  73.4 84.1 %all-to-all-start = ((bf16[4,160,1792]{2,1,0:T(8,128)(2,1)}), bf16[4,160,1792]{2,1,0:T(8,128)(2,1)S(1)}, u32[]{:S(2)}, u32[]{:S(2)}) async-start(bf16[4,160,1792]{2,1,0:T(8,128)(2,1)} %param.33), calls=%async_computation | async-start | bytes 4587520 | tf_op jit(solution)/shard_map/all_to_all | solution.py:637
  171.7 51.0 %collective-permute-start.16 = (bf16[2,256,1280]{2,1,0:T(8,128)(2,1)}, bf16[2,256,1280]{2,1,0:T(8,128)(2,1)}, u32[]{:S(2)}, u32[]{:S(2)}) collective-permute-start(bf16[2,256,1280]{2,1,0:T(8,128)(2,1)} %get-tuple-element.103.refs_0_), channel_id=1, source_target_pairs={{0,8},{8,16},{16,24},{24,0},{1,9},{9,17},{17,25},{25,1},{2,10},{10... | collective-permute-start | bytes 3932168 | tf_op jit(solution)/shard_map/ppermute | solution.py:54
  222.7 66.2 %collective-permute-start.18 = (bf16[2,256,1280]{2,1,0:T(8,128)(2,1)}, bf16[2,256,1280]{2,1,0:T(8,128)(2,1)}, u32[]{:S(2)}, u32[]{:S(2)}) collective-permute-start(bf16[2,256,1280]{2,1,0:T(8,128)(2,1)} %collective-permute-done.16.refs_0_), channel_id=1, source_target_pairs={{0,8},{8,16},{16,24},{24,0},{1,9},{9,17},{17,25},{25,1},{2,10},{10... | collective-permute-start | bytes 3932168 | tf_op jit(solution)/shard_map/ppermute | solution.py:54
  289.0 62.5 %collective-permute-start.20 = (bf16[2,256,1280]{2,1,0:T(8,128)(2,1)}, bf16[2,256,1280]{2,1,0:T(8,128)(2,1)}, u32[]{:S(2)}, u32[]{:S(2)}) collective-permute-start(bf16[2,256,1280]{2,1,0:T(8,128)(2,1)} %collective-permute-done.18.refs_0_), channel_id=1, source_target_pairs={{0,8},{8,16},{16,24},{24,0},{1,9},{9,17},{17,25},{25,1},{2,10},{10... | collective-permute-start | bytes 3932168 | tf_op jit(solution)/shard_map/ppermute | solution.py:54
  355.7 424.9 %reduce-scatter.7.cloned.1.call-start = ((), (), s32[]{:S(2)}) async-start(), calls=%async_computation.10 | async-start | bytes 7096320
  356.4 42.3 %collective-permute-start.21 = (bf16[2,256,1280]{2,1,0:T(8,128)(2,1)}, bf16[2,256,1280]{2,1,0:T(8,128)(2,1)}, u32[]{:S(2)}, u32[]{:S(2)}) collective-permute-start(bf16[2,256,1280]{2,1,0:T(8,128)(2,1)} %collective-permute-done.20.refs_0_), channel_id=1, source_target_pairs={{0,4},{4,0},{1,5},{5,1},{2,6},{6,2},{3,7},{7,3},{8,12},{12,8},{9,1... | collective-permute-start | bytes 3932168 | tf_op jit(solution)/shard_map/ppermute | solution.py:54
  449.4 50.0 %collective-permute-start.27 = (bf16[2,256,1280]{2,1,0:T(8,128)(2,1)}, bf16[2,256,1280]{2,1,0:T(8,128)(2,1)}, u32[]{:S(2)}, u32[]{:S(2)}) collective-permute-start(bf16[2,256,1280]{2,1,0:T(8,128)(2,1)} %get-tuple-element.256), channel_id=1, source_target_pairs={{0,2},{2,0},{1,3},{3,1},{4,6},{6,4},{5,7},{7,5},{8,10},{10,8},{9,1... | collective-permute-start | bytes 3932168 | tf_op jit(solution)/shard_map/ppermute | solution.py:54
  451.4 43.5 %collective-permute-start.31 = (bf16[256,1280]{1,0:T(8,128)(2,1)}, bf16[256,1280]{1,0:T(8,128)(2,1)}, u32[]{:S(2)}, u32[]{:S(2)}) collective-permute-start(bf16[256,1280]{1,0:T(8,128)(2,1)} %collective-permute-done.23), channel_id=1, source_target_pairs={{0,2},{2,0},{1,3},{3,1},{4,6},{6,4},{5,7},{7,5},{8,10},{10,8},{9,1... | collective-permute-start | bytes 1966088 | tf_op jit(solution)/shard_map/ppermute | solution.py:54
  497.4 68.8 %collective-permute-start.32 = (bf16[2,256,1280]{2,1,0:T(8,128)(2,1)}, bf16[2,256,1280]{2,1,0:T(8,128)(2,1)}, u32[]{:S(2)}, u32[]{:S(2)}) collective-permute-start(bf16[2,256,1280]{2,1,0:T(8,128)(2,1)} %pad_maximum_fusion.6.refs_0_), channel_id=1, source_target_pairs={{0,1},{1,0},{2,3},{3,2},{4,5},{5,4},{6,7},{7,6},{8,9},{9,8},{10,11... | collective-permute-start | bytes 3932168 | tf_op jit(solution)/shard_map/ppermute | solution.py:54
  498.1 59.4 %collective-permute-start.25 = (bf16[256,1280]{1,0:T(8,128)(2,1)}, bf16[256,1280]{1,0:T(8,128)(2,1)}, u32[]{:S(2)}, u32[]{:S(2)}) collective-permute-start(bf16[256,1280]{1,0:T(8,128)(2,1)} %collective-permute-done.24), channel_id=1, source_target_pairs={{0,1},{1,0},{2,3},{3,2},{4,5},{5,4},{6,7},{7,6},{8,9},{9,8},{10,11... | collective-permute-start | bytes 1966088 | tf_op jit(solution)/shard_map/ppermute | solution.py:54
  502.5 60.6 %collective-permute-start.39 = (bf16[256,1280]{1,0:T(8,128)(2,1)}, bf16[256,1280]{1,0:T(8,128)(2,1)}, u32[]{:S(2)}, u32[]{:S(2)}) collective-permute-start(bf16[256,1280]{1,0:T(8,128)(2,1)} %collective-permute-done.38), channel_id=1, source_target_pairs={{0,2},{2,0},{1,3},{3,1},{4,6},{6,4},{5,7},{7,5},{8,10},{10,8},{9,1... | collective-permute-start | bytes 1966088 | tf_op jit(solution)/shard_map/ppermute | solution.py:54
  565.6 53.5 %collective-permute-start.40 = (bf16[2,256,1280]{2,1,0:T(8,128)(2,1)}, bf16[2,256,1280]{2,1,0:T(8,128)(2,1)}, u32[]{:S(2)}, u32[]{:S(2)}) collective-permute-start(bf16[2,256,1280]{2,1,0:T(8,128)(2,1)} %pad_maximum_fusion.7.refs_0_), channel_id=1, source_target_pairs={{0,1},{1,0},{2,3},{3,2},{4,5},{5,4},{6,7},{7,6},{8,9},{9,8},{10,11... | collective-permute-start | bytes 3932168 | tf_op jit(solution)/shard_map/ppermute | solution.py:54
  589.3 60.9 %collective-permute-start.33 = (bf16[2,256,1280]{2,1,0:T(8,128)(2,1)}, bf16[2,256,1280]{2,1,0:T(8,128)(2,1)}, u32[]{:S(2)}, u32[]{:S(2)}) collective-permute-start(bf16[2,256,1280]{2,1,0:T(8,128)(2,1)} %get-tuple-element.127), channel_id=1, source_target_pairs={{0,1},{1,0},{2,3},{3,2},{4,5},{5,4},{6,7},{7,6},{8,9},{9,8},{10,11... | collective-permute-start | bytes 3932168 | tf_op jit(solution)/shard_map/ppermute | solution.py:54
  617.7 50.9 %collective-permute-start.36 = (bf16[2,256,1280]{2,1,0:T(8,128)(2,1)}, bf16[2,256,1280]{2,1,0:T(8,128)(2,1)}, u32[]{:S(2)}, u32[]{:S(2)}) collective-permute-start(bf16[2,256,1280]{2,1,0:T(8,128)(2,1)} %get-tuple-element.129), channel_id=1, source_target_pairs={{0,2},{2,0},{1,3},{3,1},{4,6},{6,4},{5,7},{7,5},{8,10},{10,8},{9,1... | collective-permute-start | bytes 3932168 | tf_op jit(solution)/shard_map/ppermute | solution.py:54
  641.2 49.7 %collective-permute-start.42 = (bf16[2,256,1280]{2,1,0:T(8,128)(2,1)}, bf16[2,256,1280]{2,1,0:T(8,128)(2,1)}, u32[]{:S(2)}, u32[]{:S(2)}) collective-permute-start(bf16[2,256,1280]{2,1,0:T(8,128)(2,1)} %get-tuple-element.142), channel_id=1, source_target_pairs={{0,1},{1,0},{2,3},{3,2},{4,5},{5,4},{6,7},{7,6},{8,9},{9,8},{10,11... | collective-permute-start | bytes 3932168 | tf_op jit(solution)/shard_map/ppermute | solution.py:54
  656.5 58.9 %collective-permute-start.45 = (bf16[2,256,1280]{2,1,0:T(8,128)(2,1)}, bf16[2,256,1280]{2,1,0:T(8,128)(2,1)}, u32[]{:S(2)}, u32[]{:S(2)}) collective-permute-start(bf16[2,256,1280]{2,1,0:T(8,128)(2,1)} %get-tuple-element.150), channel_id=1, source_target_pairs={{0,2},{2,0},{1,3},{3,1},{4,6},{6,4},{5,7},{7,5},{8,10},{10,8},{9,1... | collective-permute-start | bytes 3932168 | tf_op jit(solution)/shard_map/ppermute | solution.py:54
  673.9 36.9 %collective-permute-start.35 = (bf16[256,1280]{1,0:T(8,128)(2,1)S(1)}, bf16[256,1280]{1,0:T(8,128)(2,1)}, u32[]{:S(2)}, u32[]{:S(2)}) collective-permute-start(bf16[256,1280]{1,0:T(8,128)(2,1)S(1)} %fusion.48), channel_id=1, source_target_pairs={{0,8},{8,16},{16,24},{24,0},{1,9},{9,17},{17,25},{25,1},{2,10},{10... | collective-permute-start | bytes 1966088 | tf_op jit(solution)/shard_map/ppermute | solution.py:54
  736.5 66.4 %all-to-all-start.3 = ((bf16[4,160,1792]{2,1,0:T(8,128)(2,1)}), bf16[4,160,1792]{2,1,0:T(8,128)(2,1)}, u32[]{:S(2)}, u32[]{:S(2)}) async-start(bf16[4,160,1792]{2,1,0:T(8,128)(2,1)} %fusion), calls=%async_computation.3 | async-start | bytes 4587520 | tf_op jit(solution)/shard_map/all_to_all | solution.py:721
  741.0 168.5 %reduce-scatter.5.cloned.1.call-start = ((), (), s32[]{:S(2)}) async-start(), calls=%async_computation.8 | async-start | bytes 3379200 | tf_op jit(solution)/shard_map/reduce_scatter | solution.py:800
  755.8 99.8 %collective-permute-start.51 = (bf16[2,2,256,1280]{3,2,0,1:T(8,128)(2,1)}, bf16[2,2,256,1280]{3,2,0,1:T(8,128)(2,1)}, u32[]{:S(2)}, u32[]{:S(2)}) collective-permute-start(bf16[2,2,256,1280]{3,2,0,1:T(8,128)(2,1)} %copy.146), channel_id=1, source_target_pairs={{0,1},{1,0},{2,3},{3,2},{4,5},{5,4},{6,7},{7,6},{8,9},{9,8},{10,11... | collective-permute-start | bytes 7864328 | tf_op jit(solution)/shard_map/ppermute | solution.py:54
  776.2 95.4 %collective-permute-start.47 = (bf16[2,2,256,1280]{3,2,0,1:T(8,128)(2,1)}, bf16[2,2,256,1280]{3,2,0,1:T(8,128)(2,1)}, u32[]{:S(2)}, u32[]{:S(2)}) collective-permute-start(bf16[2,2,256,1280]{3,2,0,1:T(8,128)(2,1)} %copy.140), channel_id=1, source_target_pairs={{0,2},{2,0},{1,3},{3,1},{4,6},{6,4},{5,7},{7,5},{8,10},{10,8},{9,1... | collective-permute-start | bytes 7864328 | tf_op jit(solution)/shard_map/ppermute | solution.py:54
  815.6 54.4 %collective-permute-start.49 = (bf16[2,256,1280]{2,1,0:T(8,128)(2,1)S(1)}, bf16[2,256,1280]{2,1,0:T(8,128)(2,1)S(1)}, u32[]{:S(2)}, u32[]{:S(2)}) collective-permute-start(bf16[2,256,1280]{2,1,0:T(8,128)(2,1)S(1)} %get-tuple-element.160), channel_id=1, source_target_pairs={{0,4},{4,0},{1,5},{5,1},{2,6},{6,2},{3,7},{7,3},{8,12},{12,8},{9,1... | collective-permute-start | bytes 3932168 | tf_op jit(solution)/shard_map/ppermute | solution.py:54
  870.0 41.1 %collective-permute-start.54 = (bf16[2,256,1280]{2,1,0:T(8,128)(2,1)}, bf16[2,256,1280]{2,1,0:T(8,128)(2,1)}, u32[]{:S(2)}, u32[]{:S(2)}) collective-permute-start(bf16[2,256,1280]{2,1,0:T(8,128)(2,1)} %get-tuple-element.169), channel_id=1, source_target_pairs={{0,4},{4,0},{1,5},{5,1},{2,6},{6,2},{3,7},{7,3},{8,12},{12,8},{9,1... | collective-permute-start | bytes 3932168 | tf_op jit(solution)/shard_map/ppermute | solution.py:54
  871.6 39.6 %collective-permute-start.53 = (bf16[2,256,1280]{2,1,0:T(8,128)(2,1)}, bf16[2,256,1280]{2,1,0:T(8,128)(2,1)}, u32[]{:S(2)}, u32[]{:S(2)}) collective-permute-start(bf16[2,256,1280]{2,1,0:T(8,128)(2,1)} %add_convert_fusion.3), channel_id=1, source_target_pairs={{0,8},{8,16},{16,24},{24,0},{1,9},{9,17},{17,25},{25,1},{2,10},{10... | collective-permute-start | bytes 3932168 | tf_op jit(solution)/shard_map/ppermute | solution.py:54
  882.3 60.2 %collective-permute-start.52 = (bf16[2,256,1280]{2,1,0:T(8,128)(2,1)}, bf16[2,256,1280]{2,1,0:T(8,128)(2,1)}, u32[]{:S(2)}, u32[]{:S(2)}) collective-permute-start(bf16[2,256,1280]{2,1,0:T(8,128)(2,1)} %fusion.32), channel_id=1, source_target_pairs={{0,2},{2,0},{1,3},{3,1},{4,6},{6,4},{5,7},{7,5},{8,10},{10,8},{9,1... | collective-permute-start | bytes 3932168 | tf_op jit(solution)/shard_map/ppermute | solution.py:54
  885.5 60.1 %collective-permute-start.50 = (bf16[2,256,1280]{2,1,0:T(8,128)(2,1)}, bf16[2,256,1280]{2,1,0:T(8,128)(2,1)}, u32[]{:S(2)}, u32[]{:S(2)}) collective-permute-start(bf16[2,256,1280]{2,1,0:T(8,128)(2,1)} %fusion.31), channel_id=1, source_target_pairs={{0,1},{1,0},{2,3},{3,2},{4,5},{5,4},{6,7},{7,6},{8,9},{9,8},{10,11... | collective-permute-start | bytes 3932168 | tf_op jit(solution)/shard_map/ppermute | solution.py:54
  953.9 82.3 %all-to-all-start.4 = ((bf16[4,112,1280]{2,1,0:T(8,128)(2,1)}), bf16[4,112,1280]{2,1,0:T(8,128)(2,1)}, u32[]{:S(2)}, u32[]{:S(2)}) async-start(bf16[4,112,1280]{2,1,0:T(8,128)(2,1)} %fusion.28), calls=%async_computation.5 | async-start | bytes 2293760 | tf_op jit(solution)/shard_map/all_to_all | solution.py:721
  960.9 53.1 %collective-permute-start.70 = (bf16[4,2,2,40,1280]{4,3,2,1,0:T(8,128)(2,1)}, bf16[4,2,2,40,1280]{4,3,2,1,0:T(8,128)(2,1)}, u32[]{:S(2)}, u32[]{:S(2)}) collective-permute-start(bf16[4,2,2,40,1280]{4,3,2,1,0:T(8,128)(2,1)} %dynamic-slice_bitcast_fusion.1), channel_id=1, source_target_pairs={{0,4},{4,0},{1,5},{5,1},{2,6},{6,2},{3,7},{7,3},{8,12},{12,8},{9,1... | collective-permute-start | bytes 4915208 | tf_op jit(solution)/shard_map/ppermute | solution.py:54
  1048.1 44.1 %collective-permute-start.60 = (bf16[256,1280]{1,0:T(8,128)(2,1)S(1)}, bf16[256,1280]{1,0:T(8,128)(2,1)S(1)}, u32[]{:S(2)}, u32[]{:S(2)}) collective-permute-start(bf16[256,1280]{1,0:T(8,128)(2,1)S(1)} %fusion.52), channel_id=1, source_target_pairs={{0,8},{8,16},{16,24},{24,0},{1,9},{9,17},{17,25},{25,1},{2,10},{10... | collective-permute-start | bytes 1966088 | tf_op jit(solution)/shard_map/ppermute | solution.py:54
  (168 other events, 4846.3 us)
Sparse Core Ops, SparseCore 0:
  11.7 138.4 all-gather.3
  152.9 179.6 all-gather.5
  457.2 131.1 reduce-scatter.6
  762.5 147.0 reduce-scatter.4

commit v5 on v4

--- a/solution.py
+++ b/solution.py
@@ -70,14 +70,15 @@
     return [value] + [shift_by(value, axis, k) for k in range(1, lax.axis_size(axis))]
 
 
-def ring_sum(blocks, axis):
+def ring_sum(blocks, axis, events=()):
     n = len(blocks)
     if n == 1:
         return blocks[0].astype(F32)
     moving = blocks[1].astype(BF)
     for k in range(2, n):
-        moving = (shift(moving, axis).astype(F32) + blocks[k].astype(F32)).astype(BF)
-    return shift(moving, axis).astype(F32) + blocks[0].astype(F32)
+        moving = after(shift(moving, axis), *events)
+        moving = (moving.astype(F32) + blocks[k].astype(F32)).astype(BF)
+    return after(shift(moving, axis), *events).astype(F32) + blocks[0].astype(F32)
 
 
 def ring_blocks(arrays, axis, dim):
@@ -97,7 +98,7 @@
     return lax.optimization_barrier((value, *events))[0]
 
 
-def place_kernel(counts, columns, index_ref, *refs):
+def place_kernel(counts, cuts, index_ref, *refs):
     n = len(counts)
     pieces, outs, sems = refs[:n], refs[n:-1], refs[-1]
     t = 0
@@ -105,35 +106,35 @@
         for j in range(count):
             at = index_ref[t]
             t += 1
-            for o, (low, high) in enumerate(columns):
+            for o, (rows, low, high) in enumerate(cuts):
                 pltpu.make_async_copy(
-                    piece.at[j, :, pl.ds(low, high - low)], outs[o].at[at], sems.at[o]
+                    piece.at[j, pl.ds(*rows), pl.ds(low, high - low)], outs[o].at[at], sems.at[o]
                 ).start()
-    for o in range(len(columns)):
+    for o in range(len(cuts)):
         pltpu.make_async_copy(outs[o], outs[o], sems.at[o]).wait()
 
 
-def place(index, pieces, widths):
+def place(index, pieces, cuts):
     rows, total = pieces[0].shape[-2:]
     pieces = [piece.reshape(-1, rows, total) for piece in pieces]
     counts = [piece.shape[0] for piece in pieces]
-    edges = np.cumsum([0] + list(widths))
-    columns = [(int(low), int(high)) for low, high in zip(edges[:-1], edges[1:])]
     n = sum(counts)
     outs = pl.pallas_call(
-        functools.partial(place_kernel, counts, columns),
+        functools.partial(place_kernel, counts, cuts),
         in_specs=[pl.BlockSpec(memory_space=pltpu.SMEM)]
         + [pl.BlockSpec(memory_space=pl.ANY)] * len(pieces),
-        out_specs=[pl.BlockSpec(memory_space=pltpu.VMEM)] * len(widths),
-        scratch_shapes=[pltpu.SemaphoreType.DMA((len(widths),))],
-        out_shape=[jax.ShapeDtypeStruct((n, rows, w), pieces[0].dtype) for w in widths],
+        out_specs=[pl.BlockSpec(memory_space=pltpu.VMEM)] * len(cuts),
+        scratch_shapes=[pltpu.SemaphoreType.DMA((len(cuts),))],
+        out_shape=[
+            jax.ShapeDtypeStruct((n, c[0][1], c[2] - c[1]), pieces[0].dtype) for c in cuts
+        ],
         compiler_params=pltpu.CompilerParams(vmem_limit_bytes=VMEM_LIMIT // 2),
         cost_estimate=pl.CostEstimate(
             flops=0, bytes_accessed=4 * n * rows * total, transcendentals=0
         ),
         name="place",
     )(index, *pieces)
-    return [out.reshape(n * rows, w) for out, w in zip(outs, widths)]
+    return [out.reshape(-1, out.shape[2]) for out in outs]
 
 
 def dense_steps(nq):
@@ -155,50 +156,69 @@
     return ring_gather(one, "a") + ring_gather(two, "b")
 
 
-def dense_place(pieces, steps, widths):
+def dense_place(pieces, steps, widths, due=()):
     nq, nr, na, nb = (lax.axis_size(axis) for axis in ("q", "r", "a", "b"))
-    moved = [ring_gather(piece, "r") for piece in pieces]
-    order = [(k, *s) for k in range(nr) for part in steps for s in part]
+    rows, width = pieces[0].shape[-2:]
+    flat = [piece.reshape(-1, rows, width) for piece in pieces]
+    groups = [[0, na], [k for k in range(na + nb) if k not in (0, na)]]
+    arrays, order = [], []
+    for group in groups:
+        own = jnp.concatenate([flat[k] for k in group], axis=0)
+        if group is groups[1]:
+            own = after(own, *due)
+        entries = [s for k in group for s in steps[k]]
+        for kr, part in enumerate(ring_gather(own, "r")):
+            arrays.append(part)
+            order += [(kr, *s) for s in entries]
     kr, kq, ka, kb = (np.array(column, np.int32) for column in zip(*order))
     index = lax.rem(lax.axis_index("q") - kq + nq, nq) * nr
     index = index + lax.rem(lax.axis_index("r") - kr + nr, nr)
     index = index * na + lax.rem(lax.axis_index("a") - ka + na, na)
     index = index * nb + lax.rem(lax.axis_index("b") - kb + nb, nb)
-    arrays = [moved[p][k] for k in range(nr) for p in range(len(pieces))]
-    return place(index.astype(jnp.int32), arrays, widths)
-
-
-def dense_sum(wholes, n_rows, middle=(), late=()):
+    edges = np.cumsum([0] + list(widths))
+    cuts = [((0, rows), int(low), int(high)) for low, high in zip(edges[:-1], edges[1:])]
+    return place(index.astype(jnp.int32), arrays, cuts)
+
+
+def dense_sum_core(wholes, n_rows):
     nq, nr, na, nb = (lax.axis_size(axis) for axis in ("q", "r", "a", "b"))
     values = [whole.reshape(nq, nr, na, nb, n_rows, whole.shape[1]) for whole in wholes]
-    value = ring_sum(ring_blocks(values, "r", 1), "r").astype(BF)
-    half = nq // 2
-    one, two = value[:half], value[half:]
-    one = ring_sum(ring_blocks([one], "a", 1), "a").astype(BF)
-    two = ring_sum(ring_blocks([two], "b", 2), "b").astype(BF)
-    one, two = after(one, *middle), after(two, *middle)
+    return ring_sum(ring_blocks(values, "r", 1), "r").astype(BF)
+
+
+def dense_sum_first(value):
+    half = value.shape[0] // 2
+    one = ring_sum(ring_blocks([value[:half]], "a", 1), "a").astype(BF)
+    two = ring_sum(ring_blocks([value[half:]], "b", 2), "b").astype(BF)
+    return one, two
+
+
+def dense_sum_second(one, two):
     one = ring_sum(ring_blocks([one], "b", 1), "b")
     two = ring_sum(ring_blocks([two], "a", 1), "a")
-    value = after(jnp.concatenate([one, two], axis=0).astype(BF), *late)
+    return jnp.concatenate([one, two], axis=0).astype(BF)
+
+
+def dense_sum_last(value):
     return ring_sum(ring_blocks([value], "q", 0), "q")
 
 
-def plane_gather(rows, even, event=()):
+def plane_gather(rows, even, first=None):
     inner, outer = ("b", "a") if even else ("a", "b")
-    first = after(jnp.stack(ring_gather(rows, inner)), *event)
+    if first is None:
+        first = jnp.stack(ring_gather(rows, inner))
     parts = ring_gather(first, outer)
     return [jnp.stack(parts)] if even else parts
 
 
-def sum_start(parts, even):
-    return ring_sum(parts, "a" if even else "b")
-
-
-def sum_end(first, even, dim=0):
+def sum_start(parts, even, events=()):
+    return ring_sum(parts, "a" if even else "b", events)
+
+
+def sum_end(first, even, dim=0, events=()):
     n = first.shape[dim]
-    return ring_sum(
-        [lax.index_in_dim(first, k, dim, False) for k in range(n)], "b" if even else "a"
-    )
+    parts = [lax.index_in_dim(first, k, dim, False) for k in range(n)]
+    return ring_sum(parts, "b" if even else "a", events)
 
 
 def project_kernel(n_query, x_ref, w_ref, cos_ref, sin_ref, q_ref, kv_ref):
@@ -421,13 +441,13 @@
 
 def expert_kernel(slots, na, nb, even, n_kept, e_ref, rank_ref, *refs):
     n_in, n_sum = (1, na) if even else (nb, nb)
-    c_refs, g_ref, refs = refs[:n_in], refs[n_in], refs[n_in + 1 :]
+    c_refs, g_refs, refs = refs[:n_in], refs[n_in : 2 * n_in], refs[2 * n_in :]
     wr_ref, w1_ref, w2_ref = refs[:3]
     refs = refs[3 + n_kept :]
     d_refs, dg_ref, refs = refs[:n_sum], refs[n_sum], refs[n_sum + 1 :]
     x_ref, h_ref, dey_ref, deg_ref = refs[:4]
     y_refs = refs[4:]
-    tok = g_ref.shape[3]
+    tok = g_refs[0].shape[-2]
     experts = wr_ref.shape[0]
     me = e_ref[0]
     step = pl.program_id(0)
@@ -436,7 +456,7 @@
     slot = lax.broadcasted_iota(jnp.int32, (slots, tok), 0).astype(F32)
     for s in range(nb):
         tokens = c_refs[0][0, s] if even else c_refs[s][0]
-        cot = g_ref[0, 0, lax.rem(e_ref[3] - s + nb, nb)]
+        cot = g_refs[0][0, s, 0] if even else g_refs[s][0, 0]
         rank = rank_ref[0, s, 0]
         logits = dot(wr_ref[...], tokens, NT)
         logits = jnp.where(rank >= 0, logits, masked_value)
@@ -499,10 +519,8 @@
     even = chunk % 2 == 0
     tok, width = c[0].shape[-2:]
     experts = router_t.shape[0]
-    plane = pl.BlockSpec(
-        (1, 1, nb, tok, width),
-        lambda i, e: (lax.rem(e[1] - chunk + nq, nq), lax.rem(e[2] - i + na, na), 0, 0, 0),
-    )
+    g_one = pl.BlockSpec((1, nb, 1, tok, width), lambda i, e: (i, 0, chunk // 2, 0, 0))
+    g_two = pl.BlockSpec((1, 1, tok, width), lambda i, e: (i, chunk // 2, 0, 0))
     one = pl.BlockSpec((1, nb, tok, width), lambda i, e: (i, 0, 0, 0))
     two = pl.BlockSpec((1, tok, width), lambda i, e: (i, 0, 0))
 
@@ -525,7 +543,7 @@
         d_shapes = [jax.ShapeDtypeStruct((na, tok, width), BF)] * nb
         y_shapes = [jax.ShapeDtypeStruct((n_half, na, tok, width), BF)] * nb
     held = [*(kept or ()), *(y_kept or ())]
-    n_in = 1 + 1 + len(c) + 1 + 3
+    n_in = 1 + 1 + len(c) + len(g) + 3
     n_out = len(d_shapes) + 1
     aliases = {n_in + k: n_out + k for k in range(len(kept or ()))}
     for k in range(len(y_kept or ())):
@@ -537,7 +555,7 @@
             grid=(na,),
             in_specs=[
                 pl.BlockSpec((1, nb, 1, experts, tok), lambda i, e: (i, 0, chunk, 0, 0)),
-                *([one] if even else [two] * nb), plane,
+                *([one, g_one] if even else [two] * nb + [g_two] * nb),
                 fixed(router_t.shape), fixed(w1.shape), fixed(w2.shape),
                 *[pl.BlockSpec(memory_space=pl.ANY)] * len(held),
             ],
@@ -560,7 +578,7 @@
             flops=n_rows * width * FF * 12, bytes_accessed=30_000_000, transcendentals=n_rows * FF
         ),
         name="experts",
-    )(expert, ranks, *c, g, router_t, w1, w2, *held)
+    )(expert, ranks, *c, *g, router_t, w1, w2, *held)
     n_d = len(d_shapes)
     return out[:n_d], out[n_d], out[n_out : n_out + 4], out[n_out + 4 :]
 
@@ -633,27 +651,25 @@
     steps = dense_steps(nq)
     front_first = dense_start(front_q)
 
-    def own_rows_of(stack, event):
-        return lax.all_to_all(after(stack, event), "q", split_axis=0, concat_axis=0, tiled=True)
-
-    def own_expert(rows):
-        parts = ring_gather(rows, "r")
-        kr = np.repeat(np.arange(nr, dtype=np.int32), nq)
-        kq = np.tile(np.arange(nq, dtype=np.int32), nr)
-        index = kq * nr + lax.rem(r_at - kr + nr, nr)
-        return place(index.astype(jnp.int32), parts, [rows.shape[2]])[0]
-
-    w1_rows = own_rows_of(expert_gate_up, front_q[-1])
+    gu_rows = expert_gate_up.shape[1]
+    folded = expert_down.reshape(nq, -1, 2 * FF)
+    both = jnp.concatenate([expert_gate_up, folded], axis=1)
+
+    rest_q = ring_gather(after(rest, front_q[-1]), "q")
+    g_q = [after(grad_low, rest_q[-1])]
+    g_q.append(shift(g_q[0], "q"))
     front_pieces = dense_end(*front_first)
-    qkv_weight, front_small = dense_place(front_pieces, steps, [3 * width, 128])
-    rest = lax.all_gather(rest, ("q", "r", "a", "b"), axis=0, tiled=True)
-    g_all = lax.all_gather(grad_low, ("q", "a", "b"), axis=0, tiled=True)
-    g_all = g_all.reshape(nq, na, nb, tok, width)
+    qkv_weight, front_small = dense_place(
+        front_pieces, steps, [3 * width, 128], (rest_q[-2],)
+    )
+    for _ in range(nq - 2):
+        g_q.append(shift(g_q[-1], "q"))
+    rest_first = dense_start([after(part, *front_pieces) for part in rest_q])
 
     kv_chunks = []
     gain_one = front_small[:, 0].astype(F32)
     inv_one = rms_scale(tokens_in)
-    normed = after((tokens_in * inv_one * gain_one).astype(BF), w1_rows)
+    normed = after((tokens_in * inv_one * gain_one).astype(BF), g_q[1], *rest_first)
     queries, kv_own = project(normed, qkv_weight, *tables)
     places = [
         jnp.stack(
@@ -665,23 +681,35 @@
         ).astype(jnp.int32)
         for k in range(nq)
     ]
+    rest_pieces = dense_end(*rest_first)
     state = None
     arrived = kv_own
     for k in range(nq):
         chunk = ring_gather(arrived, "r")
+        due = ()
         if k < nq - 1:
             coming = shift(arrived, "q")
+        if k == 1:
+            g_even, g_odd = (after(jnp.stack(g_q[low::2]), *rest_pieces) for low in (0, 1))
+            g_even = jnp.stack(ring_gather(g_even, "b"))
+            g_odd = jnp.stack(ring_gather(g_odd, "a"))
         state = attend_chunk(places[k], queries, chunk, state, k == nq - 1, n_ctx)
         kv_chunks.append(chunk)
         if k < nq - 1:
-            arrived = after(coming, state[0]) if k < nq - 2 else coming
+            if k == 0:
+                due = (state[0], g_q[nq - 2], *rest_pieces)
+            if k == 1:
+                due = (state[0], g_even, g_odd)
+            if k == 2:
+                g_even, g_odd = ring_gather(g_even, "a"), ring_gather(g_odd, "b")
+                due = (state[0], *g_even, *g_odd)
+            arrived = after(coming, *due)
     mixed, lse = state
-    w1, w2 = own_expert(w1_rows), own_expert(own_rows_of(expert_down, arrived))
-
-    at_in, at_out = width + 2 * FF, width + 2 * FF + flat
-    out_weight, shared_in = rest[:, :width], rest[:, width:at_in]
-    shared_out = rest[:, at_in:at_out].reshape(-1, width)
-    rest_small = rest[:, at_out:]
+    both = lax.all_to_all(after(both, arrived), "q", split_axis=0, concat_axis=0, tiled=True)
+    out_weight, shared_in, shared_out, rest_small = dense_place(
+        rest_pieces, steps, [width, 2 * FF, flat, 128]
+    )
+    shared_out = shared_out.reshape(-1, width)
     gain_two = rest_small[:, 0].astype(F32)
     router = rest_small[:, 1 : 1 + n_experts]
     residual = tokens_in + dot(mixed, out_weight)
@@ -691,43 +719,69 @@
     router_t = router.T
     kept = None
     ys = [None, None]
-    dec_parts, dgates = [], []
+    sum_first, dgates = [], []
     c_q = ring_gather(second, "q")
+    c_start = jnp.stack(ring_gather(c_q[0], "b"))
+    both = ring_gather(after(both, c_start), "r")
+    kr = np.repeat(np.arange(nr, dtype=np.int32), nq)
+    kq = np.tile(np.arange(nq, dtype=np.int32), nr)
+    index = kq * nr + lax.rem(r_at - kr + nr, nr)
+    w1, w2 = place(
+        index.astype(jnp.int32),
+        both,
+        [((0, gu_rows), 0, 2 * FF), ((gu_rows, folded.shape[1]), 0, 2 * FF)],
+    )
+    w2 = w2.reshape(-1, width)
+    g_even = [jnp.stack(g_even)]
     for k in range(nq):
-        c = plane_gather(c_q[k], k % 2 == 0, () if k < 2 else (dgates[0],))
+        rows = c_q[k] if k < 2 else after(c_q[k], dgates[0])
+        first = c_start
+        if k:
+            first = jnp.stack(ring_gather(rows, "ba"[k % 2]))
+        if k == 1:
+            first = after(first, w1)
+        c = plane_gather(rows, k % 2 == 0, first)
         dec, dgate, kept, ys[k % 2] = expert_chunk(
-            k, nq, na, nb, expert, ranks, c, g_all, router_t, w1, w2, kept, ys[k % 2], slots
+            k, nq, na, nb, expert, ranks, c, (g_even, g_odd)[k % 2], router_t, w1, w2, kept, ys[k % 2], slots
         )
-        dec_parts.append(dec)
+        sum_first.append(sum_start(dec, k % 2 == 0))
         dgates.append(dgate.reshape(na * nb, tok))
-    dec_parts[0] = [after(v, dgates[-1]) for v in dec_parts[0]]
-    firsts = [sum_start(dec_parts[k], k % 2 == 0) for k in range(nq)]
+    firsts = sum_first
     dec_sums = [sum_end(firsts[k], k % 2 == 0) for k in range(nq)]
     xs, hs, deys, degs = kept[:4]
-    down_term = dot(after(hs, firsts[nq - 2]), deys, TN).astype(BF)
-    gate_up_term = dot(after(xs, firsts[nq - 1]), degs, TN).astype(BF)
+    down_term = dot(hs, deys, TN).astype(BF)
+    gate_up_term = dot(xs, degs, TN).astype(BF)
+    terms = [
+        gate_up_term.reshape(nq, nr, gu_rows, 2 * FF),
+        down_term.reshape(nq, nr, -1, 2 * FF),
+    ]
+    at = [lax.rem(r_at - k + nr, nr) for k in range(nr)]
+    expert_rows = ring_sum(
+        [
+            jnp.concatenate(
+                [lax.dynamic_index_in_dim(t, i, 1, keepdims=False) for t in terms], axis=1
+            )
+            for i in at
+        ],
+        "r",
+    ).astype(BF)
     moving = dec_sums[1].astype(BF)
     for k in range(2, nq):
         term = dec_sums[k]
-        if k >= nq - 2:
-            term = after(term, down_term if k == nq - 2 else gate_up_term)
+        if k == 2:
+            term = after(term, expert_rows)
         moving = (shift(moving, "q").astype(F32) + term).astype(BF)
     routed_grad = shift(moving, "q").astype(F32) + dec_sums[0]
 
-    def expert_rows(whole, *events):
-        value = whole.reshape(nq, nr, -1, whole.shape[1])
-        value = ring_sum(ring_blocks([value], "r", 1), "r").astype(BF)
-        value = after(value, *events)
-        return lax.all_to_all(value, "q", split_axis=0, concat_axis=0, tiled=True)
-
-    gate_up_rows_low = expert_rows(gate_up_term)
-
-    shared_pre = dot(second, shared_in)
+    expert_rows = lax.all_to_all(expert_rows, "q", split_axis=0, concat_axis=0, tiled=True)
+
+    later = after(second, dgates[0])
+    shared_pre = dot(later, shared_in)
     shared_gate, shared_up = shared_pre[:, :FF], shared_pre[:, FF:]
     shared_sig = jax.nn.sigmoid(shared_gate)
     shared_hidden = (shared_gate * shared_sig * shared_up).astype(BF)
 
-    logits = jnp.where(named, dot(second, router), masked_value)
+    logits = jnp.where(named, dot(later, router), masked_value)
     raised = jnp.where(named, jnp.exp(logits - jnp.max(logits, axis=1, keepdims=True)), 0.0)
     gates = raised / jnp.sum(raised, axis=1, keepdims=True)
     n_all = nq * na * nb
@@ -751,15 +805,6 @@
         ],
         axis=1,
     ).astype(BF)
-    every = ("q", "r", "a", "b")
-    shared_grad = jnp.concatenate(
-        [
-            dot(second, shared_pre_grad, TN).astype(BF),
-            dot(shared_hidden, grad_low, TN).astype(BF).reshape(width, flat),
-        ],
-        axis=1,
-    )
-    shared_grad = lax.psum_scatter(shared_grad, every, scatter_dimension=0, tiled=True)
     second_grad = (
         dot(shared_pre_grad, shared_in, NT) + dot(grad_logits, router, NT) + routed_grad
     )
@@ -768,12 +813,15 @@
     mixed_grad = residual_grad.astype(BF)
     heads_grad = dot(mixed_grad, out_weight, NT).astype(BF)
 
+    y_first = [
+        sum_start([after(v, routed_grad) for v in ys[p]], p == 0) for p in (0, 1)
+    ]
     dq = None
     moving = None
-    held = after(heads_grad, shared_grad, gate_up_rows_low)
+    held = heads_grad
     for step, k in enumerate(list(range(1, nq)) + [0]):
         if step == 2:
-            held = after(held, moving)
+            held = after(held, moving, expert_rows)
         dq, parts = attend_back_chunk(
             places[k], queries, held, mixed, lse, tables, kv_chunks[k], dq, k == 0, n_ctx
         )
@@ -783,56 +831,68 @@
             first_move = moving
         elif k:
             moving = (shift(moving, "q").astype(F32) + term).astype(BF)
-    last_move = moving
-    kv_back = finish_keys(shift(moving, "q"), term, *tables)
-
-    y_sums = []
-    for even in (True, False):
-        first = sum_start([after(v, routed_grad) for v in ys[0 if even else 1]], even)
-        y_sums.append(sum_end(after(first, first_move), even, 1))
-    y_sums = after(y_sums, kv_back)
-    routed_sum = ring_sum([y_sums[k % 2][k // 2] for k in range(nq)], "q")
-    layer_out = (residual + dot(shared_hidden, shared_out) + routed_sum).astype(BF)
-
-
-    down_rows_low = expert_rows(down_term, last_move)
-    gate_up_grad, down_grad = gate_up_rows_low.astype(F32), down_rows_low.astype(F32)
-    out_part = lax.psum_scatter(
-        dot(mixed, mixed_grad, TN).astype(BF), every, scatter_dimension=0, tiled=True
-    )
-    shared_grad, out_part = shared_grad.astype(F32), out_part.astype(F32)
-    query_grad = dense_sum([after(dot(normed, dq, TN).astype(BF), last_move)], own_rows)
+    late = dense_sum_core(
+        [
+            dot(normed, dq, TN).astype(BF),
+            dot(mixed, mixed_grad, TN).astype(BF),
+            dot(later, shared_pre_grad, TN).astype(BF),
+            dot(shared_hidden, grad_low, TN).astype(BF).reshape(width, flat),
+        ],
+        own_rows,
+    )
+    y_sums = [sum_end(after(y_first[p], dq), p == 0, 1) for p in (0, 1)]
+    late = dense_sum_first(late)
+    kv_back = finish_keys(shift(moving, "q"), after(term, *late), *tables)
+
+    gate_up_grad = expert_rows[:, :gu_rows].astype(F32)
+    down_grad = expert_rows[:, gu_rows:].reshape(nq, -1, width).astype(F32)
     normed_grad = dot(dq, qkv_weight[:, :width], NT)
     normed_grad += dot(kv_back[0], qkv_weight[:, width : 2 * width], NT)
     normed_grad += dot(kv_back[1], qkv_weight[:, 2 * width :], NT)
     attn_gain_grad = jnp.sum(normed_grad * tokens_in * inv_one, axis=0)
     input_grad = residual_grad + norm_back(normed_grad, tokens_in, inv_one, gain_one)
-    kv_weight_grad = dense_sum(
+    small_grad = jnp.concatenate(
+        [
+            attn_gain_grad[:, None],
+            ffn_gain_grad[:, None],
+            dot(second, grad_logits, TN),
+            jnp.zeros((width, 126 - n_experts), F32),
+        ],
+        axis=1,
+    ).astype(BF)
+    key_value = dense_sum_core(
         [
             dot(normed, kv_back[0], TN).astype(BF),
             dot(normed, kv_back[1], TN).astype(BF),
-            jnp.concatenate(
-                [
-                    attn_gain_grad[:, None],
-                    ffn_gain_grad[:, None],
-                    dot(second, grad_logits, TN),
-                    jnp.zeros((width, 126 - n_experts), F32),
-                ],
-                axis=1,
-            ).astype(BF),
+            small_grad,
         ],
         own_rows,
     )
+    y_sums = after(y_sums, kv_back)
+    y_terms = [y_sums[k % 2][k // 2] for k in range(nq)]
+    late = dense_sum_second(*late)
+    first_kv = dense_sum_first(key_value)
+    last_kv = dense_sum_second(*first_kv)
+    y_moving = y_terms[1].astype(BF)
+    events = [(key_value,), first_kv, (late,)]
+    for k in range(2, nq + 1):
+        y_moving = after(shift(y_moving, "q"), *events[min(k - 2, 2)])
+        routed_sum = y_moving.astype(F32) + y_terms[k % nq]
+        y_moving = routed_sum.astype(BF)
+    late_grad = dense_sum_last(after(late, *first_kv))
+    kv_weight_grad = dense_sum_last(last_kv)
+    layer_out = (residual + dot(shared_hidden, shared_out) + routed_sum).astype(BF)
+    at_out, at_shared, at_down = width, 2 * width, 2 * width + 2 * FF
     return (
         layer_out[None],
         input_grad[None],
         kv_weight_grad[:, 2 * width],
-        jnp.concatenate([query_grad, kv_weight_grad[:, : 2 * width]], axis=1),
-        out_part,
+        jnp.concatenate([late_grad[:, :at_out], kv_weight_grad[:, : 2 * width]], axis=1),
+        late_grad[:, at_out:at_shared],
         kv_weight_grad[:, 2 * width + 1],
         kv_weight_grad[:, 2 * width + 2 : 2 * width + 2 + n_experts],
-        shared_grad[:, : 2 * FF],
-        shared_grad[:, 2 * FF :].reshape(down_rows, width),
+        late_grad[:, at_shared:at_down],
+        late_grad[:, at_down:].reshape(down_rows, width),
         gate_up_grad,
         down_grad,
     )

time: 1130 us -> 1040 us (0.920)
  waiting for transfers between devices: 517 us -> 439 us
  local copies, waits for them, and re-layouts: 81.3 us -> 125 us
  starting transfers between devices: 124 us -> 81.5 us
  other arithmetic: 102 us -> 120 us
  between operations: 16.1 us -> 3.38 us
    ppermute x76 -> x88, starting transfers between devices: 94.5 us -> 62.6 us  [shift(): return lax.ppermute(value, axis, [(i, (i + 1) % n) for i in range(n)])]
    reduce_scatter x1 -> x0, waiting for transfers between devices: 24.1 us -> none  [body(): lax.psum_scatter(dot(mixed, mixed_grad, TN).astype(BF), every, scatter_di...]
    all_to_all x4 -> x2, waiting for transfers between devices: 63.9 us -> 42.7 us  [the longest x1 30 us: body(): lax.all_to_all(after(both, arrived), 'q', split_axis=0, concat_axis=0, ti...]
    dynamic_slice x0 -> x12, local copies, waits for them, and re-layouts: none -> 19.6 us  [ring_blocks(): lax.dynamic_index_in_dim(v, at, dim, keepdims=False)]
    ppermute x76 -> x88, waiting for transfers between devices: 405 us -> 386 us  [shift(): return lax.ppermute(value, axis, [(i, (i + 1) % n) for i in range(n)])]
    unnamed x230 -> x348, local copies, waits for them, and re-layouts: 32.2 us -> 50.5 us
    another operation x0 -> x3, local copies, waits for them, and re-layouts: none -> 15.4 us  [the longest x1 5.16 us: body(): shared_out = shared_out.reshape(-1, width)]
    another operation x4 -> x8, other arithmetic: 8.47 us -> 22.3 us  [the longest x2 9.83 us: body(): g_even = [jnp.stack(g_even)]]
  transfers between devices with their start and end apart: 88 -> 94, of which waited for: 41 -> 48; matrix products, arithmetic and copies ran while one was open for 20% -> 24% of each run, Pallas kernels for 18% -> 18%
where the time goes in v5:
time: 1040 us; the launch traced here: 1030 us
  waiting for transfers between devices  439 us (42%)
  Pallas kernels  196 us (19%)
  local copies, waits for them, and re-layouts  125 us (12%)
  other arithmetic  120 us (12%)
  starting transfers between devices  81.5 us (8%)
  matrix products  67.9 us (7%)
    ppermute x88, waiting for transfers between devices, shift(): return lax.ppermute(value, axis, [(i, (i + 1) % n) for i in range(n)])  386 us
    pallas_call x4, Pallas kernels, expert_chunk(): pl.pallas_call(functools.partial(expert_kernel, slots, na, nb, even, len(...  91.2 us
    dot_general x21, matrix products, dot(): return lax.dot_general(a, b, (dims, ((), ())), preferred_element_type=F32)  67.9 us
    ppermute x88, starting transfers between devices, shift(): return lax.ppermute(value, axis, [(i, (i + 1) % n) for i in range(n)])  62.6 us
    unnamed x348, local copies, waits for them, and re-layouts  50.5 us
    pallas_call x4, Pallas kernels, attend_back_chunk(): pl.pallas_call(functools.partial(attend_back_kernel, n_ctx, n, first, las...  44.5 us
    pallas_call x4, Pallas kernels, attend_chunk(): pl.pallas_call(functools.partial(attend_kernel, n_ctx, n, first, last), g...  33.5 us
    all_to_all x1, waiting for transfers between devices, body(): lax.all_to_all(after(both, arrived), 'q', split_axis=0, concat_axis=0, ti...  30 us
  transfers between devices with their start and end apart: 94, of which 48 were waited for; matrix products, arithmetic and copies ran while one was open for 24% of the time, Pallas kernels for 18%

profile of v5, /device:TPU:0, one launch (start us, length us, event | category | flops | bytes accessed | tf_op | source)
XLA Modules:
  0.0 1032.8 jit_solution(14623828653789654384)
XLA Ops:
  48.5 11.2 %collective-permute-done.9 = bf16[2,40,3968]{2,1,0:T(8,128)(2,1)S(1)} collective-permute-done((bf16[2,40,3968]{2,1,0:T(8,128)(2,1)S(1)}, bf16[2,40,3968]{2,1,0:T(8,128)(2,1)S(1)}, u32[]{:S(2)}, u32[]{:S(2)}) %collective-permute-start.9) | collective-permute-done | bytes 634912 | tf_op jit(solution)/shard_map/ppermute | solution.py:54
  63.2 12.1 %collective-permute-done.13 = bf16[40,4096]{1,0:T(8,128)(2,1)S(1)} collective-permute-done((bf16[40,4096]{1,0:T(8,128)(2,1)S(1)}, bf16[40,4096]{1,0:T(8,128)(2,1)S(1)}, u32[]{:S(2)}, u32[]{:S(2)}) %collective-permute-start.13) | collective-permute-done | bytes 327712 | tf_op jit(solution)/shard_map/ppermute | solution.py:54
  77.0 9.2 collective-permute-done.14
  98.1 12.4 %collective-permute-done.17 = bf16[256,1280]{1,0:T(8,128)(2,1)S(1)} collective-permute-done((bf16[256,1280]{1,0:T(8,128)(2,1)S(1)}, bf16[256,1280]{1,0:T(8,128)(2,1)S(1)}, u32[]{:S(2)}, u32[]{:S(2)}) %collective-permute-start.17) | collective-permute-done | bytes 655392 | tf_op jit(solution)/shard_map/ppermute | solution.py:54
  114.5 10.8 %collective-permute-done.22 = bf16[256,1280]{1,0:T(8,128)(2,1)} collective-permute-done((bf16[256,1280]{1,0:T(8,128)(2,1)S(1)}, bf16[256,1280]{1,0:T(8,128)(2,1)}, u32[]{:S(2)}, u32[]{:S(2)}) %collective-permute-start.22) | collective-permute-done | bytes 655392 | tf_op jit(solution)/shard_map/ppermute | solution.py:54
  162.1 19.4 %collective-permute-done.20.refs_0_ = bf16[2,256,1280]{2,1,0:T(8,128)(2,1)} collective-permute-done((bf16[2,256,1280]{2,1,0:T(8,128)(2,1)S(1)}, bf16[2,256,1280]{2,1,0:T(8,128)(2,1)}, u32[]{:S(2)}, u32[]{:S(2)}) %collective-permute-start.20) | collective-permute-done | bytes 1310752 | tf_op jit(solution)/shard_map/ppermute | solution.py:54
  194.1 9.2 attend.5
  205.4 14.1 %collective-permute-done.25.refs_0_ = bf16[2,256,1280]{2,1,0:T(8,128)(2,1)S(1)} collective-permute-done((bf16[2,256,1280]{2,1,0:T(8,128)(2,1)}, bf16[2,256,1280]{2,1,0:T(8,128)(2,1)S(1)}, u32[]{:S(2)}, u32[]{:S(2)}) %collective-permute-start.25) | collective-permute-done | bytes 1310752 | tf_op jit(solution)/shard_map/ppermute | solution.py:54
  272.4 10.5 %attend.7 = (bf16[256,1280]{1,0:T(8,128)(2,1)S(1)}, f32[10,256,128]{2,1,0:T(8,128)S(1)}) custom-call(s32[3]{0:T(128)S(1)} %pad_add_fusion.place_ref, bf16[256,1280]{1,0:T(8,128)(2,1)S(1)} %copy-done.42, bf16[2,256,1280]{2,1,0:T(8,128)(2,1)} %collective-permute-done.30.refs_0_, bf16[2,256,1280]{2,1,0:T(8,128)(2,1)} %collective-permute-done.34.refs_1_, ...), custom_call_target="tpu_custom_call" | custom-call | flops 2684354560 | bytes 2621440 | tf_op jit(solution)/shard_map/attend/pallas_call | solution.py:362
  286.1 15.8 %collective-permute-done.37 = bf16[256,1280]{1,0:T(8,128)(2,1)S(1)} collective-permute-done((bf16[256,1280]{1,0:T(8,128)(2,1)S(1)}, bf16[256,1280]{1,0:T(8,128)(2,1)S(1)}, u32[]{:S(2)}, u32[]{:S(2)}) %collective-permute-start.37) | collective-permute-done | bytes 655392 | tf_op jit(solution)/shard_map/ppermute | solution.py:54
  303.6 30.0 %all-to-all-done.refs_0_ = bf16[4,240,1792]{2,1,0:T(8,128)(2,1)S(1)} async-done(((bf16[4,240,1792]{2,1,0:T(8,128)(2,1)}), bf16[4,240,1792]{2,1,0:T(8,128)(2,1)S(1)}, u32[]{:S(2)}, u32[]{:S(2)}) %all-to-all-start) | async-done | bytes 3440672 | tf_op jit(solution)/shard_map/all_to_all | solution.py:708
  335.8 17.1 %collective-permute-done.40 = bf16[256,1280]{1,0:T(8,128)(2,1)} collective-permute-done((bf16[256,1280]{1,0:T(8,128)(2,1)}, bf16[256,1280]{1,0:T(8,128)(2,1)}, u32[]{:S(2)}, u32[]{:S(2)}) %collective-permute-start.40) | collective-permute-done | bytes 655392 | tf_op jit(solution)/shard_map/ppermute | solution.py:54
  396.4 23.4 %experts.4 = (bf16[2,256,1280]{2,1,0:T(8,128)(2,1)}, bf16[2,256,1280]{2,1,0:T(8,128)(2,1)}, f32[2,2,1,256]{3,2,1,0:T(1,128)}, bf16[2816,1280]{1,0:T(8,128)(2,1)}...) custom-call(s32[4]{0:T(128)} %pad_add_fusion.4.e_ref, ...), custom_call_target="tpu_custom_call" | custom-call | flops 9688842240 | bytes 30000000 | tf_op jit(solution)/shard_map/experts/pallas_call | solution.py:551
  442.8 25.7 %collective-permute-done.52 = bf16[256,1280]{1,0:T(8,128)(2,1)S(1)} collective-permute-done((bf16[256,1280]{1,0:T(8,128)(2,1)}, bf16[256,1280]{1,0:T(8,128)(2,1)S(1)}, u32[]{:S(2)}, u32[]{:S(2)}) %collective-permute-start.52) | collective-permute-done | bytes 655392 | tf_op jit(solution)/shard_map/ppermute | solution.py:54
  471.7 22.3 %experts.5 = (bf16[2,256,1280]{2,1,0:T(8,128)(2,1)}, bf16[2,256,1280]{2,1,0:T(8,128)(2,1)}, f32[2,2,1,256]{3,2,1,0:T(1,128)}, bf16[2816,1280]{1,0:T(8,128)(2,1)}...) custom-call(s32[4]{0:T(128)} %pad_add_fusion.4.e_ref, ...), custom_call_target="tpu_custom_call", output_to_operand_aliasing={{3}: (9, {}), {4}: (10, {}), {5}: (11, {}), {6}: (12, {})} | custom-call | flops 9688842240 | bytes 30000000 | tf_op jit(solution)/shard_map/experts/pallas_call | solution.py:551
  497.0 23.5 %experts.6 = (bf16[2,256,1280]{2,1,0:T(8,128)(2,1)}, bf16[2,256,1280]{2,1,0:T(8,128)(2,1)}, f32[2,2,1,256]{3,2,1,0:T(1,128)}, bf16[2816,1280]{1,0:T(8,128)(2,1)}...) custom-call(s32[4]{0:T(128)} %pad_add_fusion.4.e_ref, ...), custom_call_target="tpu_custom_call", output_to_operand_aliasing={{3}: (7, {}), {4}: (8, {}), {5}: (9, {}), {6}: (10, {}), {7... | custom-call | flops 9688842240 | bytes 30000000 | tf_op jit(solution)/shard_map/experts/pallas_call | solution.py:551
  521.5 22.1 %experts.7 = (bf16[2,256,1280]{2,1,0:T(8,128)(2,1)}, bf16[2,256,1280]{2,1,0:T(8,128)(2,1)}, f32[2,2,1,256]{3,2,1,0:T(1,128)}, bf16[2816,1280]{1,0:T(8,128)(2,1)}...) custom-call(s32[4]{0:T(128)} %pad_add_fusion.4.e_ref, ...), custom_call_target="tpu_custom_call", output_to_operand_aliasing={{3}: (9, {}), {4}: (10, {}), {5}: (11, {}), {6}: (12, {}), ... | custom-call | flops 9688842240 | bytes 30000000 | tf_op jit(solution)/shard_map/experts/pallas_call | solution.py:551
  545.7 20.8 %convolution_convert_fusion.4 = bf16[1280,1792]{1,0:T(8,128)(2,1)} fusion(bf16[2816,1280]{1,0:T(8,128)(2,1)} %get-tuple-element.171, bf16[2816,1792]{1,0:T(8,128)(2,1)} %get-tuple-element.172), kind=kOutput, calls=%fused_computation.6 | convolution fusion | flops 12920750080 | bytes 21889024 | tf_op jit(solution)/shard_map/dot_general | solution.py:45
  592.4 9.7 collective-permute-done.47
  606.4 11.5 %collective-permute-done.48 = bf16[256,1280]{1,0:T(8,128)(2,1)S(1)} collective-permute-done((bf16[256,1280]{1,0:T(8,128)(2,1)S(1)}, bf16[256,1280]{1,0:T(8,128)(2,1)S(1)}, u32[]{:S(2)}, u32[]{:S(2)}) %collective-permute-start.48) | collective-permute-done | bytes 655392 | tf_op jit(solution)/shard_map/ppermute | solution.py:54
  645.8 10.3 collective-permute-done.58
  667.0 11.5 %attend_back.4 = (f32[256,1280]{1,0:T(8,128)S(1)}, f32[2,256,1280]{2,1,0:T(8,128)S(1)}, bf16[2,256,1280]{2,1,0:T(8,128)(2,1)}) custom-call(s32[3]{0:T(128)S(1)} %pad_add_fusion.2.place_ref, bf16[256,1280]{1,0:T(8,128)(2,1)S(1)} %copy-done.43, bf16[256,1280]{1,0:T(8,128)(2,1)S(1)} %convolution_convert_fusion.8.do_ref, bf16[256,1280]{1,0:T(8,128)(2,1)S(1)} %copy-done.13, ...), custom_call_target="tpu_custom_call" | custom-call | flops 6710886400 | bytes 5242880 | tf_op jit(solution)/shard_map/attend_back/pallas_call | solution.py:423
  691.9 10.5 %attend_back.5 = (f32[256,1280]{1,0:T(8,128)S(1)}, f32[2,256,1280]{2,1,0:T(8,128)S(1)}, bf16[2,256,1280]{2,1,0:T(8,128)(2,1)S(1)}) custom-call(s32[3]{0:T(128)S(1)} %pad_add_fusion.3.place_ref, bf16[256,1280]{1,0:T(8,128)(2,1)S(1)} %copy-done.44, bf16[256,1280]{1,0:T(8,128)(2,1)S(1)} %copy-done.48, bf16[256,1280]{1,0:T(8,128)(2,1)S(1)} %copy-done.13, ...), custom_call_target="tpu_custom_call" | custom-call | flops 6710886400 | bytes 5242880 | tf_op jit(solution)/shard_map/attend_back/pallas_call | solution.py:423
  720.7 17.2 %collective-permute-done.63 = bf16[2,256,1280]{2,1,0:T(8,128)(2,1)S(1)} collective-permute-done((bf16[2,256,1280]{2,1,0:T(8,128)(2,1)S(1)}, bf16[2,256,1280]{2,1,0:T(8,128)(2,1)S(1)}, u32[]{:S(2)}, u32[]{:S(2)}) %collective-permute-start.63) | collective-permute-done | bytes 1310752 | tf_op jit(solution)/shard_map/ppermute | solution.py:54
  739.4 12.7 %all-to-all-done.2 = bf16[4,240,1792]{2,1,0:T(8,128)(2,1)} async-done(((bf16[4,240,1792]{2,1,0:T(8,128)(2,1)}), bf16[4,240,1792]{2,1,0:T(8,128)(2,1)}, u32[]{:S(2)}, u32[]{:S(2)}) %all-to-all-start.2) | async-done | bytes 3440672 | tf_op jit(solution)/shard_map/all_to_all | solution.py:776
  754.8 12.0 %attend_back.6 = (f32[256,1280]{1,0:T(8,128)S(1)}, f32[2,256,1280]{2,1,0:T(8,128)S(1)}, bf16[2,256,1280]{2,1,0:T(8,128)(2,1)}) custom-call(s32[3]{0:T(128)S(1)} %copy-done.24, bf16[256,1280]{1,0:T(8,128)(2,1)S(1)} %copy-done.45, bf16[256,1280]{1,0:T(8,128)(2,1)S(1)} %copy-done.49, bf16[256,1280]{1,0:T(8,128)(2,1)S(1)} %copy-done.13, ...), custom_call_target="tpu_custom_call" | custom-call | flops 6710886400 | bytes 5242880 | tf_op jit(solution)/shard_map/attend_back/pallas_call | solution.py:423
  766.9 10.5 %attend_back.7 = (bf16[256,1280]{1,0:T(8,128)(2,1)S(1)}, f32[2,256,1280]{2,1,0:T(8,128)S(1)}, bf16[2,256,1280]{2,1,0:T(8,128)(2,1)S(1)}) custom-call(s32[3]{0:T(128)S(1)} %copy-done.22, bf16[256,1280]{1,0:T(8,128)(2,1)S(1)} %copy-done.46, bf16[256,1280]{1,0:T(8,128)(2,1)S(1)} %copy-done.50, bf16[256,1280]{1,0:T(8,128)(2,1)S(1)} %copy-done.14, ...), custom_call_target="tpu_custom_call" | custom-call | flops 6710886400 | bytes 5242880 | tf_op jit(solution)/shard_map/attend_back/pallas_call | solution.py:423
  818.5 9.7 collective-permute-done.68
  856.3 29.6 %collective-permute-done.73 = bf16[2,2,40,5248]{3,2,0,1:T(8,128)(2,1)S(1)} collective-permute-done((bf16[2,2,40,5248]{3,2,0,1:T(8,128)(2,1)S(1)}, bf16[2,2,40,5248]{3,2,0,1:T(8,128)(2,1)S(1)}, u32[]{:S(2)}, u32[]{:S(2)}) %collective-permute-start.73) | collective-permute-done | bytes 1679392 | tf_op jit(solution)/shard_map/ppermute | solution.py:54
  930.2 16.9 %collective-permute-done.82 = bf16[2,40,5248]{2,1,0:T(8,128)(2,1)S(1)} collective-permute-done((bf16[2,40,5248]{2,1,0:T(8,128)(2,1)S(1)}, bf16[2,40,5248]{2,1,0:T(8,128)(2,1)S(1)}, u32[]{:S(2)}, u32[]{:S(2)}) %collective-permute-start.82) | collective-permute-done | bytes 839712 | tf_op jit(solution)/shard_map/ppermute | solution.py:54
  954.2 14.8 %collective-permute-done.78 = bf16[2,2,40,2688]{3,2,1,0:T(8,128)(2,1)S(1)} collective-permute-done((bf16[2,2,40,2688]{3,2,1,0:T(8,128)(2,1)S(1)}, bf16[2,2,40,2688]{3,2,1,0:T(8,128)(2,1)S(1)}, u32[]{:S(2)}, u32[]{:S(2)}) %collective-permute-start.78) | collective-permute-done | bytes 860192 | tf_op jit(solution)/shard_map/ppermute | solution.py:54
  985.7 13.8 %collective-permute-done.88 = bf16[40,5248]{1,0:T(8,128)(2,1)S(1)} collective-permute-done((bf16[40,5248]{1,0:T(8,128)(2,1)S(1)}, bf16[40,5248]{1,0:T(8,128)(2,1)S(1)}, u32[]{:S(2)}, u32[]{:S(2)}) %collective-permute-start.88) | collective-permute-done | bytes 419872 | tf_op jit(solution)/shard_map/ppermute | solution.py:54
  (721 shorter events, 529.3 us)
Async XLA Ops:
  47.6 38.6 %collective-permute-start.11 = (bf16[2,2,40,3968]{3,2,1,0:T(8,128)(2,1)S(1)}, bf16[2,2,40,3968]{3,2,1,0:T(8,128)(2,1)}, u32[]{:S(2)}, u32[]{:S(2)}) collective-permute-start(bf16[2,2,40,3968]{3,2,1,0:T(8,128)(2,1)S(1)} %pad_maximum_fusion.22), channel_id=1, source_target_pairs={{0,2},{2,0},{1,3},{3,1},{4,6},{6,4},{5,7},{7,5},{8,10},{10,8},{9,1... | collective-permute-start | bytes 3809288 | tf_op jit(solution)/shard_map/ppermute | solution.py:54
  76.9 48.4 %collective-permute-start.10 = (bf16[8,40,3968]{2,1,0:T(8,128)(2,1)S(1)}, bf16[8,40,3968]{2,1,0:T(8,128)(2,1)S(1)}, u32[]{:S(2)}, u32[]{:S(2)}) collective-permute-start(bf16[8,40,3968]{2,1,0:T(8,128)(2,1)S(1)} %pad_maximum_fusion.11.refs_0_), channel_id=1, source_target_pairs={{0,4},{4,0},{1,5},{5,1},{2,6},{6,2},{3,7},{7,3},{8,12},{12,8},{9,1... | collective-permute-start | bytes 7618568 | tf_op jit(solution)/shard_map/ppermute | solution.py:54
  88.2 37.0 %collective-permute-start.15 = (bf16[8,40,3968]{2,1,0:T(8,128)(2,1)S(1)}, bf16[8,40,3968]{2,1,0:T(8,128)(2,1)S(1)}, u32[]{:S(2)}, u32[]{:S(2)}) collective-permute-start(bf16[8,40,3968]{2,1,0:T(8,128)(2,1)S(1)} %pad_maximum_fusion.12.refs_2_), channel_id=1, source_target_pairs={{0,4},{4,0},{1,5},{5,1},{2,6},{6,2},{3,7},{7,3},{8,12},{12,8},{9,1... | collective-permute-start | bytes 7618568 | tf_op jit(solution)/shard_map/ppermute | solution.py:54
  111.9 36.8 %collective-permute-start.23 = (bf16[2,2,40,4096]{3,2,1,0:T(8,128)(2,1)}, bf16[2,2,40,4096]{3,2,1,0:T(8,128)(2,1)}, u32[]{:S(2)}, u32[]{:S(2)}) collective-permute-start(bf16[2,2,40,4096]{3,2,1,0:T(8,128)(2,1)} %pad_maximum_fusion.14), channel_id=1, source_target_pairs={{0,2},{2,0},{1,3},{3,1},{4,6},{6,4},{5,7},{7,5},{8,10},{10,8},{9,1... | collective-permute-start | bytes 3932168 | tf_op jit(solution)/shard_map/ppermute | solution.py:54
  113.7 35.0 %collective-permute-start.24 = (bf16[2,2,40,4096]{3,2,1,0:T(8,128)(2,1)}, bf16[2,2,40,4096]{3,2,1,0:T(8,128)(2,1)}, u32[]{:S(2)}, u32[]{:S(2)}) collective-permute-start(bf16[2,2,40,4096]{3,2,1,0:T(8,128)(2,1)} %pad_maximum_fusion.15), channel_id=1, source_target_pairs={{0,1},{1,0},{2,3},{3,2},{4,5},{5,4},{6,7},{7,6},{8,9},{9,8},{10,11... | collective-permute-start | bytes 3932168 | tf_op jit(solution)/shard_map/ppermute | solution.py:54
  151.5 35.0 %collective-permute-start.29 = (bf16[2,256,1280]{2,1,0:T(8,128)(2,1)}, bf16[2,256,1280]{2,1,0:T(8,128)(2,1)}, u32[]{:S(2)}, u32[]{:S(2)}) collective-permute-start(bf16[2,256,1280]{2,1,0:T(8,128)(2,1)} %pad_maximum_fusion.17), channel_id=1, source_target_pairs={{0,2},{2,0},{1,3},{3,1},{4,6},{6,4},{5,7},{7,5},{8,10},{10,8},{9,1... | collective-permute-start | bytes 3932168 | tf_op jit(solution)/shard_map/ppermute | solution.py:54
  186.0 59.6 %collective-permute-start.32 = (bf16[2,2,256,1280]{3,2,1,0:T(8,128)(2,1)}, bf16[2,2,256,1280]{3,2,1,0:T(8,128)(2,1)}, u32[]{:S(2)}, u32[]{:S(2)}) collective-permute-start(bf16[2,2,256,1280]{3,2,1,0:T(8,128)(2,1)} %get-tuple-element.304), channel_id=1, source_target_pairs={{0,2},{2,0},{1,3},{3,1},{4,6},{6,4},{5,7},{7,5},{8,10},{10,8},{9,1... | collective-permute-start | bytes 7864328 | tf_op jit(solution)/shard_map/ppermute | solution.py:54
  190.1 59.3 %collective-permute-start.33 = (bf16[2,2,256,1280]{3,2,1,0:T(8,128)(2,1)}, bf16[2,2,256,1280]{3,2,1,0:T(8,128)(2,1)}, u32[]{:S(2)}, u32[]{:S(2)}) collective-permute-start(bf16[2,2,256,1280]{3,2,1,0:T(8,128)(2,1)} %pad_maximum_fusion.6.refs_2_), channel_id=1, source_target_pairs={{0,1},{1,0},{2,3},{3,2},{4,5},{5,4},{6,7},{7,6},{8,9},{9,8},{10,11... | collective-permute-start | bytes 7864328 | tf_op jit(solution)/shard_map/ppermute | solution.py:54
  252.6 81.1 %all-to-all-start = ((bf16[4,240,1792]{2,1,0:T(8,128)(2,1)}), bf16[4,240,1792]{2,1,0:T(8,128)(2,1)S(1)}, u32[]{:S(2)}, u32[]{:S(2)}) async-start(bf16[4,240,1792]{2,1,0:T(8,128)(2,1)} %pad_maximum_fusion.2), calls=%async_computation | async-start | bytes 6881280 | tf_op jit(solution)/shard_map/all_to_all | solution.py:708
  333.6 51.1 %collective-permute-start.39 = (bf16[4,240,1792]{2,1,0:T(8,128)(2,1)S(1)}, bf16[4,240,1792]{2,1,0:T(8,128)(2,1)}, u32[]{:S(2)}, u32[]{:S(2)}) collective-permute-start(bf16[4,240,1792]{2,1,0:T(8,128)(2,1)S(1)} %all-to-all-done.refs_0_), channel_id=1, source_target_pairs={{0,4},{4,0},{1,5},{5,1},{2,6},{6,2},{3,7},{7,3},{8,12},{12,8},{9,1... | collective-permute-start | bytes 10321928 | tf_op jit(solution)/shard_map/ppermute | solution.py:54
  333.6 48.0 %collective-permute-start.38 = (bf16[2,256,1280]{2,1,0:T(8,128)(2,1)}, bf16[2,256,1280]{2,1,0:T(8,128)(2,1)}, u32[]{:S(2)}, u32[]{:S(2)}) collective-permute-start(bf16[2,256,1280]{2,1,0:T(8,128)(2,1)} %get-tuple-element.313), channel_id=1, source_target_pairs={{0,2},{2,0},{1,3},{3,1},{4,6},{6,4},{5,7},{7,5},{8,10},{10,8},{9,1... | collective-permute-start | bytes 3932168 | tf_op jit(solution)/shard_map/ppermute | solution.py:54
  371.4 52.7 %collective-permute-start.51 = (bf16[256,1280]{1,0:T(8,128)(2,1)}, bf16[256,1280]{1,0:T(8,128)(2,1)}, u32[]{:S(2)}, u32[]{:S(2)}) collective-permute-start(bf16[256,1280]{1,0:T(8,128)(2,1)} %collective-permute-done.41), channel_id=1, source_target_pairs={{0,8},{8,16},{16,24},{24,0},{1,9},{9,17},{17,25},{25,1},{2,10},{10... | collective-permute-start | bytes 1966088 | tf_op jit(solution)/shard_map/ppermute | solution.py:54
  421.3 49.3 %collective-permute-start.45 = (bf16[2,256,1280]{2,1,0:T(8,128)(2,1)}, bf16[2,256,1280]{2,1,0:T(8,128)(2,1)S(1)}, u32[]{:S(2)}, u32[]{:S(2)}) collective-permute-start(bf16[2,256,1280]{2,1,0:T(8,128)(2,1)} %pad_maximum_fusion.20.refs_0_), channel_id=1, source_target_pairs={{0,1},{1,0},{2,3},{3,2},{4,5},{5,4},{6,7},{7,6},{8,9},{9,8},{10,11... | collective-permute-start | bytes 3932168 | tf_op jit(solution)/shard_map/ppermute | solution.py:54
  422.6 196.3 %collective-permute-start.59 = (bf16[2,256,1280]{2,1,0:T(8,128)(2,1)}, bf16[2,256,1280]{2,1,0:T(8,128)(2,1)}, u32[]{:S(2)}, u32[]{:S(2)}) collective-permute-start(bf16[2,256,1280]{2,1,0:T(8,128)(2,1)} %get-tuple-element.178), channel_id=1, source_target_pairs={{0,2},{2,0},{1,3},{3,1},{4,6},{6,4},{5,7},{7,5},{8,10},{10,8},{9,1... | collective-permute-start | bytes 3932168 | tf_op jit(solution)/shard_map/ppermute | solution.py:54
  424.1 44.5 %collective-permute-start.52 = (bf16[256,1280]{1,0:T(8,128)(2,1)}, bf16[256,1280]{1,0:T(8,128)(2,1)S(1)}, u32[]{:S(2)}, u32[]{:S(2)}) collective-permute-start(bf16[256,1280]{1,0:T(8,128)(2,1)} %collective-permute-done.51), channel_id=1, source_target_pairs={{0,2},{2,0},{1,3},{3,1},{4,6},{6,4},{5,7},{7,5},{8,10},{10,8},{9,1... | collective-permute-start | bytes 1966088 | tf_op jit(solution)/shard_map/ppermute | solution.py:54
  440.8 54.5 %collective-permute-start.43 = (bf16[2,256,1280]{2,1,0:T(8,128)(2,1)}, bf16[2,256,1280]{2,1,0:T(8,128)(2,1)S(1)}, u32[]{:S(2)}, u32[]{:S(2)}) collective-permute-start(bf16[2,256,1280]{2,1,0:T(8,128)(2,1)} %get-tuple-element.311), channel_id=1, source_target_pairs={{0,2},{2,0},{1,3},{3,1},{4,6},{6,4},{5,7},{7,5},{8,10},{10,8},{9,1... | collective-permute-start | bytes 3932168 | tf_op jit(solution)/shard_map/ppermute | solution.py:54
  469.8 50.7 %collective-permute-start.53 = (bf16[2,256,1280]{2,1,0:T(8,128)(2,1)S(1)}, bf16[2,256,1280]{2,1,0:T(8,128)(2,1)S(1)}, u32[]{:S(2)}, u32[]{:S(2)}) collective-permute-start(bf16[2,256,1280]{2,1,0:T(8,128)(2,1)S(1)} %pad_maximum_fusion.21.refs_0_), channel_id=1, source_target_pairs={{0,1},{1,0},{2,3},{3,2},{4,5},{5,4},{6,7},{7,6},{8,9},{9,8},{10,11... | collective-permute-start | bytes 3932168 | tf_op jit(solution)/shard_map/ppermute | solution.py:54
  494.0 87.7 %collective-permute-start.46 = (bf16[2,256,1280]{2,1,0:T(8,128)(2,1)}, bf16[2,256,1280]{2,1,0:T(8,128)(2,1)}, u32[]{:S(2)}, u32[]{:S(2)}) collective-permute-start(bf16[2,256,1280]{2,1,0:T(8,128)(2,1)} %get-tuple-element.160), channel_id=1, source_target_pairs={{0,1},{1,0},{2,3},{3,2},{4,5},{5,4},{6,7},{7,6},{8,9},{9,8},{10,11... | collective-permute-start | bytes 3932168 | tf_op jit(solution)/shard_map/ppermute | solution.py:54
  543.6 45.4 %collective-permute-start.56 = (bf16[2,256,1280]{2,1,0:T(8,128)(2,1)}, bf16[2,256,1280]{2,1,0:T(8,128)(2,1)}, u32[]{:S(2)}, u32[]{:S(2)}) collective-permute-start(bf16[2,256,1280]{2,1,0:T(8,128)(2,1)} %get-tuple-element.176), channel_id=1, source_target_pairs={{0,1},{1,0},{2,3},{3,2},{4,5},{5,4},{6,7},{7,6},{8,9},{9,8},{10,11... | collective-permute-start | bytes 3932168 | tf_op jit(solution)/shard_map/ppermute | solution.py:54
  544.4 40.8 %collective-permute-start.49 = (bf16[2,256,1280]{2,1,0:T(8,128)(2,1)}, bf16[2,256,1280]{2,1,0:T(8,128)(2,1)}, u32[]{:S(2)}, u32[]{:S(2)}) collective-permute-start(bf16[2,256,1280]{2,1,0:T(8,128)(2,1)} %get-tuple-element.162), channel_id=1, source_target_pairs={{0,2},{2,0},{1,3},{3,1},{4,6},{6,4},{5,7},{7,5},{8,10},{10,8},{9,1... | collective-permute-start | bytes 3932168 | tf_op jit(solution)/shard_map/ppermute | solution.py:54
  591.6 40.0 %collective-permute-start.57 = (bf16[256,1280]{1,0:T(8,128)(2,1)}, bf16[256,1280]{1,0:T(8,128)(2,1)}, u32[]{:S(2)}, u32[]{:S(2)}) collective-permute-start(bf16[256,1280]{1,0:T(8,128)(2,1)} %fusion.50), channel_id=1, source_target_pairs={{0,2},{2,0},{1,3},{3,1},{4,6},{6,4},{5,7},{7,5},{8,10},{10,8},{9,1... | collective-permute-start | bytes 1966088 | tf_op jit(solution)/shard_map/ppermute | solution.py:54
  640.7 111.4 %all-to-all-start.2 = ((bf16[4,240,1792]{2,1,0:T(8,128)(2,1)}), bf16[4,240,1792]{2,1,0:T(8,128)(2,1)}, u32[]{:S(2)}, u32[]{:S(2)}) async-start(bf16[4,240,1792]{2,1,0:T(8,128)(2,1)} %add_convert_fusion.2), calls=%async_computation.2 | async-start | bytes 6881280 | tf_op jit(solution)/shard_map/all_to_all | solution.py:776
  712.4 82.6 %collective-permute-start.61 = (bf16[2,2,256,1280]{3,2,0,1:T(8,128)(2,1)}, bf16[2,2,256,1280]{3,2,0,1:T(8,128)(2,1)}, u32[]{:S(2)}, u32[]{:S(2)}) collective-permute-start(bf16[2,2,256,1280]{3,2,0,1:T(8,128)(2,1)} %copy.191), channel_id=1, source_target_pairs={{0,2},{2,0},{1,3},{3,1},{4,6},{6,4},{5,7},{7,5},{8,10},{10,8},{9,1... | collective-permute-start | bytes 7864328 | tf_op jit(solution)/shard_map/ppermute | solution.py:54
  715.2 83.0 %collective-permute-start.66 = (bf16[2,2,256,1280]{3,2,0,1:T(8,128)(2,1)}, bf16[2,2,256,1280]{3,2,0,1:T(8,128)(2,1)}, u32[]{:S(2)}, u32[]{:S(2)}) collective-permute-start(bf16[2,2,256,1280]{3,2,0,1:T(8,128)(2,1)} %copy.196), channel_id=1, source_target_pairs={{0,1},{1,0},{2,3},{3,2},{4,5},{5,4},{6,7},{7,6},{8,9},{9,8},{10,11... | collective-permute-start | bytes 7864328 | tf_op jit(solution)/shard_map/ppermute | solution.py:54
  785.3 53.9 %collective-permute-start.72 = (bf16[4,2,2,40,5248]{4,3,0,1,2:T(8,128)(2,1)}, bf16[4,2,2,40,5248]{4,3,0,1,2:T(8,128)(2,1)}, u32[]{:S(2)}, u32[]{:S(2)}) collective-permute-start(bf16[4,2,2,40,5248]{4,3,0,1,2:T(8,128)(2,1)} %pad_maximum_fusion), channel_id=1, source_target_pairs={{0,4},{4,0},{1,5},{5,1},{2,6},{6,2},{3,7},{7,3},{8,12},{12,8},{9,1... | collective-permute-start | bytes 20152328 | tf_op jit(solution)/shard_map/ppermute | solution.py:54
  794.7 33.5 %collective-permute-start.68 = (bf16[2,256,1280]{2,1,0:T(8,128)(2,1)}, bf16[2,256,1280]{2,1,0:T(8,128)(2,1)}, u32[]{:S(2)}, u32[]{:S(2)}) collective-permute-start(bf16[2,256,1280]{2,1,0:T(8,128)(2,1)} %add_convert_fusion.4), channel_id=1, source_target_pairs={{0,8},{8,16},{16,24},{24,0},{1,9},{9,17},{17,25},{25,1},{2,10},{10... | collective-permute-start | bytes 3932168 | tf_op jit(solution)/shard_map/ppermute | solution.py:54
  806.6 41.8 %collective-permute-start.67 = (bf16[2,256,1280]{2,1,0:T(8,128)(2,1)}, bf16[2,256,1280]{2,1,0:T(8,128)(2,1)}, u32[]{:S(2)}, u32[]{:S(2)}) collective-permute-start(bf16[2,256,1280]{2,1,0:T(8,128)(2,1)} %fusion.23), channel_id=1, source_target_pairs={{0,2},{2,0},{1,3},{3,1},{4,6},{6,4},{5,7},{7,5},{8,10},{10,8},{9,1... | collective-permute-start | bytes 3932168 | tf_op jit(solution)/shard_map/ppermute | solution.py:54
  831.7 59.6 %collective-permute-start.70 = (bf16[2,256,1280]{2,1,0:T(8,128)(2,1)}, bf16[2,256,1280]{2,1,0:T(8,128)(2,1)}, u32[]{:S(2)}, u32[]{:S(2)}) collective-permute-start(bf16[2,256,1280]{2,1,0:T(8,128)(2,1)} %add_convert_fusion.3), channel_id=1, source_target_pairs={{0,8},{8,16},{16,24},{24,0},{1,9},{9,17},{17,25},{25,1},{2,10},{10... | collective-permute-start | bytes 3932168 | tf_op jit(solution)/shard_map/ppermute | solution.py:54
  847.5 38.3 %collective-permute-start.73 = (bf16[2,2,40,5248]{3,2,0,1:T(8,128)(2,1)S(1)}, bf16[2,2,40,5248]{3,2,0,1:T(8,128)(2,1)S(1)}, u32[]{:S(2)}, u32[]{:S(2)}) collective-permute-start(bf16[2,2,40,5248]{3,2,0,1:T(8,128)(2,1)S(1)} %dynamic-slice_bitcast_fusion.3), channel_id=1, source_target_pairs={{0,2},{2,0},{1,3},{3,1},{4,6},{6,4},{5,7},{7,5},{8,10},{10,8},{9,1... | collective-permute-start | bytes 5038088 | tf_op jit(solution)/shard_map/ppermute | solution.py:54
  851.7 38.0 %collective-permute-start.74 = (bf16[2,2,40,5248]{3,2,0,1:T(8,128)(2,1)S(1)}, bf16[2,2,40,5248]{3,2,0,1:T(8,128)(2,1)S(1)}, u32[]{:S(2)}, u32[]{:S(2)}) collective-permute-start(bf16[2,2,40,5248]{3,2,0,1:T(8,128)(2,1)S(1)} %dynamic-slice_bitcast_fusion.2), channel_id=1, source_target_pairs={{0,1},{1,0},{2,3},{3,2},{4,5},{5,4},{6,7},{7,6},{8,9},{9,8},{10,11... | collective-permute-start | bytes 5038088 | tf_op jit(solution)/shard_map/ppermute | solution.py:54
  914.8 34.1 %collective-permute-start.75 = (bf16[256,1280]{1,0:T(8,128)(2,1)}, bf16[256,1280]{1,0:T(8,128)(2,1)}, u32[]{:S(2)}, u32[]{:S(2)}) collective-permute-start(bf16[256,1280]{1,0:T(8,128)(2,1)} %fusion.52), channel_id=1, source_target_pairs={{0,8},{8,16},{16,24},{24,0},{1,9},{9,17},{17,25},{25,1},{2,10},{10... | collective-permute-start | bytes 1966088 | tf_op jit(solution)/shard_map/ppermute | solution.py:54
  971.1 33.2 %collective-permute-start.80 = (bf16[256,1280]{1,0:T(8,128)(2,1)S(1)}, bf16[256,1280]{1,0:T(8,128)(2,1)S(1)}, u32[]{:S(2)}, u32[]{:S(2)}) collective-permute-start(bf16[256,1280]{1,0:T(8,128)(2,1)S(1)} %fusion.42), channel_id=1, source_target_pairs={{0,8},{8,16},{16,24},{24,0},{1,9},{9,17},{17,25},{25,1},{2,10},{10... | collective-permute-start | bytes 1966088 | tf_op jit(solution)/shard_map/ppermute | solution.py:54
  (233 other events, 2567.2 us)

commit v6 on v5

--- a/solution.py
+++ b/solution.py
@@ -90,6 +90,46 @@
         parts = [lax.dynamic_index_in_dim(v, at, dim, keepdims=False) for v in arrays]
         out.append(parts[0] if len(parts) == 1 else jnp.concatenate(parts, axis=-1))
     return out
+
+
+ORDER = {
+    "g": "f3",
+    "mid0": "r1",
+    "core2": "r3",
+    "rs1": "fp",
+    "norm": "rs g2",
+    "gs1": "rp",
+    "arr1": "g3 rp",
+    "arr2": "s rp",
+    "arr3": "s gf",
+    "wa": "a3",
+    "wc": "cs",
+    "c1b": "w",
+    "c2b": "k0",
+    "c3a": "k0",
+    "c3b": "k0",
+    "gu": "s2",
+    "dn": "gu",
+    "t2": "gu dn",
+    "ea": "t",
+    "sh": "k2",
+    "B2": "er",
+    "B3": "er",
+    "y1": "rg",
+    "y2": "q",
+    "fin": "late ys",
+    "y3": "b",
+    "late2": "b",
+    "kv2": "l",
+    "yz2": "kv",
+    "yz4": "l",
+    "late3": "f",
+}
+
+
+def pick(name, value, **events):
+    chosen = [events[key] for key in ORDER.get(name, "").split() if key in events]
+    return after(value, *jax.tree.leaves(chosen))
 
 
 def after(value, *events):
@@ -655,21 +695,26 @@
     folded = expert_down.reshape(nq, -1, 2 * FF)
     both = jnp.concatenate([expert_gate_up, folded], axis=1)
 
-    rest_q = ring_gather(after(rest, front_q[-1]), "q")
-    g_q = [after(grad_low, rest_q[-1])]
+    rest_q = ring_gather(pick("rest", rest, f1=front_q[1], f3=front_q[-1]), "q")
+    g_q = [pick("g", grad_low, r1=rest_q[1], r3=rest_q[-1], f3=front_q[-1])]
     g_q.append(shift(g_q[0], "q"))
+    front_first = [
+        pick(f"mid{i}", v, r1=rest_q[1], r2=rest_q[2]) for i, v in enumerate(front_first)
+    ]
     front_pieces = dense_end(*front_first)
-    qkv_weight, front_small = dense_place(
-        front_pieces, steps, [3 * width, 128], (rest_q[-2],)
-    )
+    due = [pick("core2", front_pieces[0], r1=rest_q[1], r2=rest_q[2], r3=rest_q[3], g1=g_q[1])]
+    qkv_weight, front_small = dense_place(front_pieces, steps, [3 * width, 128], due)
     for _ in range(nq - 2):
         g_q.append(shift(g_q[-1], "q"))
-    rest_first = dense_start([after(part, *front_pieces) for part in rest_q])
+    rest_first = dense_start(
+        [pick("rs1", part, fp=front_pieces, w=qkv_weight) for part in rest_q]
+    )
 
     kv_chunks = []
     gain_one = front_small[:, 0].astype(F32)
     inv_one = rms_scale(tokens_in)
-    normed = after((tokens_in * inv_one * gain_one).astype(BF), g_q[1], *rest_first)
+    normed = (tokens_in * inv_one * gain_one).astype(BF)
+    normed = pick("norm", normed, rs=rest_first, g1=g_q[1], g2=g_q[2], g3=g_q[3])
     queries, kv_own = project(normed, qkv_weight, *tables)
     places = [
         jnp.stack(
@@ -681,31 +726,33 @@
         ).astype(jnp.int32)
         for k in range(nq)
     ]
-    rest_pieces = dense_end(*rest_first)
+    rest_pieces = dense_end(*(pick("rs2", v, q=queries, w=qkv_weight) for v in rest_first))
     state = None
     arrived = kv_own
     for k in range(nq):
         chunk = ring_gather(arrived, "r")
-        due = ()
         if k < nq - 1:
             coming = shift(arrived, "q")
         if k == 1:
-            g_even, g_odd = (after(jnp.stack(g_q[low::2]), *rest_pieces) for low in (0, 1))
+            g_even, g_odd = (
+                pick("gs1", jnp.stack(g_q[low::2]), rp=rest_pieces, a1=arrived) for low in (0, 1)
+            )
             g_even = jnp.stack(ring_gather(g_even, "b"))
             g_odd = jnp.stack(ring_gather(g_odd, "a"))
         state = attend_chunk(places[k], queries, chunk, state, k == nq - 1, n_ctx)
         kv_chunks.append(chunk)
         if k < nq - 1:
             if k == 0:
-                due = (state[0], g_q[nq - 2], *rest_pieces)
+                arrived = pick("arr1", coming, s=state[0], g2=g_q[2], g3=g_q[3], rp=rest_pieces)
             if k == 1:
-                due = (state[0], g_even, g_odd)
+                arrived = pick("arr2", coming, s=state[0], gs=(g_even, g_odd), rp=rest_pieces)
             if k == 2:
                 g_even, g_odd = ring_gather(g_even, "a"), ring_gather(g_odd, "b")
-                due = (state[0], *g_even, *g_odd)
-            arrived = after(coming, *due)
+                arrived = pick("arr3", coming, s=state[0], gf=(g_even, g_odd))
     mixed, lse = state
-    both = lax.all_to_all(after(both, arrived), "q", split_axis=0, concat_axis=0, tiled=True)
+    both = pick("wa", both, a3=arrived, c3=chunk[1:], q=queries, m=mixed)
+    both = lax.all_to_all(both, "q", split_axis=0, concat_axis=0, tiled=True)
+    mixed = pick("mix", mixed, gf=(g_even, g_odd))
     out_weight, shared_in, shared_out, rest_small = dense_place(
         rest_pieces, steps, [width, 2 * FF, flat, 128]
     )
@@ -719,10 +766,12 @@
     router_t = router.T
     kept = None
     ys = [None, None]
-    sum_first, dgates = [], []
+    sum_first, dgates, decs = [], [], []
     c_q = ring_gather(second, "q")
     c_start = jnp.stack(ring_gather(c_q[0], "b"))
-    both = ring_gather(after(both, c_start), "r")
+    c_planes = [plane_gather(c_q[0], True, c_start)]
+    both = pick("wc", both, m=mixed, cs=c_start, c1=c_q[1], cp=c_planes[0])
+    both = ring_gather(both, "r")
     kr = np.repeat(np.arange(nr, dtype=np.int32), nq)
     kq = np.tile(np.arange(nq, dtype=np.int32), nr)
     index = kq * nr + lax.rem(r_at - kr + nr, nr)
@@ -734,23 +783,33 @@
     w2 = w2.reshape(-1, width)
     g_even = [jnp.stack(g_even)]
     for k in range(nq):
-        rows = c_q[k] if k < 2 else after(c_q[k], dgates[0])
-        first = c_start
         if k:
+            ready = dict(w=w1) | {f"k{i}": v for i, v in enumerate(dgates)}
+            rows = pick(f"c{k}a", c_q[k], **ready)
             first = jnp.stack(ring_gather(rows, "ba"[k % 2]))
-        if k == 1:
-            first = after(first, w1)
-        c = plane_gather(rows, k % 2 == 0, first)
+            c_planes.append(plane_gather(rows, k % 2 == 0, pick(f"c{k}b", first, **ready)))
+        c = c_planes[k]
+        ready = {f"s{i}": v for i, v in enumerate(sum_first) if v is not None}
+        if k == 3:
+            ready["e1"] = dec_one = sum_end(sum_first[1], False)
+        hold = pick(f"K{k}", ranks, **ready)
         dec, dgate, kept, ys[k % 2] = expert_chunk(
-            k, nq, na, nb, expert, ranks, c, (g_even, g_odd)[k % 2], router_t, w1, w2, kept, ys[k % 2], slots
+            k, nq, na, nb, expert, hold, c, (g_even, g_odd)[k % 2], router_t, w1, w2, kept, ys[k % 2], slots
         )
-        sum_first.append(sum_start(dec, k % 2 == 0))
         dgates.append(dgate.reshape(na * nb, tok))
+        ready = {f"k{i}": v for i, v in enumerate(dgates)}
+        decs.append(dec)
+        sum_first.append(None)
+        if k:
+            sum_first[k] = sum_start([pick(f"d{k}", v, **ready) for v in dec], k % 2 == 0)
+    ready = {f"k{i}": v for i, v in enumerate(dgates)}
+    sum_first[0] = sum_start([pick("d0", v, **ready) for v in decs[0]], True)
     firsts = sum_first
-    dec_sums = [sum_end(firsts[k], k % 2 == 0) for k in range(nq)]
+    dec_sums = [dec_one if k == 1 else sum_end(firsts[k], k % 2 == 0) for k in range(nq)]
+    ready = {f"s{i}": v for i, v in enumerate(firsts)}
     xs, hs, deys, degs = kept[:4]
-    down_term = dot(hs, deys, TN).astype(BF)
-    gate_up_term = dot(xs, degs, TN).astype(BF)
+    gate_up_term = dot(pick("gu", xs, **ready), degs, TN).astype(BF)
+    down_term = dot(pick("dn", hs, gu=gate_up_term, **ready), deys, TN).astype(BF)
     terms = [
         gate_up_term.reshape(nq, nr, gu_rows, 2 * FF),
         down_term.reshape(nq, nr, -1, 2 * FF),
@@ -768,14 +827,15 @@
     moving = dec_sums[1].astype(BF)
     for k in range(2, nq):
         term = dec_sums[k]
-        if k == 2:
-            term = after(term, expert_rows)
+        term = pick(f"t{k}", term, gu=gate_up_term, dn=down_term, er=expert_rows)
         moving = (shift(moving, "q").astype(F32) + term).astype(BF)
     routed_grad = shift(moving, "q").astype(F32) + dec_sums[0]
 
+    expert_rows = pick("ea", expert_rows, rg=routed_grad, t=moving)
     expert_rows = lax.all_to_all(expert_rows, "q", split_axis=0, concat_axis=0, tiled=True)
 
-    later = after(second, dgates[0])
+    ready = {f"k{i}": v for i, v in enumerate(dgates)}
+    later = pick("sh", second, **ready)
     shared_pre = dot(later, shared_in)
     shared_gate, shared_up = shared_pre[:, :FF], shared_pre[:, FF:]
     shared_sig = jax.nn.sigmoid(shared_gate)
@@ -814,14 +874,15 @@
     heads_grad = dot(mixed_grad, out_weight, NT).astype(BF)
 
     y_first = [
-        sum_start([after(v, routed_grad) for v in ys[p]], p == 0) for p in (0, 1)
+        sum_start([pick("y1", v, rg=routed_grad, k=dgates[3]) for v in ys[p]], p == 0)
+        for p in (0, 1)
     ]
     dq = None
     moving = None
     held = heads_grad
     for step, k in enumerate(list(range(1, nq)) + [0]):
-        if step == 2:
-            held = after(held, moving, expert_rows)
+        ready = dict(er=expert_rows, y=y_first, m=moving if step else ())
+        held = pick(f"B{step}", held, **ready)
         dq, parts = attend_back_chunk(
             places[k], queries, held, mixed, lse, tables, kv_chunks[k], dq, k == 0, n_ctx
         )
@@ -840,9 +901,11 @@
         ],
         own_rows,
     )
-    y_sums = [sum_end(after(y_first[p], dq), p == 0, 1) for p in (0, 1)]
+    y_sums = [sum_end(pick("y2", y_first[p], q=dq, m=moving, f=first_move), p == 0, 1) for p in (0, 1)]
     late = dense_sum_first(late)
-    kv_back = finish_keys(shift(moving, "q"), after(term, *late), *tables)
+    kv_back = finish_keys(
+        shift(moving, "q"), pick("fin", term, late=late, ys=y_sums), *tables
+    )
 
     gate_up_grad = expert_rows[:, :gu_rows].astype(F32)
     down_grad = expert_rows[:, gu_rows:].reshape(nq, -1, width).astype(F32)
@@ -862,24 +925,24 @@
     ).astype(BF)
     key_value = dense_sum_core(
         [
-            dot(normed, kv_back[0], TN).astype(BF),
+            pick("kv1", dot(normed, kv_back[0], TN).astype(BF), late=late, ys=y_sums),
             dot(normed, kv_back[1], TN).astype(BF),
             small_grad,
         ],
         own_rows,
     )
-    y_sums = after(y_sums, kv_back)
+    y_sums = pick("y3", y_sums, b=kv_back, kv=key_value, m=moving)
     y_terms = [y_sums[k % 2][k // 2] for k in range(nq)]
-    late = dense_sum_second(*late)
-    first_kv = dense_sum_first(key_value)
+    late = dense_sum_second(*(pick("late2", v, b=kv_back, kv=key_value) for v in late))
+    first_kv = dense_sum_first(pick("kv2", key_value, l=late))
     last_kv = dense_sum_second(*first_kv)
     y_moving = y_terms[1].astype(BF)
-    events = [(key_value,), first_kv, (late,)]
     for k in range(2, nq + 1):
-        y_moving = after(shift(y_moving, "q"), *events[min(k - 2, 2)])
+        y_moving = shift(y_moving, "q")
+        y_moving = pick(f"yz{k}", y_moving, kv=key_value, f=first_kv, l=late, z=last_kv)
         routed_sum = y_moving.astype(F32) + y_terms[k % nq]
         y_moving = routed_sum.astype(BF)
-    late_grad = dense_sum_last(after(late, *first_kv))
+    late_grad = dense_sum_last(pick("late3", late, f=first_kv, kv=key_value, z=last_kv))
     kv_weight_grad = dense_sum_last(last_kv)
     layer_out = (residual + dot(shared_hidden, shared_out) + routed_sum).astype(BF)
     at_out, at_shared, at_down = width, 2 * width, 2 * width + 2 * FF

time: 1040 us -> 1020 us (0.981)
  waiting for transfers between devices: 439 us -> 420 us
    ppermute x88, waiting for transfers between devices: 386 us -> 322 us  [shift(): return lax.ppermute(value, axis, [(i, (i + 1) % n) for i in range(n)])]
    all_to_all x1, waiting for transfers between devices: 12.7 us -> 55.2 us  [body(): lax.all_to_all(expert_rows, 'q', split_axis=0, concat_axis=0, tiled=True)]
    unnamed x348 -> x314, local copies, waits for them, and re-layouts: 50.5 us -> 37.3 us
  transfers between devices with their start and end apart: 94 -> 94, of which waited for: 48 -> 50; matrix products, arithmetic and copies ran while one was open for 24% -> 25% of each run, Pallas kernels for 18% -> 19%
where the time goes in v6:
time: 1020 us; the launch traced here: 1010 us
  waiting for transfers between devices  420 us (41%)
  Pallas kernels  199 us (20%)
  other arithmetic  128 us (13%)
  local copies, waits for them, and re-layouts  116 us (11%)
  starting transfers between devices  83.2 us (8%)
  matrix products  63.9 us (6%)
    ppermute x88, waiting for transfers between devices, shift(): return lax.ppermute(value, axis, [(i, (i + 1) % n) for i in range(n)])  322 us
    pallas_call x4, Pallas kernels, expert_chunk(): pl.pallas_call(functools.partial(expert_kernel, slots, na, nb, even, len(...  91.5 us
    dot_general x21, matrix products, dot(): return lax.dot_general(a, b, (dims, ((), ())), preferred_element_type=F32)  63.9 us
    ppermute x88, starting transfers between devices, shift(): return lax.ppermute(value, axis, [(i, (i + 1) % n) for i in range(n)])  63.6 us
    all_to_all x1, waiting for transfers between devices, body(): lax.all_to_all(expert_rows, 'q', split_axis=0, concat_axis=0, tiled=True)  55.2 us
    pallas_call x4, Pallas kernels, attend_back_chunk(): pl.pallas_call(functools.partial(attend_back_kernel, n_ctx, n, first, las...  45.3 us
    unnamed x314, local copies, waits for them, and re-layouts  37.3 us
    pallas_call x4, Pallas kernels, attend_chunk(): pl.pallas_call(functools.partial(attend_kernel, n_ctx, n, first, last), g...  35.2 us
  transfers between devices with their start and end apart: 94, of which 50 were waited for; matrix products, arithmetic and copies ran while one was open for 25% of the time, Pallas kernels for 19%

profile of v6, /device:TPU:0, one launch (start us, length us, event | category | flops | bytes accessed | tf_op | source)
XLA Modules:
  0.0 1013.2 jit_solution(14296213778462843582)
XLA Ops:
  6.3 8.8 collective-permute-done
  65.5 12.0 %collective-permute-done.16 = bf16[40,4096]{1,0:T(8,128)(2,1)S(1)} collective-permute-done((bf16[40,4096]{1,0:T(8,128)(2,1)}, bf16[40,4096]{1,0:T(8,128)(2,1)S(1)}, u32[]{:S(2)}, u32[]{:S(2)}) %collective-permute-start.16) | collective-permute-done | bytes 327712 | tf_op jit(solution)/shard_map/ppermute | solution.py:54
  95.0 12.0 %collective-permute-done.15 = bf16[2,40,4096]{2,1,0:T(8,128)(2,1)S(1)} collective-permute-done((bf16[2,40,4096]{2,1,0:T(8,128)(2,1)S(1)}, bf16[2,40,4096]{2,1,0:T(8,128)(2,1)S(1)}, u32[]{:S(2)}, u32[]{:S(2)}) %collective-permute-start.15) | collective-permute-done | bytes 655392 | tf_op jit(solution)/shard_map/ppermute | solution.py:54
  144.8 20.7 %collective-permute-done.21.refs_0_ = bf16[2,256,1280]{2,1,0:T(8,128)(2,1)} collective-permute-done((bf16[2,256,1280]{2,1,0:T(8,128)(2,1)S(1)}, bf16[2,256,1280]{2,1,0:T(8,128)(2,1)}, u32[]{:S(2)}, u32[]{:S(2)}) %collective-permute-start.21) | collective-permute-done | bytes 1310752 | tf_op jit(solution)/shard_map/ppermute | solution.py:54
  185.1 9.6 attend.5
  214.5 9.2 attend.6
  257.4 10.5 %attend.7 = (bf16[256,1280]{1,0:T(8,128)(2,1)S(1)}, f32[10,256,128]{2,1,0:T(8,128)S(1)}) custom-call(s32[3]{0:T(128)S(1)} %pad_add_fusion.place_ref, bf16[256,1280]{1,0:T(8,128)(2,1)S(1)} %copy-done.45, bf16[2,256,1280]{2,1,0:T(8,128)(2,1)} %collective-permute-done.28.refs_0_, bf16[2,256,1280]{2,1,0:T(8,128)(2,1)} %collective-permute-done.34.refs_1_, ...), custom_call_target="tpu_custom_call" | custom-call | flops 2684354560 | bytes 2621440 | tf_op jit(solution)/shard_map/attend/pallas_call | solution.py:402
  271.3 15.1 %collective-permute-done.40 = bf16[256,1280]{1,0:T(8,128)(2,1)S(1)} collective-permute-done((bf16[256,1280]{1,0:T(8,128)(2,1)S(1)}, bf16[256,1280]{1,0:T(8,128)(2,1)S(1)}, u32[]{:S(2)}, u32[]{:S(2)}) %collective-permute-start.40) | collective-permute-done | bytes 655392 | tf_op jit(solution)/shard_map/ppermute | solution.py:54
  288.0 30.6 %all-to-all-done.refs_0_ = bf16[4,240,1792]{2,1,0:T(8,128)(2,1)S(1)} async-done(((bf16[4,240,1792]{2,1,0:T(8,128)(2,1)}), bf16[4,240,1792]{2,1,0:T(8,128)(2,1)S(1)}, u32[]{:S(2)}, u32[]{:S(2)}) %all-to-all-start) | async-done | bytes 3440672 | tf_op jit(solution)/shard_map/all_to_all | solution.py:754
  319.9 17.9 %collective-permute-done.37 = bf16[256,1280]{1,0:T(8,128)(2,1)} collective-permute-done((bf16[256,1280]{1,0:T(8,128)(2,1)}, bf16[256,1280]{1,0:T(8,128)(2,1)}, u32[]{:S(2)}, u32[]{:S(2)}) %collective-permute-start.37) | collective-permute-done | bytes 655392 | tf_op jit(solution)/shard_map/ppermute | solution.py:54
  347.5 8.8 collective-permute-done.38
  382.9 23.3 %experts.4 = (bf16[2,256,1280]{2,1,0:T(8,128)(2,1)}, bf16[2,256,1280]{2,1,0:T(8,128)(2,1)}, f32[2,2,1,256]{3,2,1,0:T(1,128)}, bf16[2816,1280]{1,0:T(8,128)(2,1)}...) custom-call(s32[4]{0:T(128)} %pad_add_fusion.4.e_ref, ...), custom_call_target="tpu_custom_call" | custom-call | flops 9688842240 | bytes 30000000 | tf_op jit(solution)/shard_map/experts/pallas_call | solution.py:591
  415.9 9.2 collective-permute-done.52
  427.9 22.0 %experts.5 = (bf16[2,256,1280]{2,1,0:T(8,128)(2,1)}, bf16[2,256,1280]{2,1,0:T(8,128)(2,1)}, f32[2,2,1,256]{3,2,1,0:T(1,128)}, bf16[2816,1280]{1,0:T(8,128)(2,1)}...) custom-call(s32[4]{0:T(128)} %pad_add_fusion.4.e_ref, ...), custom_call_target="tpu_custom_call", output_to_operand_aliasing={{3}: (9, {}), {4}: (10, {}), {5}: (11, {}), {6}: (12, {})} | custom-call | flops 9688842240 | bytes 30000000 | tf_op jit(solution)/shard_map/experts/pallas_call | solution.py:591
  456.8 24.1 %experts.6 = (bf16[2,256,1280]{2,1,0:T(8,128)(2,1)}, bf16[2,256,1280]{2,1,0:T(8,128)(2,1)}, f32[2,2,1,256]{3,2,1,0:T(1,128)}, bf16[2816,1280]{1,0:T(8,128)(2,1)}...) custom-call(s32[4]{0:T(128)} %pad_add_fusion.4.e_ref, ...), custom_call_target="tpu_custom_call", output_to_operand_aliasing={{3}: (7, {}), {4}: (8, {}), {5}: (9, {}), {6}: (10, {}), {7... | custom-call | flops 9688842240 | bytes 30000000 | tf_op jit(solution)/shard_map/experts/pallas_call | solution.py:591
  503.7 22.1 %experts.7 = (bf16[2,256,1280]{2,1,0:T(8,128)(2,1)}, bf16[2,256,1280]{2,1,0:T(8,128)(2,1)}, f32[2,2,1,256]{3,2,1,0:T(1,128)}, bf16[2816,1280]{1,0:T(8,128)(2,1)}...) custom-call(s32[4]{0:T(128)} %pad_add_fusion.4.e_ref, ...), custom_call_target="tpu_custom_call", output_to_operand_aliasing={{3}: (9, {}), {4}: (10, {}), {5}: (11, {}), {6}: (12, {}), ... | custom-call | flops 9688842240 | bytes 30000000 | tf_op jit(solution)/shard_map/experts/pallas_call | solution.py:591
  531.9 21.1 %convolution_convert_fusion.4 = bf16[1280,1792]{1,0:T(8,128)(2,1)} fusion(bf16[2816,1280]{1,0:T(8,128)(2,1)} %get-tuple-element.179, bf16[2816,1792]{1,0:T(8,128)(2,1)} %get-tuple-element.180), kind=kOutput, calls=%fused_computation.6 | convolution fusion | flops 12920750080 | bytes 21889024 | tf_op jit(solution)/shard_map/dot_general | solution.py:45
  556.9 8.3 convolution_convert_fusion.7
  582.3 13.1 %collective-permute-done.48 = bf16[256,1280]{1,0:T(8,128)(2,1)S(1)} collective-permute-done((bf16[256,1280]{1,0:T(8,128)(2,1)S(1)}, bf16[256,1280]{1,0:T(8,128)(2,1)S(1)}, u32[]{:S(2)}, u32[]{:S(2)}) %collective-permute-start.48) | collective-permute-done | bytes 655392 | tf_op jit(solution)/shard_map/ppermute | solution.py:54
  628.7 8.7 collective-permute-done.57
  651.1 11.1 %attend_back.4 = (f32[256,1280]{1,0:T(8,128)S(1)}, f32[2,256,1280]{2,1,0:T(8,128)S(1)}, bf16[2,256,1280]{2,1,0:T(8,128)(2,1)S(1)}) custom-call(s32[3]{0:T(128)S(1)} %copy-done.26, bf16[256,1280]{1,0:T(8,128)(2,1)S(1)} %copy-done.46, bf16[256,1280]{1,0:T(8,128)(2,1)S(1)} %convolution_convert_fusion.8.do_ref, bf16[256,1280]{1,0:T(8,128)(2,1)S(1)} %copy-done.15, ...), custom_call_target="tpu_custom_call" | custom-call | flops 6710886400 | bytes 5242880 | tf_op jit(solution)/shard_map/attend_back/pallas_call | solution.py:463
  662.3 11.6 %attend_back.5 = (f32[256,1280]{1,0:T(8,128)S(1)}, f32[2,256,1280]{2,1,0:T(8,128)S(1)}, bf16[2,256,1280]{2,1,0:T(8,128)(2,1)}) custom-call(s32[3]{0:T(128)S(1)} %copy-done.28, bf16[256,1280]{1,0:T(8,128)(2,1)S(1)} %copy-done.46, bf16[256,1280]{1,0:T(8,128)(2,1)S(1)} %convolution_convert_fusion.8.do_ref, bf16[256,1280]{1,0:T(8,128)(2,1)S(1)} %copy-done.15, ...), custom_call_target="tpu_custom_call" | custom-call | flops 6710886400 | bytes 5242880 | tf_op jit(solution)/shard_map/attend_back/pallas_call | solution.py:463
  680.2 55.2 %all-to-all-done.2 = bf16[4,240,1792]{2,1,0:T(8,128)(2,1)} async-done(((bf16[4,240,1792]{2,1,0:T(8,128)(2,1)}), bf16[4,240,1792]{2,1,0:T(8,128)(2,1)}, u32[]{:S(2)}, u32[]{:S(2)}) %all-to-all-start.2) | async-done | bytes 3440672 | tf_op jit(solution)/shard_map/all_to_all | solution.py:835
  738.1 12.0 %attend_back.6 = (f32[256,1280]{1,0:T(8,128)S(1)}, f32[2,256,1280]{2,1,0:T(8,128)S(1)}, bf16[2,256,1280]{2,1,0:T(8,128)(2,1)}) custom-call(s32[3]{0:T(128)S(1)} %copy-done.30, bf16[256,1280]{1,0:T(8,128)(2,1)S(1)} %copy-done.47, bf16[256,1280]{1,0:T(8,128)(2,1)S(1)} %copy-done.50, bf16[256,1280]{1,0:T(8,128)(2,1)S(1)} %copy-done.15, ...), custom_call_target="tpu_custom_call" | custom-call | flops 6710886400 | bytes 5242880 | tf_op jit(solution)/shard_map/attend_back/pallas_call | solution.py:463
  750.2 10.5 %attend_back.7 = (bf16[256,1280]{1,0:T(8,128)(2,1)S(1)}, f32[2,256,1280]{2,1,0:T(8,128)S(1)}, bf16[2,256,1280]{2,1,0:T(8,128)(2,1)S(1)}) custom-call(s32[3]{0:T(128)S(1)} %copy-done.24, bf16[256,1280]{1,0:T(8,128)(2,1)S(1)} %copy-done.48, bf16[256,1280]{1,0:T(8,128)(2,1)S(1)} %copy-done.51, bf16[256,1280]{1,0:T(8,128)(2,1)S(1)} %copy-done.16, ...), custom_call_target="tpu_custom_call" | custom-call | flops 6710886400 | bytes 5242880 | tf_op jit(solution)/shard_map/attend_back/pallas_call | solution.py:463
  805.1 10.2 %collective-permute-done.68 = bf16[2,256,1280]{2,1,0:T(8,128)(2,1)} collective-permute-done((bf16[2,256,1280]{2,1,0:T(8,128)(2,1)}, bf16[2,256,1280]{2,1,0:T(8,128)(2,1)}, u32[]{:S(2)}, u32[]{:S(2)}) %collective-permute-start.68) | collective-permute-done | bytes 1310752 | tf_op jit(solution)/shard_map/ppermute | solution.py:54
  842.8 29.4 %collective-permute-done.73 = bf16[2,2,40,5248]{3,2,0,1:T(8,128)(2,1)S(1)} collective-permute-done((bf16[2,2,40,5248]{3,2,0,1:T(8,128)(2,1)S(1)}, bf16[2,2,40,5248]{3,2,0,1:T(8,128)(2,1)S(1)}, u32[]{:S(2)}, u32[]{:S(2)}) %collective-permute-start.73) | collective-permute-done | bytes 1679392 | tf_op jit(solution)/shard_map/ppermute | solution.py:54
  914.4 16.3 %collective-permute-done.80 = bf16[2,40,5248]{2,1,0:T(8,128)(2,1)S(1)} collective-permute-done((bf16[2,40,5248]{2,1,0:T(8,128)(2,1)S(1)}, bf16[2,40,5248]{2,1,0:T(8,128)(2,1)S(1)}, u32[]{:S(2)}, u32[]{:S(2)}) %collective-permute-start.80) | collective-permute-done | bytes 839712 | tf_op jit(solution)/shard_map/ppermute | solution.py:54
  938.2 14.0 %collective-permute-done.77 = bf16[256,1280]{1,0:T(8,128)(2,1)S(1)} collective-permute-done((bf16[256,1280]{1,0:T(8,128)(2,1)S(1)}, bf16[256,1280]{1,0:T(8,128)(2,1)S(1)}, u32[]{:S(2)}, u32[]{:S(2)}) %collective-permute-start.77) | collective-permute-done | bytes 655392 | tf_op jit(solution)/shard_map/ppermute | solution.py:54
  970.1 10.8 %collective-permute-done.88 = bf16[40,5248]{1,0:T(8,128)(2,1)S(1)} collective-permute-done((bf16[40,5248]{1,0:T(8,128)(2,1)S(1)}, bf16[40,5248]{1,0:T(8,128)(2,1)S(1)}, u32[]{:S(2)}, u32[]{:S(2)}) %collective-permute-start.88) | collective-permute-done | bytes 419872 | tf_op jit(solution)/shard_map/ppermute | solution.py:54
  987.4 8.3 collective-permute-done.86
  996.9 8.4 collective-permute-done.87
  (690 shorter events, 505.0 us)
Async XLA Ops:
  79.1 34.7 %collective-permute-start.11 = (bf16[8,40,3968]{2,1,0:T(8,128)(2,1)S(1)}, bf16[8,40,3968]{2,1,0:T(8,128)(2,1)S(1)}, u32[]{:S(2)}, u32[]{:S(2)}) collective-permute-start(bf16[8,40,3968]{2,1,0:T(8,128)(2,1)S(1)} %pad_maximum_fusion.11.refs_0_), channel_id=1, source_target_pairs={{0,4},{4,0},{1,5},{5,1},{2,6},{6,2},{3,7},{7,3},{8,12},{12,8},{9,1... | collective-permute-start | bytes 7618568 | tf_op jit(solution)/shard_map/ppermute | solution.py:54
  172.8 56.8 %collective-permute-start.31 = (bf16[2,2,256,1280]{3,2,1,0:T(8,128)(2,1)}, bf16[2,2,256,1280]{3,2,1,0:T(8,128)(2,1)}, u32[]{:S(2)}, u32[]{:S(2)}) collective-permute-start(bf16[2,2,256,1280]{3,2,1,0:T(8,128)(2,1)} %get-tuple-element.316), channel_id=1, source_target_pairs={{0,2},{2,0},{1,3},{3,1},{4,6},{6,4},{5,7},{7,5},{8,10},{10,8},{9,1... | collective-permute-start | bytes 7864328 | tf_op jit(solution)/shard_map/ppermute | solution.py:54
  175.8 56.5 %collective-permute-start.33 = (bf16[2,2,256,1280]{3,2,1,0:T(8,128)(2,1)}, bf16[2,2,256,1280]{3,2,1,0:T(8,128)(2,1)}, u32[]{:S(2)}, u32[]{:S(2)}) collective-permute-start(bf16[2,2,256,1280]{3,2,1,0:T(8,128)(2,1)} %pad_maximum_fusion.6.refs_2_), channel_id=1, source_target_pairs={{0,1},{1,0},{2,3},{3,2},{4,5},{5,4},{6,7},{7,6},{8,9},{9,8},{10,11... | collective-permute-start | bytes 7864328 | tf_op jit(solution)/shard_map/ppermute | solution.py:54
  204.3 33.3 %collective-permute-start.28 = (bf16[2,256,1280]{2,1,0:T(8,128)(2,1)}, bf16[2,256,1280]{2,1,0:T(8,128)(2,1)}, u32[]{:S(2)}, u32[]{:S(2)}) collective-permute-start(bf16[2,256,1280]{2,1,0:T(8,128)(2,1)} %collective-permute-done.25.refs_0_), channel_id=1, source_target_pairs={{0,8},{8,16},{16,24},{24,0},{1,9},{9,17},{17,25},{25,1},{2,10},{10... | collective-permute-start | bytes 3932168 | tf_op jit(solution)/shard_map/ppermute | solution.py:54
  237.6 81.0 %all-to-all-start = ((bf16[4,240,1792]{2,1,0:T(8,128)(2,1)}), bf16[4,240,1792]{2,1,0:T(8,128)(2,1)S(1)}, u32[]{:S(2)}, u32[]{:S(2)}) async-start(bf16[4,240,1792]{2,1,0:T(8,128)(2,1)} %pad_maximum_fusion.2), calls=%async_computation | async-start | bytes 6881280 | tf_op jit(solution)/shard_map/all_to_all | solution.py:754
  318.6 51.2 %collective-permute-start.42 = (bf16[4,240,1792]{2,1,0:T(8,128)(2,1)S(1)}, bf16[4,240,1792]{2,1,0:T(8,128)(2,1)}, u32[]{:S(2)}, u32[]{:S(2)}) collective-permute-start(bf16[4,240,1792]{2,1,0:T(8,128)(2,1)S(1)} %all-to-all-done.refs_0_), channel_id=1, source_target_pairs={{0,4},{4,0},{1,5},{5,1},{2,6},{6,2},{3,7},{7,3},{8,12},{12,8},{9,1... | collective-permute-start | bytes 10321928 | tf_op jit(solution)/shard_map/ppermute | solution.py:54
  318.6 48.1 %collective-permute-start.41 = (bf16[2,256,1280]{2,1,0:T(8,128)(2,1)}, bf16[2,256,1280]{2,1,0:T(8,128)(2,1)}, u32[]{:S(2)}, u32[]{:S(2)}) collective-permute-start(bf16[2,256,1280]{2,1,0:T(8,128)(2,1)} %get-tuple-element.323), channel_id=1, source_target_pairs={{0,2},{2,0},{1,3},{3,1},{4,6},{6,4},{5,7},{7,5},{8,10},{10,8},{9,1... | collective-permute-start | bytes 3932168 | tf_op jit(solution)/shard_map/ppermute | solution.py:54
  356.4 51.4 %collective-permute-start.39 = (bf16[256,1280]{1,0:T(8,128)(2,1)}, bf16[256,1280]{1,0:T(8,128)(2,1)}, u32[]{:S(2)}, u32[]{:S(2)}) collective-permute-start(bf16[256,1280]{1,0:T(8,128)(2,1)} %collective-permute-done.38), channel_id=1, source_target_pairs={{0,1},{1,0},{2,3},{3,2},{4,5},{5,4},{6,7},{7,6},{8,9},{9,8},{10,11... | collective-permute-start | bytes 1966088 | tf_op jit(solution)/shard_map/ppermute | solution.py:54
  357.9 49.3 %collective-permute-start.51 = (bf16[256,1280]{1,0:T(8,128)(2,1)}, bf16[256,1280]{1,0:T(8,128)(2,1)}, u32[]{:S(2)}, u32[]{:S(2)}) collective-permute-start(bf16[256,1280]{1,0:T(8,128)(2,1)} %collective-permute-done.38), channel_id=1, source_target_pairs={{0,8},{8,16},{16,24},{24,0},{1,9},{9,17},{17,25},{25,1},{2,10},{10... | collective-permute-start | bytes 1966088 | tf_op jit(solution)/shard_map/ppermute | solution.py:54
  381.4 46.5 %collective-permute-start.45 = (bf16[2,256,1280]{2,1,0:T(8,128)(2,1)}, bf16[2,256,1280]{2,1,0:T(8,128)(2,1)}, u32[]{:S(2)}, u32[]{:S(2)}) collective-permute-start(bf16[2,256,1280]{2,1,0:T(8,128)(2,1)} %pad_maximum_fusion.20.refs_0_), channel_id=1, source_target_pairs={{0,1},{1,0},{2,3},{3,2},{4,5},{5,4},{6,7},{7,6},{8,9},{9,8},{10,11... | collective-permute-start | bytes 3932168 | tf_op jit(solution)/shard_map/ppermute | solution.py:54
  410.2 43.1 %collective-permute-start.43 = (bf16[2,256,1280]{2,1,0:T(8,128)(2,1)}, bf16[2,256,1280]{2,1,0:T(8,128)(2,1)}, u32[]{:S(2)}, u32[]{:S(2)}) collective-permute-start(bf16[2,256,1280]{2,1,0:T(8,128)(2,1)} %pad_maximum_fusion.18), channel_id=1, source_target_pairs={{0,2},{2,0},{1,3},{3,1},{4,6},{6,4},{5,7},{7,5},{8,10},{10,8},{9,1... | collective-permute-start | bytes 3932168 | tf_op jit(solution)/shard_map/ppermute | solution.py:54
  415.4 66.3 %collective-permute-start.58 = (bf16[2,256,1280]{2,1,0:T(8,128)(2,1)}, bf16[2,256,1280]{2,1,0:T(8,128)(2,1)S(1)}, u32[]{:S(2)}, u32[]{:S(2)}) collective-permute-start(bf16[2,256,1280]{2,1,0:T(8,128)(2,1)} %get-tuple-element.187), channel_id=1, source_target_pairs={{0,2},{2,0},{1,3},{3,1},{4,6},{6,4},{5,7},{7,5},{8,10},{10,8},{9,1... | collective-permute-start | bytes 3932168 | tf_op jit(solution)/shard_map/ppermute | solution.py:54
  427.4 76.3 %collective-permute-start.53 = (bf16[2,256,1280]{2,1,0:T(8,128)(2,1)}, bf16[2,256,1280]{2,1,0:T(8,128)(2,1)}, u32[]{:S(2)}, u32[]{:S(2)}) collective-permute-start(bf16[2,256,1280]{2,1,0:T(8,128)(2,1)} %pad_maximum_fusion.21.refs_0_), channel_id=1, source_target_pairs={{0,1},{1,0},{2,3},{3,2},{4,5},{5,4},{6,7},{7,6},{8,9},{9,8},{10,11... | collective-permute-start | bytes 3932168 | tf_op jit(solution)/shard_map/ppermute | solution.py:54
  483.0 145.7 %collective-permute-start.59 = (bf16[256,1280]{1,0:T(8,128)(2,1)}, bf16[256,1280]{1,0:T(8,128)(2,1)}, u32[]{:S(2)}, u32[]{:S(2)}) collective-permute-start(bf16[256,1280]{1,0:T(8,128)(2,1)} %fusion.51), channel_id=1, source_target_pairs={{0,1},{1,0},{2,3},{3,2},{4,5},{5,4},{6,7},{7,6},{8,9},{9,8},{10,11... | collective-permute-start | bytes 1966088 | tf_op jit(solution)/shard_map/ppermute | solution.py:54
  483.5 43.1 %collective-permute-start.49 = (bf16[2,256,1280]{2,1,0:T(8,128)(2,1)}, bf16[2,256,1280]{2,1,0:T(8,128)(2,1)}, u32[]{:S(2)}, u32[]{:S(2)}) collective-permute-start(bf16[2,256,1280]{2,1,0:T(8,128)(2,1)} %get-tuple-element.168), channel_id=1, source_target_pairs={{0,2},{2,0},{1,3},{3,1},{4,6},{6,4},{5,7},{7,5},{8,10},{10,8},{9,1... | collective-permute-start | bytes 3932168 | tf_op jit(solution)/shard_map/ppermute | solution.py:54
  484.3 68.7 %collective-permute-start.46 = (bf16[2,256,1280]{2,1,0:T(8,128)(2,1)}, bf16[2,256,1280]{2,1,0:T(8,128)(2,1)}, u32[]{:S(2)}, u32[]{:S(2)}) collective-permute-start(bf16[2,256,1280]{2,1,0:T(8,128)(2,1)} %get-tuple-element.166), channel_id=1, source_target_pairs={{0,1},{1,0},{2,3},{3,2},{4,5},{5,4},{6,7},{7,6},{8,9},{9,8},{10,11... | collective-permute-start | bytes 3932168 | tf_op jit(solution)/shard_map/ppermute | solution.py:54
  525.8 51.6 %collective-permute-start.55 = (bf16[2,256,1280]{2,1,0:T(8,128)(2,1)}, bf16[2,256,1280]{2,1,0:T(8,128)(2,1)}, u32[]{:S(2)}, u32[]{:S(2)}) collective-permute-start(bf16[2,256,1280]{2,1,0:T(8,128)(2,1)} %get-tuple-element.185), channel_id=1, source_target_pairs={{0,1},{1,0},{2,3},{3,2},{4,5},{5,4},{6,7},{7,6},{8,9},{9,8},{10,11... | collective-permute-start | bytes 3932168 | tf_op jit(solution)/shard_map/ppermute | solution.py:54
  530.6 50.4 %collective-permute-start.50 = (bf16[256,1280]{1,0:T(8,128)(2,1)}, bf16[256,1280]{1,0:T(8,128)(2,1)}, u32[]{:S(2)}, u32[]{:S(2)}) collective-permute-start(bf16[256,1280]{1,0:T(8,128)(2,1)} %fusion.49), channel_id=1, source_target_pairs={{0,1},{1,0},{2,3},{3,2},{4,5},{5,4},{6,7},{7,6},{8,9},{9,8},{10,11... | collective-permute-start | bytes 1966088 | tf_op jit(solution)/shard_map/ppermute | solution.py:54
  575.1 43.0 %collective-permute-start.61 = (bf16[4,240,1792]{2,1,0:T(8,128)(2,1)}, bf16[4,240,1792]{2,1,0:T(8,128)(2,1)}, u32[]{:S(2)}, u32[]{:S(2)}) collective-permute-start(bf16[4,240,1792]{2,1,0:T(8,128)(2,1)} %pad_maximum_fusion.3), channel_id=1, source_target_pairs={{0,4},{4,0},{1,5},{5,1},{2,6},{6,2},{3,7},{7,3},{8,12},{12,8},{9,1... | collective-permute-start | bytes 10321928 | tf_op jit(solution)/shard_map/ppermute | solution.py:54
  580.3 34.5 %collective-permute-start.56 = (bf16[256,1280]{1,0:T(8,128)(2,1)}, bf16[256,1280]{1,0:T(8,128)(2,1)}, u32[]{:S(2)}, u32[]{:S(2)}) collective-permute-start(bf16[256,1280]{1,0:T(8,128)(2,1)} %fusion.50), channel_id=1, source_target_pairs={{0,2},{2,0},{1,3},{3,1},{4,6},{6,4},{5,7},{7,5},{8,10},{10,8},{9,1... | collective-permute-start | bytes 1966088 | tf_op jit(solution)/shard_map/ppermute | solution.py:54
  622.8 112.7 %all-to-all-start.2 = ((bf16[4,240,1792]{2,1,0:T(8,128)(2,1)}), bf16[4,240,1792]{2,1,0:T(8,128)(2,1)}, u32[]{:S(2)}, u32[]{:S(2)}) async-start(bf16[4,240,1792]{2,1,0:T(8,128)(2,1)} %add_convert_fusion.2), calls=%async_computation.2 | async-start | bytes 6881280 | tf_op jit(solution)/shard_map/all_to_all | solution.py:835
  640.9 141.2 %collective-permute-start.60 = (bf16[2,2,256,1280]{3,2,0,1:T(8,128)(2,1)}, bf16[2,2,256,1280]{3,2,0,1:T(8,128)(2,1)}, u32[]{:S(2)}, u32[]{:S(2)}) collective-permute-start(bf16[2,2,256,1280]{3,2,0,1:T(8,128)(2,1)} %copy.191), channel_id=1, source_target_pairs={{0,2},{2,0},{1,3},{3,1},{4,6},{6,4},{5,7},{7,5},{8,10},{10,8},{9,1... | collective-permute-start | bytes 7864328 | tf_op jit(solution)/shard_map/ppermute | solution.py:54
  643.6 140.9 %collective-permute-start.63 = (bf16[2,2,256,1280]{3,2,0,1:T(8,128)(2,1)}, bf16[2,2,256,1280]{3,2,0,1:T(8,128)(2,1)}, u32[]{:S(2)}, u32[]{:S(2)}) collective-permute-start(bf16[2,2,256,1280]{3,2,0,1:T(8,128)(2,1)} %copy.196), channel_id=1, source_target_pairs={{0,1},{1,0},{2,3},{3,2},{4,5},{5,4},{6,7},{7,6},{8,9},{9,8},{10,11... | collective-permute-start | bytes 7864328 | tf_op jit(solution)/shard_map/ppermute | solution.py:54
  673.9 104.1 %collective-permute-start.67 = (bf16[2,256,1280]{2,1,0:T(8,128)(2,1)}, bf16[2,256,1280]{2,1,0:T(8,128)(2,1)}, u32[]{:S(2)}, u32[]{:S(2)}) collective-permute-start(bf16[2,256,1280]{2,1,0:T(8,128)(2,1)} %get-tuple-element.210), channel_id=1, source_target_pairs={{0,4},{4,0},{1,5},{5,1},{2,6},{6,2},{3,7},{7,3},{8,12},{12,8},{9,1... | collective-permute-start | bytes 3932168 | tf_op jit(solution)/shard_map/ppermute | solution.py:54
  680.1 97.9 %collective-permute-start.66 = (bf16[2,256,1280]{2,1,0:T(8,128)(2,1)}, bf16[2,256,1280]{2,1,0:T(8,128)(2,1)}, u32[]{:S(2)}, u32[]{:S(2)}) collective-permute-start(bf16[2,256,1280]{2,1,0:T(8,128)(2,1)} %add_convert_fusion.5), channel_id=1, source_target_pairs={{0,8},{8,16},{16,24},{24,0},{1,9},{9,17},{17,25},{25,1},{2,10},{10... | collective-permute-start | bytes 3932168 | tf_op jit(solution)/shard_map/ppermute | solution.py:54
  768.6 57.0 %collective-permute-start.72 = (bf16[4,2,2,40,5248]{4,3,0,1,2:T(8,128)(2,1)}, bf16[4,2,2,40,5248]{4,3,0,1,2:T(8,128)(2,1)}, u32[]{:S(2)}, u32[]{:S(2)}) collective-permute-start(bf16[4,2,2,40,5248]{4,3,0,1,2:T(8,128)(2,1)} %pad_maximum_fusion), channel_id=1, source_target_pairs={{0,4},{4,0},{1,5},{5,1},{2,6},{6,2},{3,7},{7,3},{8,12},{12,8},{9,1... | collective-permute-start | bytes 20152328 | tf_op jit(solution)/shard_map/ppermute | solution.py:54
  782.1 33.3 %collective-permute-start.68 = (bf16[2,256,1280]{2,1,0:T(8,128)(2,1)}, bf16[2,256,1280]{2,1,0:T(8,128)(2,1)}, u32[]{:S(2)}, u32[]{:S(2)}) collective-permute-start(bf16[2,256,1280]{2,1,0:T(8,128)(2,1)} %add_convert_fusion.4), channel_id=1, source_target_pairs={{0,8},{8,16},{16,24},{24,0},{1,9},{9,17},{17,25},{25,1},{2,10},{10... | collective-permute-start | bytes 3932168 | tf_op jit(solution)/shard_map/ppermute | solution.py:54
  792.4 42.5 %collective-permute-start.64 = (bf16[2,256,1280]{2,1,0:T(8,128)(2,1)}, bf16[2,256,1280]{2,1,0:T(8,128)(2,1)}, u32[]{:S(2)}, u32[]{:S(2)}) collective-permute-start(bf16[2,256,1280]{2,1,0:T(8,128)(2,1)} %fusion.23), channel_id=1, source_target_pairs={{0,2},{2,0},{1,3},{3,1},{4,6},{6,4},{5,7},{7,5},{8,10},{10,8},{9,1... | collective-permute-start | bytes 3932168 | tf_op jit(solution)/shard_map/ppermute | solution.py:54
  818.8 59.0 %collective-permute-start.70 = (bf16[2,256,1280]{2,1,0:T(8,128)(2,1)}, bf16[2,256,1280]{2,1,0:T(8,128)(2,1)}, u32[]{:S(2)}, u32[]{:S(2)}) collective-permute-start(bf16[2,256,1280]{2,1,0:T(8,128)(2,1)} %add_convert_fusion.3), channel_id=1, source_target_pairs={{0,8},{8,16},{16,24},{24,0},{1,9},{9,17},{17,25},{25,1},{2,10},{10... | collective-permute-start | bytes 3932168 | tf_op jit(solution)/shard_map/ppermute | solution.py:54
  833.9 38.4 %collective-permute-start.73 = (bf16[2,2,40,5248]{3,2,0,1:T(8,128)(2,1)S(1)}, bf16[2,2,40,5248]{3,2,0,1:T(8,128)(2,1)S(1)}, u32[]{:S(2)}, u32[]{:S(2)}) collective-permute-start(bf16[2,2,40,5248]{3,2,0,1:T(8,128)(2,1)S(1)} %dynamic-slice_bitcast_fusion.3), channel_id=1, source_target_pairs={{0,2},{2,0},{1,3},{3,1},{4,6},{6,4},{5,7},{7,5},{8,10},{10,8},{9,1... | collective-permute-start | bytes 5038088 | tf_op jit(solution)/shard_map/ppermute | solution.py:54
  838.2 38.1 %collective-permute-start.74 = (bf16[2,2,40,5248]{3,2,0,1:T(8,128)(2,1)S(1)}, bf16[2,2,40,5248]{3,2,0,1:T(8,128)(2,1)S(1)}, u32[]{:S(2)}, u32[]{:S(2)}) collective-permute-start(bf16[2,2,40,5248]{3,2,0,1:T(8,128)(2,1)S(1)} %dynamic-slice_bitcast_fusion.2), channel_id=1, source_target_pairs={{0,1},{1,0},{2,3},{3,2},{4,5},{5,4},{6,7},{7,6},{8,9},{9,8},{10,11... | collective-permute-start | bytes 5038088 | tf_op jit(solution)/shard_map/ppermute | solution.py:54
  899.3 33.6 %collective-permute-start.75 = (bf16[256,1280]{1,0:T(8,128)(2,1)}, bf16[256,1280]{1,0:T(8,128)(2,1)}, u32[]{:S(2)}, u32[]{:S(2)}) collective-permute-start(bf16[256,1280]{1,0:T(8,128)(2,1)} %fusion.52), channel_id=1, source_target_pairs={{0,8},{8,16},{16,24},{24,0},{1,9},{9,17},{17,25},{25,1},{2,10},{10... | collective-permute-start | bytes 1966088 | tf_op jit(solution)/shard_map/ppermute | solution.py:54
  (216 other events, 2751.5 us)

commit v7 on v6

--- a/solution.py
+++ b/solution.py
@@ -93,37 +93,35 @@
 
 
 ORDER = {
-    "g": "f3",
-    "mid0": "r1",
-    "core2": "r3",
+    "g": "r1",
+    "mid1": "r1",
     "rs1": "fp",
-    "norm": "rs g2",
+    "norm": "rs g1",
     "gs1": "rp",
     "arr1": "g3 rp",
-    "arr2": "s rp",
+    "arr2": "s",
     "arr3": "s gf",
-    "wa": "a3",
-    "wc": "cs",
+    "wa": "q",
+    "wc": "cp",
     "c1b": "w",
     "c2b": "k0",
     "c3a": "k0",
-    "c3b": "k0",
-    "gu": "s2",
-    "dn": "gu",
-    "t2": "gu dn",
-    "ea": "t",
+    "K1": "s0",
+    "gu": "s0",
+    "dn": "s1",
+    "t2": "er",
     "sh": "k2",
-    "B2": "er",
+    "B1": "m",
     "B3": "er",
     "y1": "rg",
-    "y2": "q",
-    "fin": "late ys",
-    "y3": "b",
-    "late2": "b",
+    "fin": "late",
+    "kv1": "late",
     "kv2": "l",
     "yz2": "kv",
     "yz4": "l",
-    "late3": "f",
+    "late3": "kv",
+    "xg": "m",
+    "dn0": "kv",
 }
 
 
@@ -168,7 +166,7 @@
         out_shape=[
             jax.ShapeDtypeStruct((n, c[0][1], c[2] - c[1]), pieces[0].dtype) for c in cuts
         ],
-        compiler_params=pltpu.CompilerParams(vmem_limit_bytes=VMEM_LIMIT // 2),
+        compiler_params=pltpu.CompilerParams(vmem_limit_bytes=VMEM_LIMIT),
         cost_estimate=pl.CostEstimate(
             flops=0, bytes_accessed=4 * n * rows * total, transcendentals=0
         ),
@@ -310,7 +308,7 @@
             jax.ShapeDtypeStruct((tok, width), BF),
             jax.ShapeDtypeStruct((2, tok, width), BF),
         ],
-        compiler_params=pltpu.CompilerParams(vmem_limit_bytes=VMEM_LIMIT // 2),
+        compiler_params=pltpu.CompilerParams(vmem_limit_bytes=VMEM_LIMIT),
         cost_estimate=pl.CostEstimate(
             flops=6 * tok * width * width, bytes_accessed=6 * width * width, transcendentals=0
         ),
@@ -411,7 +409,7 @@
             jax.ShapeDtypeStruct((tok, width), BF if last else F32),
             jax.ShapeDtypeStruct((HEADS, tok, 128), F32),
         ],
-        compiler_params=pltpu.CompilerParams(vmem_limit_bytes=VMEM_LIMIT // 2),
+        compiler_params=pltpu.CompilerParams(vmem_limit_bytes=VMEM_LIMIT),
         cost_estimate=pl.CostEstimate(
             flops=4 * pairs * HEAD_DIM * 4, bytes_accessed=8 * tok * width, transcendentals=pairs
         ),
@@ -470,7 +468,7 @@
         ),
         out_shape=[jax.ShapeDtypeStruct((tok, width), BF if last else F32)]
         + [jax.ShapeDtypeStruct((2, tok, width), F32 if s == 0 else BF) for s in range(n)],
-        compiler_params=pltpu.CompilerParams(vmem_limit_bytes=VMEM_LIMIT // 2),
+        compiler_params=pltpu.CompilerParams(vmem_limit_bytes=VMEM_LIMIT),
         cost_estimate=pl.CostEstimate(
             flops=10 * pairs * HEAD_DIM * 4, bytes_accessed=16 * tok * width, transcendentals=pairs
         ),
@@ -767,7 +765,7 @@
     kept = None
     ys = [None, None]
     sum_first, dgates, decs = [], [], []
-    c_q = ring_gather(second, "q")
+    c_q = [second, shift(second, "q")]
     c_start = jnp.stack(ring_gather(c_q[0], "b"))
     c_planes = [plane_gather(c_q[0], True, c_start)]
     both = pick("wc", both, m=mixed, cs=c_start, c1=c_q[1], cp=c_planes[0])
@@ -781,6 +779,8 @@
         [((0, gu_rows), 0, 2 * FF), ((gu_rows, folded.shape[1]), 0, 2 * FF)],
     )
     w2 = w2.reshape(-1, width)
+    for k in range(2, nq):
+        c_q.append(shift(pick(f"cz{k}", c_q[-1], w=w1, cp=c_planes[0]), "q"))
     g_even = [jnp.stack(g_even)]
     for k in range(nq):
         if k:
@@ -898,6 +898,14 @@
             dot(mixed, mixed_grad, TN).astype(BF),
             dot(later, shared_pre_grad, TN).astype(BF),
             dot(shared_hidden, grad_low, TN).astype(BF).reshape(width, flat),
+            jnp.concatenate(
+                [
+                    ffn_gain_grad[:, None],
+                    dot(later, grad_logits, TN),
+                    jnp.zeros((width, 127 - n_experts), F32),
+                ],
+                axis=1,
+            ).astype(BF),
         ],
         own_rows,
     )
@@ -907,30 +915,22 @@
         shift(moving, "q"), pick("fin", term, late=late, ys=y_sums), *tables
     )
 
-    gate_up_grad = expert_rows[:, :gu_rows].astype(F32)
-    down_grad = expert_rows[:, gu_rows:].reshape(nq, -1, width).astype(F32)
-    normed_grad = dot(dq, qkv_weight[:, :width], NT)
-    normed_grad += dot(kv_back[0], qkv_weight[:, width : 2 * width], NT)
-    normed_grad += dot(kv_back[1], qkv_weight[:, 2 * width :], NT)
-    attn_gain_grad = jnp.sum(normed_grad * tokens_in * inv_one, axis=0)
-    input_grad = residual_grad + norm_back(normed_grad, tokens_in, inv_one, gain_one)
-    small_grad = jnp.concatenate(
-        [
-            attn_gain_grad[:, None],
-            ffn_gain_grad[:, None],
-            dot(second, grad_logits, TN),
-            jnp.zeros((width, 126 - n_experts), F32),
-        ],
-        axis=1,
-    ).astype(BF)
+    owned = pick("xg", expert_rows, b=kv_back, m=moving)
+    gate_up_grad = owned[:, :gu_rows].astype(F32)
+    down_grad = owned[:, gu_rows:].reshape(nq, -1, width).astype(F32)
     key_value = dense_sum_core(
         [
             pick("kv1", dot(normed, kv_back[0], TN).astype(BF), late=late, ys=y_sums),
             dot(normed, kv_back[1], TN).astype(BF),
-            small_grad,
         ],
         own_rows,
     )
+    ready = dict(kv=key_value)
+    normed_grad = dot(dq, qkv_weight[:, :width], NT)
+    kv_low = pick("dn0", kv_back, **ready)
+    normed_grad += dot(kv_low[0], qkv_weight[:, width : 2 * width], NT)
+    normed_grad += dot(kv_low[1], qkv_weight[:, 2 * width :], NT)
+    input_grad = residual_grad + norm_back(normed_grad, tokens_in, inv_one, gain_one)
     y_sums = pick("y3", y_sums, b=kv_back, kv=key_value, m=moving)
     y_terms = [y_sums[k % 2][k // 2] for k in range(nq)]
     late = dense_sum_second(*(pick("late2", v, b=kv_back, kv=key_value) for v in late))
@@ -946,16 +946,20 @@
     kv_weight_grad = dense_sum_last(last_kv)
     layer_out = (residual + dot(shared_hidden, shared_out) + routed_sum).astype(BF)
     at_out, at_shared, at_down = width, 2 * width, 2 * width + 2 * FF
+    at_small = at_down + flat
+    qkv_weight_grad = jnp.concatenate([late_grad[:, :at_out], kv_weight_grad], axis=1)
+    attn_gain_grad = jnp.sum(query_key_value_weight.astype(F32) * qkv_weight_grad, axis=1)
+    attn_gain_grad = attn_gain_grad / attn_gain.astype(F32)
     return (
         layer_out[None],
         input_grad[None],
-        kv_weight_grad[:, 2 * width],
-        jnp.concatenate([late_grad[:, :at_out], kv_weight_grad[:, : 2 * width]], axis=1),
+        attn_gain_grad,
+        qkv_weight_grad,
         late_grad[:, at_out:at_shared],
-        kv_weight_grad[:, 2 * width + 1],
-        kv_weight_grad[:, 2 * width + 2 : 2 * width + 2 + n_experts],
+        late_grad[:, at_small],
+        late_grad[:, at_small + 1 : at_small + 1 + n_experts],
         late_grad[:, at_shared:at_down],
-        late_grad[:, at_down:].reshape(down_rows, width),
+        late_grad[:, at_down:at_small].reshape(down_rows, width),
         gate_up_grad,
         down_grad,
     )

time: 1020 us -> 1010 us (level)
  Pallas kernels: 199 us -> 233 us
  waiting for transfers between devices: 420 us -> 398 us
  local copies, waits for them, and re-layouts: 116 us -> 97.9 us
    ppermute x88, waiting for transfers between devices: 322 us -> 356 us  [shift(): return lax.ppermute(value, axis, [(i, (i + 1) % n) for i in range(n)])]
    all_to_all x1, waiting for transfers between devices: 30.6 us -> 3.67 us  [body(): both = lax.all_to_all(both, 'q', split_axis=0, concat_axis=0, tiled=True)]
    all_to_all x1, waiting for transfers between devices: 55.2 us -> 32.6 us  [body(): lax.all_to_all(expert_rows, 'q', split_axis=0, concat_axis=0, tiled=True)]
    dynamic_slice x12 -> x9, local copies, waits for them, and re-layouts: 22.6 us -> 7.37 us  [ring_blocks(): lax.dynamic_index_in_dim(v, at, dim, keepdims=False)]
    pallas_call x3, Pallas kernels: 11.2 us -> 24 us  [place(): pl.pallas_call(functools.partial(place_kernel, counts, cuts), in_specs=[p...]
    unnamed x314 -> x198, local copies, waits for them, and re-layouts: 37.3 us -> 31.7 us
  transfers between devices with their start and end apart: 94 -> 94, of which waited for: 50 -> 41; matrix products, arithmetic and copies ran while one was open for 25% -> 27% of each run, Pallas kernels for 19% -> 23%
where the time goes in v7:
time: 1010 us; the launch traced here: 1000 us
  waiting for transfers between devices  398 us (39%)
  Pallas kernels  233 us (23%)
  other arithmetic  128 us (13%)
  local copies, waits for them, and re-layouts  97.9 us (10%)
  starting transfers between devices  79.1 us (8%)
  matrix products  62.2 us (6%)
    ppermute x88, waiting for transfers between devices, shift(): return lax.ppermute(value, axis, [(i, (i + 1) % n) for i in range(n)])  356 us
    pallas_call x4, Pallas kernels, expert_chunk(): pl.pallas_call(functools.partial(expert_kernel, slots, na, nb, even, len(...  91.4 us
    dot_general x21, matrix products, dot(): return lax.dot_general(a, b, (dims, ((), ())), preferred_element_type=F32)  62.2 us
    ppermute x88, starting transfers between devices, shift(): return lax.ppermute(value, axis, [(i, (i + 1) % n) for i in range(n)])  57.8 us
    pallas_call x4, Pallas kernels, attend_back_chunk(): pl.pallas_call(functools.partial(attend_back_kernel, n_ctx, n, first, las...  51.7 us
    pallas_call x4, Pallas kernels, attend_chunk(): pl.pallas_call(functools.partial(attend_kernel, n_ctx, n, first, last), g...  44.3 us
    all_to_all x1, waiting for transfers between devices, body(): lax.all_to_all(expert_rows, 'q', split_axis=0, concat_axis=0, tiled=True)  32.6 us
    unnamed x198, local copies, waits for them, and re-layouts  31.7 us
  transfers between devices with their start and end apart: 94, of which 41 were waited for; matrix products, arithmetic and copies ran while one was open for 27% of the time, Pallas kernels for 23%

profile of v7, /device:TPU:0, one launch (start us, length us, event | category | flops | bytes accessed | tf_op | source)
XLA Modules:
  0.0 1001.0 jit_solution(15952616974638269481)
XLA Ops:
  48.9 11.8 %collective-permute-done.9 = bf16[2,40,3968]{2,1,0:T(8,128)(2,1)S(1)} collective-permute-done((bf16[2,40,3968]{2,1,0:T(8,128)(2,1)}, bf16[2,40,3968]{2,1,0:T(8,128)(2,1)S(1)}, u32[]{:S(2)}, u32[]{:S(2)}) %collective-permute-start.9) | collective-permute-done | bytes 634912 | tf_op jit(solution)/shard_map/ppermute | solution.py:54
  64.7 12.2 %collective-permute-done.16 = bf16[40,4096]{1,0:T(8,128)(2,1)S(1)} collective-permute-done((bf16[40,4096]{1,0:T(8,128)(2,1)}, bf16[40,4096]{1,0:T(8,128)(2,1)S(1)}, u32[]{:S(2)}, u32[]{:S(2)}) %collective-permute-start.16) | collective-permute-done | bytes 327712 | tf_op jit(solution)/shard_map/ppermute | solution.py:54
  93.5 14.8 %collective-permute-done.19 = bf16[256,1280]{1,0:T(8,128)(2,1)S(1)} collective-permute-done((bf16[256,1280]{1,0:T(8,128)(2,1)S(1)}, bf16[256,1280]{1,0:T(8,128)(2,1)S(1)}, u32[]{:S(2)}, u32[]{:S(2)}) %collective-permute-start.19) | collective-permute-done | bytes 655392 | tf_op jit(solution)/shard_map/ppermute | solution.py:54
  112.3 14.1 %collective-permute-done.21 = bf16[256,1280]{1,0:T(8,128)(2,1)} collective-permute-done((bf16[256,1280]{1,0:T(8,128)(2,1)S(1)}, bf16[256,1280]{1,0:T(8,128)(2,1)}, u32[]{:S(2)}, u32[]{:S(2)}) %collective-permute-start.21) | collective-permute-done | bytes 655392 | tf_op jit(solution)/shard_map/ppermute | solution.py:54
  139.4 13.9 %project.1 = (bf16[256,1280]{1,0:T(8,128)(2,1)}, bf16[2,256,1280]{2,1,0:T(8,128)(2,1)}) custom-call(bf16[256,1280]{1,0:T(8,128)(2,1)} %fusion.29.x_ref, bf16[1280,3840]{1,0:T(8,128)(2,1)} %bitcast.354, f32[256,128]{1,0:T(8,128)} %get-tuple-element.316.cos_ref, f32[256,128]{1,0:T(8,128)} %get-tuple-element.315.sin_ref), custom_call_target="tpu_custom_call" | custom-call | flops 2516582400 | bytes 9830400 | tf_op jit(solution)/shard_map/project/pallas_call | solution.py:291
  159.8 24.8 %collective-permute-done.20.refs_0_ = bf16[2,256,1280]{2,1,0:T(8,128)(2,1)} collective-permute-done((bf16[2,256,1280]{2,1,0:T(8,128)(2,1)}, bf16[2,256,1280]{2,1,0:T(8,128)(2,1)}, u32[]{:S(2)}, u32[]{:S(2)}) %collective-permute-start.20) | collective-permute-done | bytes 1310752 | tf_op jit(solution)/shard_map/ppermute | solution.py:54
  195.8 9.7 attend.4
  205.4 11.3 %attend.5 = (f32[256,1280]{1,0:T(8,128)}, f32[10,256,128]{2,1,0:T(8,128)}) custom-call(s32[3]{0:T(128)} %pad_add_fusion.1.place_ref, bf16[256,1280]{1,0:T(8,128)(2,1)} %get-tuple-element.125.q_ref, bf16[2,256,1280]{2,1,0:T(8,128)(2,1)} %collective-permute-done.20.refs_0_, bf16[2,256,1280]{2,1,0:T(8,128)(2,1)} %collective-permute-done.26.refs_1_, ...), custom_call_target="tpu_custom_call" | custom-call | flops 2684354560 | bytes 2621440 | tf_op jit(solution)/shard_map/attend/pallas_call | solution.py:400
  228.0 11.4 %attend.6 = (f32[256,1280]{1,0:T(8,128)}, f32[10,256,128]{2,1,0:T(8,128)}) custom-call(s32[3]{0:T(128)} %pad_add_fusion.3.place_ref, bf16[256,1280]{1,0:T(8,128)(2,1)} %get-tuple-element.125.q_ref, bf16[2,256,1280]{2,1,0:T(8,128)(2,1)} %collective-permute-done.25.refs_0_, bf16[2,256,1280]{2,1,0:T(8,128)(2,1)} %collective-permute-done.29.refs_1_, ...), custom_call_target="tpu_custom_call" | custom-call | flops 2684354560 | bytes 2621440 | tf_op jit(solution)/shard_map/attend/pallas_call | solution.py:400
  239.4 9.5 collective-permute-done.33.refs_3_
  272.1 11.9 %attend.7 = (bf16[256,1280]{1,0:T(8,128)(2,1)}, f32[10,256,128]{2,1,0:T(8,128)}) custom-call(s32[3]{0:T(128)} %pad_add_fusion.place_ref, bf16[256,1280]{1,0:T(8,128)(2,1)} %get-tuple-element.125.q_ref, bf16[2,256,1280]{2,1,0:T(8,128)(2,1)} %collective-permute-done.28.refs_0_, bf16[2,256,1280]{2,1,0:T(8,128)(2,1)} %collective-permute-done.34.refs_1_, ...), custom_call_target="tpu_custom_call" | custom-call | flops 2684354560 | bytes 2621440 | tf_op jit(solution)/shard_map/attend/pallas_call | solution.py:400
  287.9 15.7 %collective-permute-done.40 = bf16[256,1280]{1,0:T(8,128)(2,1)S(1)} collective-permute-done((bf16[256,1280]{1,0:T(8,128)(2,1)S(1)}, bf16[256,1280]{1,0:T(8,128)(2,1)S(1)}, u32[]{:S(2)}, u32[]{:S(2)}) %collective-permute-start.40) | collective-permute-done | bytes 655392 | tf_op jit(solution)/shard_map/ppermute | solution.py:54
  304.3 29.7 %collective-permute-done.41 = bf16[2,256,1280]{2,1,0:T(8,128)(2,1)S(1)} collective-permute-done((bf16[2,256,1280]{2,1,0:T(8,128)(2,1)S(1)}, bf16[2,256,1280]{2,1,0:T(8,128)(2,1)S(1)}, u32[]{:S(2)}, u32[]{:S(2)}) %collective-permute-start.41) | collective-permute-done | bytes 1310752 | tf_op jit(solution)/shard_map/ppermute | solution.py:54
  340.0 18.4 %collective-permute-done.37 = bf16[256,1280]{1,0:T(8,128)(2,1)} collective-permute-done((bf16[256,1280]{1,0:T(8,128)(2,1)S(1)}, bf16[256,1280]{1,0:T(8,128)(2,1)}, u32[]{:S(2)}, u32[]{:S(2)}) %collective-permute-start.37) | collective-permute-done | bytes 655392 | tf_op jit(solution)/shard_map/ppermute | solution.py:54
  365.9 11.3 %collective-permute-done.38 = bf16[256,1280]{1,0:T(8,128)(2,1)} collective-permute-done((bf16[256,1280]{1,0:T(8,128)(2,1)}, bf16[256,1280]{1,0:T(8,128)(2,1)}, u32[]{:S(2)}, u32[]{:S(2)}) %collective-permute-start.38) | collective-permute-done | bytes 655392 | tf_op jit(solution)/shard_map/ppermute | solution.py:54
  393.5 23.2 %experts.4 = (bf16[2,256,1280]{2,1,0:T(8,128)(2,1)}, bf16[2,256,1280]{2,1,0:T(8,128)(2,1)}, f32[2,2,1,256]{3,2,1,0:T(1,128)}, bf16[2816,1280]{1,0:T(8,128)(2,1)}...) custom-call(s32[4]{0:T(128)} %pad_add_fusion.4.e_ref, ...), custom_call_target="tpu_custom_call" | custom-call | flops 9688842240 | bytes 30000000 | tf_op jit(solution)/shard_map/experts/pallas_call | solution.py:589
  439.3 22.2 %experts.5 = (bf16[2,256,1280]{2,1,0:T(8,128)(2,1)}, bf16[2,256,1280]{2,1,0:T(8,128)(2,1)}, f32[2,2,1,256]{3,2,1,0:T(1,128)}, bf16[2816,1280]{1,0:T(8,128)(2,1)}...) custom-call(s32[4]{0:T(128)} %pad_add_fusion.4.e_ref, ...), custom_call_target="tpu_custom_call", output_to_operand_aliasing={{3}: (9, {}), {4}: (10, {}), {5}: (11, {}), {6}: (12, {})} | custom-call | flops 9688842240 | bytes 30000000 | tf_op jit(solution)/shard_map/experts/pallas_call | solution.py:589
  467.1 23.7 %experts.6 = (bf16[2,256,1280]{2,1,0:T(8,128)(2,1)}, bf16[2,256,1280]{2,1,0:T(8,128)(2,1)}, f32[2,2,1,256]{3,2,1,0:T(1,128)}, bf16[2816,1280]{1,0:T(8,128)(2,1)}...) custom-call(s32[4]{0:T(128)} %pad_add_fusion.4.e_ref, ...), custom_call_target="tpu_custom_call", output_to_operand_aliasing={{3}: (7, {}), {4}: (8, {}), {5}: (9, {}), {6}: (10, {}), {7... | custom-call | flops 9688842240 | bytes 30000000 | tf_op jit(solution)/shard_map/experts/pallas_call | solution.py:589
  508.9 22.3 %experts.7 = (bf16[2,256,1280]{2,1,0:T(8,128)(2,1)}, bf16[2,256,1280]{2,1,0:T(8,128)(2,1)}, f32[2,2,1,256]{3,2,1,0:T(1,128)}, bf16[2816,1280]{1,0:T(8,128)(2,1)}...) custom-call(s32[4]{0:T(128)} %pad_add_fusion.4.e_ref, ...), custom_call_target="tpu_custom_call", output_to_operand_aliasing={{3}: (9, {}), {4}: (10, {}), {5}: (11, {}), {6}: (12, {}), ... | custom-call | flops 9688842240 | bytes 30000000 | tf_op jit(solution)/shard_map/experts/pallas_call | solution.py:589
  532.5 18.7 %convolution_convert_fusion.4 = bf16[1280,1792]{1,0:T(8,128)(2,1)S(1)} fusion(bf16[2816,1280]{1,0:T(8,128)(2,1)} %get-tuple-element.177, bf16[2816,1792]{1,0:T(8,128)(2,1)} %get-tuple-element.178), kind=kOutput, calls=%fused_computation.6 | convolution fusion | flops 12920750080 | bytes 21889024 | tf_op jit(solution)/shard_map/dot_general | solution.py:45
  583.5 10.9 %collective-permute-done.53 = bf16[256,1280]{1,0:T(8,128)(2,1)S(1)} collective-permute-done((bf16[256,1280]{1,0:T(8,128)(2,1)S(1)}, bf16[256,1280]{1,0:T(8,128)(2,1)S(1)}, u32[]{:S(2)}, u32[]{:S(2)}) %collective-permute-start.53) | collective-permute-done | bytes 655392 | tf_op jit(solution)/shard_map/ppermute | solution.py:54
  648.2 12.7 %attend_back.4 = (f32[256,1280]{1,0:T(8,128)}, f32[2,256,1280]{2,1,0:T(8,128)}, bf16[2,256,1280]{2,1,0:T(8,128)(2,1)}) custom-call(s32[3]{0:T(128)} %pad_add_fusion.1.place_ref, bf16[256,1280]{1,0:T(8,128)(2,1)} %get-tuple-element.125.q_ref, bf16[256,1280]{1,0:T(8,128)(2,1)} %convolution_convert_fusion.8.do_ref, bf16[256,1280]{1,0:T(8,128)(2,1)} %get-tuple-element.138.o_ref, ...), custom_call_target="tpu_custom_call" | custom-call | flops 6710886400 | bytes 5242880 | tf_op jit(solution)/shard_map/attend_back/pallas_call | solution.py:461
  678.6 12.9 %attend_back.5 = (f32[256,1280]{1,0:T(8,128)}, f32[2,256,1280]{2,1,0:T(8,128)}, bf16[2,256,1280]{2,1,0:T(8,128)(2,1)}) custom-call(s32[3]{0:T(128)} %pad_add_fusion.3.place_ref, bf16[256,1280]{1,0:T(8,128)(2,1)} %get-tuple-element.125.q_ref, bf16[256,1280]{1,0:T(8,128)(2,1)} %convolution_convert_fusion.8.do_ref, bf16[256,1280]{1,0:T(8,128)(2,1)} %get-tuple-element.138.o_ref, ...), custom_call_target="tpu_custom_call" | custom-call | flops 6710886400 | bytes 5242880 | tf_op jit(solution)/shard_map/attend_back/pallas_call | solution.py:461
  691.5 12.9 %attend_back.6 = (f32[256,1280]{1,0:T(8,128)}, f32[2,256,1280]{2,1,0:T(8,128)}, bf16[2,256,1280]{2,1,0:T(8,128)(2,1)}) custom-call(s32[3]{0:T(128)} %pad_add_fusion.place_ref, bf16[256,1280]{1,0:T(8,128)(2,1)} %get-tuple-element.125.q_ref, bf16[256,1280]{1,0:T(8,128)(2,1)} %convolution_convert_fusion.8.do_ref, bf16[256,1280]{1,0:T(8,128)(2,1)} %get-tuple-element.138.o_ref, ...), custom_call_target="tpu_custom_call" | custom-call | flops 6710886400 | bytes 5242880 | tf_op jit(solution)/shard_map/attend_back/pallas_call | solution.py:461
  705.0 32.6 %all-to-all-done.2 = bf16[4,240,1792]{2,1,0:T(8,128)(2,1)} async-done(((bf16[4,240,1792]{2,1,0:T(8,128)(2,1)}), bf16[4,240,1792]{2,1,0:T(8,128)(2,1)}, u32[]{:S(2)}, u32[]{:S(2)}) %all-to-all-start.2) | async-done | bytes 3440672 | tf_op jit(solution)/shard_map/all_to_all | solution.py:835
  737.5 13.0 %attend_back.7 = (bf16[256,1280]{1,0:T(8,128)(2,1)}, f32[2,256,1280]{2,1,0:T(8,128)}, bf16[2,256,1280]{2,1,0:T(8,128)(2,1)}) custom-call(s32[3]{0:T(128)} %pad_add_fusion.2.place_ref, bf16[256,1280]{1,0:T(8,128)(2,1)} %get-tuple-element.125.q_ref, bf16[256,1280]{1,0:T(8,128)(2,1)} %convolution_convert_fusion.8.do_ref, ...), custom_call_target="tpu_custom_call" | custom-call | flops 6710886400 | bytes 5242880 | tf_op jit(solution)/shard_map/attend_back/pallas_call | solution.py:461
  779.9 22.0 %collective-permute-done.67 = bf16[2,256,1280]{2,1,0:T(8,128)(2,1)S(1)} collective-permute-done((bf16[2,256,1280]{2,1,0:T(8,128)(2,1)S(1)}, bf16[2,256,1280]{2,1,0:T(8,128)(2,1)S(1)}, u32[]{:S(2)}, u32[]{:S(2)}) %collective-permute-start.67) | collective-permute-done | bytes 1310752 | tf_op jit(solution)/shard_map/ppermute | solution.py:54
  822.6 9.3 add_convert_fusion
  843.2 31.6 %collective-permute-done.72 = bf16[2,2,40,5376]{3,2,0,1:T(8,128)(2,1)S(1)} collective-permute-done((bf16[2,2,40,5376]{3,2,0,1:T(8,128)(2,1)S(1)}, bf16[2,2,40,5376]{3,2,0,1:T(8,128)(2,1)S(1)}, u32[]{:S(2)}, u32[]{:S(2)}) %collective-permute-start.72) | collective-permute-done | bytes 1720352 | tf_op jit(solution)/shard_map/ppermute | solution.py:54
  895.4 15.5 %collective-permute-done.79 = bf16[2,40,5376]{2,1,0:T(8,128)(2,1)} collective-permute-done((bf16[2,40,5376]{2,1,0:T(8,128)(2,1)S(1)}, bf16[2,40,5376]{2,1,0:T(8,128)(2,1)}, u32[]{:S(2)}, u32[]{:S(2)}) %collective-permute-start.79) | collective-permute-done | bytes 860192 | tf_op jit(solution)/shard_map/ppermute | solution.py:54
  934.5 13.9 %collective-permute-done.77 = bf16[256,1280]{1,0:T(8,128)(2,1)S(1)} collective-permute-done((bf16[256,1280]{1,0:T(8,128)(2,1)S(1)}, bf16[256,1280]{1,0:T(8,128)(2,1)S(1)}, u32[]{:S(2)}, u32[]{:S(2)}) %collective-permute-start.77) | collective-permute-done | bytes 655392 | tf_op jit(solution)/shard_map/ppermute | solution.py:54
  961.7 17.9 %collective-permute-done.83 = bf16[40,5376]{1,0:T(8,128)(2,1)S(1)} collective-permute-done((bf16[40,5376]{1,0:T(8,128)(2,1)S(1)}, bf16[40,5376]{1,0:T(8,128)(2,1)S(1)}, u32[]{:S(2)}, u32[]{:S(2)}) %collective-permute-start.83) | collective-permute-done | bytes 430112 | tf_op jit(solution)/shard_map/ppermute | solution.py:54
  (568 shorter events, 462.4 us)
Async XLA Ops:
  77.2 49.1 %collective-permute-start.11 = (bf16[8,40,3968]{2,1,0:T(8,128)(2,1)S(1)}, bf16[8,40,3968]{2,1,0:T(8,128)(2,1)S(1)}, u32[]{:S(2)}, u32[]{:S(2)}) collective-permute-start(bf16[8,40,3968]{2,1,0:T(8,128)(2,1)S(1)} %pad_maximum_fusion.10.refs_0_), channel_id=1, source_target_pairs={{0,4},{4,0},{1,5},{5,1},{2,6},{6,2},{3,7},{7,3},{8,12},{12,8},{9,1... | collective-permute-start | bytes 7618568 | tf_op jit(solution)/shard_map/ppermute | solution.py:54
  88.0 39.9 %collective-permute-start.14 = (bf16[8,40,3968]{2,1,0:T(8,128)(2,1)S(1)}, bf16[8,40,3968]{2,1,0:T(8,128)(2,1)}, u32[]{:S(2)}, u32[]{:S(2)}) collective-permute-start(bf16[8,40,3968]{2,1,0:T(8,128)(2,1)S(1)} %pad_maximum_fusion.11.refs_2_), channel_id=1, source_target_pairs={{0,4},{4,0},{1,5},{5,1},{2,6},{6,2},{3,7},{7,3},{8,12},{12,8},{9,1... | collective-permute-start | bytes 7618568 | tf_op jit(solution)/shard_map/ppermute | solution.py:54
  108.5 47.0 %collective-permute-start.24 = (bf16[2,2,40,4096]{3,2,1,0:T(8,128)(2,1)S(1)}, bf16[2,2,40,4096]{3,2,1,0:T(8,128)(2,1)}, u32[]{:S(2)}, u32[]{:S(2)}) collective-permute-start(bf16[2,2,40,4096]{3,2,1,0:T(8,128)(2,1)S(1)} %pad_maximum_fusion.14), channel_id=1, source_target_pairs={{0,1},{1,0},{2,3},{3,2},{4,5},{5,4},{6,7},{7,6},{8,9},{9,8},{10,11... | collective-permute-start | bytes 3932168 | tf_op jit(solution)/shard_map/ppermute | solution.py:54
  111.2 44.3 %collective-permute-start.23 = (bf16[2,2,40,4096]{3,2,1,0:T(8,128)(2,1)}, bf16[2,2,40,4096]{3,2,1,0:T(8,128)(2,1)}, u32[]{:S(2)}, u32[]{:S(2)}) collective-permute-start(bf16[2,2,40,4096]{3,2,1,0:T(8,128)(2,1)} %pad_maximum_fusion.13), channel_id=1, source_target_pairs={{0,2},{2,0},{1,3},{3,1},{4,6},{6,4},{5,7},{7,5},{8,10},{10,8},{9,1... | collective-permute-start | bytes 3932168 | tf_op jit(solution)/shard_map/ppermute | solution.py:54
  189.3 59.6 %collective-permute-start.33 = (bf16[2,2,256,1280]{3,2,1,0:T(8,128)(2,1)}, bf16[2,2,256,1280]{3,2,1,0:T(8,128)(2,1)}, u32[]{:S(2)}, u32[]{:S(2)}) collective-permute-start(bf16[2,2,256,1280]{3,2,1,0:T(8,128)(2,1)} %pad_maximum_fusion.5.refs_2_), channel_id=1, source_target_pairs={{0,1},{1,0},{2,3},{3,2},{4,5},{5,4},{6,7},{7,6},{8,9},{9,8},{10,11... | collective-permute-start | bytes 7864328 | tf_op jit(solution)/shard_map/ppermute | solution.py:54
  195.3 59.3 %collective-permute-start.31 = (bf16[2,2,256,1280]{3,2,1,0:T(8,128)(2,1)}, bf16[2,2,256,1280]{3,2,1,0:T(8,128)(2,1)}, u32[]{:S(2)}, u32[]{:S(2)}) collective-permute-start(bf16[2,2,256,1280]{3,2,1,0:T(8,128)(2,1)} %get-tuple-element.295), channel_id=1, source_target_pairs={{0,2},{2,0},{1,3},{3,1},{4,6},{6,4},{5,7},{7,5},{8,10},{10,8},{9,1... | collective-permute-start | bytes 7864328 | tf_op jit(solution)/shard_map/ppermute | solution.py:54
  221.0 41.2 %collective-permute-start.35 = (bf16[8,40,4096]{2,1,0:T(8,128)(2,1)}, bf16[8,40,4096]{2,1,0:T(8,128)(2,1)}, u32[]{:S(2)}, u32[]{:S(2)}) collective-permute-start(bf16[8,40,4096]{2,1,0:T(8,128)(2,1)} %pad_maximum_fusion.6.refs_0_), channel_id=1, source_target_pairs={{0,4},{4,0},{1,5},{5,1},{2,6},{6,2},{3,7},{7,3},{8,12},{12,8},{9,1... | collective-permute-start | bytes 7864328 | tf_op jit(solution)/shard_map/ppermute | solution.py:54
  256.5 82.9 %all-to-all-start = ((bf16[4,240,1792]{2,1,0:T(8,128)(2,1)}), bf16[4,240,1792]{2,1,0:T(8,128)(2,1)}, u32[]{:S(2)}, u32[]{:S(2)}) async-start(bf16[4,240,1792]{2,1,0:T(8,128)(2,1)} %pad_maximum_fusion.1), calls=%async_computation | async-start | bytes 6881280 | tf_op jit(solution)/shard_map/all_to_all | solution.py:752
  339.4 41.5 %collective-permute-start.42 = (bf16[4,240,1792]{2,1,0:T(8,128)(2,1)}, bf16[4,240,1792]{2,1,0:T(8,128)(2,1)}, u32[]{:S(2)}, u32[]{:S(2)}) collective-permute-start(bf16[4,240,1792]{2,1,0:T(8,128)(2,1)} %all-to-all-done.refs_0_), channel_id=1, source_target_pairs={{0,4},{4,0},{1,5},{5,1},{2,6},{6,2},{3,7},{7,3},{8,12},{12,8},{9,1... | collective-permute-start | bytes 10321928 | tf_op jit(solution)/shard_map/ppermute | solution.py:54
  377.2 41.9 %collective-permute-start.39 = (bf16[256,1280]{1,0:T(8,128)(2,1)}, bf16[256,1280]{1,0:T(8,128)(2,1)}, u32[]{:S(2)}, u32[]{:S(2)}) collective-permute-start(bf16[256,1280]{1,0:T(8,128)(2,1)} %collective-permute-done.38), channel_id=1, source_target_pairs={{0,1},{1,0},{2,3},{3,2},{4,5},{5,4},{6,7},{7,6},{8,9},{9,8},{10,11... | collective-permute-start | bytes 1966088 | tf_op jit(solution)/shard_map/ppermute | solution.py:54
  378.4 39.1 %collective-permute-start.46 = (bf16[256,1280]{1,0:T(8,128)(2,1)}, bf16[256,1280]{1,0:T(8,128)(2,1)}, u32[]{:S(2)}, u32[]{:S(2)}) collective-permute-start(bf16[256,1280]{1,0:T(8,128)(2,1)} %collective-permute-done.38), channel_id=1, source_target_pairs={{0,8},{8,16},{16,24},{24,0},{1,9},{9,17},{17,25},{25,1},{2,10},{10... | collective-permute-start | bytes 1966088 | tf_op jit(solution)/shard_map/ppermute | solution.py:54
  387.5 51.8 %collective-permute-start.45 = (bf16[2,256,1280]{2,1,0:T(8,128)(2,1)}, bf16[2,256,1280]{2,1,0:T(8,128)(2,1)}, u32[]{:S(2)}, u32[]{:S(2)}) collective-permute-start(bf16[2,256,1280]{2,1,0:T(8,128)(2,1)} %pad_maximum_fusion.19.refs_0_), channel_id=1, source_target_pairs={{0,1},{1,0},{2,3},{3,2},{4,5},{5,4},{6,7},{7,6},{8,9},{9,8},{10,11... | collective-permute-start | bytes 3932168 | tf_op jit(solution)/shard_map/ppermute | solution.py:54
  421.6 42.1 %collective-permute-start.43 = (bf16[2,256,1280]{2,1,0:T(8,128)(2,1)}, bf16[2,256,1280]{2,1,0:T(8,128)(2,1)}, u32[]{:S(2)}, u32[]{:S(2)}) collective-permute-start(bf16[2,256,1280]{2,1,0:T(8,128)(2,1)} %pad_maximum_fusion.17), channel_id=1, source_target_pairs={{0,2},{2,0},{1,3},{3,1},{4,6},{6,4},{5,7},{7,5},{8,10},{10,8},{9,1... | collective-permute-start | bytes 3932168 | tf_op jit(solution)/shard_map/ppermute | solution.py:54
  427.4 67.0 %collective-permute-start.54 = (bf16[2,256,1280]{2,1,0:T(8,128)(2,1)}, bf16[2,256,1280]{2,1,0:T(8,128)(2,1)}, u32[]{:S(2)}, u32[]{:S(2)}) collective-permute-start(bf16[2,256,1280]{2,1,0:T(8,128)(2,1)} %get-tuple-element.175), channel_id=1, source_target_pairs={{0,2},{2,0},{1,3},{3,1},{4,6},{6,4},{5,7},{7,5},{8,10},{10,8},{9,1... | collective-permute-start | bytes 3932168 | tf_op jit(solution)/shard_map/ppermute | solution.py:54
  438.1 70.9 %collective-permute-start.48 = (bf16[2,256,1280]{2,1,0:T(8,128)(2,1)}, bf16[2,256,1280]{2,1,0:T(8,128)(2,1)}, u32[]{:S(2)}, u32[]{:S(2)}) collective-permute-start(bf16[2,256,1280]{2,1,0:T(8,128)(2,1)} %pad_maximum_fusion.20.refs_0_), channel_id=1, source_target_pairs={{0,1},{1,0},{2,3},{3,2},{4,5},{5,4},{6,7},{7,6},{8,9},{9,8},{10,11... | collective-permute-start | bytes 3932168 | tf_op jit(solution)/shard_map/ppermute | solution.py:54
  491.6 62.4 %collective-permute-start.49 = (bf16[2,256,1280]{2,1,0:T(8,128)(2,1)}, bf16[2,256,1280]{2,1,0:T(8,128)(2,1)S(1)}, u32[]{:S(2)}, u32[]{:S(2)}) collective-permute-start(bf16[2,256,1280]{2,1,0:T(8,128)(2,1)} %get-tuple-element.170), channel_id=1, source_target_pairs={{0,1},{1,0},{2,3},{3,2},{4,5},{5,4},{6,7},{7,6},{8,9},{9,8},{10,11... | collective-permute-start | bytes 3932168 | tf_op jit(solution)/shard_map/ppermute | solution.py:54
  492.9 82.4 %collective-permute-start.52 = (bf16[2,256,1280]{2,1,0:T(8,128)(2,1)}, bf16[2,256,1280]{2,1,0:T(8,128)(2,1)}, u32[]{:S(2)}, u32[]{:S(2)}) collective-permute-start(bf16[2,256,1280]{2,1,0:T(8,128)(2,1)} %get-tuple-element.172), channel_id=1, source_target_pairs={{0,2},{2,0},{1,3},{3,1},{4,6},{6,4},{5,7},{7,5},{8,10},{10,8},{9,1... | collective-permute-start | bytes 3932168 | tf_op jit(solution)/shard_map/ppermute | solution.py:54
  497.4 133.9 %collective-permute-start.60 = (bf16[256,1280]{1,0:T(8,128)(2,1)}, bf16[256,1280]{1,0:T(8,128)(2,1)}, u32[]{:S(2)}, u32[]{:S(2)}) collective-permute-start(bf16[256,1280]{1,0:T(8,128)(2,1)} %fusion.57), channel_id=1, source_target_pairs={{0,1},{1,0},{2,3},{3,2},{4,5},{5,4},{6,7},{7,6},{8,9},{9,8},{10,11... | collective-permute-start | bytes 1966088 | tf_op jit(solution)/shard_map/ppermute | solution.py:54
  531.2 49.1 %collective-permute-start.57 = (bf16[2,256,1280]{2,1,0:T(8,128)(2,1)}, bf16[2,256,1280]{2,1,0:T(8,128)(2,1)}, u32[]{:S(2)}, u32[]{:S(2)}) collective-permute-start(bf16[2,256,1280]{2,1,0:T(8,128)(2,1)} %get-tuple-element.183), channel_id=1, source_target_pairs={{0,1},{1,0},{2,3},{3,2},{4,5},{5,4},{6,7},{7,6},{8,9},{9,8},{10,11... | collective-permute-start | bytes 3932168 | tf_op jit(solution)/shard_map/ppermute | solution.py:54
  626.2 111.3 %all-to-all-start.2 = ((bf16[4,240,1792]{2,1,0:T(8,128)(2,1)}), bf16[4,240,1792]{2,1,0:T(8,128)(2,1)}, u32[]{:S(2)}, u32[]{:S(2)}) async-start(bf16[4,240,1792]{2,1,0:T(8,128)(2,1)} %add_convert_fusion.1), calls=%async_computation.2 | async-start | bytes 6881280 | tf_op jit(solution)/shard_map/all_to_all | solution.py:835
  667.2 101.8 %collective-permute-start.61 = (bf16[2,2,256,1280]{3,2,0,1:T(8,128)(2,1)}, bf16[2,2,256,1280]{3,2,0,1:T(8,128)(2,1)}, u32[]{:S(2)}, u32[]{:S(2)}) collective-permute-start(bf16[2,2,256,1280]{3,2,0,1:T(8,128)(2,1)} %copy.164), channel_id=1, source_target_pairs={{0,1},{1,0},{2,3},{3,2},{4,5},{5,4},{6,7},{7,6},{8,9},{9,8},{10,11... | collective-permute-start | bytes 7864328 | tf_op jit(solution)/shard_map/ppermute | solution.py:54
  670.1 102.9 %collective-permute-start.75 = (bf16[2,2,256,1280]{3,2,0,1:T(8,128)(2,1)}, bf16[2,2,256,1280]{3,2,0,1:T(8,128)(2,1)}, u32[]{:S(2)}, u32[]{:S(2)}) collective-permute-start(bf16[2,2,256,1280]{3,2,0,1:T(8,128)(2,1)} %copy.183), channel_id=1, source_target_pairs={{0,2},{2,0},{1,3},{3,1},{4,6},{6,4},{5,7},{7,5},{8,10},{10,8},{9,1... | collective-permute-start | bytes 7864328 | tf_op jit(solution)/shard_map/ppermute | solution.py:54
  678.2 88.4 %collective-permute-start.65 = (bf16[2,256,1280]{2,1,0:T(8,128)(2,1)}, bf16[2,256,1280]{2,1,0:T(8,128)(2,1)}, u32[]{:S(2)}, u32[]{:S(2)}) collective-permute-start(bf16[2,256,1280]{2,1,0:T(8,128)(2,1)} %add_convert_fusion.5), channel_id=1, source_target_pairs={{0,8},{8,16},{16,24},{24,0},{1,9},{9,17},{17,25},{25,1},{2,10},{10... | collective-permute-start | bytes 3932168 | tf_op jit(solution)/shard_map/ppermute | solution.py:54
  691.5 75.0 %collective-permute-start.66 = (bf16[2,256,1280]{2,1,0:T(8,128)(2,1)}, bf16[2,256,1280]{2,1,0:T(8,128)(2,1)}, u32[]{:S(2)}, u32[]{:S(2)}) collective-permute-start(bf16[2,256,1280]{2,1,0:T(8,128)(2,1)} %get-tuple-element.195), channel_id=1, source_target_pairs={{0,4},{4,0},{1,5},{5,1},{2,6},{6,2},{3,7},{7,3},{8,12},{12,8},{9,1... | collective-permute-start | bytes 3932168 | tf_op jit(solution)/shard_map/ppermute | solution.py:54
  704.5 75.3 %collective-permute-start.68 = (bf16[2,256,1280]{2,1,0:T(8,128)(2,1)}, bf16[2,256,1280]{2,1,0:T(8,128)(2,1)}, u32[]{:S(2)}, u32[]{:S(2)}) collective-permute-start(bf16[2,256,1280]{2,1,0:T(8,128)(2,1)} %get-tuple-element.198), channel_id=1, source_target_pairs={{0,4},{4,0},{1,5},{5,1},{2,6},{6,2},{3,7},{7,3},{8,12},{12,8},{9,1... | collective-permute-start | bytes 3932168 | tf_op jit(solution)/shard_map/ppermute | solution.py:54
  766.5 56.1 %collective-permute-start.71 = (bf16[4,2,2,40,5376]{4,3,0,1,2:T(8,128)(2,1)}, bf16[4,2,2,40,5376]{4,3,0,1,2:T(8,128)(2,1)}, u32[]{:S(2)}, u32[]{:S(2)}) collective-permute-start(bf16[4,2,2,40,5376]{4,3,0,1,2:T(8,128)(2,1)} %get-tuple-element.313), channel_id=1, source_target_pairs={{0,4},{4,0},{1,5},{5,1},{2,6},{6,2},{3,7},{7,3},{8,12},{12,8},{9,1... | collective-permute-start | bytes 20643848 | tf_op jit(solution)/shard_map/ppermute | solution.py:54
  772.5 42.3 %collective-permute-start.62 = (bf16[2,256,1280]{2,1,0:T(8,128)(2,1)}, bf16[2,256,1280]{2,1,0:T(8,128)(2,1)}, u32[]{:S(2)}, u32[]{:S(2)}) collective-permute-start(bf16[2,256,1280]{2,1,0:T(8,128)(2,1)} %fusion.35), channel_id=1, source_target_pairs={{0,2},{2,0},{1,3},{3,1},{4,6},{6,4},{5,7},{7,5},{8,10},{10,8},{9,1... | collective-permute-start | bytes 3932168 | tf_op jit(solution)/shard_map/ppermute | solution.py:54
  778.5 40.2 %collective-permute-start.76 = (bf16[2,256,1280]{2,1,0:T(8,128)(2,1)}, bf16[2,256,1280]{2,1,0:T(8,128)(2,1)}, u32[]{:S(2)}, u32[]{:S(2)}) collective-permute-start(bf16[2,256,1280]{2,1,0:T(8,128)(2,1)} %fusion.36), channel_id=1, source_target_pairs={{0,1},{1,0},{2,3},{3,2},{4,5},{5,4},{6,7},{7,6},{8,9},{9,8},{10,11... | collective-permute-start | bytes 3932168 | tf_op jit(solution)/shard_map/ppermute | solution.py:54
  779.7 60.2 %collective-permute-start.70 = (bf16[2,256,1280]{2,1,0:T(8,128)(2,1)}, bf16[2,256,1280]{2,1,0:T(8,128)(2,1)}, u32[]{:S(2)}, u32[]{:S(2)}) collective-permute-start(bf16[2,256,1280]{2,1,0:T(8,128)(2,1)} %get-tuple-element.202), channel_id=1, source_target_pairs={{0,4},{4,0},{1,5},{5,1},{2,6},{6,2},{3,7},{7,3},{8,12},{12,8},{9,1... | collective-permute-start | bytes 3932168 | tf_op jit(solution)/shard_map/ppermute | solution.py:54
  804.9 75.6 %collective-permute-start.69 = (bf16[2,256,1280]{2,1,0:T(8,128)(2,1)}, bf16[2,256,1280]{2,1,0:T(8,128)(2,1)}, u32[]{:S(2)}, u32[]{:S(2)}) collective-permute-start(bf16[2,256,1280]{2,1,0:T(8,128)(2,1)} %add_convert_fusion.3), channel_id=1, source_target_pairs={{0,8},{8,16},{16,24},{24,0},{1,9},{9,17},{17,25},{25,1},{2,10},{10... | collective-permute-start | bytes 3932168 | tf_op jit(solution)/shard_map/ppermute | solution.py:54
  835.6 39.2 %collective-permute-start.72 = (bf16[2,2,40,5376]{3,2,0,1:T(8,128)(2,1)S(1)}, bf16[2,2,40,5376]{3,2,0,1:T(8,128)(2,1)S(1)}, u32[]{:S(2)}, u32[]{:S(2)}) collective-permute-start(bf16[2,2,40,5376]{3,2,0,1:T(8,128)(2,1)S(1)} %dynamic-slice_bitcast_fusion.3), channel_id=1, source_target_pairs={{0,2},{2,0},{1,3},{3,1},{4,6},{6,4},{5,7},{7,5},{8,10},{10,8},{9,1... | collective-permute-start | bytes 5160968 | tf_op jit(solution)/shard_map/ppermute | solution.py:54
  838.3 86.0 %collective-permute-start.63 = (bf16[256,1280]{1,0:T(8,128)(2,1)}, bf16[256,1280]{1,0:T(8,128)(2,1)}, u32[]{:S(2)}, u32[]{:S(2)}) collective-permute-start(bf16[256,1280]{1,0:T(8,128)(2,1)} %fusion.58), channel_id=1, source_target_pairs={{0,8},{8,16},{16,24},{24,0},{1,9},{9,17},{17,25},{25,1},{2,10},{10... | collective-permute-start | bytes 1966088 | tf_op jit(solution)/shard_map/ppermute | solution.py:54
  (154 other events, 1969.5 us)

commit v8 on v7

--- a/solution.py
+++ b/solution.py
@@ -93,34 +93,32 @@
 
 
 ORDER = {
-    "g": "r1",
+    "rest": "f3",
+    "g": "r3",
     "mid1": "r1",
     "rs1": "fp",
-    "norm": "rs g1",
+    "norm": "rs g2",
     "gs1": "rp",
-    "arr1": "g3 rp",
-    "arr2": "s",
+    "arr2": "s gs",
     "arr3": "s gf",
     "wa": "q",
     "wc": "cp",
     "c1b": "w",
-    "c2b": "k0",
-    "c3a": "k0",
+    "c2b": "w",
+    "c3a": "w",
     "K1": "s0",
-    "gu": "s0",
+    "gu": "s1",
     "dn": "s1",
     "t2": "er",
-    "sh": "k2",
     "B1": "m",
     "B3": "er",
     "y1": "rg",
     "fin": "late",
-    "kv1": "late",
+    "late2": "b",
     "kv2": "l",
     "yz2": "kv",
-    "yz4": "l",
     "late3": "kv",
-    "xg": "m",
+    "cz3": "cp",
     "dn0": "kv",
 }
 
@@ -166,7 +164,7 @@
         out_shape=[
             jax.ShapeDtypeStruct((n, c[0][1], c[2] - c[1]), pieces[0].dtype) for c in cuts
         ],
-        compiler_params=pltpu.CompilerParams(vmem_limit_bytes=VMEM_LIMIT),
+        compiler_params=pltpu.CompilerParams(vmem_limit_bytes=VMEM_LIMIT // 2),
         cost_estimate=pl.CostEstimate(
             flops=0, bytes_accessed=4 * n * rows * total, transcendentals=0
         ),
@@ -308,7 +306,7 @@
             jax.ShapeDtypeStruct((tok, width), BF),
             jax.ShapeDtypeStruct((2, tok, width), BF),
         ],
-        compiler_params=pltpu.CompilerParams(vmem_limit_bytes=VMEM_LIMIT),
+        compiler_params=pltpu.CompilerParams(vmem_limit_bytes=VMEM_LIMIT // 2),
         cost_estimate=pl.CostEstimate(
             flops=6 * tok * width * width, bytes_accessed=6 * width * width, transcendentals=0
         ),
@@ -409,7 +407,7 @@
             jax.ShapeDtypeStruct((tok, width), BF if last else F32),
             jax.ShapeDtypeStruct((HEADS, tok, 128), F32),
         ],
-        compiler_params=pltpu.CompilerParams(vmem_limit_bytes=VMEM_LIMIT),
+        compiler_params=pltpu.CompilerParams(vmem_limit_bytes=VMEM_LIMIT // 2),
         cost_estimate=pl.CostEstimate(
             flops=4 * pairs * HEAD_DIM * 4, bytes_accessed=8 * tok * width, transcendentals=pairs
         ),
@@ -468,7 +466,7 @@
         ),
         out_shape=[jax.ShapeDtypeStruct((tok, width), BF if last else F32)]
         + [jax.ShapeDtypeStruct((2, tok, width), F32 if s == 0 else BF) for s in range(n)],
-        compiler_params=pltpu.CompilerParams(vmem_limit_bytes=VMEM_LIMIT),
+        compiler_params=pltpu.CompilerParams(vmem_limit_bytes=VMEM_LIMIT // 2),
         cost_estimate=pl.CostEstimate(
             flops=10 * pairs * HEAD_DIM * 4, bytes_accessed=16 * tok * width, transcendentals=pairs
         ),

time: 1010 us -> 981 us (0.971)
  Pallas kernels: 233 us -> 199 us
  local copies, waits for them, and re-layouts: 97.9 us -> 128 us
  waiting for transfers between devices: 398 us -> 377 us
    unnamed x198 -> x352, local copies, waits for them, and re-layouts: 31.7 us -> 69.1 us
    ppermute x88, waiting for transfers between devices: 356 us -> 341 us  [shift(): return lax.ppermute(value, axis, [(i, (i + 1) % n) for i in range(n)])]
    pallas_call x3, Pallas kernels: 24 us -> 11.4 us  [place(): pl.pallas_call(functools.partial(place_kernel, counts, cuts), in_specs=[p...]
  transfers between devices with their start and end apart: 94 -> 94, of which waited for: 41 -> 44; matrix products, arithmetic and copies ran while one was open for 27% -> 26% of each run, Pallas kernels for 23% -> 21%
where the time goes in v8:
time: 981 us; the launch traced here: 969 us
  waiting for transfers between devices  377 us (38%)
  Pallas kernels  199 us (20%)
  local copies, waits for them, and re-layouts  128 us (13%)
  other arithmetic  123 us (13%)
  starting transfers between devices  77.8 us (8%)
  matrix products  60.6 us (6%)
    ppermute x88, waiting for transfers between devices, shift(): return lax.ppermute(value, axis, [(i, (i + 1) % n) for i in range(n)])  341 us
    pallas_call x4, Pallas kernels, expert_chunk(): pl.pallas_call(functools.partial(expert_kernel, slots, na, nb, even, len(...  91.1 us
    unnamed x352, local copies, waits for them, and re-layouts  69.1 us
    dot_general x21, matrix products, dot(): return lax.dot_general(a, b, (dims, ((), ())), preferred_element_type=F32)  60.6 us
    ppermute x88, starting transfers between devices, shift(): return lax.ppermute(value, axis, [(i, (i + 1) % n) for i in range(n)])  57.1 us
    pallas_call x4, Pallas kernels, attend_back_chunk(): pl.pallas_call(functools.partial(attend_back_kernel, n_ctx, n, first, las...  46 us
    pallas_call x4, Pallas kernels, attend_chunk(): pl.pallas_call(functools.partial(attend_kernel, n_ctx, n, first, last), g...  35.5 us
    all_to_all x1, waiting for transfers between devices, body(): lax.all_to_all(expert_rows, 'q', split_axis=0, concat_axis=0, tiled=True)  25.4 us
  transfers between devices with their start and end apart: 94, of which 44 were waited for; matrix products, arithmetic and copies ran while one was open for 26% of the time, Pallas kernels for 21%

profile of v8, /device:TPU:0, one launch (start us, length us, event | category | flops | bytes accessed | tf_op | source)
XLA Modules:
  0.0 969.1 jit_solution(14523921463897916471)
XLA Ops:
  6.3 8.8 collective-permute-done
  50.8 9.8 %collective-permute-done.9 = bf16[2,40,3968]{2,1,0:T(8,128)(2,1)} collective-permute-done((bf16[2,40,3968]{2,1,0:T(8,128)(2,1)}, bf16[2,40,3968]{2,1,0:T(8,128)(2,1)}, u32[]{:S(2)}, u32[]{:S(2)}) %collective-permute-start.9) | collective-permute-done | bytes 634912 | tf_op jit(solution)/shard_map/ppermute | solution.py:54
  67.1 9.7 collective-permute-done.16
  92.5 16.0 %collective-permute-done.19 = bf16[256,1280]{1,0:T(8,128)(2,1)S(1)} collective-permute-done((bf16[256,1280]{1,0:T(8,128)(2,1)S(1)}, bf16[256,1280]{1,0:T(8,128)(2,1)S(1)}, u32[]{:S(2)}, u32[]{:S(2)}) %collective-permute-start.19) | collective-permute-done | bytes 655392 | tf_op jit(solution)/shard_map/ppermute | solution.py:54
  113.3 13.5 %collective-permute-done.20 = bf16[256,1280]{1,0:T(8,128)(2,1)} collective-permute-done((bf16[256,1280]{1,0:T(8,128)(2,1)S(1)}, bf16[256,1280]{1,0:T(8,128)(2,1)}, u32[]{:S(2)}, u32[]{:S(2)}) %collective-permute-start.20) | collective-permute-done | bytes 655392 | tf_op jit(solution)/shard_map/ppermute | solution.py:54
  153.7 24.3 %collective-permute-done.21.refs_0_ = bf16[2,256,1280]{2,1,0:T(8,128)(2,1)} collective-permute-done((bf16[2,256,1280]{2,1,0:T(8,128)(2,1)S(1)}, bf16[2,256,1280]{2,1,0:T(8,128)(2,1)}, u32[]{:S(2)}, u32[]{:S(2)}) %collective-permute-start.21) | collective-permute-done | bytes 1310752 | tf_op jit(solution)/shard_map/ppermute | solution.py:54
  195.2 9.6 attend.5
  223.8 9.4 attend.6
  261.6 10.5 %attend.7 = (bf16[256,1280]{1,0:T(8,128)(2,1)S(1)}, f32[10,256,128]{2,1,0:T(8,128)S(1)}) custom-call(s32[3]{0:T(128)S(1)} %pad_add_fusion.place_ref, bf16[256,1280]{1,0:T(8,128)(2,1)S(1)} %copy-done.42, bf16[2,256,1280]{2,1,0:T(8,128)(2,1)} %collective-permute-done.30.refs_0_, bf16[2,256,1280]{2,1,0:T(8,128)(2,1)} %collective-permute-done.34.refs_1_, ...), custom_call_target="tpu_custom_call" | custom-call | flops 2684354560 | bytes 2621440 | tf_op jit(solution)/shard_map/attend/pallas_call | solution.py:398
  276.0 15.4 %collective-permute-done.39 = bf16[256,1280]{1,0:T(8,128)(2,1)S(1)} collective-permute-done((bf16[256,1280]{1,0:T(8,128)(2,1)S(1)}, bf16[256,1280]{1,0:T(8,128)(2,1)S(1)}, u32[]{:S(2)}, u32[]{:S(2)}) %collective-permute-start.39) | collective-permute-done | bytes 655392 | tf_op jit(solution)/shard_map/ppermute | solution.py:54
  295.2 28.7 %collective-permute-done.40 = bf16[2,256,1280]{2,1,0:T(8,128)(2,1)} collective-permute-done((bf16[2,256,1280]{2,1,0:T(8,128)(2,1)}, bf16[2,256,1280]{2,1,0:T(8,128)(2,1)}, u32[]{:S(2)}, u32[]{:S(2)}) %collective-permute-start.40) | collective-permute-done | bytes 1310752 | tf_op jit(solution)/shard_map/ppermute | solution.py:54
  351.3 13.9 %collective-permute-done.37 = bf16[256,1280]{1,0:T(8,128)(2,1)S(1)} collective-permute-done((bf16[256,1280]{1,0:T(8,128)(2,1)S(1)}, bf16[256,1280]{1,0:T(8,128)(2,1)S(1)}, u32[]{:S(2)}, u32[]{:S(2)}) %collective-permute-start.37) | collective-permute-done | bytes 655392 | tf_op jit(solution)/shard_map/ppermute | solution.py:54
  369.8 13.5 %collective-permute-done.38 = bf16[256,1280]{1,0:T(8,128)(2,1)S(1)} collective-permute-done((bf16[256,1280]{1,0:T(8,128)(2,1)S(1)}, bf16[256,1280]{1,0:T(8,128)(2,1)S(1)}, u32[]{:S(2)}, u32[]{:S(2)}) %collective-permute-start.38) | collective-permute-done | bytes 655392 | tf_op jit(solution)/shard_map/ppermute | solution.py:54
  410.0 23.2 %experts.4 = (bf16[2,256,1280]{2,1,0:T(8,128)(2,1)}, bf16[2,256,1280]{2,1,0:T(8,128)(2,1)}, f32[2,2,1,256]{3,2,1,0:T(1,128)}, bf16[2816,1280]{1,0:T(8,128)(2,1)}...) custom-call(s32[4]{0:T(128)} %pad_add_fusion.4.e_ref, ...), custom_call_target="tpu_custom_call" | custom-call | flops 9688842240 | bytes 30000000 | tf_op jit(solution)/shard_map/experts/pallas_call | solution.py:587
  436.6 22.2 %experts.5 = (bf16[2,256,1280]{2,1,0:T(8,128)(2,1)}, bf16[2,256,1280]{2,1,0:T(8,128)(2,1)}, f32[2,2,1,256]{3,2,1,0:T(1,128)}, bf16[2816,1280]{1,0:T(8,128)(2,1)}...) custom-call(s32[4]{0:T(128)} %pad_add_fusion.4.e_ref, ...), custom_call_target="tpu_custom_call", output_to_operand_aliasing={{3}: (9, {}), {4}: (10, {}), {5}: (11, {}), {6}: (12, {})} | custom-call | flops 9688842240 | bytes 30000000 | tf_op jit(solution)/shard_map/experts/pallas_call | solution.py:587
  461.8 23.5 %experts.6 = (bf16[2,256,1280]{2,1,0:T(8,128)(2,1)}, bf16[2,256,1280]{2,1,0:T(8,128)(2,1)}, f32[2,2,1,256]{3,2,1,0:T(1,128)}, bf16[2816,1280]{1,0:T(8,128)(2,1)}...) custom-call(s32[4]{0:T(128)} %pad_add_fusion.4.e_ref, ...), custom_call_target="tpu_custom_call", output_to_operand_aliasing={{3}: (7, {}), {4}: (8, {}), {5}: (9, {}), {6}: (10, {}), {7... | custom-call | flops 9688842240 | bytes 30000000 | tf_op jit(solution)/shard_map/experts/pallas_call | solution.py:587
  488.0 22.2 %experts.7 = (bf16[2,256,1280]{2,1,0:T(8,128)(2,1)}, bf16[2,256,1280]{2,1,0:T(8,128)(2,1)}, f32[2,2,1,256]{3,2,1,0:T(1,128)}, bf16[2816,1280]{1,0:T(8,128)(2,1)}...) custom-call(s32[4]{0:T(128)} %pad_add_fusion.4.e_ref, ...), custom_call_target="tpu_custom_call", output_to_operand_aliasing={{3}: (9, {}), {4}: (10, {}), {5}: (11, {}), {6}: (12, {}), ... | custom-call | flops 9688842240 | bytes 30000000 | tf_op jit(solution)/shard_map/experts/pallas_call | solution.py:587
  514.2 21.3 %convolution_convert_fusion.4 = bf16[1280,1792]{1,0:T(8,128)(2,1)} fusion(bf16[2816,1280]{1,0:T(8,128)(2,1)} %get-tuple-element.172, bf16[2816,1792]{1,0:T(8,128)(2,1)} %get-tuple-element.173), kind=kOutput, calls=%fused_computation.6 | convolution fusion | flops 12920750080 | bytes 21889024 | tf_op jit(solution)/shard_map/dot_general | solution.py:45
  535.6 8.2 convolution_convert_fusion.7
  560.1 9.8 %collective-permute-done.53 = bf16[256,1280]{1,0:T(8,128)(2,1)S(1)} collective-permute-done((bf16[256,1280]{1,0:T(8,128)(2,1)S(1)}, bf16[256,1280]{1,0:T(8,128)(2,1)S(1)}, u32[]{:S(2)}, u32[]{:S(2)}) %collective-permute-start.53) | collective-permute-done | bytes 655392 | tf_op jit(solution)/shard_map/ppermute | solution.py:54
  604.7 8.7 collective-permute-done.58
  624.0 11.7 %attend_back.4 = (f32[256,1280]{1,0:T(8,128)S(1)}, f32[2,256,1280]{2,1,0:T(8,128)S(1)}, bf16[2,256,1280]{2,1,0:T(8,128)(2,1)}) custom-call(s32[3]{0:T(128)S(1)} %pad_add_fusion.1.place_ref, bf16[256,1280]{1,0:T(8,128)(2,1)S(1)} %copy-done.43, bf16[256,1280]{1,0:T(8,128)(2,1)S(1)} %convolution_convert_fusion.8.do_ref, bf16[256,1280]{1,0:T(8,128)(2,1)S(1)} %copy-done.18, ...), custom_call_target="tpu_custom_call" | custom-call | flops 6710886400 | bytes 5242880 | tf_op jit(solution)/shard_map/attend_back/pallas_call | solution.py:459
  657.7 12.0 %attend_back.5 = (f32[256,1280]{1,0:T(8,128)S(1)}, f32[2,256,1280]{2,1,0:T(8,128)S(1)}, bf16[2,256,1280]{2,1,0:T(8,128)(2,1)}) custom-call(s32[3]{0:T(128)S(1)} %copy-done.27, bf16[256,1280]{1,0:T(8,128)(2,1)S(1)} %copy-done.44, bf16[256,1280]{1,0:T(8,128)(2,1)S(1)} %copy-done.47, bf16[256,1280]{1,0:T(8,128)(2,1)S(1)} %copy-done.18, ...), custom_call_target="tpu_custom_call" | custom-call | flops 6710886400 | bytes 5242880 | tf_op jit(solution)/shard_map/attend_back/pallas_call | solution.py:459
  671.2 11.2 %attend_back.6 = (f32[256,1280]{1,0:T(8,128)S(1)}, f32[2,256,1280]{2,1,0:T(8,128)S(1)}, bf16[2,256,1280]{2,1,0:T(8,128)(2,1)S(1)}) custom-call(s32[3]{0:T(128)S(1)} %copy-done.29, bf16[256,1280]{1,0:T(8,128)(2,1)S(1)} %copy-done.44, bf16[256,1280]{1,0:T(8,128)(2,1)S(1)} %copy-done.47, bf16[256,1280]{1,0:T(8,128)(2,1)S(1)} %copy-done.18, ...), custom_call_target="tpu_custom_call" | custom-call | flops 6710886400 | bytes 5242880 | tf_op jit(solution)/shard_map/attend_back/pallas_call | solution.py:459
  686.1 25.4 %all-to-all-done.2 = bf16[4,240,1792]{2,1,0:T(8,128)(2,1)} async-done(((bf16[4,240,1792]{2,1,0:T(8,128)(2,1)}), bf16[4,240,1792]{2,1,0:T(8,128)(2,1)}, u32[]{:S(2)}, u32[]{:S(2)}) %all-to-all-start.2) | async-done | bytes 3440672 | tf_op jit(solution)/shard_map/all_to_all | solution.py:833
  720.1 11.1 %attend_back.7 = (bf16[256,1280]{1,0:T(8,128)(2,1)S(1)}, f32[2,256,1280]{2,1,0:T(8,128)S(1)}, bf16[2,256,1280]{2,1,0:T(8,128)(2,1)}) custom-call(s32[3]{0:T(128)S(1)} %copy-done.25, bf16[256,1280]{1,0:T(8,128)(2,1)S(1)} %copy-done.45, bf16[256,1280]{1,0:T(8,128)(2,1)S(1)} %copy-done.48, bf16[256,1280]{1,0:T(8,128)(2,1)S(1)} %copy-done.19, ...), custom_call_target="tpu_custom_call" | custom-call | flops 6710886400 | bytes 5242880 | tf_op jit(solution)/shard_map/attend_back/pallas_call | solution.py:459
  773.8 10.2 %collective-permute-done.67 = bf16[2,256,1280]{2,1,0:T(8,128)(2,1)} collective-permute-done((bf16[2,256,1280]{2,1,0:T(8,128)(2,1)}, bf16[2,256,1280]{2,1,0:T(8,128)(2,1)}, u32[]{:S(2)}, u32[]{:S(2)}) %collective-permute-start.67) | collective-permute-done | bytes 1310752 | tf_op jit(solution)/shard_map/ppermute | solution.py:54
  792.2 9.3 add_convert_fusion
  814.1 29.6 %collective-permute-done.73 = bf16[2,2,40,5376]{3,2,0,1:T(8,128)(2,1)S(1)} collective-permute-done((bf16[2,2,40,5376]{3,2,0,1:T(8,128)(2,1)S(1)}, bf16[2,2,40,5376]{3,2,0,1:T(8,128)(2,1)S(1)}, u32[]{:S(2)}, u32[]{:S(2)}) %collective-permute-start.73) | collective-permute-done | bytes 1720352 | tf_op jit(solution)/shard_map/ppermute | solution.py:54
  865.1 15.0 %collective-permute-done.79 = bf16[2,40,5376]{2,1,0:T(8,128)(2,1)S(1)} collective-permute-done((bf16[2,40,5376]{2,1,0:T(8,128)(2,1)S(1)}, bf16[2,40,5376]{2,1,0:T(8,128)(2,1)S(1)}, u32[]{:S(2)}, u32[]{:S(2)}) %collective-permute-start.79) | collective-permute-done | bytes 860192 | tf_op jit(solution)/shard_map/ppermute | solution.py:54
  903.4 13.9 %collective-permute-done.77 = bf16[256,1280]{1,0:T(8,128)(2,1)S(1)} collective-permute-done((bf16[256,1280]{1,0:T(8,128)(2,1)S(1)}, bf16[256,1280]{1,0:T(8,128)(2,1)S(1)}, u32[]{:S(2)}, u32[]{:S(2)}) %collective-permute-start.77) | collective-permute-done | bytes 655392 | tf_op jit(solution)/shard_map/ppermute | solution.py:54
  929.9 17.8 %collective-permute-done.83 = bf16[40,5376]{1,0:T(8,128)(2,1)S(1)} collective-permute-done((bf16[40,5376]{1,0:T(8,128)(2,1)S(1)}, bf16[40,5376]{1,0:T(8,128)(2,1)S(1)}, u32[]{:S(2)}, u32[]{:S(2)}) %collective-permute-start.83) | collective-permute-done | bytes 430112 | tf_op jit(solution)/shard_map/ppermute | solution.py:54
  (723 shorter events, 476.5 us)
Async XLA Ops:
  67.0 59.8 %collective-permute-start.11 = (bf16[8,40,3968]{2,1,0:T(8,128)(2,1)S(1)}, bf16[8,40,3968]{2,1,0:T(8,128)(2,1)S(1)}, u32[]{:S(2)}, u32[]{:S(2)}) collective-permute-start(bf16[8,40,3968]{2,1,0:T(8,128)(2,1)S(1)} %pad_maximum_fusion.10.refs_0_), channel_id=1, source_target_pairs={{0,4},{4,0},{1,5},{5,1},{2,6},{6,2},{3,7},{7,3},{8,12},{12,8},{9,1... | collective-permute-start | bytes 7618568 | tf_op jit(solution)/shard_map/ppermute | solution.py:54
  88.9 37.9 %collective-permute-start.14 = (bf16[8,40,3968]{2,1,0:T(8,128)(2,1)S(1)}, bf16[8,40,3968]{2,1,0:T(8,128)(2,1)S(1)}, u32[]{:S(2)}, u32[]{:S(2)}) collective-permute-start(bf16[8,40,3968]{2,1,0:T(8,128)(2,1)S(1)} %pad_maximum_fusion.11.refs_2_), channel_id=1, source_target_pairs={{0,4},{4,0},{1,5},{5,1},{2,6},{6,2},{3,7},{7,3},{8,12},{12,8},{9,1... | collective-permute-start | bytes 7618568 | tf_op jit(solution)/shard_map/ppermute | solution.py:54
  109.9 39.5 %collective-permute-start.26 = (bf16[2,2,40,4096]{3,2,1,0:T(8,128)(2,1)}, bf16[2,2,40,4096]{3,2,1,0:T(8,128)(2,1)}, u32[]{:S(2)}, u32[]{:S(2)}) collective-permute-start(bf16[2,2,40,4096]{3,2,1,0:T(8,128)(2,1)} %pad_maximum_fusion.14), channel_id=1, source_target_pairs={{0,1},{1,0},{2,3},{3,2},{4,5},{5,4},{6,7},{7,6},{8,9},{9,8},{10,11... | collective-permute-start | bytes 3932168 | tf_op jit(solution)/shard_map/ppermute | solution.py:54
  112.8 36.7 %collective-permute-start.25 = (bf16[2,2,40,4096]{3,2,1,0:T(8,128)(2,1)}, bf16[2,2,40,4096]{3,2,1,0:T(8,128)(2,1)}, u32[]{:S(2)}, u32[]{:S(2)}) collective-permute-start(bf16[2,2,40,4096]{3,2,1,0:T(8,128)(2,1)} %pad_maximum_fusion.13), channel_id=1, source_target_pairs={{0,2},{2,0},{1,3},{3,1},{4,6},{6,4},{5,7},{7,5},{8,10},{10,8},{9,1... | collective-permute-start | bytes 3932168 | tf_op jit(solution)/shard_map/ppermute | solution.py:54
  153.7 35.4 %collective-permute-start.24 = (bf16[2,256,1280]{2,1,0:T(8,128)(2,1)S(1)}, bf16[2,256,1280]{2,1,0:T(8,128)(2,1)S(1)}, u32[]{:S(2)}, u32[]{:S(2)}) collective-permute-start(bf16[2,256,1280]{2,1,0:T(8,128)(2,1)S(1)} %get-tuple-element.126.refs_0_), channel_id=1, source_target_pairs={{0,4},{4,0},{1,5},{5,1},{2,6},{6,2},{3,7},{7,3},{8,12},{12,8},{9,1... | collective-permute-start | bytes 3932168 | tf_op jit(solution)/shard_map/ppermute | solution.py:54
  182.7 58.5 %collective-permute-start.33 = (bf16[2,2,256,1280]{3,2,1,0:T(8,128)(2,1)}, bf16[2,2,256,1280]{3,2,1,0:T(8,128)(2,1)}, u32[]{:S(2)}, u32[]{:S(2)}) collective-permute-start(bf16[2,2,256,1280]{3,2,1,0:T(8,128)(2,1)} %pad_maximum_fusion.5.refs_2_), channel_id=1, source_target_pairs={{0,1},{1,0},{2,3},{3,2},{4,5},{5,4},{6,7},{7,6},{8,9},{9,8},{10,11... | collective-permute-start | bytes 7864328 | tf_op jit(solution)/shard_map/ppermute | solution.py:54
  188.6 58.3 %collective-permute-start.32 = (bf16[2,2,256,1280]{3,2,1,0:T(8,128)(2,1)}, bf16[2,2,256,1280]{3,2,1,0:T(8,128)(2,1)}, u32[]{:S(2)}, u32[]{:S(2)}) collective-permute-start(bf16[2,2,256,1280]{3,2,1,0:T(8,128)(2,1)} %get-tuple-element.293), channel_id=1, source_target_pairs={{0,2},{2,0},{1,3},{3,1},{4,6},{6,4},{5,7},{7,5},{8,10},{10,8},{9,1... | collective-permute-start | bytes 7864328 | tf_op jit(solution)/shard_map/ppermute | solution.py:54
  214.8 39.4 %collective-permute-start.35 = (bf16[8,40,4096]{2,1,0:T(8,128)(2,1)}, bf16[8,40,4096]{2,1,0:T(8,128)(2,1)}, u32[]{:S(2)}, u32[]{:S(2)}) collective-permute-start(bf16[8,40,4096]{2,1,0:T(8,128)(2,1)} %pad_maximum_fusion.6.refs_0_), channel_id=1, source_target_pairs={{0,4},{4,0},{1,5},{5,1},{2,6},{6,2},{3,7},{7,3},{8,12},{12,8},{9,1... | collective-permute-start | bytes 7864328 | tf_op jit(solution)/shard_map/ppermute | solution.py:54
  218.8 35.4 %collective-permute-start.36 = (bf16[8,40,4096]{2,1,0:T(8,128)(2,1)}, bf16[8,40,4096]{2,1,0:T(8,128)(2,1)}, u32[]{:S(2)}, u32[]{:S(2)}) collective-permute-start(bf16[8,40,4096]{2,1,0:T(8,128)(2,1)} %pad_maximum_fusion.7.refs_2_), channel_id=1, source_target_pairs={{0,4},{4,0},{1,5},{5,1},{2,6},{6,2},{3,7},{7,3},{8,12},{12,8},{9,1... | collective-permute-start | bytes 7864328 | tf_op jit(solution)/shard_map/ppermute | solution.py:54
  250.2 81.8 %all-to-all-start = ((bf16[4,240,1792]{2,1,0:T(8,128)(2,1)}), bf16[4,240,1792]{2,1,0:T(8,128)(2,1)S(1)}, u32[]{:S(2)}, u32[]{:S(2)}) async-start(bf16[4,240,1792]{2,1,0:T(8,128)(2,1)} %pad_maximum_fusion.1), calls=%async_computation | async-start | bytes 6881280 | tf_op jit(solution)/shard_map/all_to_all | solution.py:750
  332.0 57.1 %collective-permute-start.42 = (bf16[4,240,1792]{2,1,0:T(8,128)(2,1)S(1)}, bf16[4,240,1792]{2,1,0:T(8,128)(2,1)}, u32[]{:S(2)}, u32[]{:S(2)}) collective-permute-start(bf16[4,240,1792]{2,1,0:T(8,128)(2,1)S(1)} %all-to-all-done.refs_0_), channel_id=1, source_target_pairs={{0,4},{4,0},{1,5},{5,1},{2,6},{6,2},{3,7},{7,3},{8,12},{12,8},{9,1... | collective-permute-start | bytes 10321928 | tf_op jit(solution)/shard_map/ppermute | solution.py:54
  395.7 40.9 %collective-permute-start.48 = (bf16[2,256,1280]{2,1,0:T(8,128)(2,1)}, bf16[2,256,1280]{2,1,0:T(8,128)(2,1)}, u32[]{:S(2)}, u32[]{:S(2)}) collective-permute-start(bf16[2,256,1280]{2,1,0:T(8,128)(2,1)} %pad_maximum_fusion.20.refs_0_), channel_id=1, source_target_pairs={{0,1},{1,0},{2,3},{3,2},{4,5},{5,4},{6,7},{7,6},{8,9},{9,8},{10,11... | collective-permute-start | bytes 3932168 | tf_op jit(solution)/shard_map/ppermute | solution.py:54
  408.5 51.6 %collective-permute-start.46 = (bf16[2,256,1280]{2,1,0:T(8,128)(2,1)}, bf16[2,256,1280]{2,1,0:T(8,128)(2,1)S(1)}, u32[]{:S(2)}, u32[]{:S(2)}) collective-permute-start(bf16[2,256,1280]{2,1,0:T(8,128)(2,1)} %pad_maximum_fusion.19), channel_id=1, source_target_pairs={{0,2},{2,0},{1,3},{3,1},{4,6},{6,4},{5,7},{7,5},{8,10},{10,8},{9,1... | collective-permute-start | bytes 3932168 | tf_op jit(solution)/shard_map/ppermute | solution.py:54
  434.0 140.1 %collective-permute-start.59 = (bf16[2,256,1280]{2,1,0:T(8,128)(2,1)}, bf16[2,256,1280]{2,1,0:T(8,128)(2,1)}, u32[]{:S(2)}, u32[]{:S(2)}) collective-permute-start(bf16[2,256,1280]{2,1,0:T(8,128)(2,1)} %get-tuple-element.180), channel_id=1, source_target_pairs={{0,2},{2,0},{1,3},{3,1},{4,6},{6,4},{5,7},{7,5},{8,10},{10,8},{9,1... | collective-permute-start | bytes 3932168 | tf_op jit(solution)/shard_map/ppermute | solution.py:54
  435.7 51.2 %collective-permute-start.44 = (bf16[2,256,1280]{2,1,0:T(8,128)(2,1)S(1)}, bf16[2,256,1280]{2,1,0:T(8,128)(2,1)S(1)}, u32[]{:S(2)}, u32[]{:S(2)}) collective-permute-start(bf16[2,256,1280]{2,1,0:T(8,128)(2,1)S(1)} %pad_maximum_fusion.18.refs_0_), channel_id=1, source_target_pairs={{0,1},{1,0},{2,3},{3,2},{4,5},{5,4},{6,7},{7,6},{8,9},{9,8},{10,11... | collective-permute-start | bytes 3932168 | tf_op jit(solution)/shard_map/ppermute | solution.py:54
  458.8 52.0 %collective-permute-start.49 = (bf16[2,256,1280]{2,1,0:T(8,128)(2,1)}, bf16[2,256,1280]{2,1,0:T(8,128)(2,1)S(1)}, u32[]{:S(2)}, u32[]{:S(2)}) collective-permute-start(bf16[2,256,1280]{2,1,0:T(8,128)(2,1)} %get-tuple-element.167), channel_id=1, source_target_pairs={{0,1},{1,0},{2,3},{3,2},{4,5},{5,4},{6,7},{7,6},{8,9},{9,8},{10,11... | collective-permute-start | bytes 3932168 | tf_op jit(solution)/shard_map/ppermute | solution.py:54
  485.3 65.4 %collective-permute-start.52 = (bf16[2,256,1280]{2,1,0:T(8,128)(2,1)}, bf16[2,256,1280]{2,1,0:T(8,128)(2,1)}, u32[]{:S(2)}, u32[]{:S(2)}) collective-permute-start(bf16[2,256,1280]{2,1,0:T(8,128)(2,1)} %get-tuple-element.169), channel_id=1, source_target_pairs={{0,2},{2,0},{1,3},{3,1},{4,6},{6,4},{5,7},{7,5},{8,10},{10,8},{9,1... | collective-permute-start | bytes 3932168 | tf_op jit(solution)/shard_map/ppermute | solution.py:54
  510.2 46.1 %collective-permute-start.56 = (bf16[2,256,1280]{2,1,0:T(8,128)(2,1)}, bf16[2,256,1280]{2,1,0:T(8,128)(2,1)}, u32[]{:S(2)}, u32[]{:S(2)}) collective-permute-start(bf16[2,256,1280]{2,1,0:T(8,128)(2,1)} %get-tuple-element.178), channel_id=1, source_target_pairs={{0,1},{1,0},{2,3},{3,2},{4,5},{5,4},{6,7},{7,6},{8,9},{9,8},{10,11... | collective-permute-start | bytes 3932168 | tf_op jit(solution)/shard_map/ppermute | solution.py:54
  513.5 41.5 %collective-permute-start.50 = (bf16[256,1280]{1,0:T(8,128)(2,1)}, bf16[256,1280]{1,0:T(8,128)(2,1)}, u32[]{:S(2)}, u32[]{:S(2)}) collective-permute-start(bf16[256,1280]{1,0:T(8,128)(2,1)} %fusion.54), channel_id=1, source_target_pairs={{0,2},{2,0},{1,3},{3,1},{4,6},{6,4},{5,7},{7,5},{8,10},{10,8},{9,1... | collective-permute-start | bytes 1966088 | tf_op jit(solution)/shard_map/ppermute | solution.py:54
  599.3 112.3 %all-to-all-start.2 = ((bf16[4,240,1792]{2,1,0:T(8,128)(2,1)}), bf16[4,240,1792]{2,1,0:T(8,128)(2,1)}, u32[]{:S(2)}, u32[]{:S(2)}) async-start(bf16[4,240,1792]{2,1,0:T(8,128)(2,1)} %add_convert_fusion.1), calls=%async_computation.2 | async-start | bytes 6881280 | tf_op jit(solution)/shard_map/all_to_all | solution.py:833
  646.6 104.6 %collective-permute-start.61 = (bf16[2,2,256,1280]{3,2,0,1:T(8,128)(2,1)}, bf16[2,2,256,1280]{3,2,0,1:T(8,128)(2,1)}, u32[]{:S(2)}, u32[]{:S(2)}) collective-permute-start(bf16[2,2,256,1280]{3,2,0,1:T(8,128)(2,1)} %copy.164), channel_id=1, source_target_pairs={{0,1},{1,0},{2,3},{3,2},{4,5},{5,4},{6,7},{7,6},{8,9},{9,8},{10,11... | collective-permute-start | bytes 7864328 | tf_op jit(solution)/shard_map/ppermute | solution.py:54
  649.1 107.5 %collective-permute-start.75 = (bf16[2,2,256,1280]{3,2,0,1:T(8,128)(2,1)}, bf16[2,2,256,1280]{3,2,0,1:T(8,128)(2,1)}, u32[]{:S(2)}, u32[]{:S(2)}) collective-permute-start(bf16[2,2,256,1280]{3,2,0,1:T(8,128)(2,1)} %copy.183), channel_id=1, source_target_pairs={{0,2},{2,0},{1,3},{3,1},{4,6},{6,4},{5,7},{7,5},{8,10},{10,8},{9,1... | collective-permute-start | bytes 7864328 | tf_op jit(solution)/shard_map/ppermute | solution.py:54
  657.2 89.9 %collective-permute-start.65 = (bf16[2,256,1280]{2,1,0:T(8,128)(2,1)}, bf16[2,256,1280]{2,1,0:T(8,128)(2,1)}, u32[]{:S(2)}, u32[]{:S(2)}) collective-permute-start(bf16[2,256,1280]{2,1,0:T(8,128)(2,1)} %add_convert_fusion.5), channel_id=1, source_target_pairs={{0,8},{8,16},{16,24},{24,0},{1,9},{9,17},{17,25},{25,1},{2,10},{10... | collective-permute-start | bytes 3932168 | tf_op jit(solution)/shard_map/ppermute | solution.py:54
  671.2 75.4 %collective-permute-start.66 = (bf16[2,256,1280]{2,1,0:T(8,128)(2,1)}, bf16[2,256,1280]{2,1,0:T(8,128)(2,1)}, u32[]{:S(2)}, u32[]{:S(2)}) collective-permute-start(bf16[2,256,1280]{2,1,0:T(8,128)(2,1)} %get-tuple-element.194), channel_id=1, source_target_pairs={{0,4},{4,0},{1,5},{5,1},{2,6},{6,2},{3,7},{7,3},{8,12},{12,8},{9,1... | collective-permute-start | bytes 3932168 | tf_op jit(solution)/shard_map/ppermute | solution.py:54
  746.5 45.6 %collective-permute-start.71 = (bf16[4,2,2,40,5376]{4,3,0,1,2:T(8,128)(2,1)}, bf16[4,2,2,40,5376]{4,3,0,1,2:T(8,128)(2,1)}, u32[]{:S(2)}, u32[]{:S(2)}) collective-permute-start(bf16[4,2,2,40,5376]{4,3,0,1,2:T(8,128)(2,1)} %get-tuple-element.311), channel_id=1, source_target_pairs={{0,4},{4,0},{1,5},{5,1},{2,6},{6,2},{3,7},{7,3},{8,12},{12,8},{9,1... | collective-permute-start | bytes 20643848 | tf_op jit(solution)/shard_map/ppermute | solution.py:54
  762.9 43.0 %collective-permute-start.76 = (bf16[2,256,1280]{2,1,0:T(8,128)(2,1)}, bf16[2,256,1280]{2,1,0:T(8,128)(2,1)}, u32[]{:S(2)}, u32[]{:S(2)}) collective-permute-start(bf16[2,256,1280]{2,1,0:T(8,128)(2,1)} %fusion.36), channel_id=1, source_target_pairs={{0,1},{1,0},{2,3},{3,2},{4,5},{5,4},{6,7},{7,6},{8,9},{9,8},{10,11... | collective-permute-start | bytes 3932168 | tf_op jit(solution)/shard_map/ppermute | solution.py:54
  773.8 37.3 %collective-permute-start.70 = (bf16[2,256,1280]{2,1,0:T(8,128)(2,1)}, bf16[2,256,1280]{2,1,0:T(8,128)(2,1)}, u32[]{:S(2)}, u32[]{:S(2)}) collective-permute-start(bf16[2,256,1280]{2,1,0:T(8,128)(2,1)} %get-tuple-element.201), channel_id=1, source_target_pairs={{0,4},{4,0},{1,5},{5,1},{2,6},{6,2},{3,7},{7,3},{8,12},{12,8},{9,1... | collective-permute-start | bytes 3932168 | tf_op jit(solution)/shard_map/ppermute | solution.py:54
  787.3 62.6 %collective-permute-start.69 = (bf16[2,256,1280]{2,1,0:T(8,128)(2,1)}, bf16[2,256,1280]{2,1,0:T(8,128)(2,1)}, u32[]{:S(2)}, u32[]{:S(2)}) collective-permute-start(bf16[2,256,1280]{2,1,0:T(8,128)(2,1)} %add_convert_fusion.3), channel_id=1, source_target_pairs={{0,8},{8,16},{16,24},{24,0},{1,9},{9,17},{17,25},{25,1},{2,10},{10... | collective-permute-start | bytes 3932168 | tf_op jit(solution)/shard_map/ppermute | solution.py:54
  792.0 100.5 %collective-permute-start.63 = (bf16[256,1280]{1,0:T(8,128)(2,1)}, bf16[256,1280]{1,0:T(8,128)(2,1)}, u32[]{:S(2)}, u32[]{:S(2)}) collective-permute-start(bf16[256,1280]{1,0:T(8,128)(2,1)} %fusion.58), channel_id=1, source_target_pairs={{0,8},{8,16},{16,24},{24,0},{1,9},{9,17},{17,25},{25,1},{2,10},{10... | collective-permute-start | bytes 1966088 | tf_op jit(solution)/shard_map/ppermute | solution.py:54
  805.0 38.7 %collective-permute-start.73 = (bf16[2,2,40,5376]{3,2,0,1:T(8,128)(2,1)S(1)}, bf16[2,2,40,5376]{3,2,0,1:T(8,128)(2,1)S(1)}, u32[]{:S(2)}, u32[]{:S(2)}) collective-permute-start(bf16[2,2,40,5376]{3,2,0,1:T(8,128)(2,1)S(1)} %dynamic-slice_bitcast_fusion.2), channel_id=1, source_target_pairs={{0,1},{1,0},{2,3},{3,2},{4,5},{5,4},{6,7},{7,6},{8,9},{9,8},{10,11... | collective-permute-start | bytes 5160968 | tf_op jit(solution)/shard_map/ppermute | solution.py:54
  809.8 38.4 %collective-permute-start.72 = (bf16[2,2,40,5376]{3,2,0,1:T(8,128)(2,1)S(1)}, bf16[2,2,40,5376]{3,2,0,1:T(8,128)(2,1)S(1)}, u32[]{:S(2)}, u32[]{:S(2)}) collective-permute-start(bf16[2,2,40,5376]{3,2,0,1:T(8,128)(2,1)S(1)} %dynamic-slice_bitcast_fusion.3), channel_id=1, source_target_pairs={{0,2},{2,0},{1,3},{3,1},{4,6},{6,4},{5,7},{7,5},{8,10},{10,8},{9,1... | collective-permute-start | bytes 5160968 | tf_op jit(solution)/shard_map/ppermute | solution.py:54
  918.2 41.4 %collective-permute-start.78 = (bf16[256,1280]{1,0:T(8,128)(2,1)}, bf16[256,1280]{1,0:T(8,128)(2,1)}, u32[]{:S(2)}, u32[]{:S(2)}) collective-permute-start(bf16[256,1280]{1,0:T(8,128)(2,1)} %fusion.39), channel_id=1, source_target_pairs={{0,8},{8,16},{16,24},{24,0},{1,9},{9,17},{17,25},{25,1},{2,10},{10... | collective-permute-start | bytes 1966088 | tf_op jit(solution)/shard_map/ppermute | solution.py:54
  (231 other events, 2505.7 us)

commit v9 on v6

--- a/solution.py
+++ b/solution.py
@@ -93,37 +93,39 @@
 
 
 ORDER = {
-    "g": "f3",
-    "mid0": "r1",
+    "rest": "f1",
+    "g": "r3",
+    "mid1": "r2",
     "core2": "r3",
     "rs1": "fp",
-    "norm": "rs g2",
+    "norm": "g2",
     "gs1": "rp",
     "arr1": "g3 rp",
-    "arr2": "s rp",
+    "arr2": "gs",
     "arr3": "s gf",
-    "wa": "a3",
-    "wc": "cs",
+    "wa": "q",
+    "wc": "m",
     "c1b": "w",
     "c2b": "k0",
-    "c3a": "k0",
+    "c3a": "w",
     "c3b": "k0",
-    "gu": "s2",
-    "dn": "gu",
-    "t2": "gu dn",
-    "ea": "t",
+    "gu": "s1",
+    "dn": "s1",
+    "t2": "er",
     "sh": "k2",
-    "B2": "er",
+    "B1": "m",
     "B3": "er",
     "y1": "rg",
-    "y2": "q",
-    "fin": "late ys",
-    "y3": "b",
-    "late2": "b",
+    "fin": "late",
+    "kv1": "ys",
     "kv2": "l",
-    "yz2": "kv",
-    "yz4": "l",
-    "late3": "f",
+    "yz3": "kv",
+    "yz4": "z",
+    "late3": "kv",
+    "cz2": "w",
+    "cz3": "cp",
+    "xg": "m",
+    "dn0": "kv",
 }
 
 

time: 1020 us -> 978 us (0.959)
  waiting for transfers between devices: 420 us -> 356 us
    all_to_all x1, waiting for transfers between devices: 55.2 us -> 13.6 us  [body(): lax.all_to_all(expert_rows, 'q', split_axis=0, concat_axis=0, tiled=True)]
    all_to_all x1, waiting for transfers between devices: 30.6 us -> 0.01 us  [body(): both = lax.all_to_all(both, 'q', split_axis=0, concat_axis=0, tiled=True)]
    unnamed x314 -> x328, local copies, waits for them, and re-layouts: 37.3 us -> 57.5 us
    ppermute x88, waiting for transfers between devices: 322 us -> 336 us  [shift(): return lax.ppermute(value, axis, [(i, (i + 1) % n) for i in range(n)])]
  transfers between devices with their start and end apart: 94 -> 94, of which waited for: 50 -> 41; matrix products, arithmetic and copies ran while one was open for 25% -> 27% of each run, Pallas kernels for 19% -> 21%
where the time goes in v9:
time: 978 us; the launch traced here: 967 us
  waiting for transfers between devices  356 us (36%)
  Pallas kernels  203 us (21%)
  local copies, waits for them, and re-layouts  123 us (13%)
  other arithmetic  120 us (12%)
  starting transfers between devices  91.1 us (9%)
  matrix products  70.4 us (7%)
    ppermute x88, waiting for transfers between devices, shift(): return lax.ppermute(value, axis, [(i, (i + 1) % n) for i in range(n)])  336 us
    pallas_call x4, Pallas kernels, expert_chunk(): pl.pallas_call(functools.partial(expert_kernel, slots, na, nb, even, len(...  91.5 us
    ppermute x88, starting transfers between devices, shift(): return lax.ppermute(value, axis, [(i, (i + 1) % n) for i in range(n)])  70.8 us
    dot_general x21, matrix products, dot(): return lax.dot_general(a, b, (dims, ((), ())), preferred_element_type=F32)  70.4 us
    unnamed x328, local copies, waits for them, and re-layouts  57.5 us
    pallas_call x4, Pallas kernels, attend_back_chunk(): pl.pallas_call(functools.partial(attend_back_kernel, n_ctx, n, first, las...  46 us
    pallas_call x4, Pallas kernels, attend_chunk(): pl.pallas_call(functools.partial(attend_kernel, n_ctx, n, first, last), g...  37.4 us
  transfers between devices with their start and end apart: 94, of which 41 were waited for; matrix products, arithmetic and copies ran while one was open for 27% of the time, Pallas kernels for 21%

profile of v9, /device:TPU:0, one launch (start us, length us, event | category | flops | bytes accessed | tf_op | source)
XLA Modules:
  0.0 966.9 jit_solution(9005635103740334158)
XLA Ops:
  6.3 8.8 collective-permute-done
  51.6 11.3 %collective-permute-done.9 = bf16[2,40,3968]{2,1,0:T(8,128)(2,1)S(1)} collective-permute-done((bf16[2,40,3968]{2,1,0:T(8,128)(2,1)S(1)}, bf16[2,40,3968]{2,1,0:T(8,128)(2,1)S(1)}, u32[]{:S(2)}, u32[]{:S(2)}) %collective-permute-start.9) | collective-permute-done | bytes 634912 | tf_op jit(solution)/shard_map/ppermute | solution.py:54
  65.1 12.0 %collective-permute-done.16 = bf16[40,4096]{1,0:T(8,128)(2,1)S(1)} collective-permute-done((bf16[40,4096]{1,0:T(8,128)(2,1)S(1)}, bf16[40,4096]{1,0:T(8,128)(2,1)S(1)}, u32[]{:S(2)}, u32[]{:S(2)}) %collective-permute-start.16) | collective-permute-done | bytes 327712 | tf_op jit(solution)/shard_map/ppermute | solution.py:54
  93.3 17.3 %collective-permute-done.18 = bf16[256,1280]{1,0:T(8,128)(2,1)} collective-permute-done((bf16[256,1280]{1,0:T(8,128)(2,1)S(1)}, bf16[256,1280]{1,0:T(8,128)(2,1)}, u32[]{:S(2)}, u32[]{:S(2)}) %collective-permute-start.18) | collective-permute-done | bytes 655392 | tf_op jit(solution)/shard_map/ppermute | solution.py:54
  126.0 9.2 project.1
  148.2 18.9 %collective-permute-done.19.refs_0_ = bf16[2,256,1280]{2,1,0:T(8,128)(2,1)} collective-permute-done((bf16[2,256,1280]{2,1,0:T(8,128)(2,1)}, bf16[2,256,1280]{2,1,0:T(8,128)(2,1)}, u32[]{:S(2)}, u32[]{:S(2)}) %collective-permute-start.19) | collective-permute-done | bytes 1310752 | tf_op jit(solution)/shard_map/ppermute | solution.py:54
  187.0 14.1 %collective-permute-done.25.refs_0_ = bf16[2,256,1280]{2,1,0:T(8,128)(2,1)} collective-permute-done((bf16[2,256,1280]{2,1,0:T(8,128)(2,1)}, bf16[2,256,1280]{2,1,0:T(8,128)(2,1)}, u32[]{:S(2)}, u32[]{:S(2)}) %collective-permute-start.25) | collective-permute-done | bytes 1310752 | tf_op jit(solution)/shard_map/ppermute | solution.py:54
  212.2 8.5 attend.4
  220.8 9.2 attend.5
  230.0 9.2 attend.6
  245.1 36.6 %collective-permute-done.28.refs_0_ = bf16[2,256,1280]{2,1,0:T(8,128)(2,1)} collective-permute-done((bf16[2,256,1280]{2,1,0:T(8,128)(2,1)}, bf16[2,256,1280]{2,1,0:T(8,128)(2,1)}, u32[]{:S(2)}, u32[]{:S(2)}) %collective-permute-start.28) | collective-permute-done | bytes 1310752 | tf_op jit(solution)/shard_map/ppermute | solution.py:54
  289.2 10.5 %attend.7 = (bf16[256,1280]{1,0:T(8,128)(2,1)S(1)}, f32[10,256,128]{2,1,0:T(8,128)S(1)}) custom-call(s32[3]{0:T(128)S(1)} %pad_add_fusion.place_ref, bf16[256,1280]{1,0:T(8,128)(2,1)S(1)} %copy-done.42, bf16[2,256,1280]{2,1,0:T(8,128)(2,1)} %collective-permute-done.28.refs_0_, bf16[2,256,1280]{2,1,0:T(8,128)(2,1)} %collective-permute-done.34.refs_1_, ...), custom_call_target="tpu_custom_call" | custom-call | flops 2684354560 | bytes 2621440 | tf_op jit(solution)/shard_map/attend/pallas_call | solution.py:404
  306.3 14.2 %collective-permute-start.37 = (bf16[256,1280]{1,0:T(8,128)(2,1)S(1)}, bf16[256,1280]{1,0:T(8,128)(2,1)}, u32[]{:S(2)}, u32[]{:S(2)}) collective-permute-start(bf16[256,1280]{1,0:T(8,128)(2,1)S(1)} %multiply_convert_fusion), channel_id=1, source_target_pairs={{0,8},{8,16},{16,24},{24,0},{1,9},{9,17},{17,25},{25,1},{2,10},{10... | collective-permute-start | bytes 1966088 | tf_op jit(solution)/shard_map/ppermute | solution.py:54
  322.0 12.7 %collective-permute-done.37 = bf16[256,1280]{1,0:T(8,128)(2,1)} collective-permute-done((bf16[256,1280]{1,0:T(8,128)(2,1)S(1)}, bf16[256,1280]{1,0:T(8,128)(2,1)}, u32[]{:S(2)}, u32[]{:S(2)}) %collective-permute-start.37) | collective-permute-done | bytes 655392 | tf_op jit(solution)/shard_map/ppermute | solution.py:54
  345.2 8.4 collective-permute-done.38
  360.3 22.6 %collective-permute-done.44 = bf16[256,1280]{1,0:T(8,128)(2,1)} collective-permute-done((bf16[256,1280]{1,0:T(8,128)(2,1)}, bf16[256,1280]{1,0:T(8,128)(2,1)}, u32[]{:S(2)}, u32[]{:S(2)}) %collective-permute-start.44) | collective-permute-done | bytes 655392 | tf_op jit(solution)/shard_map/ppermute | solution.py:54
  405.3 23.4 %experts.4 = (bf16[2,256,1280]{2,1,0:T(8,128)(2,1)}, bf16[2,256,1280]{2,1,0:T(8,128)(2,1)}, f32[2,2,1,256]{3,2,1,0:T(1,128)}, bf16[2816,1280]{1,0:T(8,128)(2,1)}...) custom-call(s32[4]{0:T(128)} %pad_add_fusion.4.e_ref, ...), custom_call_target="tpu_custom_call" | custom-call | flops 9688842240 | bytes 30000000 | tf_op jit(solution)/shard_map/experts/pallas_call | solution.py:593
  438.5 22.2 %experts.5 = (bf16[2,256,1280]{2,1,0:T(8,128)(2,1)}, bf16[2,256,1280]{2,1,0:T(8,128)(2,1)}, f32[2,2,1,256]{3,2,1,0:T(1,128)}, bf16[2816,1280]{1,0:T(8,128)(2,1)}...) custom-call(s32[4]{0:T(128)} %pad_add_fusion.4.e_ref, ...), custom_call_target="tpu_custom_call", output_to_operand_aliasing={{3}: (9, {}), {4}: (10, {}), {5}: (11, {}), {6}: (12, {})} | custom-call | flops 9688842240 | bytes 30000000 | tf_op jit(solution)/shard_map/experts/pallas_call | solution.py:593
  464.6 23.9 %experts.6 = (bf16[2,256,1280]{2,1,0:T(8,128)(2,1)}, bf16[2,256,1280]{2,1,0:T(8,128)(2,1)}, f32[2,2,1,256]{3,2,1,0:T(1,128)}, bf16[2816,1280]{1,0:T(8,128)(2,1)}...) custom-call(s32[4]{0:T(128)} %pad_add_fusion.4.e_ref, ...), custom_call_target="tpu_custom_call", output_to_operand_aliasing={{3}: (7, {}), {4}: (8, {}), {5}: (9, {}), {6}: (10, {}), {7... | custom-call | flops 9688842240 | bytes 30000000 | tf_op jit(solution)/shard_map/experts/pallas_call | solution.py:593
  503.9 22.1 %experts.7 = (bf16[2,256,1280]{2,1,0:T(8,128)(2,1)}, bf16[2,256,1280]{2,1,0:T(8,128)(2,1)}, f32[2,2,1,256]{3,2,1,0:T(1,128)}, bf16[2816,1280]{1,0:T(8,128)(2,1)}...) custom-call(s32[4]{0:T(128)} %pad_add_fusion.4.e_ref, ...), custom_call_target="tpu_custom_call", output_to_operand_aliasing={{3}: (9, {}), {4}: (10, {}), {5}: (11, {}), {6}: (12, {}), ... | custom-call | flops 9688842240 | bytes 30000000 | tf_op jit(solution)/shard_map/experts/pallas_call | solution.py:593
  531.1 20.3 %convolution_convert_fusion.4 = bf16[1280,1792]{1,0:T(8,128)(2,1)} fusion(bf16[2816,1280]{1,0:T(8,128)(2,1)} %get-tuple-element.175, bf16[2816,1792]{1,0:T(8,128)(2,1)} %get-tuple-element.176), kind=kOutput, calls=%fused_computation.6 | convolution fusion | flops 12920750080 | bytes 21889024 | tf_op jit(solution)/shard_map/dot_general | solution.py:45
  551.5 8.2 convolution_convert_fusion.7
  618.7 11.4 %collective-permute-done.58 = bf16[256,1280]{1,0:T(8,128)(2,1)} collective-permute-done((bf16[256,1280]{1,0:T(8,128)(2,1)}, bf16[256,1280]{1,0:T(8,128)(2,1)}, u32[]{:S(2)}, u32[]{:S(2)}) %collective-permute-start.58) | collective-permute-done | bytes 655392 | tf_op jit(solution)/shard_map/ppermute | solution.py:54
  641.0 11.5 %attend_back.4 = (f32[256,1280]{1,0:T(8,128)S(1)}, f32[2,256,1280]{2,1,0:T(8,128)S(1)}, bf16[2,256,1280]{2,1,0:T(8,128)(2,1)}) custom-call(s32[3]{0:T(128)S(1)} %pad_add_fusion.2.place_ref, bf16[256,1280]{1,0:T(8,128)(2,1)S(1)} %copy-done.43, bf16[256,1280]{1,0:T(8,128)(2,1)S(1)} %convolution_convert_fusion.8.do_ref, bf16[256,1280]{1,0:T(8,128)(2,1)S(1)} %copy-done.16, ...), custom_call_target="tpu_custom_call" | custom-call | flops 6710886400 | bytes 5242880 | tf_op jit(solution)/shard_map/attend_back/pallas_call | solution.py:465
  686.4 11.6 %attend_back.5 = (f32[256,1280]{1,0:T(8,128)S(1)}, f32[2,256,1280]{2,1,0:T(8,128)S(1)}, bf16[2,256,1280]{2,1,0:T(8,128)(2,1)}) custom-call(s32[3]{0:T(128)S(1)} %copy-done.27, bf16[256,1280]{1,0:T(8,128)(2,1)S(1)} %copy-done.44, bf16[256,1280]{1,0:T(8,128)(2,1)S(1)} %copy-done.47, bf16[256,1280]{1,0:T(8,128)(2,1)S(1)} %copy-done.16, ...), custom_call_target="tpu_custom_call" | custom-call | flops 6710886400 | bytes 5242880 | tf_op jit(solution)/shard_map/attend_back/pallas_call | solution.py:465
  699.8 11.7 %attend_back.6 = (f32[256,1280]{1,0:T(8,128)S(1)}, f32[2,256,1280]{2,1,0:T(8,128)S(1)}, bf16[2,256,1280]{2,1,0:T(8,128)(2,1)}) custom-call(s32[3]{0:T(128)S(1)} %copy-done.29, bf16[256,1280]{1,0:T(8,128)(2,1)S(1)} %copy-done.44, bf16[256,1280]{1,0:T(8,128)(2,1)S(1)} %copy-done.47, bf16[256,1280]{1,0:T(8,128)(2,1)S(1)} %copy-done.16, ...), custom_call_target="tpu_custom_call" | custom-call | flops 6710886400 | bytes 5242880 | tf_op jit(solution)/shard_map/attend_back/pallas_call | solution.py:465
  714.3 13.6 %all-to-all-done.2 = bf16[4,240,1792]{2,1,0:T(8,128)(2,1)} async-done(((bf16[4,240,1792]{2,1,0:T(8,128)(2,1)}), bf16[4,240,1792]{2,1,0:T(8,128)(2,1)}, u32[]{:S(2)}, u32[]{:S(2)}) %all-to-all-start.2) | async-done | bytes 3440672 | tf_op jit(solution)/shard_map/all_to_all | solution.py:837
  733.8 11.2 %attend_back.7 = (bf16[256,1280]{1,0:T(8,128)(2,1)S(1)}, f32[2,256,1280]{2,1,0:T(8,128)S(1)}, bf16[2,256,1280]{2,1,0:T(8,128)(2,1)S(1)}) custom-call(s32[3]{0:T(128)S(1)} %copy-done.25, bf16[256,1280]{1,0:T(8,128)(2,1)S(1)} %copy-done.45, bf16[256,1280]{1,0:T(8,128)(2,1)S(1)} %copy-done.48, bf16[256,1280]{1,0:T(8,128)(2,1)S(1)} %copy-done.17, ...), custom_call_target="tpu_custom_call" | custom-call | flops 6710886400 | bytes 5242880 | tf_op jit(solution)/shard_map/attend_back/pallas_call | solution.py:465
  778.6 8.4 collective-permute-done.62
  820.1 26.9 %collective-permute-done.75 = bf16[2,2,40,5248]{3,2,0,1:T(8,128)(2,1)S(1)} collective-permute-done((bf16[2,2,40,5248]{3,2,0,1:T(8,128)(2,1)S(1)}, bf16[2,2,40,5248]{3,2,0,1:T(8,128)(2,1)S(1)}, u32[]{:S(2)}, u32[]{:S(2)}) %collective-permute-start.75) | collective-permute-done | bytes 1679392 | tf_op jit(solution)/shard_map/ppermute | solution.py:54
  903.4 10.3 %collective-permute-done.88 = bf16[40,5248]{1,0:T(8,128)(2,1)S(1)} collective-permute-done((bf16[40,5248]{1,0:T(8,128)(2,1)S(1)}, bf16[40,5248]{1,0:T(8,128)(2,1)S(1)}, u32[]{:S(2)}, u32[]{:S(2)}) %collective-permute-start.88) | collective-permute-done | bytes 419872 | tf_op jit(solution)/shard_map/ppermute | solution.py:54
  914.1 13.6 %collective-permute-done.78 = bf16[256,1280]{1,0:T(8,128)(2,1)S(1)} collective-permute-done((bf16[256,1280]{1,0:T(8,128)(2,1)S(1)}, bf16[256,1280]{1,0:T(8,128)(2,1)S(1)}, u32[]{:S(2)}, u32[]{:S(2)}) %collective-permute-start.78) | collective-permute-done | bytes 655392 | tf_op jit(solution)/shard_map/ppermute | solution.py:54
  (704 shorter events, 490.1 us)
Async XLA Ops:
  51.0 34.9 %collective-permute-start.13 = (bf16[2,2,40,3968]{3,2,1,0:T(8,128)(2,1)S(1)}, bf16[2,2,40,3968]{3,2,1,0:T(8,128)(2,1)}, u32[]{:S(2)}, u32[]{:S(2)}) collective-permute-start(bf16[2,2,40,3968]{3,2,1,0:T(8,128)(2,1)S(1)} %pad_maximum_fusion.23), channel_id=1, source_target_pairs={{0,2},{2,0},{1,3},{3,1},{4,6},{6,4},{5,7},{7,5},{8,10},{10,8},{9,1... | collective-permute-start | bytes 3809288 | tf_op jit(solution)/shard_map/ppermute | solution.py:54
  78.7 35.5 %collective-permute-start.12 = (bf16[8,40,3968]{2,1,0:T(8,128)(2,1)S(1)}, bf16[8,40,3968]{2,1,0:T(8,128)(2,1)S(1)}, u32[]{:S(2)}, u32[]{:S(2)}) collective-permute-start(bf16[8,40,3968]{2,1,0:T(8,128)(2,1)S(1)} %pad_maximum_fusion.11.refs_0_), channel_id=1, source_target_pairs={{0,4},{4,0},{1,5},{5,1},{2,6},{6,2},{3,7},{7,3},{8,12},{12,8},{9,1... | collective-permute-start | bytes 7618568 | tf_op jit(solution)/shard_map/ppermute | solution.py:54
  171.4 36.6 %collective-permute-start.31 = (bf16[2,256,1280]{2,1,0:T(8,128)(2,1)}, bf16[2,256,1280]{2,1,0:T(8,128)(2,1)}, u32[]{:S(2)}, u32[]{:S(2)}) collective-permute-start(bf16[2,256,1280]{2,1,0:T(8,128)(2,1)} %get-tuple-element.121.refs_0_), channel_id=1, source_target_pairs={{0,4},{4,0},{1,5},{5,1},{2,6},{6,2},{3,7},{7,3},{8,12},{12,8},{9,1... | collective-permute-start | bytes 3932168 | tf_op jit(solution)/shard_map/ppermute | solution.py:54
  171.4 132.3 %all-to-all-start = ((bf16[4,240,1792]{2,1,0:T(8,128)(2,1)}), bf16[4,240,1792]{2,1,0:T(8,128)(2,1)S(1)}, u32[]{:S(2)}, u32[]{:S(2)}) async-start(bf16[4,240,1792]{2,1,0:T(8,128)(2,1)} %pad_maximum_fusion.2), calls=%async_computation | async-start | bytes 6881280 | tf_op jit(solution)/shard_map/all_to_all | solution.py:756
  179.9 61.4 %collective-permute-start.33 = (bf16[2,2,256,1280]{3,2,1,0:T(8,128)(2,1)}, bf16[2,2,256,1280]{3,2,1,0:T(8,128)(2,1)}, u32[]{:S(2)}, u32[]{:S(2)}) collective-permute-start(bf16[2,2,256,1280]{3,2,1,0:T(8,128)(2,1)} %pad_maximum_fusion.6.refs_2_), channel_id=1, source_target_pairs={{0,1},{1,0},{2,3},{3,2},{4,5},{5,4},{6,7},{7,6},{8,9},{9,8},{10,11... | collective-permute-start | bytes 7864328 | tf_op jit(solution)/shard_map/ppermute | solution.py:54
  185.5 59.6 %collective-permute-start.32 = (bf16[2,2,256,1280]{3,2,1,0:T(8,128)(2,1)}, bf16[2,2,256,1280]{3,2,1,0:T(8,128)(2,1)}, u32[]{:S(2)}, u32[]{:S(2)}) collective-permute-start(bf16[2,2,256,1280]{3,2,1,0:T(8,128)(2,1)} %get-tuple-element.306), channel_id=1, source_target_pairs={{0,2},{2,0},{1,3},{3,1},{4,6},{6,4},{5,7},{7,5},{8,10},{10,8},{9,1... | collective-permute-start | bytes 7864328 | tf_op jit(solution)/shard_map/ppermute | solution.py:54
  208.0 73.8 %collective-permute-start.35 = (bf16[8,40,4096]{2,1,0:T(8,128)(2,1)}, bf16[8,40,4096]{2,1,0:T(8,128)(2,1)}, u32[]{:S(2)}, u32[]{:S(2)}) collective-permute-start(bf16[8,40,4096]{2,1,0:T(8,128)(2,1)} %pad_maximum_fusion.7.refs_0_), channel_id=1, source_target_pairs={{0,4},{4,0},{1,5},{5,1},{2,6},{6,2},{3,7},{7,3},{8,12},{12,8},{9,1... | collective-permute-start | bytes 7864328 | tf_op jit(solution)/shard_map/ppermute | solution.py:54
  209.6 72.2 %collective-permute-start.36 = (bf16[8,40,4096]{2,1,0:T(8,128)(2,1)}, bf16[8,40,4096]{2,1,0:T(8,128)(2,1)}, u32[]{:S(2)}, u32[]{:S(2)}) collective-permute-start(bf16[8,40,4096]{2,1,0:T(8,128)(2,1)} %pad_maximum_fusion.8.refs_2_), channel_id=1, source_target_pairs={{0,4},{4,0},{1,5},{5,1},{2,6},{6,2},{3,7},{7,3},{8,12},{12,8},{9,1... | collective-permute-start | bytes 7864328 | tf_op jit(solution)/shard_map/ppermute | solution.py:54
  210.7 71.0 %collective-permute-start.28 = (bf16[2,256,1280]{2,1,0:T(8,128)(2,1)}, bf16[2,256,1280]{2,1,0:T(8,128)(2,1)}, u32[]{:S(2)}, u32[]{:S(2)}) collective-permute-start(bf16[2,256,1280]{2,1,0:T(8,128)(2,1)} %collective-permute-done.25.refs_0_), channel_id=1, source_target_pairs={{0,8},{8,16},{16,24},{24,0},{1,9},{9,17},{17,25},{25,1},{2,10},{10... | collective-permute-start | bytes 3932168 | tf_op jit(solution)/shard_map/ppermute | solution.py:54
  303.7 87.1 %collective-permute-start.42 = (bf16[4,240,1792]{2,1,0:T(8,128)(2,1)S(1)}, bf16[4,240,1792]{2,1,0:T(8,128)(2,1)}, u32[]{:S(2)}, u32[]{:S(2)}) collective-permute-start(bf16[4,240,1792]{2,1,0:T(8,128)(2,1)S(1)} %all-to-all-done.refs_0_), channel_id=1, source_target_pairs={{0,4},{4,0},{1,5},{5,1},{2,6},{6,2},{3,7},{7,3},{8,12},{12,8},{9,1... | collective-permute-start | bytes 10321928 | tf_op jit(solution)/shard_map/ppermute | solution.py:54
  339.0 46.4 %collective-permute-start.41 = (bf16[2,256,1280]{2,1,0:T(8,128)(2,1)}, bf16[2,256,1280]{2,1,0:T(8,128)(2,1)}, u32[]{:S(2)}, u32[]{:S(2)}) collective-permute-start(bf16[2,256,1280]{2,1,0:T(8,128)(2,1)} %get-tuple-element.313), channel_id=1, source_target_pairs={{0,2},{2,0},{1,3},{3,1},{4,6},{6,4},{5,7},{7,5},{8,10},{10,8},{9,1... | collective-permute-start | bytes 3932168 | tf_op jit(solution)/shard_map/ppermute | solution.py:54
  340.6 42.3 %collective-permute-start.44 = (bf16[256,1280]{1,0:T(8,128)(2,1)}, bf16[256,1280]{1,0:T(8,128)(2,1)}, u32[]{:S(2)}, u32[]{:S(2)}) collective-permute-start(bf16[256,1280]{1,0:T(8,128)(2,1)} %collective-permute-done.37), channel_id=1, source_target_pairs={{0,2},{2,0},{1,3},{3,1},{4,6},{6,4},{5,7},{7,5},{8,10},{10,8},{9,1... | collective-permute-start | bytes 1966088 | tf_op jit(solution)/shard_map/ppermute | solution.py:54
  360.3 43.5 %collective-permute-start.46 = (bf16[256,1280]{1,0:T(8,128)(2,1)}, bf16[256,1280]{1,0:T(8,128)(2,1)}, u32[]{:S(2)}, u32[]{:S(2)}) collective-permute-start(bf16[256,1280]{1,0:T(8,128)(2,1)} %collective-permute-done.38), channel_id=1, source_target_pairs={{0,8},{8,16},{16,24},{24,0},{1,9},{9,17},{17,25},{25,1},{2,10},{10... | collective-permute-start | bytes 1966088 | tf_op jit(solution)/shard_map/ppermute | solution.py:54
  397.5 41.0 %collective-permute-start.45 = (bf16[2,256,1280]{2,1,0:T(8,128)(2,1)}, bf16[2,256,1280]{2,1,0:T(8,128)(2,1)}, u32[]{:S(2)}, u32[]{:S(2)}) collective-permute-start(bf16[2,256,1280]{2,1,0:T(8,128)(2,1)} %pad_maximum_fusion.21.refs_0_), channel_id=1, source_target_pairs={{0,1},{1,0},{2,3},{3,2},{4,5},{5,4},{6,7},{7,6},{8,9},{9,8},{10,11... | collective-permute-start | bytes 3932168 | tf_op jit(solution)/shard_map/ppermute | solution.py:54
  434.3 56.4 %collective-permute-start.59 = (bf16[2,256,1280]{2,1,0:T(8,128)(2,1)}, bf16[2,256,1280]{2,1,0:T(8,128)(2,1)}, u32[]{:S(2)}, u32[]{:S(2)}) collective-permute-start(bf16[2,256,1280]{2,1,0:T(8,128)(2,1)} %get-tuple-element.183), channel_id=1, source_target_pairs={{0,2},{2,0},{1,3},{3,1},{4,6},{6,4},{5,7},{7,5},{8,10},{10,8},{9,1... | collective-permute-start | bytes 3932168 | tf_op jit(solution)/shard_map/ppermute | solution.py:54
  438.2 65.7 %collective-permute-start.48 = (bf16[2,256,1280]{2,1,0:T(8,128)(2,1)}, bf16[2,256,1280]{2,1,0:T(8,128)(2,1)}, u32[]{:S(2)}, u32[]{:S(2)}) collective-permute-start(bf16[2,256,1280]{2,1,0:T(8,128)(2,1)} %pad_maximum_fusion.22.refs_0_), channel_id=1, source_target_pairs={{0,1},{1,0},{2,3},{3,2},{4,5},{5,4},{6,7},{7,6},{8,9},{9,8},{10,11... | collective-permute-start | bytes 3932168 | tf_op jit(solution)/shard_map/ppermute | solution.py:54
  489.2 37.7 %collective-permute-start.49 = (bf16[2,256,1280]{2,1,0:T(8,128)(2,1)}, bf16[2,256,1280]{2,1,0:T(8,128)(2,1)S(1)}, u32[]{:S(2)}, u32[]{:S(2)}) collective-permute-start(bf16[2,256,1280]{2,1,0:T(8,128)(2,1)} %get-tuple-element.170), channel_id=1, source_target_pairs={{0,1},{1,0},{2,3},{3,2},{4,5},{5,4},{6,7},{7,6},{8,9},{9,8},{10,11... | collective-permute-start | bytes 3932168 | tf_op jit(solution)/shard_map/ppermute | solution.py:54
  490.2 76.5 %collective-permute-start.52 = (bf16[2,256,1280]{2,1,0:T(8,128)(2,1)}, bf16[2,256,1280]{2,1,0:T(8,128)(2,1)}, u32[]{:S(2)}, u32[]{:S(2)}) collective-permute-start(bf16[2,256,1280]{2,1,0:T(8,128)(2,1)} %get-tuple-element.172), channel_id=1, source_target_pairs={{0,2},{2,0},{1,3},{3,1},{4,6},{6,4},{5,7},{7,5},{8,10},{10,8},{9,1... | collective-permute-start | bytes 3932168 | tf_op jit(solution)/shard_map/ppermute | solution.py:54
  493.3 125.4 %collective-permute-start.60 = (bf16[256,1280]{1,0:T(8,128)(2,1)}, bf16[256,1280]{1,0:T(8,128)(2,1)}, u32[]{:S(2)}, u32[]{:S(2)}) collective-permute-start(bf16[256,1280]{1,0:T(8,128)(2,1)} %fusion.56), channel_id=1, source_target_pairs={{0,1},{1,0},{2,3},{3,2},{4,5},{5,4},{6,7},{7,6},{8,9},{9,8},{10,11... | collective-permute-start | bytes 1966088 | tf_op jit(solution)/shard_map/ppermute | solution.py:54
  526.0 48.6 %collective-permute-start.56 = (bf16[2,256,1280]{2,1,0:T(8,128)(2,1)}, bf16[2,256,1280]{2,1,0:T(8,128)(2,1)}, u32[]{:S(2)}, u32[]{:S(2)}) collective-permute-start(bf16[2,256,1280]{2,1,0:T(8,128)(2,1)} %get-tuple-element.181), channel_id=1, source_target_pairs={{0,1},{1,0},{2,3},{3,2},{4,5},{5,4},{6,7},{7,6},{8,9},{9,8},{10,11... | collective-permute-start | bytes 3932168 | tf_op jit(solution)/shard_map/ppermute | solution.py:54
  529.6 41.2 %collective-permute-start.50 = (bf16[256,1280]{1,0:T(8,128)(2,1)}, bf16[256,1280]{1,0:T(8,128)(2,1)}, u32[]{:S(2)}, u32[]{:S(2)}) collective-permute-start(bf16[256,1280]{1,0:T(8,128)(2,1)} %fusion.53), channel_id=1, source_target_pairs={{0,2},{2,0},{1,3},{3,1},{4,6},{6,4},{5,7},{7,5},{8,10},{10,8},{9,1... | collective-permute-start | bytes 1966088 | tf_op jit(solution)/shard_map/ppermute | solution.py:54
  613.3 114.6 %all-to-all-start.2 = ((bf16[4,240,1792]{2,1,0:T(8,128)(2,1)}), bf16[4,240,1792]{2,1,0:T(8,128)(2,1)}, u32[]{:S(2)}, u32[]{:S(2)}) async-start(bf16[4,240,1792]{2,1,0:T(8,128)(2,1)} %add_convert_fusion.2), calls=%async_computation.2 | async-start | bytes 6881280 | tf_op jit(solution)/shard_map/all_to_all | solution.py:837
  678.1 73.8 %collective-permute-start.61 = (bf16[2,2,256,1280]{3,2,0,1:T(8,128)(2,1)}, bf16[2,2,256,1280]{3,2,0,1:T(8,128)(2,1)}, u32[]{:S(2)}, u32[]{:S(2)}) collective-permute-start(bf16[2,2,256,1280]{3,2,0,1:T(8,128)(2,1)} %copy.191), channel_id=1, source_target_pairs={{0,1},{1,0},{2,3},{3,2},{4,5},{5,4},{6,7},{7,6},{8,9},{9,8},{10,11... | collective-permute-start | bytes 7864328 | tf_op jit(solution)/shard_map/ppermute | solution.py:54
  680.7 74.8 %collective-permute-start.64 = (bf16[2,2,256,1280]{3,2,0,1:T(8,128)(2,1)}, bf16[2,2,256,1280]{3,2,0,1:T(8,128)(2,1)}, u32[]{:S(2)}, u32[]{:S(2)}) collective-permute-start(bf16[2,2,256,1280]{3,2,0,1:T(8,128)(2,1)} %copy.193), channel_id=1, source_target_pairs={{0,2},{2,0},{1,3},{3,1},{4,6},{6,4},{5,7},{7,5},{8,10},{10,8},{9,1... | collective-permute-start | bytes 7864328 | tf_op jit(solution)/shard_map/ppermute | solution.py:54
  685.9 76.4 %collective-permute-start.68 = (bf16[2,256,1280]{2,1,0:T(8,128)(2,1)}, bf16[2,256,1280]{2,1,0:T(8,128)(2,1)}, u32[]{:S(2)}, u32[]{:S(2)}) collective-permute-start(bf16[2,256,1280]{2,1,0:T(8,128)(2,1)} %add_convert_fusion.5), channel_id=1, source_target_pairs={{0,8},{8,16},{16,24},{24,0},{1,9},{9,17},{17,25},{25,1},{2,10},{10... | collective-permute-start | bytes 3932168 | tf_op jit(solution)/shard_map/ppermute | solution.py:54
  699.6 61.9 %collective-permute-start.69 = (bf16[2,256,1280]{2,1,0:T(8,128)(2,1)}, bf16[2,256,1280]{2,1,0:T(8,128)(2,1)}, u32[]{:S(2)}, u32[]{:S(2)}) collective-permute-start(bf16[2,256,1280]{2,1,0:T(8,128)(2,1)} %get-tuple-element.199), channel_id=1, source_target_pairs={{0,4},{4,0},{1,5},{5,1},{2,6},{6,2},{3,7},{7,3},{8,12},{12,8},{9,1... | collective-permute-start | bytes 3932168 | tf_op jit(solution)/shard_map/ppermute | solution.py:54
  714.0 81.2 %collective-permute-start.71 = (bf16[2,256,1280]{2,1,0:T(8,128)(2,1)}, bf16[2,256,1280]{2,1,0:T(8,128)(2,1)}, u32[]{:S(2)}, u32[]{:S(2)}) collective-permute-start(bf16[2,256,1280]{2,1,0:T(8,128)(2,1)} %get-tuple-element.202), channel_id=1, source_target_pairs={{0,4},{4,0},{1,5},{5,1},{2,6},{6,2},{3,7},{7,3},{8,12},{12,8},{9,1... | collective-permute-start | bytes 3932168 | tf_op jit(solution)/shard_map/ppermute | solution.py:54
  751.9 52.5 %collective-permute-start.74 = (bf16[4,2,2,40,5248]{4,3,0,1,2:T(8,128)(2,1)}, bf16[4,2,2,40,5248]{4,3,0,1,2:T(8,128)(2,1)}, u32[]{:S(2)}, u32[]{:S(2)}) collective-permute-start(bf16[4,2,2,40,5248]{4,3,0,1,2:T(8,128)(2,1)} %pad_maximum_fusion), channel_id=1, source_target_pairs={{0,4},{4,0},{1,5},{5,1},{2,6},{6,2},{3,7},{7,3},{8,12},{12,8},{9,1... | collective-permute-start | bytes 20152328 | tf_op jit(solution)/shard_map/ppermute | solution.py:54
  804.3 52.3 %collective-permute-start.72 = (bf16[2,256,1280]{2,1,0:T(8,128)(2,1)}, bf16[2,256,1280]{2,1,0:T(8,128)(2,1)}, u32[]{:S(2)}, u32[]{:S(2)}) collective-permute-start(bf16[2,256,1280]{2,1,0:T(8,128)(2,1)} %add_convert_fusion.3), channel_id=1, source_target_pairs={{0,8},{8,16},{16,24},{24,0},{1,9},{9,17},{17,25},{25,1},{2,10},{10... | collective-permute-start | bytes 3932168 | tf_op jit(solution)/shard_map/ppermute | solution.py:54
  809.4 37.6 %collective-permute-start.75 = (bf16[2,2,40,5248]{3,2,0,1:T(8,128)(2,1)S(1)}, bf16[2,2,40,5248]{3,2,0,1:T(8,128)(2,1)S(1)}, u32[]{:S(2)}, u32[]{:S(2)}) collective-permute-start(bf16[2,2,40,5248]{3,2,0,1:T(8,128)(2,1)S(1)} %dynamic-slice_bitcast_fusion.3), channel_id=1, source_target_pairs={{0,2},{2,0},{1,3},{3,1},{4,6},{6,4},{5,7},{7,5},{8,10},{10,8},{9,1... | collective-permute-start | bytes 5038088 | tf_op jit(solution)/shard_map/ppermute | solution.py:54
  815.8 85.9 %collective-permute-start.66 = (bf16[256,1280]{1,0:T(8,128)(2,1)}, bf16[256,1280]{1,0:T(8,128)(2,1)}, u32[]{:S(2)}, u32[]{:S(2)}) collective-permute-start(bf16[256,1280]{1,0:T(8,128)(2,1)} %fusion.40), channel_id=1, source_target_pairs={{0,8},{8,16},{16,24},{24,0},{1,9},{9,17},{17,25},{25,1},{2,10},{10... | collective-permute-start | bytes 1966088 | tf_op jit(solution)/shard_map/ppermute | solution.py:54
  816.1 37.6 %collective-permute-start.76 = (bf16[2,2,40,5248]{3,2,0,1:T(8,128)(2,1)S(1)}, bf16[2,2,40,5248]{3,2,0,1:T(8,128)(2,1)S(1)}, u32[]{:S(2)}, u32[]{:S(2)}) collective-permute-start(bf16[2,2,40,5248]{3,2,0,1:T(8,128)(2,1)S(1)} %dynamic-slice_bitcast_fusion.2), channel_id=1, source_target_pairs={{0,1},{1,0},{2,3},{3,2},{4,5},{5,4},{6,7},{7,6},{8,9},{9,8},{10,11... | collective-permute-start | bytes 5038088 | tf_op jit(solution)/shard_map/ppermute | solution.py:54
  (223 other events, 2556.3 us)

commit v10 on v9

--- a/solution.py
+++ b/solution.py
@@ -98,12 +98,12 @@
     "mid1": "r2",
     "core2": "r3",
     "rs1": "fp",
-    "norm": "g2",
     "gs1": "rp",
     "arr1": "g3 rp",
     "arr2": "gs",
     "arr3": "s gf",
     "wa": "q",
+    "mix": "gf",
     "wc": "m",
     "c1b": "w",
     "c2b": "k0",
@@ -120,7 +120,7 @@
     "kv1": "ys",
     "kv2": "l",
     "yz3": "kv",
-    "yz4": "z",
+    "yz4": "f",
     "late3": "kv",
     "cz2": "w",
     "cz3": "cp",

time: 978 us -> 973 us (level)
    unnamed x328 -> x320, local copies, waits for them, and re-layouts: 57.5 us -> 56.1 us
  transfers between devices with their start and end apart: 94 -> 94, of which waited for: 41 -> 39; matrix products, arithmetic and copies ran while one was open for 27% -> 26% of each run, Pallas kernels for 21% -> 21%
where the time goes in v10:
time: 973 us; the launch traced here: 962 us
  waiting for transfers between devices  358 us (37%)
  Pallas kernels  203 us (21%)
  local copies, waits for them, and re-layouts  121 us (12%)
  other arithmetic  118 us (12%)
  starting transfers between devices  91.9 us (9%)
  matrix products  66.6 us (7%)
    ppermute x88, waiting for transfers between devices, shift(): return lax.ppermute(value, axis, [(i, (i + 1) % n) for i in range(n)])  338 us
    pallas_call x4, Pallas kernels, expert_chunk(): pl.pallas_call(functools.partial(expert_kernel, slots, na, nb, even, len(...  91.5 us
    ppermute x88, starting transfers between devices, shift(): return lax.ppermute(value, axis, [(i, (i + 1) % n) for i in range(n)])  71.6 us
    dot_general x21, matrix products, dot(): return lax.dot_general(a, b, (dims, ((), ())), preferred_element_type=F32)  66.6 us
    unnamed x320, local copies, waits for them, and re-layouts  56.1 us
    pallas_call x4, Pallas kernels, attend_back_chunk(): pl.pallas_call(functools.partial(attend_back_kernel, n_ctx, n, first, las...  46.1 us
    pallas_call x4, Pallas kernels, attend_chunk(): pl.pallas_call(functools.partial(attend_kernel, n_ctx, n, first, last), g...  37.4 us
  transfers between devices with their start and end apart: 94, of which 39 were waited for; matrix products, arithmetic and copies ran while one was open for 26% of the time, Pallas kernels for 21%

profile of v10, /device:TPU:0, one launch (start us, length us, event | category | flops | bytes accessed | tf_op | source)
XLA Modules:
  0.0 962.2 jit_solution(12541607716198293303)
XLA Ops:
  6.3 8.8 collective-permute-done
  51.6 11.3 %collective-permute-done.9 = bf16[2,40,3968]{2,1,0:T(8,128)(2,1)S(1)} collective-permute-done((bf16[2,40,3968]{2,1,0:T(8,128)(2,1)S(1)}, bf16[2,40,3968]{2,1,0:T(8,128)(2,1)S(1)}, u32[]{:S(2)}, u32[]{:S(2)}) %collective-permute-start.9) | collective-permute-done | bytes 634912 | tf_op jit(solution)/shard_map/ppermute | solution.py:54
  65.8 12.2 %collective-permute-done.17 = bf16[40,4096]{1,0:T(8,128)(2,1)S(1)} collective-permute-done((bf16[40,4096]{1,0:T(8,128)(2,1)}, bf16[40,4096]{1,0:T(8,128)(2,1)S(1)}, u32[]{:S(2)}, u32[]{:S(2)}) %collective-permute-start.17) | collective-permute-done | bytes 327712 | tf_op jit(solution)/shard_map/ppermute | solution.py:54
  94.1 17.3 %collective-permute-done.19 = bf16[256,1280]{1,0:T(8,128)(2,1)} collective-permute-done((bf16[256,1280]{1,0:T(8,128)(2,1)S(1)}, bf16[256,1280]{1,0:T(8,128)(2,1)}, u32[]{:S(2)}, u32[]{:S(2)}) %collective-permute-start.19) | collective-permute-done | bytes 655392 | tf_op jit(solution)/shard_map/ppermute | solution.py:54
  125.7 9.2 project.1
  148.0 18.9 %collective-permute-done.16.refs_0_ = bf16[2,256,1280]{2,1,0:T(8,128)(2,1)} collective-permute-done((bf16[2,256,1280]{2,1,0:T(8,128)(2,1)}, bf16[2,256,1280]{2,1,0:T(8,128)(2,1)}, u32[]{:S(2)}, u32[]{:S(2)}) %collective-permute-start.16) | collective-permute-done | bytes 1310752 | tf_op jit(solution)/shard_map/ppermute | solution.py:54
  187.0 13.8 %collective-permute-done.25.refs_0_ = bf16[2,256,1280]{2,1,0:T(8,128)(2,1)} collective-permute-done((bf16[2,256,1280]{2,1,0:T(8,128)(2,1)}, bf16[2,256,1280]{2,1,0:T(8,128)(2,1)}, u32[]{:S(2)}, u32[]{:S(2)}) %collective-permute-start.25) | collective-permute-done | bytes 1310752 | tf_op jit(solution)/shard_map/ppermute | solution.py:54
  211.4 8.5 attend.4
  220.0 9.2 attend.5
  229.2 9.2 attend.6
  245.1 36.4 %collective-permute-done.28.refs_0_ = bf16[2,256,1280]{2,1,0:T(8,128)(2,1)} collective-permute-done((bf16[2,256,1280]{2,1,0:T(8,128)(2,1)}, bf16[2,256,1280]{2,1,0:T(8,128)(2,1)}, u32[]{:S(2)}, u32[]{:S(2)}) %collective-permute-start.28) | collective-permute-done | bytes 1310752 | tf_op jit(solution)/shard_map/ppermute | solution.py:54
  288.9 10.5 %attend.7 = (bf16[256,1280]{1,0:T(8,128)(2,1)S(1)}, f32[10,256,128]{2,1,0:T(8,128)S(1)}) custom-call(s32[3]{0:T(128)S(1)} %pad_add_fusion.place_ref, bf16[256,1280]{1,0:T(8,128)(2,1)S(1)} %copy-done.41, bf16[2,256,1280]{2,1,0:T(8,128)(2,1)} %collective-permute-done.28.refs_0_, bf16[2,256,1280]{2,1,0:T(8,128)(2,1)} %collective-permute-done.34.refs_1_, ...), custom_call_target="tpu_custom_call" | custom-call | flops 2684354560 | bytes 2621440 | tf_op jit(solution)/shard_map/attend/pallas_call | solution.py:404
  306.0 14.2 %collective-permute-start.37 = (bf16[256,1280]{1,0:T(8,128)(2,1)S(1)}, bf16[256,1280]{1,0:T(8,128)(2,1)}, u32[]{:S(2)}, u32[]{:S(2)}) collective-permute-start(bf16[256,1280]{1,0:T(8,128)(2,1)S(1)} %multiply_convert_fusion), channel_id=1, source_target_pairs={{0,8},{8,16},{16,24},{24,0},{1,9},{9,17},{17,25},{25,1},{2,10},{10... | collective-permute-start | bytes 1966088 | tf_op jit(solution)/shard_map/ppermute | solution.py:54
  321.6 12.7 %collective-permute-done.37 = bf16[256,1280]{1,0:T(8,128)(2,1)} collective-permute-done((bf16[256,1280]{1,0:T(8,128)(2,1)S(1)}, bf16[256,1280]{1,0:T(8,128)(2,1)}, u32[]{:S(2)}, u32[]{:S(2)}) %collective-permute-start.37) | collective-permute-done | bytes 655392 | tf_op jit(solution)/shard_map/ppermute | solution.py:54
  344.9 8.4 collective-permute-done.38
  360.0 22.6 %collective-permute-done.44 = bf16[256,1280]{1,0:T(8,128)(2,1)} collective-permute-done((bf16[256,1280]{1,0:T(8,128)(2,1)}, bf16[256,1280]{1,0:T(8,128)(2,1)}, u32[]{:S(2)}, u32[]{:S(2)}) %collective-permute-start.44) | collective-permute-done | bytes 655392 | tf_op jit(solution)/shard_map/ppermute | solution.py:54
  405.0 23.4 %experts.4 = (bf16[2,256,1280]{2,1,0:T(8,128)(2,1)}, bf16[2,256,1280]{2,1,0:T(8,128)(2,1)}, f32[2,2,1,256]{3,2,1,0:T(1,128)}, bf16[2816,1280]{1,0:T(8,128)(2,1)}...) custom-call(s32[4]{0:T(128)} %pad_add_fusion.4.e_ref, ...), custom_call_target="tpu_custom_call" | custom-call | flops 9688842240 | bytes 30000000 | tf_op jit(solution)/shard_map/experts/pallas_call | solution.py:593
  438.5 22.2 %experts.5 = (bf16[2,256,1280]{2,1,0:T(8,128)(2,1)}, bf16[2,256,1280]{2,1,0:T(8,128)(2,1)}, f32[2,2,1,256]{3,2,1,0:T(1,128)}, bf16[2816,1280]{1,0:T(8,128)(2,1)}...) custom-call(s32[4]{0:T(128)} %pad_add_fusion.4.e_ref, ...), custom_call_target="tpu_custom_call", output_to_operand_aliasing={{3}: (9, {}), {4}: (10, {}), {5}: (11, {}), {6}: (12, {})} | custom-call | flops 9688842240 | bytes 30000000 | tf_op jit(solution)/shard_map/experts/pallas_call | solution.py:593
  464.2 23.9 %experts.6 = (bf16[2,256,1280]{2,1,0:T(8,128)(2,1)}, bf16[2,256,1280]{2,1,0:T(8,128)(2,1)}, f32[2,2,1,256]{3,2,1,0:T(1,128)}, bf16[2816,1280]{1,0:T(8,128)(2,1)}...) custom-call(s32[4]{0:T(128)} %pad_add_fusion.4.e_ref, ...), custom_call_target="tpu_custom_call", output_to_operand_aliasing={{3}: (7, {}), {4}: (8, {}), {5}: (9, {}), {6}: (10, {}), {7... | custom-call | flops 9688842240 | bytes 30000000 | tf_op jit(solution)/shard_map/experts/pallas_call | solution.py:593
  503.5 22.1 %experts.7 = (bf16[2,256,1280]{2,1,0:T(8,128)(2,1)}, bf16[2,256,1280]{2,1,0:T(8,128)(2,1)}, f32[2,2,1,256]{3,2,1,0:T(1,128)}, bf16[2816,1280]{1,0:T(8,128)(2,1)}...) custom-call(s32[4]{0:T(128)} %pad_add_fusion.4.e_ref, ...), custom_call_target="tpu_custom_call", output_to_operand_aliasing={{3}: (9, {}), {4}: (10, {}), {5}: (11, {}), {6}: (12, {}), ... | custom-call | flops 9688842240 | bytes 30000000 | tf_op jit(solution)/shard_map/experts/pallas_call | solution.py:593
  530.8 20.3 %convolution_convert_fusion.4 = bf16[1280,1792]{1,0:T(8,128)(2,1)} fusion(bf16[2816,1280]{1,0:T(8,128)(2,1)} %get-tuple-element.175, bf16[2816,1792]{1,0:T(8,128)(2,1)} %get-tuple-element.176), kind=kOutput, calls=%fused_computation.6 | convolution fusion | flops 12920750080 | bytes 21889024 | tf_op jit(solution)/shard_map/dot_general | solution.py:45
  618.4 11.3 %collective-permute-done.58 = bf16[256,1280]{1,0:T(8,128)(2,1)} collective-permute-done((bf16[256,1280]{1,0:T(8,128)(2,1)}, bf16[256,1280]{1,0:T(8,128)(2,1)}, u32[]{:S(2)}, u32[]{:S(2)}) %collective-permute-start.58) | collective-permute-done | bytes 655392 | tf_op jit(solution)/shard_map/ppermute | solution.py:54
  640.6 11.6 %attend_back.4 = (f32[256,1280]{1,0:T(8,128)S(1)}, f32[2,256,1280]{2,1,0:T(8,128)S(1)}, bf16[2,256,1280]{2,1,0:T(8,128)(2,1)}) custom-call(s32[3]{0:T(128)S(1)} %pad_add_fusion.2.place_ref, bf16[256,1280]{1,0:T(8,128)(2,1)S(1)} %copy-done.42, bf16[256,1280]{1,0:T(8,128)(2,1)S(1)} %convolution_convert_fusion.8.do_ref, bf16[256,1280]{1,0:T(8,128)(2,1)S(1)} %copy-done.16, ...), custom_call_target="tpu_custom_call" | custom-call | flops 6710886400 | bytes 5242880 | tf_op jit(solution)/shard_map/attend_back/pallas_call | solution.py:465
  686.0 11.6 %attend_back.5 = (f32[256,1280]{1,0:T(8,128)S(1)}, f32[2,256,1280]{2,1,0:T(8,128)S(1)}, bf16[2,256,1280]{2,1,0:T(8,128)(2,1)}) custom-call(s32[3]{0:T(128)S(1)} %copy-done.26, bf16[256,1280]{1,0:T(8,128)(2,1)S(1)} %copy-done.43, bf16[256,1280]{1,0:T(8,128)(2,1)S(1)} %copy-done.46, bf16[256,1280]{1,0:T(8,128)(2,1)S(1)} %copy-done.16, ...), custom_call_target="tpu_custom_call" | custom-call | flops 6710886400 | bytes 5242880 | tf_op jit(solution)/shard_map/attend_back/pallas_call | solution.py:465
  699.4 11.7 %attend_back.6 = (f32[256,1280]{1,0:T(8,128)S(1)}, f32[2,256,1280]{2,1,0:T(8,128)S(1)}, bf16[2,256,1280]{2,1,0:T(8,128)(2,1)}) custom-call(s32[3]{0:T(128)S(1)} %copy-done.28, bf16[256,1280]{1,0:T(8,128)(2,1)S(1)} %copy-done.43, bf16[256,1280]{1,0:T(8,128)(2,1)S(1)} %copy-done.46, bf16[256,1280]{1,0:T(8,128)(2,1)S(1)} %copy-done.16, ...), custom_call_target="tpu_custom_call" | custom-call | flops 6710886400 | bytes 5242880 | tf_op jit(solution)/shard_map/attend_back/pallas_call | solution.py:465
  713.9 13.6 %all-to-all-done.2 = bf16[4,240,1792]{2,1,0:T(8,128)(2,1)} async-done(((bf16[4,240,1792]{2,1,0:T(8,128)(2,1)}), bf16[4,240,1792]{2,1,0:T(8,128)(2,1)}, u32[]{:S(2)}, u32[]{:S(2)}) %all-to-all-start.2) | async-done | bytes 3440672 | tf_op jit(solution)/shard_map/all_to_all | solution.py:837
  732.3 11.2 %attend_back.7 = (bf16[256,1280]{1,0:T(8,128)(2,1)S(1)}, f32[2,256,1280]{2,1,0:T(8,128)S(1)}, bf16[2,256,1280]{2,1,0:T(8,128)(2,1)S(1)}) custom-call(s32[3]{0:T(128)S(1)} %copy-done.24, bf16[256,1280]{1,0:T(8,128)(2,1)S(1)} %copy-done.44, bf16[256,1280]{1,0:T(8,128)(2,1)S(1)} %copy-done.47, bf16[256,1280]{1,0:T(8,128)(2,1)S(1)} %copy-done.16, ...), custom_call_target="tpu_custom_call" | custom-call | flops 6710886400 | bytes 5242880 | tf_op jit(solution)/shard_map/attend_back/pallas_call | solution.py:465
  777.1 8.3 collective-permute-done.62
  818.7 26.8 %collective-permute-done.75 = bf16[2,2,40,5248]{3,2,0,1:T(8,128)(2,1)S(1)} collective-permute-done((bf16[2,2,40,5248]{3,2,0,1:T(8,128)(2,1)S(1)}, bf16[2,2,40,5248]{3,2,0,1:T(8,128)(2,1)S(1)}, u32[]{:S(2)}, u32[]{:S(2)}) %collective-permute-start.75) | collective-permute-done | bytes 1679392 | tf_op jit(solution)/shard_map/ppermute | solution.py:54
  907.6 12.2 %collective-permute-done.89 = bf16[40,5248]{1,0:T(8,128)(2,1)S(1)} collective-permute-done((bf16[40,5248]{1,0:T(8,128)(2,1)S(1)}, bf16[40,5248]{1,0:T(8,128)(2,1)S(1)}, u32[]{:S(2)}, u32[]{:S(2)}) %collective-permute-start.89) | collective-permute-done | bytes 419872 | tf_op jit(solution)/shard_map/ppermute | solution.py:54
  922.5 11.3 %collective-permute-done.78 = bf16[256,1280]{1,0:T(8,128)(2,1)S(1)} collective-permute-done((bf16[256,1280]{1,0:T(8,128)(2,1)S(1)}, bf16[256,1280]{1,0:T(8,128)(2,1)S(1)}, u32[]{:S(2)}, u32[]{:S(2)}) %collective-permute-start.78) | collective-permute-done | bytes 655392 | tf_op jit(solution)/shard_map/ppermute | solution.py:54
  943.0 8.7 collective-permute-done.86
  (696 shorter events, 485.8 us)
Async XLA Ops:
  51.0 34.9 %collective-permute-start.13 = (bf16[2,2,40,3968]{3,2,1,0:T(8,128)(2,1)S(1)}, bf16[2,2,40,3968]{3,2,1,0:T(8,128)(2,1)}, u32[]{:S(2)}, u32[]{:S(2)}) collective-permute-start(bf16[2,2,40,3968]{3,2,1,0:T(8,128)(2,1)S(1)} %pad_maximum_fusion.22), channel_id=1, source_target_pairs={{0,2},{2,0},{1,3},{3,1},{4,6},{6,4},{5,7},{7,5},{8,10},{10,8},{9,1... | collective-permute-start | bytes 3809288 | tf_op jit(solution)/shard_map/ppermute | solution.py:54
  171.2 36.1 %collective-permute-start.31 = (bf16[2,256,1280]{2,1,0:T(8,128)(2,1)}, bf16[2,256,1280]{2,1,0:T(8,128)(2,1)}, u32[]{:S(2)}, u32[]{:S(2)}) collective-permute-start(bf16[2,256,1280]{2,1,0:T(8,128)(2,1)} %get-tuple-element.119.refs_0_), channel_id=1, source_target_pairs={{0,4},{4,0},{1,5},{5,1},{2,6},{6,2},{3,7},{7,3},{8,12},{12,8},{9,1... | collective-permute-start | bytes 3932168 | tf_op jit(solution)/shard_map/ppermute | solution.py:54
  171.2 132.3 %all-to-all-start = ((bf16[4,240,1792]{2,1,0:T(8,128)(2,1)}), bf16[4,240,1792]{2,1,0:T(8,128)(2,1)S(1)}, u32[]{:S(2)}, u32[]{:S(2)}) async-start(bf16[4,240,1792]{2,1,0:T(8,128)(2,1)} %pad_maximum_fusion.2), calls=%async_computation | async-start | bytes 6881280 | tf_op jit(solution)/shard_map/all_to_all | solution.py:756
  179.7 60.8 %collective-permute-start.33 = (bf16[2,2,256,1280]{3,2,1,0:T(8,128)(2,1)}, bf16[2,2,256,1280]{3,2,1,0:T(8,128)(2,1)}, u32[]{:S(2)}, u32[]{:S(2)}) collective-permute-start(bf16[2,2,256,1280]{3,2,1,0:T(8,128)(2,1)} %pad_maximum_fusion.6.refs_2_), channel_id=1, source_target_pairs={{0,1},{1,0},{2,3},{3,2},{4,5},{5,4},{6,7},{7,6},{8,9},{9,8},{10,11... | collective-permute-start | bytes 7864328 | tf_op jit(solution)/shard_map/ppermute | solution.py:54
  185.5 59.6 %collective-permute-start.32 = (bf16[2,2,256,1280]{3,2,1,0:T(8,128)(2,1)}, bf16[2,2,256,1280]{3,2,1,0:T(8,128)(2,1)}, u32[]{:S(2)}, u32[]{:S(2)}) collective-permute-start(bf16[2,2,256,1280]{3,2,1,0:T(8,128)(2,1)} %get-tuple-element.306), channel_id=1, source_target_pairs={{0,2},{2,0},{1,3},{3,1},{4,6},{6,4},{5,7},{7,5},{8,10},{10,8},{9,1... | collective-permute-start | bytes 7864328 | tf_op jit(solution)/shard_map/ppermute | solution.py:54
  207.3 74.2 %collective-permute-start.35 = (bf16[8,40,4096]{2,1,0:T(8,128)(2,1)}, bf16[8,40,4096]{2,1,0:T(8,128)(2,1)}, u32[]{:S(2)}, u32[]{:S(2)}) collective-permute-start(bf16[8,40,4096]{2,1,0:T(8,128)(2,1)} %pad_maximum_fusion.7.refs_0_), channel_id=1, source_target_pairs={{0,4},{4,0},{1,5},{5,1},{2,6},{6,2},{3,7},{7,3},{8,12},{12,8},{9,1... | collective-permute-start | bytes 7864328 | tf_op jit(solution)/shard_map/ppermute | solution.py:54
  208.9 72.7 %collective-permute-start.36 = (bf16[8,40,4096]{2,1,0:T(8,128)(2,1)}, bf16[8,40,4096]{2,1,0:T(8,128)(2,1)}, u32[]{:S(2)}, u32[]{:S(2)}) collective-permute-start(bf16[8,40,4096]{2,1,0:T(8,128)(2,1)} %pad_maximum_fusion.8.refs_2_), channel_id=1, source_target_pairs={{0,4},{4,0},{1,5},{5,1},{2,6},{6,2},{3,7},{7,3},{8,12},{12,8},{9,1... | collective-permute-start | bytes 7864328 | tf_op jit(solution)/shard_map/ppermute | solution.py:54
  209.9 71.5 %collective-permute-start.28 = (bf16[2,256,1280]{2,1,0:T(8,128)(2,1)}, bf16[2,256,1280]{2,1,0:T(8,128)(2,1)}, u32[]{:S(2)}, u32[]{:S(2)}) collective-permute-start(bf16[2,256,1280]{2,1,0:T(8,128)(2,1)} %collective-permute-done.25.refs_0_), channel_id=1, source_target_pairs={{0,8},{8,16},{16,24},{24,0},{1,9},{9,17},{17,25},{25,1},{2,10},{10... | collective-permute-start | bytes 3932168 | tf_op jit(solution)/shard_map/ppermute | solution.py:54
  303.5 87.0 %collective-permute-start.42 = (bf16[4,240,1792]{2,1,0:T(8,128)(2,1)S(1)}, bf16[4,240,1792]{2,1,0:T(8,128)(2,1)}, u32[]{:S(2)}, u32[]{:S(2)}) collective-permute-start(bf16[4,240,1792]{2,1,0:T(8,128)(2,1)S(1)} %all-to-all-done.refs_0_), channel_id=1, source_target_pairs={{0,4},{4,0},{1,5},{5,1},{2,6},{6,2},{3,7},{7,3},{8,12},{12,8},{9,1... | collective-permute-start | bytes 10321928 | tf_op jit(solution)/shard_map/ppermute | solution.py:54
  338.6 46.4 %collective-permute-start.41 = (bf16[2,256,1280]{2,1,0:T(8,128)(2,1)}, bf16[2,256,1280]{2,1,0:T(8,128)(2,1)}, u32[]{:S(2)}, u32[]{:S(2)}) collective-permute-start(bf16[2,256,1280]{2,1,0:T(8,128)(2,1)} %get-tuple-element.313), channel_id=1, source_target_pairs={{0,2},{2,0},{1,3},{3,1},{4,6},{6,4},{5,7},{7,5},{8,10},{10,8},{9,1... | collective-permute-start | bytes 3932168 | tf_op jit(solution)/shard_map/ppermute | solution.py:54
  340.7 41.9 %collective-permute-start.44 = (bf16[256,1280]{1,0:T(8,128)(2,1)}, bf16[256,1280]{1,0:T(8,128)(2,1)}, u32[]{:S(2)}, u32[]{:S(2)}) collective-permute-start(bf16[256,1280]{1,0:T(8,128)(2,1)} %collective-permute-done.37), channel_id=1, source_target_pairs={{0,2},{2,0},{1,3},{3,1},{4,6},{6,4},{5,7},{7,5},{8,10},{10,8},{9,1... | collective-permute-start | bytes 1966088 | tf_op jit(solution)/shard_map/ppermute | solution.py:54
  353.3 34.9 %collective-permute-start.39 = (bf16[256,1280]{1,0:T(8,128)(2,1)}, bf16[256,1280]{1,0:T(8,128)(2,1)S(1)}, u32[]{:S(2)}, u32[]{:S(2)}) collective-permute-start(bf16[256,1280]{1,0:T(8,128)(2,1)} %collective-permute-done.38), channel_id=1, source_target_pairs={{0,1},{1,0},{2,3},{3,2},{4,5},{5,4},{6,7},{7,6},{8,9},{9,8},{10,11... | collective-permute-start | bytes 1966088 | tf_op jit(solution)/shard_map/ppermute | solution.py:54
  360.0 43.5 %collective-permute-start.46 = (bf16[256,1280]{1,0:T(8,128)(2,1)}, bf16[256,1280]{1,0:T(8,128)(2,1)}, u32[]{:S(2)}, u32[]{:S(2)}) collective-permute-start(bf16[256,1280]{1,0:T(8,128)(2,1)} %collective-permute-done.38), channel_id=1, source_target_pairs={{0,8},{8,16},{16,24},{24,0},{1,9},{9,17},{17,25},{25,1},{2,10},{10... | collective-permute-start | bytes 1966088 | tf_op jit(solution)/shard_map/ppermute | solution.py:54
  397.1 41.4 %collective-permute-start.45 = (bf16[2,256,1280]{2,1,0:T(8,128)(2,1)}, bf16[2,256,1280]{2,1,0:T(8,128)(2,1)}, u32[]{:S(2)}, u32[]{:S(2)}) collective-permute-start(bf16[2,256,1280]{2,1,0:T(8,128)(2,1)} %pad_maximum_fusion.20.refs_0_), channel_id=1, source_target_pairs={{0,1},{1,0},{2,3},{3,2},{4,5},{5,4},{6,7},{7,6},{8,9},{9,8},{10,11... | collective-permute-start | bytes 3932168 | tf_op jit(solution)/shard_map/ppermute | solution.py:54
  434.0 56.3 %collective-permute-start.59 = (bf16[2,256,1280]{2,1,0:T(8,128)(2,1)}, bf16[2,256,1280]{2,1,0:T(8,128)(2,1)}, u32[]{:S(2)}, u32[]{:S(2)}) collective-permute-start(bf16[2,256,1280]{2,1,0:T(8,128)(2,1)} %get-tuple-element.183), channel_id=1, source_target_pairs={{0,2},{2,0},{1,3},{3,1},{4,6},{6,4},{5,7},{7,5},{8,10},{10,8},{9,1... | collective-permute-start | bytes 3932168 | tf_op jit(solution)/shard_map/ppermute | solution.py:54
  437.9 65.6 %collective-permute-start.48 = (bf16[2,256,1280]{2,1,0:T(8,128)(2,1)}, bf16[2,256,1280]{2,1,0:T(8,128)(2,1)}, u32[]{:S(2)}, u32[]{:S(2)}) collective-permute-start(bf16[2,256,1280]{2,1,0:T(8,128)(2,1)} %pad_maximum_fusion.21.refs_0_), channel_id=1, source_target_pairs={{0,1},{1,0},{2,3},{3,2},{4,5},{5,4},{6,7},{7,6},{8,9},{9,8},{10,11... | collective-permute-start | bytes 3932168 | tf_op jit(solution)/shard_map/ppermute | solution.py:54
  488.9 37.7 %collective-permute-start.49 = (bf16[2,256,1280]{2,1,0:T(8,128)(2,1)}, bf16[2,256,1280]{2,1,0:T(8,128)(2,1)S(1)}, u32[]{:S(2)}, u32[]{:S(2)}) collective-permute-start(bf16[2,256,1280]{2,1,0:T(8,128)(2,1)} %get-tuple-element.170), channel_id=1, source_target_pairs={{0,1},{1,0},{2,3},{3,2},{4,5},{5,4},{6,7},{7,6},{8,9},{9,8},{10,11... | collective-permute-start | bytes 3932168 | tf_op jit(solution)/shard_map/ppermute | solution.py:54
  489.8 76.6 %collective-permute-start.52 = (bf16[2,256,1280]{2,1,0:T(8,128)(2,1)}, bf16[2,256,1280]{2,1,0:T(8,128)(2,1)}, u32[]{:S(2)}, u32[]{:S(2)}) collective-permute-start(bf16[2,256,1280]{2,1,0:T(8,128)(2,1)} %get-tuple-element.172), channel_id=1, source_target_pairs={{0,2},{2,0},{1,3},{3,1},{4,6},{6,4},{5,7},{7,5},{8,10},{10,8},{9,1... | collective-permute-start | bytes 3932168 | tf_op jit(solution)/shard_map/ppermute | solution.py:54
  492.9 125.4 %collective-permute-start.60 = (bf16[256,1280]{1,0:T(8,128)(2,1)}, bf16[256,1280]{1,0:T(8,128)(2,1)}, u32[]{:S(2)}, u32[]{:S(2)}) collective-permute-start(bf16[256,1280]{1,0:T(8,128)(2,1)} %fusion.63), channel_id=1, source_target_pairs={{0,1},{1,0},{2,3},{3,2},{4,5},{5,4},{6,7},{7,6},{8,9},{9,8},{10,11... | collective-permute-start | bytes 1966088 | tf_op jit(solution)/shard_map/ppermute | solution.py:54
  525.6 48.7 %collective-permute-start.56 = (bf16[2,256,1280]{2,1,0:T(8,128)(2,1)}, bf16[2,256,1280]{2,1,0:T(8,128)(2,1)}, u32[]{:S(2)}, u32[]{:S(2)}) collective-permute-start(bf16[2,256,1280]{2,1,0:T(8,128)(2,1)} %get-tuple-element.181), channel_id=1, source_target_pairs={{0,1},{1,0},{2,3},{3,2},{4,5},{5,4},{6,7},{7,6},{8,9},{9,8},{10,11... | collective-permute-start | bytes 3932168 | tf_op jit(solution)/shard_map/ppermute | solution.py:54
  529.2 41.2 %collective-permute-start.50 = (bf16[256,1280]{1,0:T(8,128)(2,1)}, bf16[256,1280]{1,0:T(8,128)(2,1)}, u32[]{:S(2)}, u32[]{:S(2)}) collective-permute-start(bf16[256,1280]{1,0:T(8,128)(2,1)} %fusion.60), channel_id=1, source_target_pairs={{0,2},{2,0},{1,3},{3,1},{4,6},{6,4},{5,7},{7,5},{8,10},{10,8},{9,1... | collective-permute-start | bytes 1966088 | tf_op jit(solution)/shard_map/ppermute | solution.py:54
  613.0 114.5 %all-to-all-start.2 = ((bf16[4,240,1792]{2,1,0:T(8,128)(2,1)}), bf16[4,240,1792]{2,1,0:T(8,128)(2,1)}, u32[]{:S(2)}, u32[]{:S(2)}) async-start(bf16[4,240,1792]{2,1,0:T(8,128)(2,1)} %add_convert_fusion.2), calls=%async_computation.2 | async-start | bytes 6881280 | tf_op jit(solution)/shard_map/all_to_all | solution.py:837
  677.7 72.7 %collective-permute-start.61 = (bf16[2,2,256,1280]{3,2,0,1:T(8,128)(2,1)}, bf16[2,2,256,1280]{3,2,0,1:T(8,128)(2,1)}, u32[]{:S(2)}, u32[]{:S(2)}) collective-permute-start(bf16[2,2,256,1280]{3,2,0,1:T(8,128)(2,1)} %copy.191), channel_id=1, source_target_pairs={{0,1},{1,0},{2,3},{3,2},{4,5},{5,4},{6,7},{7,6},{8,9},{9,8},{10,11... | collective-permute-start | bytes 7864328 | tf_op jit(solution)/shard_map/ppermute | solution.py:54
  680.4 73.7 %collective-permute-start.64 = (bf16[2,2,256,1280]{3,2,0,1:T(8,128)(2,1)}, bf16[2,2,256,1280]{3,2,0,1:T(8,128)(2,1)}, u32[]{:S(2)}, u32[]{:S(2)}) collective-permute-start(bf16[2,2,256,1280]{3,2,0,1:T(8,128)(2,1)} %copy.193), channel_id=1, source_target_pairs={{0,2},{2,0},{1,3},{3,1},{4,6},{6,4},{5,7},{7,5},{8,10},{10,8},{9,1... | collective-permute-start | bytes 7864328 | tf_op jit(solution)/shard_map/ppermute | solution.py:54
  685.5 75.3 %collective-permute-start.68 = (bf16[2,256,1280]{2,1,0:T(8,128)(2,1)}, bf16[2,256,1280]{2,1,0:T(8,128)(2,1)}, u32[]{:S(2)}, u32[]{:S(2)}) collective-permute-start(bf16[2,256,1280]{2,1,0:T(8,128)(2,1)} %add_convert_fusion.5), channel_id=1, source_target_pairs={{0,8},{8,16},{16,24},{24,0},{1,9},{9,17},{17,25},{25,1},{2,10},{10... | collective-permute-start | bytes 3932168 | tf_op jit(solution)/shard_map/ppermute | solution.py:54
  699.2 60.8 %collective-permute-start.69 = (bf16[2,256,1280]{2,1,0:T(8,128)(2,1)}, bf16[2,256,1280]{2,1,0:T(8,128)(2,1)}, u32[]{:S(2)}, u32[]{:S(2)}) collective-permute-start(bf16[2,256,1280]{2,1,0:T(8,128)(2,1)} %get-tuple-element.199), channel_id=1, source_target_pairs={{0,4},{4,0},{1,5},{5,1},{2,6},{6,2},{3,7},{7,3},{8,12},{12,8},{9,1... | collective-permute-start | bytes 3932168 | tf_op jit(solution)/shard_map/ppermute | solution.py:54
  713.6 80.2 %collective-permute-start.71 = (bf16[2,256,1280]{2,1,0:T(8,128)(2,1)}, bf16[2,256,1280]{2,1,0:T(8,128)(2,1)}, u32[]{:S(2)}, u32[]{:S(2)}) collective-permute-start(bf16[2,256,1280]{2,1,0:T(8,128)(2,1)} %get-tuple-element.202), channel_id=1, source_target_pairs={{0,4},{4,0},{1,5},{5,1},{2,6},{6,2},{3,7},{7,3},{8,12},{12,8},{9,1... | collective-permute-start | bytes 3932168 | tf_op jit(solution)/shard_map/ppermute | solution.py:54
  750.4 52.5 %collective-permute-start.74 = (bf16[4,2,2,40,5248]{4,3,0,1,2:T(8,128)(2,1)}, bf16[4,2,2,40,5248]{4,3,0,1,2:T(8,128)(2,1)}, u32[]{:S(2)}, u32[]{:S(2)}) collective-permute-start(bf16[4,2,2,40,5248]{4,3,0,1,2:T(8,128)(2,1)} %pad_maximum_fusion), channel_id=1, source_target_pairs={{0,4},{4,0},{1,5},{5,1},{2,6},{6,2},{3,7},{7,3},{8,12},{12,8},{9,1... | collective-permute-start | bytes 20152328 | tf_op jit(solution)/shard_map/ppermute | solution.py:54
  802.9 51.9 %collective-permute-start.72 = (bf16[2,256,1280]{2,1,0:T(8,128)(2,1)}, bf16[2,256,1280]{2,1,0:T(8,128)(2,1)}, u32[]{:S(2)}, u32[]{:S(2)}) collective-permute-start(bf16[2,256,1280]{2,1,0:T(8,128)(2,1)} %add_convert_fusion.3), channel_id=1, source_target_pairs={{0,8},{8,16},{16,24},{24,0},{1,9},{9,17},{17,25},{25,1},{2,10},{10... | collective-permute-start | bytes 3932168 | tf_op jit(solution)/shard_map/ppermute | solution.py:54
  808.0 37.6 %collective-permute-start.75 = (bf16[2,2,40,5248]{3,2,0,1:T(8,128)(2,1)S(1)}, bf16[2,2,40,5248]{3,2,0,1:T(8,128)(2,1)S(1)}, u32[]{:S(2)}, u32[]{:S(2)}) collective-permute-start(bf16[2,2,40,5248]{3,2,0,1:T(8,128)(2,1)S(1)} %dynamic-slice_bitcast_fusion.3), channel_id=1, source_target_pairs={{0,2},{2,0},{1,3},{3,1},{4,6},{6,4},{5,7},{7,5},{8,10},{10,8},{9,1... | collective-permute-start | bytes 5038088 | tf_op jit(solution)/shard_map/ppermute | solution.py:54
  814.4 82.7 %collective-permute-start.66 = (bf16[256,1280]{1,0:T(8,128)(2,1)}, bf16[256,1280]{1,0:T(8,128)(2,1)}, u32[]{:S(2)}, u32[]{:S(2)}) collective-permute-start(bf16[256,1280]{1,0:T(8,128)(2,1)} %fusion.47), channel_id=1, source_target_pairs={{0,8},{8,16},{16,24},{24,0},{1,9},{9,17},{17,25},{25,1},{2,10},{10... | collective-permute-start | bytes 1966088 | tf_op jit(solution)/shard_map/ppermute | solution.py:54
  814.7 37.6 %collective-permute-start.76 = (bf16[2,2,40,5248]{3,2,0,1:T(8,128)(2,1)S(1)}, bf16[2,2,40,5248]{3,2,0,1:T(8,128)(2,1)S(1)}, u32[]{:S(2)}, u32[]{:S(2)}) collective-permute-start(bf16[2,2,40,5248]{3,2,0,1:T(8,128)(2,1)S(1)} %dynamic-slice_bitcast_fusion.2), channel_id=1, source_target_pairs={{0,1},{1,0},{2,3},{3,2},{4,5},{5,4},{6,7},{7,6},{8,9},{9,8},{10,11... | collective-permute-start | bytes 5038088 | tf_op jit(solution)/shard_map/ppermute | solution.py:54
  (219 other events, 2508.8 us)
